TPU v7x, 32 devices: a whole 2x2x4 slice. The times are simulated.
32 devices in a mesh: geo: 4 (over x, core), dist: 8 (over z, y).
Axes of the slice: x: 2, y: 2, z: 4, core: 2. Of those that a mesh axis runs over, the one named last changes fastest.
Arguments:
- estimates: bfloat16 [3072, 7424], P(('geo', 'dist')), may hold values from -4 to 4
- factors: bfloat16 [3072, 7424], P(('geo', 'dist')), may hold values from -0.625 to 0.625
- variances: bfloat16 [3072, 116], P(('geo', 'dist')), may hold values from 0.019897461 to 0.5
- intersection_tracts: int32 [1024, 32], P('dist'), may hold values from 0 to 3071, as said below
- intersection_weights: int32 [1024, 32], P('dist'), may hold values from 1 to 256
Outputs:
- marginal: float32 [1024, 7424], P('dist')
- covariance: float32 [1024, 13456], P('dist')
Inputs may be any that keep to these rules, and one draw needn't show every extreme that they name: `intersection_tracts`: each district's intersections are 32 different tracts among 64 consecutive ones, counted cyclically over the region.
All inputs are finite; a program needn't handle non-finite values.
Results may differ from a plain program's by a relative error of at most 0.0003.
Values may be sent and summed in bfloat16 or wider, within the bound.
No kernel may reach another device: no remote copies, remote signals or barrier semaphores. Data moves between devices by JAX's collectives and lax.ppermute only.
A program may use at most 128 MiB of HBM per device.

v0:
```python
import jax
import jax.numpy as jnp
from jax import lax
from jax.sharding import PartitionSpec as P


def assemble(est_sum, fac_sum, var_sum):
    count = est_sum.shape[0]
    ages = var_sum.shape[1]
    shaped = fac_sum.reshape(count, ages, fac_sum.shape[1] // ages)
    outer = jnp.einsum("dik,djk->dij", shaped, shaped, precision=lax.Precision.HIGHEST)
    outer = outer + var_sum[:, :, None] * jnp.eye(ages, dtype=jnp.float32)[None, :, :]
    return (est_sum, outer.reshape(count, ages * ages))


def shards(estimates, factors, variances, intersection_tracts, intersection_weights):
    geo_index = lax.axis_index("geo")
    block = estimates.shape[0] * lax.axis_size("dist")
    local_ids = intersection_tracts - geo_index * block
    positions = jnp.arange(block, dtype=jnp.int32)
    onehot = (local_ids[:, :, None] == positions[None, None, :]).astype(jnp.float32)
    share = intersection_weights.astype(jnp.float32) / 256.0
    weight_mat = jnp.sum(onehot * share[:, :, None], axis=1).astype(jnp.bfloat16)
    square_mat = jnp.sum(onehot * (share * share)[:, :, None], axis=1)
    est_new = jnp.dot(
        weight_mat,
        lax.all_gather(estimates, "dist", axis=0, tiled=True),
        preferred_element_type=jnp.float32,
    )
    fac_new = jnp.dot(
        weight_mat,
        lax.all_gather(factors, "dist", axis=0, tiled=True),
        preferred_element_type=jnp.float32,
    )
    var_new = jnp.dot(
        square_mat,
        lax.all_gather(variances, "dist", axis=0, tiled=True).astype(jnp.float32),
        precision=lax.Precision.HIGHEST,
    )
    est_sum, fac_sum, var_sum = lax.psum((est_new, fac_new, var_new), "geo")
    return assemble(est_sum, fac_sum, var_sum)


def solution(mesh):
    return jax.shard_map(
        shards,
        mesh=mesh,
        in_specs=(
            P(("geo", "dist"), None),
            P(("geo", "dist"), None),
            P(("geo", "dist"), None),
            P("dist", None),
            P("dist", None),
        ),
        out_specs=(P("dist", None), P("dist", None)),
        check_vma=False,
    )
```

profile of v0, /device:TPU:0, one launch (start us, length us, event | category | flops | bytes accessed | tf_op | source)
XLA Modules:
  0.0 539.0 jit_solution(7276167828935466784)
XLA Ops:
  7.2 0.0 all-gather.5.cloned.1.call-start
  7.2 0.7 all-gather.5.cloned.1.call-update
  7.9 0.0 all-gather.3.cloned.1.call-start
  7.9 0.7 all-gather.3.cloned.1.call-update
  8.6 0.0 all-reduce.3.cloned.1.call-start
  8.7 0.7 convert_multiply_fusion
  9.4 0.1 copy.24
  9.5 0.7 broadcast_subtract_fusion
  10.2 0.1 copy.20
  10.3 0.1 copy.21
  10.4 13.2 %select_reduce_fusion = (f32[128,768]{1,0:T(8,128)S(1)}, bf16[128,768]{1,0:T(8,128)(2,1)S(1)}) fusion(f32[128,32]{1,0:T(8,128)S(1)} %copy.24, s32[128,32]{1,0:T(8,128)S(1)} %copy.20, f32[128,32]{1,0:T(8,128)S(1)} %copy.21), kind=kLoop, calls=%fused_computation | loop fusion | flops 15532032 | bytes 638976 | tf_op jit(solution)/shard_map/reduce_sum | solution.py:24
  23.6 151.3 %all-gather.5.cloned.1.call-done = bf16[768,7424]{1,0:T(8,128)(2,1)} async-done(((bf16[96,7424]{1,0:T(8,128)(2,1)}), bf16[768,7424]{1,0:T(8,128)(2,1)}) %all-gather.5.cloned.1.call-update) | async-done | bytes 11403280 | tf_op jit(solution)/shard_map/all_gather | solution.py:32
  175.0 10.6 %fusion.7 = f32[128,7424]{0,1:T(8,128)} fusion(bf16[128,768]{1,0:T(8,128)(2,1)S(1)} %get-tuple-element.5, bf16[768,7424]{1,0:T(8,128)(2,1)} %all-gather.5.cloned.1.call-done), kind=kOutput, calls=%fused_computation.14 | convolution fusion | flops 1459617792 | bytes 15400960 | tf_op jit(solution)/shard_map/dot_general | solution.py:30
  185.6 5.5 %copy.23 = f32[128,116,64]{1,2,0:T(8,128)} copy(f32[128,116,64]{0,2,1:T(8,128)} %bitcast.9) | data formatting | bytes 7602176 | tf_op jit(solution)/shard_map/reshape | solution.py:10
  191.1 0.0 copy-start
  191.1 146.3 %all-gather.3.cloned.1.call-done = bf16[768,7424]{1,0:T(8,128)(2,1)} async-done(((bf16[96,7424]{1,0:T(8,128)(2,1)}), bf16[768,7424]{1,0:T(8,128)(2,1)}) %all-gather.3.cloned.1.call-update) | async-done | bytes 11403280 | tf_op jit(solution)/shard_map/all_gather | solution.py:27
  337.4 7.8 %fusion.8 = f32[128,7424]{1,0:T(8,128)} fusion(bf16[128,768]{1,0:T(8,128)(2,1)S(1)} %get-tuple-element.5, bf16[768,7424]{1,0:T(8,128)(2,1)} %all-gather.3.cloned.1.call-done), kind=kOutput, calls=%fused_computation.15 | convolution fusion | flops 1459617792 | bytes 15400960 | tf_op jit(solution)/shard_map/dot_general | solution.py:25
  345.2 0.0 all-reduce.3.cloned.1.call-update
  345.2 0.0 copy-done
  345.3 30.6 %all_gather.11 = bf16[768,116]{1,0:T(8,128)(2,1)S(1)} all-gather(bf16[96,116]{1,0:T(8,128)(2,1)S(1)} %copy-done), channel_id=1, replica_groups=mesh['geo'=4,'dist'=8] {'dist'}, dimensions={0}, use_global_device_ids=true | all-gather | bytes 200448 | tf_op jit(solution)/shard_map/all_gather | solution.py:37
  375.9 0.4 fusion.6
  376.2 13.0 %psum.23 = f32[128,116]{0,1:T(8,128)S(1)} all-reduce(f32[128,116]{0,1:T(8,128)S(1)} %fusion.6), channel_id=1, replica_groups=mesh['geo'=4,'dist'=8] {'geo'}, use_global_device_ids=true, to_apply=%region_4.0 | all-reduce | flops 14848 | bytes 118784 | tf_op jit(solution)/shard_map/psum | solution.py:40
  389.3 0.1 copy.25
  389.4 102.1 %all-reduce.3.cloned.1.call-done = (f32[128,7424]{1,0:T(8,128)}, f32[128,116,64]{1,2,0:T(8,128)}) async-done(((f32[128,7424]{1,0:T(8,128)}, f32[128,116,64]{1,2,0:T(8,128)}), (f32[128,7424]{1,0:T(8,128)}, f32[128,116,64]{1,2,0:T(8,128)})) %all-reduce.3.cloned.1.call-update) | async-done | bytes 7602192 | tf_op jit(solution)/shard_map/psum | solution.py:40
  491.5 20.0 %multiply_add_fusion = f32[128,116,116]{2,1,0:T(8,128)} fusion(f32[116,116]{1,0:T(8,128)S(1)} %fusion.4, f32[128,116]{1,0:T(8,128)S(1)} %copy.25, f32[128,116,64]{1,2,0:T(8,128)} %get-tuple-element.7), kind=kOutput, calls=%fused_computation.3 | convolution fusion | flops 1326223360 | bytes 10803776 | tf_op jit(solution)/shard_map/dik,djk->dij/dot_general | solution.py:11
  511.5 8.5 %reshape.24 = f32[128,13456]{1,0:T(8,128)} reshape(f32[128,116,116]{2,1,0:T(8,128)} %multiply_add_fusion) | data formatting | bytes 13778944 | tf_op jit(solution)/shard_map/reshape | solution.py:13
  520.0 8.2 %copy.28 = f32[128,13456]{0,1:T(8,128)} copy(f32[128,13456]{1,0:T(8,128)} %reshape.24) | data formatting | bytes 13778944 | tf_op jit(solution)/shard_map/reshape | solution.py:13
  528.2 4.2 copy.31
  (1 shorter events, 0.0 us)
Async XLA Ops:
  7.2 167.8 %all-gather.5.cloned.1.call-start = ((), (), s32[]{:S(2)}) async-start(), calls=%async_computation.1 | async-start | bytes 12828672 | tf_op jit(solution)/shard_map/all_gather | solution.py:32
  7.9 329.5 %all-gather.3.cloned.1.call-start = ((), (), s32[]{:S(2)}) async-start(), calls=%async_computation | async-start | bytes 12828672 | tf_op jit(solution)/shard_map/all_gather | solution.py:27
  8.6 482.9 %all-reduce.3.cloned.1.call-start = ((), (), s32[]{:S(2)}) async-start(), calls=%async_computation.2 | async-start | bytes 15990784 | tf_op jit(solution)/shard_map/psum | solution.py:40
  191.1 154.2 %copy-start = (bf16[96,116]{1,0:T(8,128)(2,1)S(1)}, bf16[96,116]{1,0:T(8,128)(2,1)}, u32[]{:S(2)}) copy-start(bf16[96,116]{1,0:T(8,128)(2,1)} %param.7) | copy-start | bytes 66820
Sparse Core Ops, SparseCore 0:
  10.2 164.7 all-gather.4
  177.2 160.2 all-gather.2
  345.4 146.1 all-reduce.2
where the time goes:
time: 540 us; the launch traced here: 539 us
  waiting for transfers between devices  401 us (74%)
  blocking collectives  43.6 us (8%)
  matrix products  38.8 us (7%)
  local copies, waits for them, and re-layouts  26.8 us (5%)
  other arithmetic  14.6 us (3%)
  between operations  13.8 us (3%)
    all_gather x1, waiting for transfers between devices, shards(): lax.all_gather(factors, 'dist', axis=0, tiled=True)  151 us
    all_gather x1, waiting for transfers between devices, shards(): lax.all_gather(estimates, 'dist', axis=0, tiled=True)  146 us
    psum x1, waiting for transfers between devices, shards(): est_sum, fac_sum, var_sum = lax.psum((est_new, fac_new, var_new), 'geo')  102 us
    all_gather x1, blocking collectives, shards(): lax.all_gather(variances, 'dist', axis=0, tiled=True).astype(jnp.float32)  30.6 us
    dot_general x1, matrix products, assemble(): jnp.einsum('dik,djk->dij', shaped, shaped, precision=lax.Precision.HIGHEST)  20 us
    reshape x2, local copies, waits for them, and re-layouts, assemble(): return (est_sum, outer.reshape(count, ages * ages))  16.8 us
    reduce_sum x1, other arithmetic, shards(): square_mat = jnp.sum(onehot * (share * share)[:, :, None], axis=1)  13.2 us
    psum x1, blocking collectives, shards(): est_sum, fac_sum, var_sum = lax.psum((est_new, fac_new, var_new), 'geo')  13 us
  transfers between devices with their start and end apart: 3, of which 3 were waited for; matrix products, arithmetic and copies ran while one was open for 6% of the time, Pallas kernels for 0%

commit v1 on v0

v1 whole, which is shorter than its diff:
```python
import functools
import jax
import jax.numpy as jnp
from jax import lax
from jax.experimental import pallas as pl
from jax.experimental.pallas import tpu as pltpu
from jax.sharding import PartitionSpec as P

LANES = 128
CORES = 2
DEPTH = 4
TOP = 32767.0
VMEM_BYTES = 48 * 1024 * 1024


def tile(i, count=1):
    return pl.ds(i * LANES, count * LANES)


def encode(read, write, count):
    top = jnp.abs(read(0))
    for i in range(1, count):
        top = jnp.maximum(top, jnp.abs(read(i)))
    power = jnp.floor(jnp.log2(jnp.maximum(top, 1e-30))) + 1.0
    gain = jnp.exp2(-power) * TOP
    for i in range(count):
        level = jnp.clip(jnp.round(read(i) * gain), -TOP, TOP)
        write(i, level.astype(jnp.int32).astype(jnp.int16))
    write(count, power.astype(jnp.int32).astype(jnp.int16))


def step_of(power):
    return jnp.exp2(power.astype(jnp.int32).astype(jnp.float32)) * (1.0 / TOP)


def decode(level, step):
    return level.astype(jnp.int32).astype(jnp.float32) * step


def weights_kernel(tract_ref, ids_ref, weight_ref, out_ref):
    tracts = tract_ref[0:1, :]
    rows = ids_ref.shape[0]
    for r in range(0, rows, 8):
        ids = ids_ref[r:r + 8, :]
        share = weight_ref[r:r + 8, :].astype(jnp.float32) * (1.0 / 256.0)
        total = jnp.zeros((8, tracts.shape[1]), jnp.float32)
        for k in range(ids.shape[1]):
            total = total + jnp.where(ids[:, k:k + 1] == tracts, share[:, k:k + 1], 0.0)
        out_ref[r:r + 8, :] = total.astype(jnp.bfloat16)


def build_weights(tracts, ids, weights):
    rows, each = ids.shape
    width = tracts.shape[1]
    step = 128
    return pl.pallas_call(
        weights_kernel,
        grid=(rows // step,),
        in_specs=[
            pl.BlockSpec((8, width), lambda i: (0, 0)),
            pl.BlockSpec((step, each), lambda i: (i, 0)),
            pl.BlockSpec((step, each), lambda i: (i, 0)),
        ],
        out_specs=pl.BlockSpec((step, width), lambda i: (i, 0)),
        out_shape=jax.ShapeDtypeStruct((rows, width), jnp.bfloat16),
        compiler_params=pltpu.CompilerParams(vmem_limit_bytes=VMEM_BYTES),
        cost_estimate=pl.CostEstimate(flops=rows * width * each * 3, bytes_accessed=rows * width * 2, transcendentals=0),
        name="build_weights",
    )(tracts, ids, weights)


def sums_kernel(parts, has_var, flag_ref, w_ref, *refs):
    data = refs[:parts]
    own_ref = refs[parts]
    outs = refs[parts + 1:parts + DEPTH]
    acc_ref = refs[parts + DEPTH]
    depth = data[0].shape[0]
    count = acc_ref.shape[1] // LANES
    k = pl.program_id(0)

    def weighted(get, columns):
        total = None
        for j in range(parts):
            part = jnp.dot(get(j), data[j][:, columns], preferred_element_type=jnp.float32)
            total = part if total is None else total + part
        return total

    def weights(j):
        return w_ref[:, j * depth:(j + 1) * depth]

    acc_ref[...] = weighted(weights, slice(None))
    if has_var:
        @pl.when(flag_ref[0] == 1)
        def _():
            def square(j):
                w = weights(j).astype(jnp.float32)
                return w * w

            def high(j):
                return square(j).astype(jnp.bfloat16)

            def low(j):
                s = square(j)
                return (s - s.astype(jnp.bfloat16).astype(jnp.float32)).astype(jnp.bfloat16)

            last = tile(count - 1)
            acc_ref[:, last] = weighted(high, last) + weighted(low, last)

    @pl.when(k == 0)
    def _():
        own_ref[...] = acc_ref[...]

    for i in range(1, DEPTH):
        out = outs[i - 1]

        @pl.when(k == i)
        def _(out=out):
            def write(t, value):
                out[:, tile(t)] = value
            encode(lambda t: acc_ref[:, tile(t)], write, count)


def partial_sums(flag, w, data, has_var):
    rows = w.shape[0] // DEPTH
    depth, columns = data[0].shape
    count = columns // LANES
    parts = len(data)
    coded = jax.ShapeDtypeStruct((rows, (count + 1) * LANES), jnp.int16)
    whole = lambda i, s: (0, 0)
    return pl.pallas_call(
        functools.partial(sums_kernel, parts, has_var),
        grid_spec=pltpu.PrefetchScalarGridSpec(
            num_scalar_prefetch=1,
            grid=(DEPTH,),
            in_specs=[pl.BlockSpec((rows, w.shape[1]), lambda i, s: (i, 0))]
            + [pl.BlockSpec((depth, columns), whole)] * parts,
            out_specs=[pl.BlockSpec((rows, columns), whole)]
            + [pl.BlockSpec(coded.shape, whole)] * (DEPTH - 1),
            scratch_shapes=[pltpu.VMEM((rows, columns), jnp.float32)],
        ),
        out_shape=[jax.ShapeDtypeStruct((rows, columns), jnp.float32)] + [coded] * (DEPTH - 1),
        compiler_params=pltpu.CompilerParams(vmem_limit_bytes=VMEM_BYTES),
        cost_estimate=pl.CostEstimate(
            flops=2 * rows * DEPTH * w.shape[1] * columns,
            bytes_accessed=2 * depth * parts * columns + rows * columns * 10,
            transcendentals=0,
        ),
        name="partial_sums",
    )(flag, w, *data)


def combine_kernel(own_ref, *refs):
    others, out_ref, acc_ref = refs[:-2], refs[-2], refs[-1]
    count = acc_ref.shape[1] // LANES
    steps = [step_of(o[:, tile(count)]) for o in others]
    for t in range(count):
        total = own_ref[:, tile(t)]
        for o, step in zip(others, steps):
            total = total + decode(o[:, tile(t)], step)
        acc_ref[:, tile(t)] = total

    def write(t, value):
        out_ref[:, tile(t)] = value
    encode(lambda t: acc_ref[:, tile(t)], write, count)


def combine(own, others):
    rows, columns = own.shape
    wide = columns + LANES
    step = 32
    return pl.pallas_call(
        combine_kernel,
        grid=(rows // step,),
        in_specs=[pl.BlockSpec((step, columns), lambda i: (i, 0))]
        + [pl.BlockSpec((step, wide), lambda i: (i, 0))] * len(others),
        out_specs=pl.BlockSpec((step, wide), lambda i: (i, 0)),
        out_shape=jax.ShapeDtypeStruct((rows, wide), jnp.int16),
        scratch_shapes=[pltpu.VMEM((step, columns), jnp.float32)],
        compiler_params=pltpu.CompilerParams(vmem_limit_bytes=VMEM_BYTES),
        cost_estimate=pl.CostEstimate(flops=rows * columns * 16, bytes_accessed=rows * columns * 12, transcendentals=0),
        name="combine",
    )(own, *others)


def place(order_ref, pieces, dest_ref, each, total, groups):
    count = pieces[0].shape[1] // LANES - 1

    def store(r, start):
        step = step_of(pieces[r][:, tile(count)])
        for t in range(count):
            where = pl.ds(pl.multiple_of((start + t) * LANES, LANES), LANES)
            dest_ref[:, where] = decode(pieces[r][:, tile(t)], step)

    for last in (True, False):
        for r in range(groups):
            group = order_ref[r]

            @pl.when((group == groups - 1) == last)
            def _(r=r, group=group):
                store(r, jnp.minimum(group * each, total - each))


def marginal_kernel(each, total, order_ref, *refs):
    place(order_ref, refs[:-1], refs[-1], each, total, len(refs) - 1)


def marginal(order, pieces, each, total):
    rows, wide = pieces[0].shape
    step = 32
    return pl.pallas_call(
        functools.partial(marginal_kernel, each, total),
        grid_spec=pltpu.PrefetchScalarGridSpec(
            num_scalar_prefetch=1,
            grid=(rows // step,),
            in_specs=[pl.BlockSpec((step, wide), lambda i, s: (i, 0))] * len(pieces),
            out_specs=pl.BlockSpec((step, total * LANES), lambda i, s: (i, 0)),
        ),
        out_shape=jax.ShapeDtypeStruct((rows, total * LANES), jnp.float32),
        compiler_params=pltpu.CompilerParams(vmem_limit_bytes=VMEM_BYTES),
        cost_estimate=pl.CostEstimate(
            flops=rows * total * LANES * 2, bytes_accessed=rows * total * LANES * 6, transcendentals=0
        ),
        name="marginal",
    )(order, *pieces)


def covariance_kernel(each, total, ages, rank, order_ref, *refs):
    pieces, out_ref = refs[:-4], refs[-4]
    load_ref, age_ref, cov_ref = refs[-3:]
    pitch = age_ref.shape[0] // 8
    place(order_ref, pieces, load_ref, each, total, len(pieces))
    per_tile = LANES // rank
    wide = cov_ref.shape[1]
    row_id = lax.broadcasted_iota(jnp.int32, (ages, ages), 0)
    col_id = lax.broadcasted_iota(jnp.int32, (ages, ages), 1)
    diagonal = row_id == col_id
    contract = (((1,), (1,)), ((), ()))
    for base in range(0, load_ref.shape[0], 8):
        rows = slice(base, base + 8)
        for t in range(ages // per_tile):
            value = load_ref[rows, tile(t)]
            for p in range(per_tile):
                age_ref[pl.ds(per_tile * t + p, 8, stride=pitch), :] = (
                    value if p == 0 else pltpu.roll(value, LANES - p * rank, 1)
                )
        for d in range(8):
            mine = age_ref[d * pitch:d * pitch + ages, :rank]
            high = mine.astype(jnp.bfloat16)
            low = (mine - high.astype(jnp.float32)).astype(jnp.bfloat16)
            outer = (
                lax.dot_general(high, high, contract, preferred_element_type=jnp.float32)
                + lax.dot_general(high, low, contract, preferred_element_type=jnp.float32)
                + lax.dot_general(low, high, contract, preferred_element_type=jnp.float32)
            )
            noise = load_ref[base + d:base + d + 1, (total - 1) * LANES:(total - 1) * LANES + ages]
            outer = outer + jnp.where(diagonal, noise, 0.0)
            cov_ref[d * pitch:d * pitch + ages, :ages] = outer
        for i in range(ages):
            out_ref[rows, i * ages:(i + 1) * ages] = cov_ref[pl.ds(i, 8, stride=pitch), :][:, :ages]


def covariance(order, pieces, each, total, ages, rank):
    rows, wide = pieces[0].shape
    step = 16
    pitch = -(-ages // 8) * 8
    return pl.pallas_call(
        functools.partial(covariance_kernel, each, total, ages, rank),
        grid_spec=pltpu.PrefetchScalarGridSpec(
            num_scalar_prefetch=1,
            grid=(rows // step,),
            in_specs=[pl.BlockSpec((step, wide), lambda i, s: (i, 0))] * len(pieces),
            out_specs=pl.BlockSpec((step, ages * ages), lambda i, s: (i, 0)),
            scratch_shapes=[
                pltpu.VMEM((step, total * LANES), jnp.float32),
                pltpu.VMEM((8 * pitch, LANES), jnp.float32),
                pltpu.VMEM((8 * pitch, LANES), jnp.float32),
            ],
        ),
        out_shape=jax.ShapeDtypeStruct((rows, ages * ages), jnp.float32),
        compiler_params=pltpu.CompilerParams(vmem_limit_bytes=VMEM_BYTES),
        cost_estimate=pl.CostEstimate(
            flops=rows * ages * ages * rank * 32, bytes_accessed=rows * ages * ages * 4, transcendentals=0
        ),
        name="covariance",
    )(order, *pieces)


def shards(groups, parts, estimates, factors, variances, intersection_tracts, intersection_weights):
    xs = groups // CORES
    ys = parts // DEPTH
    rows = estimates.shape[0]
    ages = variances.shape[1]
    rank = factors.shape[1] // ages
    geo = lax.axis_index("geo")
    dist = lax.axis_index("dist")
    x, core = geo // CORES, geo % CORES
    z, y = dist // ys, dist % ys
    shifts = [(dx, dc) for dx in range(xs) for dc in range(CORES)]

    def geo_shift(value, dx, dc):
        if dx == 0 and dc == 0:
            return value
        perm = [(a * CORES + b, (a + dx) % xs * CORES + (b + dc) % CORES) for a in range(xs) for b in range(CORES)]
        return lax.ppermute(value, "geo", perm)

    def y_shift(value, dy):
        if dy == 0:
            return value
        perm = [(a * ys + b, a * ys + (b + dy) % ys) for a in range(DEPTH) for b in range(ys)]
        return lax.ppermute(value, "dist", perm)

    def z_shift(value, dz):
        if dz % DEPTH == 0:
            return value
        perm = [(a * ys + b, (a + dz) % DEPTH * ys + b) for a in range(DEPTH) for b in range(ys)]
        return lax.ppermute(value, "dist", perm)

    queries = jnp.concatenate([intersection_tracts, intersection_weights], axis=1)
    queries = jnp.concatenate([z_shift(queries, -k) for k in range(DEPTH)], axis=0)
    each = intersection_tracts.shape[1]

    bases = [
        (((x - dx) % xs * CORES + (core - dc) % CORES) * parts + z * ys + (y - dy) % ys) * rows
        for dy in range(ys) for dx, dc in shifts
    ]
    tracts = jnp.concatenate([base + jnp.arange(rows, dtype=jnp.int32) for base in bases])
    tracts = jnp.broadcast_to(tracts[None, :], (8, tracts.shape[0]))
    w = build_weights(tracts, queries[:, :each], queries[:, each:])

    variances = jnp.pad(variances, ((0, 0), (0, -ages % LANES)))
    loads = jnp.concatenate([factors, variances], axis=1)
    order = jnp.stack([(x - dx) % xs * CORES + (core - dc) % CORES for dx, dc in shifts]).astype(jnp.int32)
    flag = (geo == groups - 1).astype(jnp.int32).reshape(1)

    def collect(array, has_var):
        total = array.shape[1] // LANES
        count = -(-total // groups)
        pieces = []
        for dx, dc in shifts:
            target = (x + dx) % xs * CORES + (core + dc) % CORES
            start = jnp.minimum(target * count, total - count) * LANES
            piece = lax.dynamic_slice(array, (0, start), (rows, count * LANES))
            pieces.append(geo_shift(piece, dx, dc))
        data = [
            jnp.concatenate([y_shift(piece, dy) for piece in pieces], axis=0) for dy in range(ys)
        ]
        own, *outs = partial_sums(flag, w, data, has_var)
        others = [z_shift(out, k + 1) for k, out in enumerate(outs)]
        mine = combine(own, others)
        rowwise = [geo_shift(mine, dx, 0) for dx in range(xs)]
        gathered = [geo_shift(rowwise[dx], 0, dc) for dx, dc in shifts]
        return gathered, count, total

    load_pieces, load_count, load_total = collect(loads, True)
    mean_pieces, mean_count, mean_total = collect(estimates, False)
    cov = covariance(order, load_pieces, load_count, load_total, ages, rank)
    mean = marginal(order, mean_pieces, mean_count, mean_total)
    return mean, cov


def solution(mesh):
    return jax.shard_map(
        functools.partial(shards, mesh.shape["geo"], mesh.shape["dist"]),
        mesh=mesh,
        in_specs=(
            P(("geo", "dist"), None),
            P(("geo", "dist"), None),
            P(("geo", "dist"), None),
            P("dist", None),
            P("dist", None),
        ),
        out_specs=(P("dist", None), P("dist", None)),
        check_vma=False,
    )
```

time: 540 us -> 198 us (0.37)
  the two profiles are of different devices: /device:TPU:0 before, /device:TPU:11 now
where the time goes in v1:
time: 198 us
  waiting for transfers between devices  116 us (59%)
  Pallas kernels  38.9 us (20%)
  starting transfers between devices  23.2 us (12%)
  local copies, waits for them, and re-layouts  11.2 us (6%)
  other arithmetic  8.05 us (4%)
    ppermute x9, waiting for transfers between devices, z_shift(): return lax.ppermute(value, 'dist', perm)  59.1 us
    ppermute x8, waiting for transfers between devices, y_shift(): return lax.ppermute(value, 'dist', perm)  29.4 us
    ppermute x12, waiting for transfers between devices, geo_shift(): return lax.ppermute(value, 'geo', perm)  27.2 us
    pallas_call x1, Pallas kernels, covariance(): pl.pallas_call(functools.partial(covariance_kernel, each, total, ages, ra...  15.1 us
    pallas_call x2, Pallas kernels, partial_sums(): pl.pallas_call(functools.partial(sums_kernel, parts, has_var), grid_spec=...  11.7 us
    unnamed x5, local copies, waits for them, and re-layouts  9.84 us
    ppermute x9, starting transfers between devices, z_shift(): return lax.ppermute(value, 'dist', perm)  8.27 us
    ppermute x12, starting transfers between devices, geo_shift(): return lax.ppermute(value, 'geo', perm)  7.94 us
  transfers between devices with their start and end apart: 29, of which 14 were waited for; matrix products, arithmetic and copies ran while one was open for 9% of the time, Pallas kernels for 18%

profile of v1, /device:TPU:11, one launch (start us, length us, event | category | flops | bytes accessed | tf_op | source)
XLA Modules:
  0.0 197.9 jit_solution(16159403107673750657)
XLA Ops:
  0.6 0.8 copy.7
  1.4 0.8 copy.8
  2.3 0.7 pad_add_fusion.1
  3.1 2.3 %collective-permute-start.1 = (s32[128,64]{1,0:T(8,128)}, s32[128,64]{1,0:T(8,128)S(1)}, u32[]{:S(2)}, u32[]{:S(2)}) collective-permute-start(s32[128,64]{1,0:T(8,128)} %pad_add_fusion.1), channel_id=1, source_target_pairs={{0,4},{1,5},{2,6},{3,7},{4,0},{5,1},{6,2},{7,3},{8,12},{9,13},{10,... | collective-permute-start | bytes 98312 | tf_op jit(solution)/shard_map/ppermute | solution.py:316
  5.5 2.2 %collective-permute-start.2 = (s32[128,64]{1,0:T(8,128)}, s32[128,64]{1,0:T(8,128)}, u32[]{:S(2)}, u32[]{:S(2)}) collective-permute-start(s32[128,64]{1,0:T(8,128)} %pad_add_fusion.1), channel_id=1, source_target_pairs={{0,2},{1,3},{2,4},{3,5},{4,6},{5,7},{6,0},{7,1},{8,10},{9,11},{10,... | collective-permute-start | bytes 98312 | tf_op jit(solution)/shard_map/ppermute | solution.py:316
  7.7 1.6 fusion.1
  9.4 1.6 collective-permute-start.16
  11.3 1.0 constant_dynamic-slice_fusion.7
  12.3 1.4 collective-permute-start.18
  13.7 1.2 collective-permute-start.19
  15.0 0.4 collective-permute-start.3
  15.5 0.9 pad_add_fusion
  16.8 4.5 %collective-permute-done.17 = bf16[96,1920]{1,0:T(8,128)(2,1)} collective-permute-done((bf16[96,1920]{1,0:T(8,128)(2,1)S(1)}, bf16[96,1920]{1,0:T(8,128)(2,1)}, u32[]{:S(2)}, u32[]{:S(2)}) %collective-permute-start.17) | collective-permute-done | bytes 368672 | tf_op jit(solution)/shard_map/ppermute | solution.py:304
  21.3 1.4 collective-permute-start.5
  22.7 7.0 %collective-permute-done.18 = bf16[96,1920]{1,0:T(8,128)(2,1)S(1)} collective-permute-done((bf16[96,1920]{1,0:T(8,128)(2,1)S(1)}, bf16[96,1920]{1,0:T(8,128)(2,1)S(1)}, u32[]{:S(2)}, u32[]{:S(2)}) %collective-permute-start.18) | collective-permute-done | bytes 368672 | tf_op jit(solution)/shard_map/ppermute | solution.py:304
  29.7 1.2 collective-permute-start.20
  31.1 1.2 collective-permute-start.22
  32.5 7.6 %build_weights.1.w_ref = bf16[512,768]{1,0:T(8,128)(2,1)S(1)} custom-call(s32[8,768]{1,0:T(8,128)S(1)} %broadcast_in_dim.2.tract_ref, s32[512,32]{1,0:T(8,128)S(1)} %get-tuple-element.29.ids_ref, s32[512,32]{1,0:T(8,128)S(1)} %get-tuple-element.28.weight_ref), custom_call_target="tpu_custom_call" | custom-call | flops 37748736 | bytes 786432 | tf_op jit(solution)/shard_map/build_weights/pallas_call | solution.py:56
  40.1 1.2 pad_maximum_fusion.2.refs_0_
  41.6 3.7 %collective-permute-done.5 = bf16[96,1920]{1,0:T(8,128)(2,1)S(1)} collective-permute-done((bf16[96,1920]{1,0:T(8,128)(2,1)}, bf16[96,1920]{1,0:T(8,128)(2,1)S(1)}, u32[]{:S(2)}, u32[]{:S(2)}) %collective-permute-start.5) | collective-permute-done | bytes 368672 | tf_op jit(solution)/shard_map/ppermute | solution.py:304
  45.3 1.2 collective-permute-start.7
  46.8 1.4 collective-permute-done.21
  48.1 1.2 collective-permute-start.9
  49.4 6.7 %collective-permute-done.22 = bf16[96,1920]{1,0:T(8,128)(2,1)S(1)} collective-permute-done((bf16[96,1920]{1,0:T(8,128)(2,1)S(1)}, bf16[96,1920]{1,0:T(8,128)(2,1)S(1)}, u32[]{:S(2)}, u32[]{:S(2)}) %collective-permute-start.22) | collective-permute-done | bytes 368672 | tf_op jit(solution)/shard_map/ppermute | solution.py:310
  56.0 1.2 pad_maximum_fusion.3.refs_1_
  57.3 6.4 %partial_sums.3 = (f32[128,1920]{1,0:T(8,128)S(1)}, s16[128,2048]{1,0:T(8,128)(2,1)S(1)}, s16[128,2048]{1,0:T(8,128)(2,1)S(1)}, s16[128,2048]{1,0:T(8,128)(2,1)S(1)}) custom-call(s32[1]{0:T(128)} %bitcast.4.flag_ref, bf16[512,768]{1,0:T(8,128)(2,1)S(1)} %build_weights.1.w_ref, bf16[384,1920]{1,0:T(8,128)(2,1)S(1)} %pad_maximum_fusion.2.refs_0_, ...), custom_call_target="tpu_custom_call" | custom-call | flops 1509949440 | bytes 5406720 | tf_op jit(solution)/shard_map/partial_sums/pallas_call | solution.py:130
  63.7 1.1 pad_maximum_fusion.refs_0_
  64.8 1.4 collective-permute-start.24
  66.2 5.6 %collective-permute-done.7 = bf16[96,1920]{1,0:T(8,128)(2,1)S(1)} collective-permute-done((bf16[96,1920]{1,0:T(8,128)(2,1)}, bf16[96,1920]{1,0:T(8,128)(2,1)S(1)}, u32[]{:S(2)}, u32[]{:S(2)}) %collective-permute-start.7) | collective-permute-done | bytes 368672 | tf_op jit(solution)/shard_map/ppermute | solution.py:310
  71.8 7.9 %collective-permute-done.8 = bf16[96,1920]{1,0:T(8,128)(2,1)S(1)} collective-permute-done((bf16[96,1920]{1,0:T(8,128)(2,1)S(1)}, bf16[96,1920]{1,0:T(8,128)(2,1)S(1)}, u32[]{:S(2)}, u32[]{:S(2)}) %collective-permute-start.8) | collective-permute-done | bytes 368672 | tf_op jit(solution)/shard_map/ppermute | solution.py:310
  79.7 7.9 %collective-permute-done.9 = bf16[96,1920]{1,0:T(8,128)(2,1)S(1)} collective-permute-done((bf16[96,1920]{1,0:T(8,128)(2,1)S(1)}, bf16[96,1920]{1,0:T(8,128)(2,1)S(1)}, u32[]{:S(2)}, u32[]{:S(2)}) %collective-permute-start.9) | collective-permute-done | bytes 368672 | tf_op jit(solution)/shard_map/ppermute | solution.py:310
  87.6 1.2 pad_maximum_fusion.1.refs_1_
  88.8 5.3 %partial_sums.2 = (f32[128,1920]{1,0:T(8,128)S(1)}, s16[128,2048]{1,0:T(8,128)(2,1)S(1)}, s16[128,2048]{1,0:T(8,128)(2,1)S(1)}, s16[128,2048]{1,0:T(8,128)(2,1)S(1)}) custom-call(s32[1]{0:T(128)} %bitcast.4.flag_ref, bf16[512,768]{1,0:T(8,128)(2,1)S(1)} %build_weights.1.w_ref, bf16[384,1920]{1,0:T(8,128)(2,1)S(1)} %pad_maximum_fusion.refs_0_, ...), custom_call_target="tpu_custom_call" | custom-call | flops 1509949440 | bytes 5406720 | tf_op jit(solution)/shard_map/partial_sums/pallas_call | solution.py:130
  94.2 1.3 collective-permute-start.11
  95.5 0.7 collective-permute-start.12
  96.3 12.9 %collective-permute-done.24.refs_1_ = s16[128,2048]{1,0:T(8,128)(2,1)S(1)} collective-permute-done((s16[128,2048]{1,0:T(8,128)(2,1)S(1)}, s16[128,2048]{1,0:T(8,128)(2,1)S(1)}, u32[]{:S(2)}, u32[]{:S(2)}) %collective-permute-start.24) | collective-permute-done | bytes 524320 | tf_op jit(solution)/shard_map/ppermute | solution.py:316
  109.2 24.6 %collective-permute-done.25.refs_2_ = s16[128,2048]{1,0:T(8,128)(2,1)S(1)} collective-permute-done((s16[128,2048]{1,0:T(8,128)(2,1)S(1)}, s16[128,2048]{1,0:T(8,128)(2,1)S(1)}, u32[]{:S(2)}, u32[]{:S(2)}) %collective-permute-start.25) | collective-permute-done | bytes 524320 | tf_op jit(solution)/shard_map/ppermute | solution.py:316
  133.7 0.7 combine.3.refs_0_
  134.5 8.3 %collective-permute-done.10.refs_0_ = s16[128,2048]{1,0:T(8,128)(2,1)S(1)} collective-permute-done((s16[128,2048]{1,0:T(8,128)(2,1)S(1)}, s16[128,2048]{1,0:T(8,128)(2,1)S(1)}, u32[]{:S(2)}, u32[]{:S(2)}) %collective-permute-start.10) | collective-permute-done | bytes 524320 | tf_op jit(solution)/shard_map/ppermute | solution.py:316
  142.9 11.2 %collective-permute-done.11.refs_1_ = s16[128,2048]{1,0:T(8,128)(2,1)S(1)} collective-permute-done((s16[128,2048]{1,0:T(8,128)(2,1)S(1)}, s16[128,2048]{1,0:T(8,128)(2,1)S(1)}, u32[]{:S(2)}, u32[]{:S(2)}) %collective-permute-start.11) | collective-permute-done | bytes 524320 | tf_op jit(solution)/shard_map/ppermute | solution.py:316
  154.1 2.1 %collective-permute-done.12.refs_2_ = s16[128,2048]{1,0:T(8,128)(2,1)S(1)} collective-permute-done((s16[128,2048]{1,0:T(8,128)(2,1)S(1)}, s16[128,2048]{1,0:T(8,128)(2,1)S(1)}, u32[]{:S(2)}, u32[]{:S(2)}) %collective-permute-start.12) | collective-permute-done | bytes 524320 | tf_op jit(solution)/shard_map/ppermute | solution.py:316
  156.2 0.7 combine.2.refs_0_
  157.0 0.5 collective-permute-start.26
  158.0 12.0 %collective-permute-done.14.refs_2_ = s16[128,2048]{1,0:T(8,128)(2,1)S(1)} collective-permute-done((s16[128,2048]{1,0:T(8,128)(2,1)S(1)}, s16[128,2048]{1,0:T(8,128)(2,1)S(1)}, u32[]{:S(2)}, u32[]{:S(2)}) %collective-permute-start.14) | collective-permute-done | bytes 524320 | tf_op jit(solution)/shard_map/ppermute | solution.py:304
  170.1 1.3 collective-permute-start.15
  171.4 15.1 %covariance.1 = f32[128,13456]{1,0:T(8,128)} custom-call(s32[4]{0:T(128)S(1)} %pad_add_fusion.2.order_ref, s16[128,2048]{1,0:T(8,128)(2,1)S(1)} %combine.3.refs_0_, s16[128,2048]{1,0:T(8,128)(2,1)S(1)} %collective-permute-done.26.refs_1_, s16[128,2048]{1,0:T(8,128)(2,1)S(1)} %collective-permute-done.27.refs_2_, ...), custom_call_target="tpu_custom_call" | custom-call | flops 3527409664 | bytes 6889472 | tf_op jit(solution)/shard_map/covariance/pallas_call | solution.py:266
  186.5 8.2 %copy.9 = f32[128,13456]{0,1:T(8,128)} copy(f32[128,13456]{1,0:T(8,128)} %covariance.1) | data formatting | bytes 13778944
  194.7 3.1 %marginal.1 = f32[128,7424]{1,0:T(8,128)} custom-call(s32[4]{0:T(128)S(1)} %pad_add_fusion.2.order_ref, s16[128,2048]{1,0:T(8,128)(2,1)S(1)} %combine.2.refs_0_, s16[128,2048]{1,0:T(8,128)(2,1)S(1)} %collective-permute-done.13.refs_1_, s16[128,2048]{1,0:T(8,128)(2,1)S(1)} %collective-permute-done.14.refs_2_, s16[128,2048]{1,0:T(8,128)(2,1)S(1)} %collective-permute-done.15.refs_3_), custom_call_target="tpu_custom_call" | custom-call | flops 1900544 | bytes 5701632 | tf_op jit(solution)/shard_map/marginal/pallas_call | solution.py:210
  (39 shorter events, 2.8 us)
Async XLA Ops:
  3.0 9.3 %collective-permute-start = (s32[128,64]{1,0:T(8,128)}, s32[128,64]{1,0:T(8,128)S(1)}, u32[]{:S(2)}, u32[]{:S(2)}) collective-permute-start(s32[128,64]{1,0:T(8,128)} %pad_add_fusion.1), channel_id=1, source_target_pairs={{0,6},{1,7},{2,0},{3,1},{4,2},{5,3},{6,4},{7,5},{8,14},{9,15},{10,... | collective-permute-start | bytes 98312 | tf_op jit(solution)/shard_map/ppermute | solution.py:316
  3.1 10.6 %collective-permute-start.1 = (s32[128,64]{1,0:T(8,128)}, s32[128,64]{1,0:T(8,128)S(1)}, u32[]{:S(2)}, u32[]{:S(2)}) collective-permute-start(s32[128,64]{1,0:T(8,128)} %pad_add_fusion.1), channel_id=1, source_target_pairs={{0,4},{1,5},{2,6},{3,7},{4,0},{5,1},{6,2},{7,3},{8,12},{9,13},{10,... | collective-permute-start | bytes 98312 | tf_op jit(solution)/shard_map/ppermute | solution.py:316
  5.5 9.5 %collective-permute-start.2 = (s32[128,64]{1,0:T(8,128)}, s32[128,64]{1,0:T(8,128)}, u32[]{:S(2)}, u32[]{:S(2)}) collective-permute-start(s32[128,64]{1,0:T(8,128)} %pad_add_fusion.1), channel_id=1, source_target_pairs={{0,2},{1,3},{2,4},{3,5},{4,6},{5,7},{6,0},{7,1},{8,10},{9,11},{10,... | collective-permute-start | bytes 98312 | tf_op jit(solution)/shard_map/ppermute | solution.py:316
  7.6 3.6 %copy-start = (bf16[96,7424]{1,0:T(8,128)(2,1)S(1)}, bf16[96,7424]{1,0:T(8,128)(2,1)}, u32[]{:S(2)}) copy-start(bf16[96,7424]{1,0:T(8,128)(2,1)} %param.5) | copy-start | bytes 4276228
  9.4 7.0 %collective-permute-start.16 = (bf16[96,1920]{1,0:T(8,128)(2,1)S(1)}, bf16[96,1920]{1,0:T(8,128)(2,1)}, u32[]{:S(2)}, u32[]{:S(2)}) collective-permute-start(bf16[96,1920]{1,0:T(8,128)(2,1)S(1)} %get-tuple-element.23), channel_id=1, source_target_pairs={{0,8},{8,0},{16,24},{24,16},{1,9},{9,1},{17,25},{25,17},{2,10},{10... | collective-permute-start | bytes 1105928 | tf_op jit(solution)/shard_map/ppermute | solution.py:304
  11.0 10.3 %collective-permute-start.17 = (bf16[96,1920]{1,0:T(8,128)(2,1)S(1)}, bf16[96,1920]{1,0:T(8,128)(2,1)}, u32[]{:S(2)}, u32[]{:S(2)}) collective-permute-start(bf16[96,1920]{1,0:T(8,128)(2,1)S(1)} %get-tuple-element.22), channel_id=1, source_target_pairs={{0,16},{8,24},{16,0},{24,8},{1,17},{9,25},{17,1},{25,9},{2,18},{10... | collective-permute-start | bytes 1105928 | tf_op jit(solution)/shard_map/ppermute | solution.py:304
  12.3 17.4 %collective-permute-start.18 = (bf16[96,1920]{1,0:T(8,128)(2,1)S(1)}, bf16[96,1920]{1,0:T(8,128)(2,1)S(1)}, u32[]{:S(2)}, u32[]{:S(2)}) collective-permute-start(bf16[96,1920]{1,0:T(8,128)(2,1)S(1)} %get-tuple-element.21), channel_id=1, source_target_pairs={{0,24},{8,16},{16,8},{24,0},{1,25},{9,17},{17,9},{25,1},{2,26},{10... | collective-permute-start | bytes 1105928 | tf_op jit(solution)/shard_map/ppermute | solution.py:304
  13.7 17.2 %collective-permute-start.19 = (bf16[96,1920]{1,0:T(8,128)(2,1)S(1)}, bf16[96,1920]{1,0:T(8,128)(2,1)S(1)}, u32[]{:S(2)}, u32[]{:S(2)}) collective-permute-start(bf16[96,1920]{1,0:T(8,128)(2,1)S(1)} %get-tuple-element.20), channel_id=1, source_target_pairs={{0,1},{1,0},{2,3},{3,2},{4,5},{5,4},{6,7},{7,6},{8,9},{9,8},{10,11... | collective-permute-start | bytes 1105928 | tf_op jit(solution)/shard_map/ppermute | solution.py:310
  15.0 16.2 %collective-permute-start.3 = (bf16[96,1920]{1,0:T(8,128)(2,1)}, bf16[96,1920]{1,0:T(8,128)(2,1)}, u32[]{:S(2)}, u32[]{:S(2)}) collective-permute-start(bf16[96,1920]{1,0:T(8,128)(2,1)} %get-tuple-element.25), channel_id=1, source_target_pairs={{0,8},{8,0},{16,24},{24,16},{1,9},{9,1},{17,25},{25,17},{2,10},{10... | collective-permute-start | bytes 1105928 | tf_op jit(solution)/shard_map/ppermute | solution.py:304
  16.5 24.8 %collective-permute-start.4 = (bf16[96,1920]{1,0:T(8,128)(2,1)}, bf16[96,1920]{1,0:T(8,128)(2,1)S(1)}, u32[]{:S(2)}, u32[]{:S(2)}) collective-permute-start(bf16[96,1920]{1,0:T(8,128)(2,1)} %get-tuple-element.27), channel_id=1, source_target_pairs={{0,16},{8,24},{16,0},{24,8},{1,17},{9,25},{17,1},{25,9},{2,18},{10... | collective-permute-start | bytes 1105928 | tf_op jit(solution)/shard_map/ppermute | solution.py:304
  21.3 24.0 %collective-permute-start.5 = (bf16[96,1920]{1,0:T(8,128)(2,1)}, bf16[96,1920]{1,0:T(8,128)(2,1)S(1)}, u32[]{:S(2)}, u32[]{:S(2)}) collective-permute-start(bf16[96,1920]{1,0:T(8,128)(2,1)} %get-tuple-element.26), channel_id=1, source_target_pairs={{0,24},{8,16},{16,8},{24,0},{1,25},{9,17},{17,9},{25,1},{2,26},{10... | collective-permute-start | bytes 1105928 | tf_op jit(solution)/shard_map/ppermute | solution.py:304
  29.7 16.9 %collective-permute-start.20 = (bf16[96,1920]{1,0:T(8,128)(2,1)}, bf16[96,1920]{1,0:T(8,128)(2,1)S(1)}, u32[]{:S(2)}, u32[]{:S(2)}) collective-permute-start(bf16[96,1920]{1,0:T(8,128)(2,1)} %collective-permute-done.16), channel_id=1, source_target_pairs={{0,1},{1,0},{2,3},{3,2},{4,5},{5,4},{6,7},{7,6},{8,9},{9,8},{10,11... | collective-permute-start | bytes 1105928 | tf_op jit(solution)/shard_map/ppermute | solution.py:310
  30.9 17.2 %collective-permute-start.21 = (bf16[96,1920]{1,0:T(8,128)(2,1)}, bf16[96,1920]{1,0:T(8,128)(2,1)S(1)}, u32[]{:S(2)}, u32[]{:S(2)}) collective-permute-start(bf16[96,1920]{1,0:T(8,128)(2,1)} %collective-permute-done.17), channel_id=1, source_target_pairs={{0,1},{1,0},{2,3},{3,2},{4,5},{5,4},{6,7},{7,6},{8,9},{9,8},{10,11... | collective-permute-start | bytes 1105928 | tf_op jit(solution)/shard_map/ppermute | solution.py:310
  31.1 24.9 %collective-permute-start.22 = (bf16[96,1920]{1,0:T(8,128)(2,1)S(1)}, bf16[96,1920]{1,0:T(8,128)(2,1)S(1)}, u32[]{:S(2)}, u32[]{:S(2)}) collective-permute-start(bf16[96,1920]{1,0:T(8,128)(2,1)S(1)} %collective-permute-done.18), channel_id=1, source_target_pairs={{0,1},{1,0},{2,3},{3,2},{4,5},{5,4},{6,7},{7,6},{8,9},{9,8},{10,11... | collective-permute-start | bytes 1105928 | tf_op jit(solution)/shard_map/ppermute | solution.py:310
  41.3 23.5 %collective-permute-start.6 = (bf16[96,1920]{1,0:T(8,128)(2,1)S(1)}, bf16[96,1920]{1,0:T(8,128)(2,1)S(1)}, u32[]{:S(2)}, u32[]{:S(2)}) collective-permute-start(bf16[96,1920]{1,0:T(8,128)(2,1)S(1)} %get-tuple-element.24), channel_id=1, source_target_pairs={{0,1},{1,0},{2,3},{3,2},{4,5},{5,4},{6,7},{7,6},{8,9},{9,8},{10,11... | collective-permute-start | bytes 1105928 | tf_op jit(solution)/shard_map/ppermute | solution.py:310
  45.3 26.5 %collective-permute-start.7 = (bf16[96,1920]{1,0:T(8,128)(2,1)}, bf16[96,1920]{1,0:T(8,128)(2,1)S(1)}, u32[]{:S(2)}, u32[]{:S(2)}) collective-permute-start(bf16[96,1920]{1,0:T(8,128)(2,1)} %collective-permute-done.3), channel_id=1, source_target_pairs={{0,1},{1,0},{2,3},{3,2},{4,5},{5,4},{6,7},{7,6},{8,9},{9,8},{10,11... | collective-permute-start | bytes 1105928 | tf_op jit(solution)/shard_map/ppermute | solution.py:310
  46.5 33.2 %collective-permute-start.8 = (bf16[96,1920]{1,0:T(8,128)(2,1)S(1)}, bf16[96,1920]{1,0:T(8,128)(2,1)S(1)}, u32[]{:S(2)}, u32[]{:S(2)}) collective-permute-start(bf16[96,1920]{1,0:T(8,128)(2,1)S(1)} %collective-permute-done.4), channel_id=1, source_target_pairs={{0,1},{1,0},{2,3},{3,2},{4,5},{5,4},{6,7},{7,6},{8,9},{9,8},{10,11... | collective-permute-start | bytes 1105928 | tf_op jit(solution)/shard_map/ppermute | solution.py:310
  48.1 39.5 %collective-permute-start.9 = (bf16[96,1920]{1,0:T(8,128)(2,1)S(1)}, bf16[96,1920]{1,0:T(8,128)(2,1)S(1)}, u32[]{:S(2)}, u32[]{:S(2)}) collective-permute-start(bf16[96,1920]{1,0:T(8,128)(2,1)S(1)} %collective-permute-done.5), channel_id=1, source_target_pairs={{0,1},{1,0},{2,3},{3,2},{4,5},{5,4},{6,7},{7,6},{8,9},{9,8},{10,11... | collective-permute-start | bytes 1105928 | tf_op jit(solution)/shard_map/ppermute | solution.py:310
  63.6 31.9 %collective-permute-start.23 = (s16[128,2048]{1,0:T(8,128)(2,1)S(1)}, s16[128,2048]{1,0:T(8,128)(2,1)S(1)}, u32[]{:S(2)}, u32[]{:S(2)}) collective-permute-start(s16[128,2048]{1,0:T(8,128)(2,1)S(1)} %get-tuple-element.15), channel_id=1, source_target_pairs={{0,2},{1,3},{2,4},{3,5},{4,6},{5,7},{6,0},{7,1},{8,10},{9,11},{10,... | collective-permute-start | bytes 1572872 | tf_op jit(solution)/shard_map/ppermute | solution.py:316
  64.8 44.4 %collective-permute-start.24 = (s16[128,2048]{1,0:T(8,128)(2,1)S(1)}, s16[128,2048]{1,0:T(8,128)(2,1)S(1)}, u32[]{:S(2)}, u32[]{:S(2)}) collective-permute-start(s16[128,2048]{1,0:T(8,128)(2,1)S(1)} %get-tuple-element.16), channel_id=1, source_target_pairs={{0,4},{1,5},{2,6},{3,7},{4,0},{5,1},{6,2},{7,3},{8,12},{9,13},{10,... | collective-permute-start | bytes 1572872 | tf_op jit(solution)/shard_map/ppermute | solution.py:316
  71.8 61.9 %collective-permute-start.25 = (s16[128,2048]{1,0:T(8,128)(2,1)S(1)}, s16[128,2048]{1,0:T(8,128)(2,1)S(1)}, u32[]{:S(2)}, u32[]{:S(2)}) collective-permute-start(s16[128,2048]{1,0:T(8,128)(2,1)S(1)} %get-tuple-element.17), channel_id=1, source_target_pairs={{0,6},{1,7},{2,0},{3,1},{4,2},{5,3},{6,4},{7,5},{8,14},{9,15},{10,... | collective-permute-start | bytes 1572872 | tf_op jit(solution)/shard_map/ppermute | solution.py:316
  94.2 48.7 %collective-permute-start.10 = (s16[128,2048]{1,0:T(8,128)(2,1)S(1)}, s16[128,2048]{1,0:T(8,128)(2,1)S(1)}, u32[]{:S(2)}, u32[]{:S(2)}) collective-permute-start(s16[128,2048]{1,0:T(8,128)(2,1)S(1)} %get-tuple-element.11), channel_id=1, source_target_pairs={{0,2},{1,3},{2,4},{3,5},{4,6},{5,7},{6,0},{7,1},{8,10},{9,11},{10,... | collective-permute-start | bytes 1572872 | tf_op jit(solution)/shard_map/ppermute | solution.py:316
  94.2 59.9 %collective-permute-start.11 = (s16[128,2048]{1,0:T(8,128)(2,1)S(1)}, s16[128,2048]{1,0:T(8,128)(2,1)S(1)}, u32[]{:S(2)}, u32[]{:S(2)}) collective-permute-start(s16[128,2048]{1,0:T(8,128)(2,1)S(1)} %get-tuple-element.12), channel_id=1, source_target_pairs={{0,4},{1,5},{2,6},{3,7},{4,0},{5,1},{6,2},{7,3},{8,12},{9,13},{10,... | collective-permute-start | bytes 1572872 | tf_op jit(solution)/shard_map/ppermute | solution.py:316
  95.5 60.7 %collective-permute-start.12 = (s16[128,2048]{1,0:T(8,128)(2,1)S(1)}, s16[128,2048]{1,0:T(8,128)(2,1)S(1)}, u32[]{:S(2)}, u32[]{:S(2)}) collective-permute-start(s16[128,2048]{1,0:T(8,128)(2,1)S(1)} %get-tuple-element.13), channel_id=1, source_target_pairs={{0,6},{1,7},{2,0},{3,1},{4,2},{5,3},{6,4},{7,5},{8,14},{9,15},{10,... | collective-permute-start | bytes 1572872 | tf_op jit(solution)/shard_map/ppermute | solution.py:316
  134.5 23.1 %collective-permute-start.27 = (s16[128,2048]{1,0:T(8,128)(2,1)S(1)}, s16[128,2048]{1,0:T(8,128)(2,1)S(1)}, u32[]{:S(2)}, u32[]{:S(2)}) collective-permute-start(s16[128,2048]{1,0:T(8,128)(2,1)S(1)} %combine.3.refs_0_), channel_id=1, source_target_pairs={{0,16},{8,24},{16,0},{24,8},{1,17},{9,25},{17,1},{25,9},{2,18},{10... | collective-permute-start | bytes 1572872 | tf_op jit(solution)/shard_map/ppermute | solution.py:304
  156.9 13.1 %collective-permute-start.14 = (s16[128,2048]{1,0:T(8,128)(2,1)S(1)}, s16[128,2048]{1,0:T(8,128)(2,1)S(1)}, u32[]{:S(2)}, u32[]{:S(2)}) collective-permute-start(s16[128,2048]{1,0:T(8,128)(2,1)S(1)} %combine.2.refs_0_), channel_id=1, source_target_pairs={{0,16},{8,24},{16,0},{24,8},{1,17},{9,25},{17,1},{25,9},{2,18},{10... | collective-permute-start | bytes 1572872 | tf_op jit(solution)/shard_map/ppermute | solution.py:304
  157.0 14.4 %collective-permute-start.26 = (s16[128,2048]{1,0:T(8,128)(2,1)S(1)}, s16[128,2048]{1,0:T(8,128)(2,1)S(1)}, u32[]{:S(2)}, u32[]{:S(2)}) collective-permute-start(s16[128,2048]{1,0:T(8,128)(2,1)S(1)} %combine.3.refs_0_), channel_id=1, source_target_pairs={{0,8},{8,0},{16,24},{24,16},{1,9},{9,1},{17,25},{25,17},{2,10},{10... | collective-permute-start | bytes 1572872 | tf_op jit(solution)/shard_map/ppermute | solution.py:304
  157.5 13.9 %collective-permute-start.28 = (s16[128,2048]{1,0:T(8,128)(2,1)S(1)}, s16[128,2048]{1,0:T(8,128)(2,1)S(1)}, u32[]{:S(2)}, u32[]{:S(2)}) collective-permute-start(s16[128,2048]{1,0:T(8,128)(2,1)S(1)} %collective-permute-done.27.refs_2_), channel_id=1, source_target_pairs={{0,8},{8,0},{16,24},{24,16},{1,9},{9,1},{17,25},{25,17},{2,10},{10... | collective-permute-start | bytes 1572872 | tf_op jit(solution)/shard_map/ppermute | solution.py:304
  157.6 37.1 %collective-permute-start.13 = (s16[128,2048]{1,0:T(8,128)(2,1)S(1)}, s16[128,2048]{1,0:T(8,128)(2,1)S(1)}, u32[]{:S(2)}, u32[]{:S(2)}) collective-permute-start(s16[128,2048]{1,0:T(8,128)(2,1)S(1)} %combine.2.refs_0_), channel_id=1, source_target_pairs={{0,8},{8,0},{16,24},{24,16},{1,9},{9,1},{17,25},{25,17},{2,10},{10... | collective-permute-start | bytes 1572872 | tf_op jit(solution)/shard_map/ppermute | solution.py:304
  170.1 24.7 %collective-permute-start.15 = (s16[128,2048]{1,0:T(8,128)(2,1)S(1)}, s16[128,2048]{1,0:T(8,128)(2,1)S(1)}, u32[]{:S(2)}, u32[]{:S(2)}) collective-permute-start(s16[128,2048]{1,0:T(8,128)(2,1)S(1)} %collective-permute-done.14.refs_2_), channel_id=1, source_target_pairs={{0,8},{8,0},{16,24},{24,16},{1,9},{9,1},{17,25},{25,17},{2,10},{10... | collective-permute-start | bytes 1572872 | tf_op jit(solution)/shard_map/ppermute | solution.py:304

commit v2 on v0

v2 whole, which is shorter than its diff:
```python
import functools
import jax
import jax.numpy as jnp
from jax import lax
from jax.experimental import pallas as pl
from jax.experimental.pallas import tpu as pltpu
from jax.sharding import PartitionSpec as P

LANES = 128
CORES = 2
DEPTH = 4
SCALES = 16
TOP = 32767.0
VMEM_BYTES = 48 * 1024 * 1024
BEFORE = (((0,), (0,)), ((), ()))
AFTER = (((1,), (1,)), ((), ()))


def params():
    return pltpu.CompilerParams(vmem_limit_bytes=VMEM_BYTES)


def cost(flops, moved):
    return pl.CostEstimate(flops=flops, bytes_accessed=moved, transcendentals=0)


def twice(value):
    return jnp.concatenate([value, value], axis=0)


def encode(src, src_base, dst, dst_base, height):
    half = height // 2
    powers = []
    for h in range(2):
        top = jnp.abs(src[pl.ds(src_base + h * half, 8), :])
        for r in range(8, half, 8):
            top = jnp.maximum(top, jnp.abs(src[pl.ds(src_base + h * half + r, 8), :]))
        power = jnp.floor(jnp.log2(jnp.maximum(top, 1e-30))) + 1.0
        gain = twice(jnp.exp2(-power) * TOP)
        for r in range(h * half, (h + 1) * half, 16):
            level = jnp.clip(jnp.round(src[pl.ds(src_base + r, 16), :] * gain), -TOP, TOP)
            dst[pl.ds(dst_base + r, 16), :] = level.astype(jnp.int32).astype(jnp.int16)
        powers.append(power)
    both = jnp.concatenate(powers, axis=0)
    dst[pl.ds(dst_base + height, SCALES), :] = both.astype(jnp.int32).astype(jnp.int16)


def steps_of(coded, base, height):
    power = coded[pl.ds(base + height, SCALES), :].astype(jnp.int32).astype(jnp.float32)
    step = jnp.exp2(power) * (1.0 / TOP)
    return [twice(step[:8]), twice(step[8:])]


def decode(coded, row, step):
    return coded[pl.ds(row, 16), :].astype(jnp.int32).astype(jnp.float32) * step


def weights_kernel(rows, base_ref, query_ref, out_ref):
    each = query_ref.shape[0] // 2
    row_id = lax.broadcasted_iota(jnp.int32, (16, LANES), 0)

    def piece(j, carry):
        for u in range(DEPTH):
            lanes = slice(u * LANES, (u + 1) * LANES)
            for r in range(0, rows, 16):
                tract = row_id + (base_ref[j] + r)
                total = jnp.zeros((16, LANES), jnp.float32)
                for k in range(each):
                    share = query_ref[each + k:each + k + 1, lanes].astype(jnp.float32) * (1.0 / 256.0)
                    total = jnp.where(query_ref[k:k + 1, lanes] == tract, share, total)
                where = pl.ds(pl.multiple_of(j * rows + r, 16), 16)
                out_ref[where, lanes] = total.astype(jnp.bfloat16)
        return carry

    lax.fori_loop(0, out_ref.shape[0] // rows, piece, 0)


def build_weights(bases, queries, rows):
    pieces = bases.shape[0]
    width = queries.shape[1]
    shape = (pieces * rows, width)
    return pl.pallas_call(
        functools.partial(weights_kernel, rows),
        grid_spec=pltpu.PrefetchScalarGridSpec(
            num_scalar_prefetch=1,
            grid=(1,),
            in_specs=[pl.BlockSpec(queries.shape, lambda i, s: (0, 0))],
            out_specs=pl.BlockSpec(shape, lambda i, s: (0, 0)),
        ),
        out_shape=jax.ShapeDtypeStruct(shape, jnp.bfloat16),
        compiler_params=params(),
        cost_estimate=cost(shape[0] * width * queries.shape[0], shape[0] * width * 2),
        name="build_weights",
    )(bases, queries)


def sums_kernel(parts, has_var, flag_ref, w_ref, *refs):
    data = refs[:parts]
    own_ref, near_ref, far_ref, acc_ref = refs[parts:]
    depth, columns = data[0].shape
    coded = columns + SCALES

    def weighted(get, t):
        total = None
        for j in range(parts):
            part = lax.dot_general(
                data[j][:, t * LANES:(t + 1) * LANES],
                get(w_ref[j * depth:(j + 1) * depth, :]),
                BEFORE,
                preferred_element_type=jnp.float32,
            )
            total = part if total is None else total + part
        return total

    def put(t, value):
        where = slice(t * LANES, (t + 1) * LANES)
        own_ref[where, :] = value[:, :LANES]
        for u in range(1, DEPTH):
            acc_ref[u - 1, where, :] = value[:, u * LANES:(u + 1) * LANES]

    for t in range(columns // LANES):
        put(t, weighted(lambda w: w, t))

    if has_var:
        @pl.when(flag_ref[0] == 1)
        def _():
            def square(w):
                wide = w.astype(jnp.float32)
                return wide * wide

            def high(w):
                return square(w).astype(jnp.bfloat16)

            def low(w):
                s = square(w)
                return (s - s.astype(jnp.bfloat16).astype(jnp.float32)).astype(jnp.bfloat16)

            t = columns // LANES - 1
            put(t, weighted(high, t) + weighted(low, t))

    encode(acc_ref.at[0], 0, near_ref, 0, columns)
    encode(acc_ref.at[1], 0, far_ref, 0, columns)
    encode(acc_ref.at[2], 0, far_ref, coded, columns)


def partial_sums(flag, w, data, has_var):
    depth, columns = data[0].shape
    parts = len(data)
    coded = columns + SCALES
    whole = lambda i, s: (0, 0)
    shapes = [
        jax.ShapeDtypeStruct((columns, LANES), jnp.float32),
        jax.ShapeDtypeStruct((coded, LANES), jnp.int16),
        jax.ShapeDtypeStruct((2 * coded, LANES), jnp.int16),
    ]
    return pl.pallas_call(
        functools.partial(sums_kernel, parts, has_var),
        grid_spec=pltpu.PrefetchScalarGridSpec(
            num_scalar_prefetch=1,
            grid=(1,),
            in_specs=[pl.BlockSpec(w.shape, whole)] + [pl.BlockSpec((depth, columns), whole)] * parts,
            out_specs=[pl.BlockSpec(s.shape, whole) for s in shapes],
            scratch_shapes=[pltpu.VMEM((DEPTH - 1, columns, LANES), jnp.float32)],
        ),
        out_shape=shapes,
        compiler_params=params(),
        cost_estimate=cost(2 * w.shape[0] * w.shape[1] * columns, 2 * depth * parts * columns + columns * LANES * 10),
        name="partial_sums",
    )(flag, w, *data)


def middle_kernel(own_ref, other_ref, near_ref, end_ref, acc_ref):
    height = acc_ref.shape[0]
    for u, out in enumerate((near_ref, end_ref)):
        base = u * (height + SCALES)
        mine = steps_of(own_ref, base, height)
        theirs = steps_of(other_ref, base, height)
        for r in range(0, height, 16):
            h = r * 2 // height
            acc_ref[r:r + 16, :] = decode(own_ref, base + r, mine[h]) + decode(other_ref, base + r, theirs[h])
        encode(acc_ref, 0, out, 0, height)


def middle(own, other):
    coded = own.shape[0] // 2
    shape = jax.ShapeDtypeStruct((coded, LANES), jnp.int16)
    return pl.pallas_call(
        middle_kernel,
        out_shape=[shape, shape],
        scratch_shapes=[pltpu.VMEM((coded - SCALES, LANES), jnp.float32)],
        compiler_params=params(),
        cost_estimate=cost(coded * LANES * 32, coded * LANES * 12),
        name="middle",
    )(own, other)


def combine_kernel(own_ref, *refs):
    others, out_ref, acc_ref = refs[:-2], refs[-2], refs[-1]
    height = acc_ref.shape[0]
    steps = [steps_of(o, 0, height) for o in others]
    for r in range(0, height, 16):
        total = own_ref[r:r + 16, :]
        for o, step in zip(others, steps):
            total = total + decode(o, r, step[r * 2 // height])
        acc_ref[r:r + 16, :] = total
    encode(acc_ref, 0, out_ref, 0, height)


def combine(own, others):
    height = own.shape[0]
    shape = (height + SCALES, LANES)
    return pl.pallas_call(
        combine_kernel,
        out_shape=jax.ShapeDtypeStruct(shape, jnp.int16),
        scratch_shapes=[pltpu.VMEM((height, LANES), jnp.float32)],
        compiler_params=params(),
        cost_estimate=cost(height * LANES * 16, height * LANES * 12),
        name="combine",
    )(own, *others)


def each_piece(place_ref, pieces, tiles, do):
    groups = place_ref.shape[0] // 2
    for upper in (1, 0):
        for r in range(groups):
            @pl.when(place_ref[groups + r] == upper)
            def _(r=r):
                first = 0
                for c, count in enumerate(tiles):
                    do((place_ref[r] + first) * LANES, pieces[c * groups + r], count * LANES)
                    first += count


def marginal_kernel(tiles, place_ref, *refs):
    pieces, out_ref, tile_ref = refs[:-2], refs[-2], refs[-1]

    def do(start, piece, height):
        steps = steps_of(piece, 0, height)
        for t in range(0, height, LANES):
            for r in range(0, LANES, 16):
                tile_ref[r:r + 16, :] = decode(piece, t + r, steps[(t + r) * 2 // height])
            out_ref[:, pl.ds(pl.multiple_of(start + t, LANES), LANES)] = tile_ref[...].T

    each_piece(place_ref, pieces, tiles, do)


def marginal(places, pieces, tiles, total):
    shape = (LANES, total * LANES)
    return pl.pallas_call(
        functools.partial(marginal_kernel, tiles),
        grid_spec=pltpu.PrefetchScalarGridSpec(
            num_scalar_prefetch=1,
            grid=(1,),
            in_specs=[pl.BlockSpec(p.shape, lambda i, s: (0, 0)) for p in pieces],
            out_specs=pl.BlockSpec(shape, lambda i, s: (0, 0)),
            scratch_shapes=[pltpu.VMEM((LANES, LANES), jnp.float32)],
        ),
        out_shape=jax.ShapeDtypeStruct(shape, jnp.float32),
        compiler_params=params(),
        cost_estimate=cost(shape[0] * shape[1] * 4, shape[0] * shape[1] * 6),
        name="marginal",
    )(places, *pieces)


def covariance_kernel(tiles, total, ages, rank, place_ref, *refs):
    pieces, out_ref = refs[:-4], refs[-4]
    load_ref, age_ref, cov_ref = refs[-3:]
    pitch = -(-ages // 8) * 8
    left = lax.broadcasted_iota(jnp.int32, (LANES, LANES), 1) < rank

    def do(start, piece, height):
        steps = steps_of(piece, 0, height)
        for r in range(0, height, 16):
            load_ref[pl.ds(pl.multiple_of(start + r, 16), 16), :] = decode(piece, r, steps[r * 2 // height])

    each_piece(place_ref, pieces, tiles, do)

    def turn(t, carry):
        value = load_ref[pl.ds(pl.multiple_of(t * LANES, LANES), LANES), :].T
        swapped = pltpu.roll(value, rank, 1)
        age_ref[pl.ds(2 * t, LANES, stride=pitch), :] = jnp.where(left, value, swapped)
        age_ref[pl.ds(2 * t + 1, LANES, stride=pitch), :] = jnp.where(left, swapped, value)
        return carry

    lax.fori_loop(0, ages * rank // LANES, turn, 0)

    def outer(d, carry):
        start = pl.multiple_of(d * pitch, 8)
        mine = age_ref[pl.ds(start, LANES), :]
        high = mine.astype(jnp.bfloat16).astype(jnp.float32)
        low = mine - high
        mixed = jnp.where(left, high, low).astype(jnp.bfloat16)
        product = lax.dot_general(
            jnp.concatenate([mixed, mixed], axis=1),
            jnp.concatenate([high.astype(jnp.bfloat16), low.astype(jnp.bfloat16)], axis=1),
            AFTER,
            preferred_element_type=jnp.float32,
        )
        cov_ref[pl.ds(start, pitch), :] = product[:pitch]
        return carry

    lax.fori_loop(0, LANES, outer, 0, unroll=4)

    def store(m, carry):
        base = pl.multiple_of(m * (2 * ages), 8)
        for p in range(2):
            value = cov_ref[pl.ds(2 * m + p, LANES, stride=pitch), :].T
            out_ref[pl.ds(base + p * ages, ages), :] = value[:ages]
        return carry

    lax.fori_loop(0, ages // 2, store, 0)
    for i in range(ages):
        row = i * (ages + 1)
        out_ref[row:row + 1, :] += load_ref[(total - 1) * LANES + i:(total - 1) * LANES + i + 1, :]


def covariance(places, pieces, tiles, total, ages, rank):
    pitch = -(-ages // 8) * 8
    shape = (ages * ages, LANES)
    tall = (LANES * pitch + LANES - pitch, LANES)
    return pl.pallas_call(
        functools.partial(covariance_kernel, tiles, total, ages, rank),
        grid_spec=pltpu.PrefetchScalarGridSpec(
            num_scalar_prefetch=1,
            grid=(1,),
            in_specs=[pl.BlockSpec(p.shape, lambda i, s: (0, 0)) for p in pieces],
            out_specs=pl.BlockSpec(shape, lambda i, s: (0, 0)),
            scratch_shapes=[
                pltpu.VMEM((total * LANES, LANES), jnp.float32),
                pltpu.VMEM(tall, jnp.float32),
                pltpu.VMEM(tall, jnp.float32),
            ],
        ),
        out_shape=jax.ShapeDtypeStruct(shape, jnp.float32),
        compiler_params=params(),
        cost_estimate=cost(LANES * ages * ages * rank * 32, shape[0] * shape[1] * 4),
        name="covariance",
    )(places, *pieces)


def shards(groups, parts, estimates, factors, variances, intersection_tracts, intersection_weights):
    xs = groups // CORES
    ys = parts // DEPTH
    rows = estimates.shape[0]
    ages = variances.shape[1]
    rank = factors.shape[1] // ages
    geo = lax.axis_index("geo")
    dist = lax.axis_index("dist")
    x, core = geo // CORES, geo % CORES
    z, y = dist // ys, dist % ys

    def geo_shift(value, dx, dc):
        if dx == 0 and dc == 0:
            return value
        perm = [(a * CORES + b, (a + dx) % xs * CORES + (b + dc) % CORES) for a in range(xs) for b in range(CORES)]
        return lax.ppermute(value, "geo", perm)

    def y_shift(value, dy):
        if dy == 0:
            return value
        perm = [(a * ys + b, a * ys + (b + dy) % ys) for a in range(DEPTH) for b in range(ys)]
        return lax.ppermute(value, "dist", perm)

    def z_send(value, pairs):
        perm = [(a * ys + b, c * ys + b) for a, c in pairs for b in range(ys)]
        return lax.ppermute(value, "dist", perm)

    near = ((0, 1), (1, 0), (2, 3), (3, 2))
    mirror = ((0, 3), (1, 2), (2, 1), (3, 0))
    across = ((0, 2), (1, 3), (2, 0), (3, 1))
    queries = jnp.concatenate([intersection_tracts.T, intersection_weights.T], axis=0)
    in_middle = (z == 1) | (z == 2)
    at_mirror, at_across = z_send(queries, mirror), z_send(queries, across)
    queries = jnp.concatenate(
        [
            queries,
            z_send(queries, near),
            jnp.where(in_middle, at_mirror, at_across),
            jnp.where(in_middle, at_across, at_mirror),
        ],
        axis=1,
    )

    bases = jnp.stack([
        (((x - dx) % xs * CORES + (core - dc) % CORES) * parts + z * ys + (y - dy) % ys) * rows
        for dy in range(ys) for dx in range(xs) for dc in range(CORES)
    ]).astype(jnp.int32)
    w = build_weights(bases, queries, rows)
    flag = ((core == CORES - 1) & (x == xs - 1)).astype(jnp.int32).reshape(1)

    variances = jnp.pad(variances, ((0, 0), (0, -ages % LANES)))
    loads = jnp.concatenate([factors, variances], axis=1)

    def halves(array):
        total = array.shape[1] // LANES
        width = -(-total // groups) * xs

        def half(c):
            return lax.dynamic_slice(array, (0, jnp.where(c == 0, 0, total - width) * LANES), (rows, width * LANES))

        return jnp.concatenate([half(core), geo_shift(half(1 - core), 0, 1)], axis=0)

    def collect(both, first, count, each, has_var):
        def part(group):
            return lax.dynamic_slice(
                both, (0, (group * each + first) * LANES), (both.shape[0], count * LANES)
            )
        by_x = [geo_shift(part((x + dx) % xs), dx, 0) for dx in range(xs)]
        data = [y_shift(value, dy) for dy in range(ys) for value in by_x]
        own, close, far = partial_sums(flag, w, data, has_var)
        far_in = z_send(far, ((0, 1), (3, 2)))
        close_in = z_send(close, near)
        to_middle, to_end = middle(far, far_in)
        middle_in = z_send(to_middle, ((1, 2), (2, 1)))
        end_in = z_send(to_end, ((1, 3), (2, 0)))
        mine = combine(own, [close_in, middle_in, end_in])
        along = [geo_shift(mine, dx, 0) for dx in range(xs)]
        return [geo_shift(along[dx], 0, dc) for dx in range(xs) for dc in range(CORES)]

    def places(total):
        each = -(-total // groups)
        starts, uppers = [], []
        for dx in range(xs):
            for dc in range(CORES):
                c, a = (core - dc) % CORES, (x - dx) % xs
                starts.append(jnp.where(c == 0, 0, total - each * xs) + a * each)
                uppers.append(c)
        return jnp.stack(starts + uppers).astype(jnp.int32)

    def split(each):
        return (each // 2, each - each // 2)

    load_total = loads.shape[1] // LANES
    mean_total = estimates.shape[1] // LANES
    load_each, mean_each = -(-load_total // groups), -(-mean_total // groups)
    load_tiles = split(load_each)
    mean_tiles = split(mean_each)[::-1]
    load_half = halves(loads)
    mean_half = halves(estimates)
    load_pieces, mean_pieces = [], []
    first = 0
    for i, count in enumerate(load_tiles):
        load_pieces += collect(load_half, first, count, load_each, i == len(load_tiles) - 1)
        first += count
    first = 0
    for count in mean_tiles:
        mean_pieces += collect(mean_half, first, count, mean_each, False)
        first += count
    cov = covariance(places(load_total), load_pieces, load_tiles, load_total, ages, rank)
    mean = marginal(places(mean_total), mean_pieces, mean_tiles, mean_total)
    return mean, cov.T


def solution(mesh):
    return jax.shard_map(
        functools.partial(shards, mesh.shape["geo"], mesh.shape["dist"]),
        mesh=mesh,
        in_specs=(
            P(("geo", "dist"), None),
            P(("geo", "dist"), None),
            P(("geo", "dist"), None),
            P("dist", None),
            P("dist", None),
        ),
        out_specs=(P("dist", None), P("dist", None)),
        check_vma=False,
    )
```

time: 540 us -> 202 us (0.37)
  waiting for transfers between devices: 401 us -> 87.7 us
  starting transfers between devices: 0.11 us -> 52.9 us
  Pallas kernels: 0 us -> 47 us
  blocking collectives: 43.6 us -> 0 us
  matrix products: 38.8 us -> 0 us
  local copies, waits for them, and re-layouts: 26.8 us -> 5.33 us
  between operations: 13.8 us -> 1.01 us
  other arithmetic: 14.6 us -> 7.82 us
    all_gather x2 -> x0, waiting for transfers between devices: 298 us -> none  [the longest x1 151 us: shards(): lax.all_gather(factors, 'dist', axis=0, tiled=True)]
    psum x1 -> x0, waiting for transfers between devices: 102 us -> none  [shards(): est_sum, fac_sum, var_sum = lax.psum((est_new, fac_new, var_new), 'geo')]
    ppermute x0 -> x45, waiting for transfers between devices: none -> 87.7 us  [the longest x19 52.2 us: z_send(): return lax.ppermute(value, 'dist', perm)]
    ppermute x0 -> x45, starting transfers between devices: none -> 52.9 us  [the longest x19 30.9 us: z_send(): return lax.ppermute(value, 'dist', perm)]
    pallas_call x0 -> x15, Pallas kernels: none -> 47 us  [the longest x1 28.3 us: covariance(): pl.pallas_call(functools.partial(covariance_kernel, tiles, total, ages, r...]
    dot_general x4 -> x0, matrix products: 38.8 us -> none  [the longest x1 20 us: assemble(): jnp.einsum('dik,djk->dij', shaped, shaped, precision=lax.Precision.HIGHEST)]
    all_gather x1 -> x0, blocking collectives: 30.6 us -> none  [shards(): lax.all_gather(variances, 'dist', axis=0, tiled=True).astype(jnp.float32)]
    reshape x3 -> x0, local copies, waits for them, and re-layouts: 22.2 us -> none  [the longest x2 16.8 us: assemble(): return (est_sum, outer.reshape(count, ages * ages))]
  transfers between devices with their start and end apart: 3 -> 45, of which waited for: 3 -> 15; matrix products, arithmetic and copies ran while one was open for 6% -> 4% of each run, Pallas kernels for 0% -> 9%
where the time goes in v2:
time: 202 us
  waiting for transfers between devices  87.7 us (43%)
  starting transfers between devices  52.9 us (26%)
  Pallas kernels  47 us (23%)
  other arithmetic  7.82 us (4%)
  local copies, waits for them, and re-layouts  5.33 us (3%)
    ppermute x19, waiting for transfers between devices, z_send(): return lax.ppermute(value, 'dist', perm)  52.2 us
    ppermute x19, starting transfers between devices, z_send(): return lax.ppermute(value, 'dist', perm)  30.9 us
    pallas_call x1, Pallas kernels, covariance(): pl.pallas_call(functools.partial(covariance_kernel, tiles, total, ages, r...  28.3 us
    ppermute x18, waiting for transfers between devices, geo_shift(): return lax.ppermute(value, 'geo', perm)  22.6 us
    ppermute x8, waiting for transfers between devices, y_shift(): return lax.ppermute(value, 'dist', perm)  12.9 us
    ppermute x18, starting transfers between devices, geo_shift(): return lax.ppermute(value, 'geo', perm)  11.6 us
    ppermute x8, starting transfers between devices, y_shift(): return lax.ppermute(value, 'dist', perm)  10.4 us
    pallas_call x4, Pallas kernels, partial_sums(): pl.pallas_call(functools.partial(sums_kernel, parts, has_var), grid_spec=...  6.92 us
  transfers between devices with their start and end apart: 45, of which 15 were waited for; matrix products, arithmetic and copies ran while one was open for 4% of the time, Pallas kernels for 9%

profile of v2, /device:TPU:0, one launch (start us, length us, event | category | flops | bytes accessed | tf_op | source)
XLA Modules:
  0.0 201.7 jit_solution(12958985860724949234)
XLA Ops:
  0.7 1.5 fusion.1
  3.6 2.3 %constant_dynamic-slice_fusion.2 = (bf16[96,3840]{1,0:T(8,128)(2,1)}, bf16[96,3840]{1,0:T(8,128)(2,1)S(1)}) fusion(bf16[96,7424]{1,0:T(8,128)(2,1)} %param.5, s32[]{:T(128)S(6)} %select_n.219, s32[]{:T(128)S(6)} %select_n.217), kind=kLoop, calls=%fused_computation.33 | loop fusion | bytes 2949128 | tf_op jit(solution)/shard_map/dynamic_slice | solution.py:399
  6.0 4.1 %collective-permute-start.2 = (s32[64,128]{1,0:T(8,128)S(1)}, s32[64,128]{1,0:T(8,128)S(1)}, u32[]{:S(2)}, u32[]{:S(2)}) collective-permute-start(s32[64,128]{1,0:T(8,128)S(1)} %pad_add_fusion.1), channel_id=1, source_target_pairs={{0,4},{1,5},{2,6},{3,7},{4,0},{5,1},{6,2},{7,3},{8,12},{9,13},{10,... | collective-permute-start | bytes 98312 | tf_op jit(solution)/shard_map/ppermute | solution.py:366
  10.1 1.3 collective-permute-start.1
  11.7 1.1 fusion.7
  12.8 1.6 collective-permute-start.25
  14.3 1.8 fusion.2
  16.2 1.5 collective-permute-start.26
  19.1 1.5 collective-permute-start.4
  20.6 1.8 fusion.8
  23.8 1.5 collective-permute-start.36
  25.4 1.6 collective-permute-done.26.refs_2_
  27.7 1.7 collective-permute-start.27
  29.5 17.0 %collective-permute-done.14.refs_1_ = bf16[192,896]{1,0:T(8,128)(2,1)S(1)} collective-permute-done((bf16[192,896]{1,0:T(8,128)(2,1)}, bf16[192,896]{1,0:T(8,128)(2,1)S(1)}, u32[]{:S(2)}, u32[]{:S(2)}) %collective-permute-start.14) | collective-permute-done | bytes 344096 | tf_op jit(solution)/shard_map/ppermute | solution.py:356
  46.5 1.5 collective-permute-start.5
  48.5 1.5 collective-permute-start.6
  50.6 1.5 collective-permute-start.16
  52.9 4.9 %build_weights.1.w_ref = bf16[768,512]{1,0:T(8,128)(2,1)S(1)} custom-call(s32[8]{0:T(128)S(1)} %stack.84.base_ref, s32[64,512]{1,0:T(8,128)S(1)} %pad_add_fusion.query_ref), custom_call_target="tpu_custom_call" | custom-call | flops 25165824 | bytes 786432 | tf_op jit(solution)/shard_map/build_weights/pallas_call | solution.py:82
  58.8 2.3 %partial_sums.6 = (f32[896,128]{1,0:T(8,128)S(1)}, s16[912,128]{1,0:T(8,128)(2,1)S(1)}, s16[1824,128]{1,0:T(8,128)(2,1)S(1)}) custom-call(s32[1]{0:T(128)} %bitcast.6.flag_ref, bf16[768,512]{1,0:T(8,128)(2,1)S(1)} %build_weights.1.w_ref, bf16[192,896]{1,0:T(8,128)(2,1)S(1)} %get-tuple-element.45.refs_0_, ...), custom_call_target="tpu_custom_call" | custom-call | flops 704643072 | bytes 2523136 | tf_op jit(solution)/shard_map/partial_sums/pallas_call | solution.py:156
  61.1 3.5 %collective-permute-start.29 = (s16[1824,128]{1,0:T(8,128)(2,1)S(1)}, s16[1824,128]{1,0:T(8,128)(2,1)S(1)}, u32[]{:S(2)}, u32[]{:S(2)}) collective-permute-start(s16[1824,128]{1,0:T(8,128)(2,1)S(1)} %get-tuple-element.34.own_ref), channel_id=1, source_target_pairs={{0,2},{1,3},{6,4},{7,5},{8,10},{9,11},{14,12},{15,13},{16,18},{17,... | collective-permute-start | bytes 1400840 | tf_op jit(solution)/shard_map/ppermute | solution.py:366
  64.6 2.3 %collective-permute-done.37.refs_3_ = bf16[192,1024]{1,0:T(8,128)(2,1)S(1)} collective-permute-done((bf16[192,1024]{1,0:T(8,128)(2,1)S(1)}, bf16[192,1024]{1,0:T(8,128)(2,1)S(1)}, u32[]{:S(2)}, u32[]{:S(2)}) %collective-permute-start.37) | collective-permute-done | bytes 393248 | tf_op jit(solution)/shard_map/ppermute | solution.py:362
  67.0 1.5 collective-permute-start.28
  68.5 1.6 partial_sums.7
  70.1 5.2 %collective-permute-done.6.refs_3_ = bf16[192,1024]{1,0:T(8,128)(2,1)S(1)} collective-permute-done((bf16[192,1024]{1,0:T(8,128)(2,1)S(1)}, bf16[192,1024]{1,0:T(8,128)(2,1)S(1)}, u32[]{:S(2)}, u32[]{:S(2)}) %collective-permute-start.6) | collective-permute-done | bytes 393248 | tf_op jit(solution)/shard_map/ppermute | solution.py:362
  75.4 3.5 %collective-permute-start.39 = (s16[2080,128]{1,0:T(8,128)(2,1)S(1)}, s16[2080,128]{1,0:T(8,128)(2,1)S(1)}, u32[]{:S(2)}, u32[]{:S(2)}) collective-permute-start(s16[2080,128]{1,0:T(8,128)(2,1)S(1)} %get-tuple-element.39.own_ref), channel_id=1, source_target_pairs={{0,2},{1,3},{6,4},{7,5},{8,10},{9,11},{14,12},{15,13},{16,18},{17,... | collective-permute-start | bytes 1597448 | tf_op jit(solution)/shard_map/ppermute | solution.py:366
  78.9 1.6 partial_sums.4
  80.5 2.3 %collective-permute-done.15.refs_2_ = bf16[192,896]{1,0:T(8,128)(2,1)S(1)} collective-permute-done((bf16[192,896]{1,0:T(8,128)(2,1)S(1)}, bf16[192,896]{1,0:T(8,128)(2,1)S(1)}, u32[]{:S(2)}, u32[]{:S(2)}) %collective-permute-start.15) | collective-permute-done | bytes 344096 | tf_op jit(solution)/shard_map/ppermute | solution.py:362
  82.8 3.5 %collective-permute-start.8 = (s16[2080,128]{1,0:T(8,128)(2,1)S(1)}, s16[2080,128]{1,0:T(8,128)(2,1)S(1)}, u32[]{:S(2)}, u32[]{:S(2)}) collective-permute-start(s16[2080,128]{1,0:T(8,128)(2,1)S(1)} %get-tuple-element.24.own_ref), channel_id=1, source_target_pairs={{0,2},{1,3},{6,4},{7,5},{8,10},{9,11},{14,12},{15,13},{16,18},{17,... | collective-permute-start | bytes 1597448 | tf_op jit(solution)/shard_map/ppermute | solution.py:366
  86.2 1.4 collective-permute-done.16.refs_3_
  87.6 1.4 partial_sums.5
  89.0 3.2 %collective-permute-start.18 = (s16[1824,128]{1,0:T(8,128)(2,1)S(1)}, s16[1824,128]{1,0:T(8,128)(2,1)S(1)}, u32[]{:S(2)}, u32[]{:S(2)}) collective-permute-start(s16[1824,128]{1,0:T(8,128)(2,1)S(1)} %get-tuple-element.29.own_ref), channel_id=1, source_target_pairs={{0,2},{1,3},{6,4},{7,5},{8,10},{9,11},{14,12},{15,13},{16,18},{17,... | collective-permute-start | bytes 1400840 | tf_op jit(solution)/shard_map/ppermute | solution.py:366
  92.3 2.0 collective-permute-start.7
  94.8 22.5 %collective-permute-done.17.refs_0_ = s16[912,128]{1,0:T(8,128)(2,1)S(1)} collective-permute-done((s16[912,128]{1,0:T(8,128)(2,1)S(1)}, s16[912,128]{1,0:T(8,128)(2,1)S(1)}, u32[]{:S(2)}, u32[]{:S(2)}) %collective-permute-start.17) | collective-permute-done | bytes 233504 | tf_op jit(solution)/shard_map/ppermute | solution.py:366
  117.9 1.3 collective-permute-start.31
  120.8 1.3 collective-permute-start.20
  123.3 1.3 collective-permute-start.10
  124.6 10.1 %collective-permute-done.31.refs_2_ = s16[912,128]{1,0:T(8,128)(2,1)S(1)} collective-permute-done((s16[912,128]{1,0:T(8,128)(2,1)S(1)}, s16[912,128]{1,0:T(8,128)(2,1)S(1)}, u32[]{:S(2)}, u32[]{:S(2)}) %collective-permute-start.31) | collective-permute-done | bytes 233504 | tf_op jit(solution)/shard_map/ppermute | solution.py:366
  135.9 8.9 %collective-permute-done.20.refs_2_ = s16[912,128]{1,0:T(8,128)(2,1)S(1)} collective-permute-done((s16[912,128]{1,0:T(8,128)(2,1)S(1)}, s16[912,128]{1,0:T(8,128)(2,1)S(1)}, u32[]{:S(2)}, u32[]{:S(2)}) %collective-permute-start.20) | collective-permute-done | bytes 233504 | tf_op jit(solution)/shard_map/ppermute | solution.py:366
  144.8 1.5 collective-permute-start.41
  146.6 1.6 collective-permute-start.33
  148.4 7.0 %collective-permute-done.10.refs_2_ = s16[1040,128]{1,0:T(8,128)(2,1)S(1)} collective-permute-done((s16[1040,128]{1,0:T(8,128)(2,1)S(1)}, s16[1040,128]{1,0:T(8,128)(2,1)S(1)}, u32[]{:S(2)}, u32[]{:S(2)}) %collective-permute-start.10) | collective-permute-done | bytes 266272 | tf_op jit(solution)/shard_map/ppermute | solution.py:366
  155.4 1.5 collective-permute-start.22
  157.9 3.3 %collective-permute-done.41.refs_2_ = s16[1040,128]{1,0:T(8,128)(2,1)S(1)} collective-permute-done((s16[1040,128]{1,0:T(8,128)(2,1)S(1)}, s16[1040,128]{1,0:T(8,128)(2,1)S(1)}, u32[]{:S(2)}, u32[]{:S(2)}) %collective-permute-start.41) | collective-permute-done | bytes 266272 | tf_op jit(solution)/shard_map/ppermute | solution.py:366
  161.5 1.6 collective-permute-start.43
  163.7 2.4 %collective-permute-done.12.refs_2_ = s16[1040,128]{1,0:T(8,128)(2,1)S(1)} collective-permute-done((s16[1040,128]{1,0:T(8,128)(2,1)S(1)}, s16[1040,128]{1,0:T(8,128)(2,1)S(1)}, u32[]{:S(2)}, u32[]{:S(2)}) %collective-permute-start.12) | collective-permute-done | bytes 266272 | tf_op jit(solution)/shard_map/ppermute | solution.py:356
  166.5 2.3 %collective-permute-done.43.refs_6_ = s16[1040,128]{1,0:T(8,128)(2,1)S(1)} collective-permute-done((s16[1040,128]{1,0:T(8,128)(2,1)S(1)}, s16[1040,128]{1,0:T(8,128)(2,1)S(1)}, u32[]{:S(2)}, u32[]{:S(2)}) %collective-permute-start.43) | collective-permute-done | bytes 266272 | tf_op jit(solution)/shard_map/ppermute | solution.py:356
  169.6 3.8 %marginal.1 = f32[128,7424]{1,0:T(8,128)} custom-call(s32[8]{0:T(128)S(1)} %stack.75.place_ref, s16[1040,128]{1,0:T(8,128)(2,1)S(1)} %combine.4.refs_0_, s16[1040,128]{1,0:T(8,128)(2,1)S(1)} %collective-permute-done.11.refs_1_, s16[1040,128]{1,0:T(8,128)(2,1)S(1)} %collective-permute-done.12.refs_2_, s16[1040,128]{1,0:T(8,128)(2,1)S(1)} %collective-permute-done.13.refs_3_, ...), custom_call_target="tpu_custom_call" | custom-call | flops 3801088 | bytes 5701632 | tf_op jit(solution)/shard_map/marginal/pallas_call | solution.py:249
  173.5 28.3 %covariance.1 = f32[13456,128]{1,0:T(8,128)} custom-call(s32[8]{0:T(128)S(1)} %stack.89.place_ref, s16[912,128]{1,0:T(8,128)(2,1)S(1)} %combine.6.refs_0_, s16[912,128]{1,0:T(8,128)(2,1)} %collective-permute-done.32.refs_1_, s16[912,128]{1,0:T(8,128)(2,1)S(1)} %collective-permute-done.33.refs_2_, s16[912,128]{1,0:T(8,128)(2,1)} %collective-permute-done.34.refs_3_, ...), custom_call_target="tpu_custom_call" | custom-call | flops 3527409664 | bytes 6889472 | tf_op jit(solution)/shard_map/covariance/pallas_call | solution.py:321
  (80 shorter events, 17.0 us)
Async XLA Ops:
  3.2 8.5 %collective-permute-start.24 = (bf16[96,3840]{1,0:T(8,128)(2,1)}, bf16[96,3840]{1,0:T(8,128)(2,1)}, u32[]{:S(2)}, u32[]{:S(2)}) collective-permute-start(bf16[96,3840]{1,0:T(8,128)(2,1)} %get-tuple-element.50), channel_id=1, source_target_pairs={{0,8},{8,0},{16,24},{24,16},{1,9},{9,1},{17,25},{25,17},{2,10},{10... | collective-permute-start | bytes 2211848 | tf_op jit(solution)/shard_map/ppermute | solution.py:356
  3.6 2.4 %copy-start.3 = (s32[128,32]{0,1:T(8,128)S(1)}, s32[128,32]{0,1:T(8,128)}, u32[]{:S(2)}) copy-start(s32[128,32]{0,1:T(8,128)} %param.9) | copy-start | bytes 49156
  3.6 2.4 %copy-start.4 = (s32[128,32]{0,1:T(8,128)S(1)}, s32[128,32]{0,1:T(8,128)}, u32[]{:S(2)}) copy-start(s32[128,32]{0,1:T(8,128)} %param.8) | copy-start | bytes 49156
  5.9 10.3 %collective-permute-start.3 = (bf16[96,3840]{1,0:T(8,128)(2,1)}, bf16[96,3840]{1,0:T(8,128)(2,1)S(1)}, u32[]{:S(2)}, u32[]{:S(2)}) collective-permute-start(bf16[96,3840]{1,0:T(8,128)(2,1)} %get-tuple-element.52), channel_id=1, source_target_pairs={{0,8},{8,0},{16,24},{24,16},{1,9},{9,1},{17,25},{25,17},{2,10},{10... | collective-permute-start | bytes 2211848 | tf_op jit(solution)/shard_map/ppermute | solution.py:356
  6.0 12.6 %collective-permute-start.2 = (s32[64,128]{1,0:T(8,128)S(1)}, s32[64,128]{1,0:T(8,128)S(1)}, u32[]{:S(2)}, u32[]{:S(2)}) collective-permute-start(s32[64,128]{1,0:T(8,128)S(1)} %pad_add_fusion.1), channel_id=1, source_target_pairs={{0,4},{1,5},{2,6},{3,7},{4,0},{5,1},{6,2},{7,3},{8,12},{9,13},{10,... | collective-permute-start | bytes 98312 | tf_op jit(solution)/shard_map/ppermute | solution.py:366
  10.1 9.0 %collective-permute-start.1 = (s32[64,128]{1,0:T(8,128)S(1)}, s32[64,128]{1,0:T(8,128)S(1)}, u32[]{:S(2)}, u32[]{:S(2)}) collective-permute-start(s32[64,128]{1,0:T(8,128)S(1)} %pad_add_fusion.1), channel_id=1, source_target_pairs={{0,6},{1,7},{2,4},{3,5},{4,2},{5,3},{6,0},{7,1},{8,14},{9,15},{10,... | collective-permute-start | bytes 98312 | tf_op jit(solution)/shard_map/ppermute | solution.py:366
  11.5 10.9 %collective-permute-start = (s32[64,128]{1,0:T(8,128)S(1)}, s32[64,128]{1,0:T(8,128)}, u32[]{:S(2)}, u32[]{:S(2)}) collective-permute-start(s32[64,128]{1,0:T(8,128)S(1)} %pad_add_fusion.1), channel_id=1, source_target_pairs={{0,2},{1,3},{2,0},{3,1},{4,6},{5,7},{6,4},{7,5},{8,10},{9,11},{10,... | collective-permute-start | bytes 98312 | tf_op jit(solution)/shard_map/ppermute | solution.py:366
  12.8 11.1 %collective-permute-start.25 = (bf16[192,896]{1,0:T(8,128)(2,1)S(1)}, bf16[192,896]{1,0:T(8,128)(2,1)S(1)}, u32[]{:S(2)}, u32[]{:S(2)}) collective-permute-start(bf16[192,896]{1,0:T(8,128)(2,1)S(1)} %get-tuple-element.44), channel_id=1, source_target_pairs={{0,16},{8,24},{16,0},{24,8},{1,17},{9,25},{17,1},{25,9},{2,18},{10... | collective-permute-start | bytes 1032200 | tf_op jit(solution)/shard_map/ppermute | solution.py:356
  16.2 2.4 %copy-start.2 = (bf16[96,3840]{1,0:T(8,128)(2,1)}, bf16[96,3840]{1,0:T(8,128)(2,1)S(1)}, u32[]{:S(2)}) copy-start(bf16[96,3840]{1,0:T(8,128)(2,1)S(1)} %collective-permute-done.3) | copy-start | bytes 2211844
  16.2 10.8 %collective-permute-start.26 = (bf16[192,896]{1,0:T(8,128)(2,1)S(1)}, bf16[192,896]{1,0:T(8,128)(2,1)S(1)}, u32[]{:S(2)}, u32[]{:S(2)}) collective-permute-start(bf16[192,896]{1,0:T(8,128)(2,1)S(1)} %get-tuple-element.45.refs_0_), channel_id=1, source_target_pairs={{0,1},{1,0},{2,3},{3,2},{4,5},{5,4},{6,7},{7,6},{8,9},{9,8},{10,11... | collective-permute-start | bytes 1032200 | tf_op jit(solution)/shard_map/ppermute | solution.py:362
  18.6 29.4 %collective-permute-start.35 = (bf16[192,1024]{1,0:T(8,128)(2,1)}, bf16[192,1024]{1,0:T(8,128)(2,1)S(1)}, u32[]{:S(2)}, u32[]{:S(2)}) collective-permute-start(bf16[192,1024]{1,0:T(8,128)(2,1)} %get-tuple-element.42), channel_id=1, source_target_pairs={{0,16},{8,24},{16,0},{24,8},{1,17},{9,25},{17,1},{25,9},{2,18},{10... | collective-permute-start | bytes 1179656 | tf_op jit(solution)/shard_map/ppermute | solution.py:356
  19.1 29.4 %collective-permute-start.4 = (bf16[192,1024]{1,0:T(8,128)(2,1)}, bf16[192,1024]{1,0:T(8,128)(2,1)S(1)}, u32[]{:S(2)}, u32[]{:S(2)}) collective-permute-start(bf16[192,1024]{1,0:T(8,128)(2,1)} %get-tuple-element.48), channel_id=1, source_target_pairs={{0,16},{8,24},{16,0},{24,8},{1,17},{9,25},{17,1},{25,9},{2,18},{10... | collective-permute-start | bytes 1179656 | tf_op jit(solution)/shard_map/ppermute | solution.py:356
  22.4 24.1 %collective-permute-start.14 = (bf16[192,896]{1,0:T(8,128)(2,1)}, bf16[192,896]{1,0:T(8,128)(2,1)S(1)}, u32[]{:S(2)}, u32[]{:S(2)}) collective-permute-start(bf16[192,896]{1,0:T(8,128)(2,1)} %get-tuple-element.46), channel_id=1, source_target_pairs={{0,16},{8,24},{16,0},{24,8},{1,17},{9,25},{17,1},{25,9},{2,18},{10... | collective-permute-start | bytes 1032200 | tf_op jit(solution)/shard_map/ppermute | solution.py:356
  23.8 26.2 %collective-permute-start.36 = (bf16[192,1024]{1,0:T(8,128)(2,1)S(1)}, bf16[192,1024]{1,0:T(8,128)(2,1)S(1)}, u32[]{:S(2)}, u32[]{:S(2)}) collective-permute-start(bf16[192,1024]{1,0:T(8,128)(2,1)S(1)} %get-tuple-element.43.refs_0_), channel_id=1, source_target_pairs={{0,1},{1,0},{2,3},{3,2},{4,5},{5,4},{6,7},{7,6},{8,9},{9,8},{10,11... | collective-permute-start | bytes 1179656 | tf_op jit(solution)/shard_map/ppermute | solution.py:362
  27.7 22.9 %collective-permute-start.27 = (bf16[192,896]{1,0:T(8,128)(2,1)S(1)}, bf16[192,896]{1,0:T(8,128)(2,1)}, u32[]{:S(2)}, u32[]{:S(2)}) collective-permute-start(bf16[192,896]{1,0:T(8,128)(2,1)S(1)} %collective-permute-done.25.refs_1_), channel_id=1, source_target_pairs={{0,1},{1,0},{2,3},{3,2},{4,5},{5,4},{6,7},{7,6},{8,9},{9,8},{10,11... | collective-permute-start | bytes 1032200 | tf_op jit(solution)/shard_map/ppermute | solution.py:362
  46.5 14.6 %collective-permute-start.5 = (bf16[192,1024]{1,0:T(8,128)(2,1)S(1)}, bf16[192,1024]{1,0:T(8,128)(2,1)S(1)}, u32[]{:S(2)}, u32[]{:S(2)}) collective-permute-start(bf16[192,1024]{1,0:T(8,128)(2,1)S(1)} %get-tuple-element.49.refs_0_), channel_id=1, source_target_pairs={{0,1},{1,0},{2,3},{3,2},{4,5},{5,4},{6,7},{7,6},{8,9},{9,8},{10,11... | collective-permute-start | bytes 1179656 | tf_op jit(solution)/shard_map/ppermute | solution.py:362
  48.0 19.0 %collective-permute-start.37 = (bf16[192,1024]{1,0:T(8,128)(2,1)S(1)}, bf16[192,1024]{1,0:T(8,128)(2,1)S(1)}, u32[]{:S(2)}, u32[]{:S(2)}) collective-permute-start(bf16[192,1024]{1,0:T(8,128)(2,1)S(1)} %collective-permute-done.35.refs_1_), channel_id=1, source_target_pairs={{0,1},{1,0},{2,3},{3,2},{4,5},{5,4},{6,7},{7,6},{8,9},{9,8},{10,11... | collective-permute-start | bytes 1179656 | tf_op jit(solution)/shard_map/ppermute | solution.py:362
  48.5 26.9 %collective-permute-start.6 = (bf16[192,1024]{1,0:T(8,128)(2,1)S(1)}, bf16[192,1024]{1,0:T(8,128)(2,1)S(1)}, u32[]{:S(2)}, u32[]{:S(2)}) collective-permute-start(bf16[192,1024]{1,0:T(8,128)(2,1)S(1)} %collective-permute-done.4.refs_1_), channel_id=1, source_target_pairs={{0,1},{1,0},{2,3},{3,2},{4,5},{5,4},{6,7},{7,6},{8,9},{9,8},{10,11... | collective-permute-start | bytes 1179656 | tf_op jit(solution)/shard_map/ppermute | solution.py:362
  50.1 32.7 %collective-permute-start.15 = (bf16[192,896]{1,0:T(8,128)(2,1)S(1)}, bf16[192,896]{1,0:T(8,128)(2,1)S(1)}, u32[]{:S(2)}, u32[]{:S(2)}) collective-permute-start(bf16[192,896]{1,0:T(8,128)(2,1)S(1)} %get-tuple-element.47.refs_0_), channel_id=1, source_target_pairs={{0,1},{1,0},{2,3},{3,2},{4,5},{5,4},{6,7},{7,6},{8,9},{9,8},{10,11... | collective-permute-start | bytes 1032200 | tf_op jit(solution)/shard_map/ppermute | solution.py:362
  50.6 37.0 %collective-permute-start.16 = (bf16[192,896]{1,0:T(8,128)(2,1)S(1)}, bf16[192,896]{1,0:T(8,128)(2,1)S(1)}, u32[]{:S(2)}, u32[]{:S(2)}) collective-permute-start(bf16[192,896]{1,0:T(8,128)(2,1)S(1)} %collective-permute-done.14.refs_1_), channel_id=1, source_target_pairs={{0,1},{1,0},{2,3},{3,2},{4,5},{5,4},{6,7},{7,6},{8,9},{9,8},{10,11... | collective-permute-start | bytes 1032200 | tf_op jit(solution)/shard_map/ppermute | solution.py:362
  61.1 31.2 %collective-permute-start.29 = (s16[1824,128]{1,0:T(8,128)(2,1)S(1)}, s16[1824,128]{1,0:T(8,128)(2,1)S(1)}, u32[]{:S(2)}, u32[]{:S(2)}) collective-permute-start(s16[1824,128]{1,0:T(8,128)(2,1)S(1)} %get-tuple-element.34.own_ref), channel_id=1, source_target_pairs={{0,2},{1,3},{6,4},{7,5},{8,10},{9,11},{14,12},{15,13},{16,18},{17,... | collective-permute-start | bytes 1400840 | tf_op jit(solution)/shard_map/ppermute | solution.py:366
  67.0 25.3 %collective-permute-start.28 = (s16[912,128]{1,0:T(8,128)(2,1)S(1)}, s16[912,128]{1,0:T(8,128)(2,1)S(1)}, u32[]{:S(2)}, u32[]{:S(2)}) collective-permute-start(s16[912,128]{1,0:T(8,128)(2,1)S(1)} %get-tuple-element.33), channel_id=1, source_target_pairs={{0,2},{1,3},{2,0},{3,1},{4,6},{5,7},{6,4},{7,5},{8,10},{9,11},{10,... | collective-permute-start | bytes 700424 | tf_op jit(solution)/shard_map/ppermute | solution.py:366
  75.4 47.2 %collective-permute-start.39 = (s16[2080,128]{1,0:T(8,128)(2,1)S(1)}, s16[2080,128]{1,0:T(8,128)(2,1)S(1)}, u32[]{:S(2)}, u32[]{:S(2)}) collective-permute-start(s16[2080,128]{1,0:T(8,128)(2,1)S(1)} %get-tuple-element.39.own_ref), channel_id=1, source_target_pairs={{0,2},{1,3},{6,4},{7,5},{8,10},{9,11},{14,12},{15,13},{16,18},{17,... | collective-permute-start | bytes 1597448 | tf_op jit(solution)/shard_map/ppermute | solution.py:366
  82.8 38.0 %collective-permute-start.8 = (s16[2080,128]{1,0:T(8,128)(2,1)S(1)}, s16[2080,128]{1,0:T(8,128)(2,1)S(1)}, u32[]{:S(2)}, u32[]{:S(2)}) collective-permute-start(s16[2080,128]{1,0:T(8,128)(2,1)S(1)} %get-tuple-element.24.own_ref), channel_id=1, source_target_pairs={{0,2},{1,3},{6,4},{7,5},{8,10},{9,11},{14,12},{15,13},{16,18},{17,... | collective-permute-start | bytes 1597448 | tf_op jit(solution)/shard_map/ppermute | solution.py:366
  89.0 28.9 %collective-permute-start.18 = (s16[1824,128]{1,0:T(8,128)(2,1)S(1)}, s16[1824,128]{1,0:T(8,128)(2,1)S(1)}, u32[]{:S(2)}, u32[]{:S(2)}) collective-permute-start(s16[1824,128]{1,0:T(8,128)(2,1)S(1)} %get-tuple-element.29.own_ref), channel_id=1, source_target_pairs={{0,2},{1,3},{6,4},{7,5},{8,10},{9,11},{14,12},{15,13},{16,18},{17,... | collective-permute-start | bytes 1400840 | tf_op jit(solution)/shard_map/ppermute | solution.py:366
  92.2 25.0 %collective-permute-start.17 = (s16[912,128]{1,0:T(8,128)(2,1)S(1)}, s16[912,128]{1,0:T(8,128)(2,1)S(1)}, u32[]{:S(2)}, u32[]{:S(2)}) collective-permute-start(s16[912,128]{1,0:T(8,128)(2,1)S(1)} %get-tuple-element.28), channel_id=1, source_target_pairs={{0,2},{1,3},{2,0},{3,1},{4,6},{5,7},{6,4},{7,5},{8,10},{9,11},{10,... | collective-permute-start | bytes 700424 | tf_op jit(solution)/shard_map/ppermute | solution.py:366
  92.3 27.8 %collective-permute-start.7 = (s16[1040,128]{1,0:T(8,128)(2,1)S(1)}, s16[1040,128]{1,0:T(8,128)(2,1)S(1)}, u32[]{:S(2)}, u32[]{:S(2)}) collective-permute-start(s16[1040,128]{1,0:T(8,128)(2,1)S(1)} %get-tuple-element.23), channel_id=1, source_target_pairs={{0,2},{1,3},{2,0},{3,1},{4,6},{5,7},{6,4},{7,5},{8,10},{9,11},{10,... | collective-permute-start | bytes 798728 | tf_op jit(solution)/shard_map/ppermute | solution.py:366
  117.2 6.0 %collective-permute-start.30 = (s16[912,128]{1,0:T(8,128)(2,1)S(1)}, s16[912,128]{1,0:T(8,128)(2,1)S(1)}, u32[]{:S(2)}, u32[]{:S(2)}) collective-permute-start(s16[912,128]{1,0:T(8,128)(2,1)S(1)} %get-tuple-element.35), channel_id=1, source_target_pairs={{2,4},{3,5},{4,2},{5,3},{10,12},{11,13},{12,10},{13,11},{18,20},{1... | collective-permute-start | bytes 700424 | tf_op jit(solution)/shard_map/ppermute | solution.py:366
  117.9 16.8 %collective-permute-start.31 = (s16[912,128]{1,0:T(8,128)(2,1)S(1)}, s16[912,128]{1,0:T(8,128)(2,1)S(1)}, u32[]{:S(2)}, u32[]{:S(2)}) collective-permute-start(s16[912,128]{1,0:T(8,128)(2,1)S(1)} %get-tuple-element.36), channel_id=1, source_target_pairs={{2,6},{3,7},{4,0},{5,1},{10,14},{11,15},{12,8},{13,9},{18,22},{19,... | collective-permute-start | bytes 700424 | tf_op jit(solution)/shard_map/ppermute | solution.py:366
  120.1 15.1 %collective-permute-start.19 = (s16[912,128]{1,0:T(8,128)(2,1)S(1)}, s16[912,128]{1,0:T(8,128)(2,1)S(1)}, u32[]{:S(2)}, u32[]{:S(2)}) collective-permute-start(s16[912,128]{1,0:T(8,128)(2,1)S(1)} %get-tuple-element.30), channel_id=1, source_target_pairs={{2,4},{3,5},{4,2},{5,3},{10,12},{11,13},{12,10},{13,11},{18,20},{1... | collective-permute-start | bytes 700424 | tf_op jit(solution)/shard_map/ppermute | solution.py:366
  120.8 24.0 %collective-permute-start.20 = (s16[912,128]{1,0:T(8,128)(2,1)S(1)}, s16[912,128]{1,0:T(8,128)(2,1)S(1)}, u32[]{:S(2)}, u32[]{:S(2)}) collective-permute-start(s16[912,128]{1,0:T(8,128)(2,1)S(1)} %get-tuple-element.31), channel_id=1, source_target_pairs={{2,6},{3,7},{4,0},{5,1},{10,14},{11,15},{12,8},{13,9},{18,22},{19,... | collective-permute-start | bytes 700424 | tf_op jit(solution)/shard_map/ppermute | solution.py:366
  122.6 24.0 %collective-permute-start.9 = (s16[1040,128]{1,0:T(8,128)(2,1)S(1)}, s16[1040,128]{1,0:T(8,128)(2,1)S(1)}, u32[]{:S(2)}, u32[]{:S(2)}) collective-permute-start(s16[1040,128]{1,0:T(8,128)(2,1)S(1)} %get-tuple-element.25), channel_id=1, source_target_pairs={{2,4},{3,5},{4,2},{5,3},{10,12},{11,13},{12,10},{13,11},{18,20},{1... | collective-permute-start | bytes 798728 | tf_op jit(solution)/shard_map/ppermute | solution.py:366
  123.3 32.1 %collective-permute-start.10 = (s16[1040,128]{1,0:T(8,128)(2,1)S(1)}, s16[1040,128]{1,0:T(8,128)(2,1)S(1)}, u32[]{:S(2)}, u32[]{:S(2)}) collective-permute-start(s16[1040,128]{1,0:T(8,128)(2,1)S(1)} %get-tuple-element.26), channel_id=1, source_target_pairs={{2,6},{3,7},{4,0},{5,1},{10,14},{11,15},{12,8},{13,9},{18,22},{19,... | collective-permute-start | bytes 798728 | tf_op jit(solution)/shard_map/ppermute | solution.py:366
  134.7 22.6 %collective-permute-start.38 = (s16[1040,128]{1,0:T(8,128)(2,1)S(1)}, s16[1040,128]{1,0:T(8,128)(2,1)S(1)}, u32[]{:S(2)}, u32[]{:S(2)}) collective-permute-start(s16[1040,128]{1,0:T(8,128)(2,1)S(1)} %get-tuple-element.38), channel_id=1, source_target_pairs={{0,2},{1,3},{2,0},{3,1},{4,6},{5,7},{6,4},{7,5},{8,10},{9,11},{10,... | collective-permute-start | bytes 798728 | tf_op jit(solution)/shard_map/ppermute | solution.py:366
  135.2 22.7 %collective-permute-start.40 = (s16[1040,128]{1,0:T(8,128)(2,1)S(1)}, s16[1040,128]{1,0:T(8,128)(2,1)S(1)}, u32[]{:S(2)}, u32[]{:S(2)}) collective-permute-start(s16[1040,128]{1,0:T(8,128)(2,1)S(1)} %get-tuple-element.40), channel_id=1, source_target_pairs={{2,4},{3,5},{4,2},{5,3},{10,12},{11,13},{12,10},{13,11},{18,20},{1... | collective-permute-start | bytes 798728 | tf_op jit(solution)/shard_map/ppermute | solution.py:366
  144.8 16.4 %collective-permute-start.41 = (s16[1040,128]{1,0:T(8,128)(2,1)S(1)}, s16[1040,128]{1,0:T(8,128)(2,1)S(1)}, u32[]{:S(2)}, u32[]{:S(2)}) collective-permute-start(s16[1040,128]{1,0:T(8,128)(2,1)S(1)} %get-tuple-element.41), channel_id=1, source_target_pairs={{2,6},{3,7},{4,0},{5,1},{10,14},{11,15},{12,8},{13,9},{18,22},{19,... | collective-permute-start | bytes 798728 | tf_op jit(solution)/shard_map/ppermute | solution.py:366
  146.6 16.5 %collective-permute-start.33 = (s16[912,128]{1,0:T(8,128)(2,1)S(1)}, s16[912,128]{1,0:T(8,128)(2,1)S(1)}, u32[]{:S(2)}, u32[]{:S(2)}) collective-permute-start(s16[912,128]{1,0:T(8,128)(2,1)S(1)} %combine.6.refs_0_), channel_id=1, source_target_pairs={{0,16},{8,24},{16,0},{24,8},{1,17},{9,25},{17,1},{25,9},{2,18},{10... | collective-permute-start | bytes 700424 | tf_op jit(solution)/shard_map/ppermute | solution.py:356
  155.4 8.2 %collective-permute-start.22 = (s16[912,128]{1,0:T(8,128)(2,1)S(1)}, s16[912,128]{1,0:T(8,128)(2,1)S(1)}, u32[]{:S(2)}, u32[]{:S(2)}) collective-permute-start(s16[912,128]{1,0:T(8,128)(2,1)S(1)} %combine.5.refs_4_), channel_id=1, source_target_pairs={{0,16},{8,24},{16,0},{24,8},{1,17},{9,25},{17,1},{25,9},{2,18},{10... | collective-permute-start | bytes 700424 | tf_op jit(solution)/shard_map/ppermute | solution.py:356
  157.3 8.7 %collective-permute-start.12 = (s16[1040,128]{1,0:T(8,128)(2,1)S(1)}, s16[1040,128]{1,0:T(8,128)(2,1)S(1)}, u32[]{:S(2)}, u32[]{:S(2)}) collective-permute-start(s16[1040,128]{1,0:T(8,128)(2,1)S(1)} %combine.4.refs_0_), channel_id=1, source_target_pairs={{0,16},{8,24},{16,0},{24,8},{1,17},{9,25},{17,1},{25,9},{2,18},{10... | collective-permute-start | bytes 798728 | tf_op jit(solution)/shard_map/ppermute | solution.py:356
  161.5 7.4 %collective-permute-start.43 = (s16[1040,128]{1,0:T(8,128)(2,1)S(1)}, s16[1040,128]{1,0:T(8,128)(2,1)S(1)}, u32[]{:S(2)}, u32[]{:S(2)}) collective-permute-start(s16[1040,128]{1,0:T(8,128)(2,1)S(1)} %combine.7.refs_4_), channel_id=1, source_target_pairs={{0,16},{8,24},{16,0},{24,8},{1,17},{9,25},{17,1},{25,9},{2,18},{10... | collective-permute-start | bytes 798728 | tf_op jit(solution)/shard_map/ppermute | solution.py:356
  163.1 5.8 %collective-permute-start.11 = (s16[1040,128]{1,0:T(8,128)(2,1)S(1)}, s16[1040,128]{1,0:T(8,128)(2,1)S(1)}, u32[]{:S(2)}, u32[]{:S(2)}) collective-permute-start(s16[1040,128]{1,0:T(8,128)(2,1)S(1)} %combine.4.refs_0_), channel_id=1, source_target_pairs={{0,8},{8,0},{16,24},{24,16},{1,9},{9,1},{17,25},{25,17},{2,10},{10... | collective-permute-start | bytes 798728 | tf_op jit(solution)/shard_map/ppermute | solution.py:356
  163.1 2.9 %collective-permute-start.21 = (s16[912,128]{1,0:T(8,128)(2,1)S(1)}, s16[912,128]{1,0:T(8,128)(2,1)S(1)}, u32[]{:S(2)}, u32[]{:S(2)}) collective-permute-start(s16[912,128]{1,0:T(8,128)(2,1)S(1)} %combine.5.refs_4_), channel_id=1, source_target_pairs={{0,8},{8,0},{16,24},{24,16},{1,9},{9,1},{17,25},{25,17},{2,10},{10... | collective-permute-start | bytes 700424 | tf_op jit(solution)/shard_map/ppermute | solution.py:356
  163.6 5.8 %collective-permute-start.23 = (s16[912,128]{1,0:T(8,128)(2,1)S(1)}, s16[912,128]{1,0:T(8,128)(2,1)S(1)}, u32[]{:S(2)}, u32[]{:S(2)}) collective-permute-start(s16[912,128]{1,0:T(8,128)(2,1)S(1)} %collective-permute-done.22.refs_6_), channel_id=1, source_target_pairs={{0,8},{8,0},{16,24},{24,16},{1,9},{9,1},{17,25},{25,17},{2,10},{10... | collective-permute-start | bytes 700424 | tf_op jit(solution)/shard_map/ppermute | solution.py:356
  166.0 3.6 %collective-permute-start.13 = (s16[1040,128]{1,0:T(8,128)(2,1)S(1)}, s16[1040,128]{1,0:T(8,128)(2,1)S(1)}, u32[]{:S(2)}, u32[]{:S(2)}) collective-permute-start(s16[1040,128]{1,0:T(8,128)(2,1)S(1)} %collective-permute-done.12.refs_2_), channel_id=1, source_target_pairs={{0,8},{8,0},{16,24},{24,16},{1,9},{9,1},{17,25},{25,17},{2,10},{10... | collective-permute-start | bytes 798728 | tf_op jit(solution)/shard_map/ppermute | solution.py:356
  166.0 7.4 %collective-permute-start.42 = (s16[1040,128]{1,0:T(8,128)(2,1)S(1)}, s16[1040,128]{1,0:T(8,128)(2,1)S(1)}, u32[]{:S(2)}, u32[]{:S(2)}) collective-permute-start(s16[1040,128]{1,0:T(8,128)(2,1)S(1)} %combine.7.refs_4_), channel_id=1, source_target_pairs={{0,8},{8,0},{16,24},{24,16},{1,9},{9,1},{17,25},{25,17},{2,10},{10... | collective-permute-start | bytes 798728 | tf_op jit(solution)/shard_map/ppermute | solution.py:356
  168.9 4.6 %collective-permute-start.44 = (s16[1040,128]{1,0:T(8,128)(2,1)S(1)}, s16[1040,128]{1,0:T(8,128)(2,1)S(1)}, u32[]{:S(2)}, u32[]{:S(2)}) collective-permute-start(s16[1040,128]{1,0:T(8,128)(2,1)S(1)} %collective-permute-done.43.refs_6_), channel_id=1, source_target_pairs={{0,8},{8,0},{16,24},{24,16},{1,9},{9,1},{17,25},{25,17},{2,10},{10... | collective-permute-start | bytes 798728 | tf_op jit(solution)/shard_map/ppermute | solution.py:356
  168.9 4.6 %collective-permute-start.32 = (s16[912,128]{1,0:T(8,128)(2,1)S(1)}, s16[912,128]{1,0:T(8,128)(2,1)}, u32[]{:S(2)}, u32[]{:S(2)}) collective-permute-start(s16[912,128]{1,0:T(8,128)(2,1)S(1)} %combine.6.refs_0_), channel_id=1, source_target_pairs={{0,8},{8,0},{16,24},{24,16},{1,9},{9,1},{17,25},{25,17},{2,10},{10... | collective-permute-start | bytes 700424 | tf_op jit(solution)/shard_map/ppermute | solution.py:356
  169.4 4.1 %collective-permute-start.34 = (s16[912,128]{1,0:T(8,128)(2,1)S(1)}, s16[912,128]{1,0:T(8,128)(2,1)}, u32[]{:S(2)}, u32[]{:S(2)}) collective-permute-start(s16[912,128]{1,0:T(8,128)(2,1)S(1)} %collective-permute-done.33.refs_2_), channel_id=1, source_target_pairs={{0,8},{8,0},{16,24},{24,16},{1,9},{9,1},{17,25},{25,17},{2,10},{10... | collective-permute-start | bytes 700424 | tf_op jit(solution)/shard_map/ppermute | solution.py:356
  (2 other events, 1.7 us)

commit v3 on v2

--- a/solution.py
+++ b/solution.py
@@ -22,6 +22,10 @@
 
 def cost(flops, moved):
     return pl.CostEstimate(flops=flops, bytes_accessed=moved, transcendentals=0)
+
+
+def after(value, *others):
+    return lax.optimization_barrier((value, *others))[0]
 
 
 def twice(value):
@@ -282,7 +286,7 @@
         age_ref[pl.ds(2 * t + 1, LANES, stride=pitch), :] = jnp.where(left, swapped, value)
         return carry
 
-    lax.fori_loop(0, ages * rank // LANES, turn, 0)
+    lax.fori_loop(0, ages * rank // LANES, turn, 0, unroll=True)
 
     def outer(d, carry):
         start = pl.multiple_of(d * pitch, 8)
@@ -299,7 +303,7 @@
         cov_ref[pl.ds(start, pitch), :] = product[:pitch]
         return carry
 
-    lax.fori_loop(0, LANES, outer, 0, unroll=4)
+    lax.fori_loop(0, LANES, outer, 0, unroll=16)
 
     def store(m, carry):
         base = pl.multiple_of(m * (2 * ages), 8)
@@ -308,7 +312,7 @@
             out_ref[pl.ds(base + p * ages, ages), :] = value[:ages]
         return carry
 
-    lax.fori_loop(0, ages // 2, store, 0)
+    lax.fori_loop(0, ages // 2, store, 0, unroll=True)
     for i in range(ages):
         row = i * (ages + 1)
         out_ref[row:row + 1, :] += load_ref[(total - 1) * LANES + i:(total - 1) * LANES + i + 1, :]
@@ -391,29 +395,37 @@
     variances = jnp.pad(variances, ((0, 0), (0, -ages % LANES)))
     loads = jnp.concatenate([factors, variances], axis=1)
 
-    def halves(array):
+    def half(array, c):
         total = array.shape[1] // LANES
         width = -(-total // groups) * xs
-
-        def half(c):
-            return lax.dynamic_slice(array, (0, jnp.where(c == 0, 0, total - width) * LANES), (rows, width * LANES))
-
-        return jnp.concatenate([half(core), geo_shift(half(1 - core), 0, 1)], axis=0)
-
-    def collect(both, first, count, each, has_var):
-        def part(group):
-            return lax.dynamic_slice(
-                both, (0, (group * each + first) * LANES), (both.shape[0], count * LANES)
-            )
-        by_x = [geo_shift(part((x + dx) % xs), dx, 0) for dx in range(xs)]
-        data = [y_shift(value, dy) for dy in range(ys) for value in by_x]
-        own, close, far = partial_sums(flag, w, data, has_var)
+        return lax.dynamic_slice(array, (0, jnp.where(c == 0, 0, total - width) * LANES), (rows, width * LANES))
+
+    def swap(array):
+        return geo_shift(half(array, 1 - core), 0, 1)
+
+    def part(both, group, each, first, count):
+        return lax.dynamic_slice(both, (0, (group * each + first) * LANES), (both.shape[0], count * LANES))
+
+    def along_x(both, chunk, *done):
+        mine = part(both, x, *chunk)
+        others = [geo_shift(after(part(both, (x + dx) % xs, *chunk), *done), dx, 0) for dx in range(1, xs)]
+        return [mine] + others
+
+    def along_y(by_x, *done):
+        mine = [after(by_x[0], *done)] + by_x[1:]
+        return mine + [y_shift(value, dy) for dy in range(1, ys) for value in mine]
+
+    def along_z(data, has_var, *done):
+        own, close, far = partial_sums(flag, after(w, *done), data, has_var)
         far_in = z_send(far, ((0, 1), (3, 2)))
         close_in = z_send(close, near)
         to_middle, to_end = middle(far, far_in)
         middle_in = z_send(to_middle, ((1, 2), (2, 1)))
         end_in = z_send(to_end, ((1, 3), (2, 0)))
-        mine = combine(own, [close_in, middle_in, end_in])
+        return far, own, [close_in, middle_in, end_in]
+
+    def spread(own, others, *done):
+        mine = combine(after(own, *done), others)
         along = [geo_shift(mine, dx, 0) for dx in range(xs)]
         return [geo_shift(along[dx], 0, dc) for dx in range(xs) for dc in range(CORES)]
 
@@ -435,18 +447,29 @@
     load_each, mean_each = -(-load_total // groups), -(-mean_total // groups)
     load_tiles = split(load_each)
     mean_tiles = split(mean_each)[::-1]
-    load_half = halves(loads)
-    mean_half = halves(estimates)
+
+    def chunks(each, tiles):
+        return [(each, sum(tiles[:i]), count) for i, count in enumerate(tiles)]
+
+    load_chunks, mean_chunks = chunks(load_each, load_tiles), chunks(mean_each, mean_tiles)
+    load_both = jnp.concatenate([half(loads, core), swap(loads)], axis=0)
+    by_x, by_y, by_z = [], [], []
+    for chunk in load_chunks:
+        by_x.append(along_x(load_both, chunk, *by_x[-1:], queries))
+    mean_both = jnp.concatenate([half(estimates, core), swap(after(estimates, by_x[0]))], axis=0)
+    for chunk in mean_chunks:
+        by_x.append(along_x(mean_both, chunk, *by_x[-1:]))
+    for values in by_x:
+        by_y.append(along_y(values, *by_y[-1:]))
+    for i, values in enumerate(by_y):
+        done = [far for far, _, _ in by_z[-1:]]
+        by_z.append(along_z(values, i == len(load_chunks) - 1, *done))
     load_pieces, mean_pieces = [], []
-    first = 0
-    for i, count in enumerate(load_tiles):
-        load_pieces += collect(load_half, first, count, load_each, i == len(load_tiles) - 1)
-        first += count
-    first = 0
-    for count in mean_tiles:
-        mean_pieces += collect(mean_half, first, count, mean_each, False)
-        first += count
+    for _, own, others in by_z[:len(load_chunks)]:
+        load_pieces += spread(own, others, *load_pieces[:1])
     cov = covariance(places(load_total), load_pieces, load_tiles, load_total, ages, rank)
+    for _, own, others in by_z[len(load_chunks):]:
+        mean_pieces += spread(own, others, cov, *mean_pieces[:1])
     mean = marginal(places(mean_total), mean_pieces, mean_tiles, mean_total)
     return mean, cov.T
 

time: 202 us -> 169 us (0.84)
  waiting for transfers between devices: 87.7 us -> 69 us
  Pallas kernels: 47 us -> 35.3 us
  starting transfers between devices: 52.9 us -> 48.2 us
    ppermute x19, waiting for transfers between devices: 52.2 us -> 20.6 us  [z_send(): return lax.ppermute(value, 'dist', perm)]
    pallas_call x1, Pallas kernels: 28.3 us -> 13.2 us  [covariance(): pl.pallas_call(functools.partial(covariance_kernel, tiles, total, ages, r...]
    ppermute x8, waiting for transfers between devices: 12.9 us -> 24.7 us  [y_shift(): return lax.ppermute(value, 'dist', perm)]
    ppermute x19, starting transfers between devices: 30.9 us -> 27.3 us  [z_send(): return lax.ppermute(value, 'dist', perm)]
    unnamed x10 -> x36, local copies, waits for them, and re-layouts: 1.71 us -> 4.87 us
    pallas_call x4, Pallas kernels: 1.28 us -> 3.7 us  [combine(): pl.pallas_call(combine_kernel, out_shape=jax.ShapeDtypeStruct(shape, jnp....]
    ppermute x8, starting transfers between devices: 10.4 us -> 8.1 us  [y_shift(): return lax.ppermute(value, 'dist', perm)]
  transfers between devices with their start and end apart: 45 -> 45, of which waited for: 15 -> 15; matrix products, arithmetic and copies ran while one was open for 4% -> 3% of each run, Pallas kernels for 9% -> 19%
where the time goes in v3:
time: 169 us; the launch traced here: 167 us
  waiting for transfers between devices  69 us (41%)
  starting transfers between devices  48.2 us (29%)
  Pallas kernels  35.3 us (21%)
  local copies, waits for them, and re-layouts  7.19 us (4%)
  other arithmetic  6.48 us (4%)
    ppermute x19, starting transfers between devices, z_send(): return lax.ppermute(value, 'dist', perm)  27.3 us
    ppermute x8, waiting for transfers between devices, y_shift(): return lax.ppermute(value, 'dist', perm)  24.7 us
    ppermute x18, waiting for transfers between devices, geo_shift(): return lax.ppermute(value, 'geo', perm)  23.6 us
    ppermute x19, waiting for transfers between devices, z_send(): return lax.ppermute(value, 'dist', perm)  20.6 us
    pallas_call x1, Pallas kernels, covariance(): pl.pallas_call(functools.partial(covariance_kernel, tiles, total, ages, r...  13.2 us
    ppermute x18, starting transfers between devices, geo_shift(): return lax.ppermute(value, 'geo', perm)  12.7 us
    ppermute x8, starting transfers between devices, y_shift(): return lax.ppermute(value, 'dist', perm)  8.1 us
    pallas_call x4, Pallas kernels, partial_sums(): pl.pallas_call(functools.partial(sums_kernel, parts, has_var), grid_spec=...  7.89 us
  transfers between devices with their start and end apart: 45, of which 15 were waited for; matrix products, arithmetic and copies ran while one was open for 3% of the time, Pallas kernels for 19%

profile of v3, /device:TPU:0, one launch (start us, length us, event | category | flops | bytes accessed | tf_op | source)
XLA Modules:
  0.0 167.2 jit_solution(13224932935535386478)
XLA Ops:
  0.7 1.6 fusion.1
  3.7 3.7 %collective-permute-start.2 = (s32[64,128]{1,0:T(8,128)S(1)}, s32[64,128]{1,0:T(8,128)S(1)}, u32[]{:S(2)}, u32[]{:S(2)}) collective-permute-start(s32[64,128]{1,0:T(8,128)S(1)} %pad_add_fusion.1), channel_id=1, source_target_pairs={{0,4},{1,5},{2,6},{3,7},{4,0},{5,1},{6,2},{7,3},{8,12},{9,13},{10,... | collective-permute-start | bytes 98312 | tf_op jit(solution)/shard_map/ppermute | solution.py:370
  7.4 1.3 collective-permute-start.1
  9.5 3.7 %collective-permute-done.1 = s32[64,128]{1,0:T(8,128)S(1)} collective-permute-done((s32[64,128]{1,0:T(8,128)S(1)}, s32[64,128]{1,0:T(8,128)S(1)}, u32[]{:S(2)}, u32[]{:S(2)}) %collective-permute-start.1) | collective-permute-done | bytes 32800 | tf_op jit(solution)/shard_map/ppermute | solution.py:370
  14.2 1.5 collective-permute-start.4
  15.7 7.8 %collective-permute-done.4.refs_1_ = bf16[192,896]{1,0:T(8,128)(2,1)S(1)} collective-permute-done((bf16[192,896]{1,0:T(8,128)(2,1)}, bf16[192,896]{1,0:T(8,128)(2,1)S(1)}, u32[]{:S(2)}, u32[]{:S(2)}) %collective-permute-start.4) | collective-permute-done | bytes 344096 | tf_op jit(solution)/shard_map/ppermute | solution.py:360
  24.5 1.5 collective-permute-start.5
  26.1 1.1 fusion.4
  27.2 1.6 collective-permute-start.7
  29.3 6.1 %collective-permute-done.5.refs_2_ = bf16[192,896]{1,0:T(8,128)(2,1)S(1)} collective-permute-done((bf16[192,896]{1,0:T(8,128)(2,1)S(1)}, bf16[192,896]{1,0:T(8,128)(2,1)S(1)}, u32[]{:S(2)}, u32[]{:S(2)}) %collective-permute-start.5) | collective-permute-done | bytes 344096 | tf_op jit(solution)/shard_map/ppermute | solution.py:366
  35.4 7.0 %collective-permute-done.6.refs_3_ = bf16[192,896]{1,0:T(8,128)(2,1)S(1)} collective-permute-done((bf16[192,896]{1,0:T(8,128)(2,1)S(1)}, bf16[192,896]{1,0:T(8,128)(2,1)S(1)}, u32[]{:S(2)}, u32[]{:S(2)}) %collective-permute-start.6) | collective-permute-done | bytes 344096 | tf_op jit(solution)/shard_map/ppermute | solution.py:366
  42.4 1.5 collective-permute-start.8
  44.4 1.8 %fusion.3 = (bf16[192,1024]{1,0:T(8,128)(2,1)}, bf16[192,1024]{1,0:T(8,128)(2,1)S(1)}) fusion(s32[]{:T(128)S(6)} %select_n.214, bf16[96,3840]{1,0:T(8,128)(2,1)S(1)} %constant_dynamic-slice_fusion.1, bf16[96,3840]{1,0:T(8,128)(2,1)} %collective-permute-done.10, s32[]{:T(128)S(6)} %select_n.212), kind=kLoop, calls=%fused_computation.20 | loop fusion | flops 1572864 | bytes 2261000 | tf_op jit(solution)/shard_map/concatenate | solution.py:459
  46.3 1.6 collective-permute-start.11
  47.9 4.8 %build_weights.1.w_ref = bf16[768,512]{1,0:T(8,128)(2,1)S(1)} custom-call(s32[8]{0:T(128)S(1)} %stack.84.base_ref, s32[64,512]{1,0:T(8,128)S(1)} %pad_add_fusion.query_ref), custom_call_target="tpu_custom_call" | custom-call | flops 25165824 | bytes 786432 | tf_op jit(solution)/shard_map/build_weights/pallas_call | solution.py:86
  55.7 1.4 partial_sums.4
  57.1 1.8 %collective-permute-start.15 = (s16[1824,128]{1,0:T(8,128)(2,1)S(1)}, s16[1824,128]{1,0:T(8,128)(2,1)S(1)}, u32[]{:S(2)}, u32[]{:S(2)}) collective-permute-start(s16[1824,128]{1,0:T(8,128)(2,1)S(1)} %get-tuple-element.37.own_ref), channel_id=1, source_target_pairs={{0,2},{1,3},{6,4},{7,5},{8,10},{9,11},{14,12},{15,13},{16,18},{17,... | collective-permute-start | bytes 1400840 | tf_op jit(solution)/shard_map/ppermute | solution.py:370
  58.8 1.1 fusion.6
  59.9 1.7 %collective-permute-done.9.refs_3_ = bf16[192,1024]{1,0:T(8,128)(2,1)} collective-permute-done((bf16[192,1024]{1,0:T(8,128)(2,1)}, bf16[192,1024]{1,0:T(8,128)(2,1)}, u32[]{:S(2)}, u32[]{:S(2)}) %collective-permute-start.9) | collective-permute-done | bytes 393248 | tf_op jit(solution)/shard_map/ppermute | solution.py:366
  61.7 1.5 collective-permute-start.12
  63.2 1.5 collective-permute-start.35
  65.2 2.9 %partial_sums.5 = (f32[1024,128]{1,0:T(8,128)S(1)}, s16[1040,128]{1,0:T(8,128)(2,1)S(1)}, s16[2080,128]{1,0:T(8,128)(2,1)S(1)}) custom-call(s32[1]{0:T(128)} %bitcast.6.flag_ref, bf16[768,512]{1,0:T(8,128)(2,1)S(1)} %build_weights.1.w_ref, bf16[192,1024]{1,0:T(8,128)(2,1)S(1)} %get-tuple-element.39.refs_0_, ...), custom_call_target="tpu_custom_call" | custom-call | flops 805306368 | bytes 2883584 | tf_op jit(solution)/shard_map/partial_sums/pallas_call | solution.py:160
  68.1 1.8 %collective-permute-start.22 = (s16[2080,128]{1,0:T(8,128)(2,1)S(1)}, s16[2080,128]{1,0:T(8,128)(2,1)S(1)}, u32[]{:S(2)}, u32[]{:S(2)}) collective-permute-start(s16[2080,128]{1,0:T(8,128)(2,1)S(1)} %get-tuple-element.41.own_ref), channel_id=1, source_target_pairs={{0,2},{1,3},{6,4},{7,5},{8,10},{9,11},{14,12},{15,13},{16,18},{17,... | collective-permute-start | bytes 1597448 | tf_op jit(solution)/shard_map/ppermute | solution.py:370
  69.8 1.9 %collective-permute-done.35.refs_1_ = bf16[192,896]{1,0:T(8,128)(2,1)S(1)} collective-permute-done((bf16[192,896]{1,0:T(8,128)(2,1)S(1)}, bf16[192,896]{1,0:T(8,128)(2,1)S(1)}, u32[]{:S(2)}, u32[]{:S(2)}) %collective-permute-start.35) | collective-permute-done | bytes 344096 | tf_op jit(solution)/shard_map/ppermute | solution.py:360
  72.2 1.5 collective-permute-done.12.refs_2_
  73.7 8.4 %collective-permute-done.13.refs_3_ = bf16[192,1024]{1,0:T(8,128)(2,1)S(1)} collective-permute-done((bf16[192,1024]{1,0:T(8,128)(2,1)S(1)}, bf16[192,1024]{1,0:T(8,128)(2,1)S(1)}, u32[]{:S(2)}, u32[]{:S(2)}) %collective-permute-start.13) | collective-permute-done | bytes 393248 | tf_op jit(solution)/shard_map/ppermute | solution.py:366
  82.1 1.5 collective-permute-start.36
  84.8 1.3 collective-permute-start.17
  86.6 8.2 %collective-permute-done.14.refs_0_ = s16[912,128]{1,0:T(8,128)(2,1)S(1)} collective-permute-done((s16[912,128]{1,0:T(8,128)(2,1)S(1)}, s16[912,128]{1,0:T(8,128)(2,1)S(1)}, u32[]{:S(2)}, u32[]{:S(2)}) %collective-permute-start.14) | collective-permute-done | bytes 233504 | tf_op jit(solution)/shard_map/ppermute | solution.py:370
  95.4 1.3 collective-permute-start.24
  96.7 2.3 %partial_sums.6 = (f32[1024,128]{1,0:T(8,128)S(1)}, s16[1040,128]{1,0:T(8,128)(2,1)}, s16[2080,128]{1,0:T(8,128)(2,1)S(1)}) custom-call(s32[1]{0:T(128)} %bitcast.6.flag_ref, bf16[768,512]{1,0:T(8,128)(2,1)S(1)} %build_weights.1.w_ref, bf16[192,1024]{1,0:T(8,128)(2,1)S(1)} %get-tuple-element.44.refs_0_, ...), custom_call_target="tpu_custom_call" | custom-call | flops 805306368 | bytes 2883584 | tf_op jit(solution)/shard_map/partial_sums/pallas_call | solution.py:160
  99.0 6.6 %collective-permute-start.29 = (s16[2080,128]{1,0:T(8,128)(2,1)S(1)}, s16[2080,128]{1,0:T(8,128)(2,1)S(1)}, u32[]{:S(2)}, u32[]{:S(2)}) collective-permute-start(s16[2080,128]{1,0:T(8,128)(2,1)S(1)} %get-tuple-element.58.own_ref), channel_id=1, source_target_pairs={{0,2},{1,3},{6,4},{7,5},{8,10},{9,11},{14,12},{15,13},{16,18},{17,... | collective-permute-start | bytes 1597448 | tf_op jit(solution)/shard_map/ppermute | solution.py:370
  105.6 1.4 partial_sums.7
  107.1 1.5 collective-permute-start.39
  110.6 1.5 collective-permute-start.26
  112.7 7.2 %collective-permute-done.19.refs_2_ = s16[912,128]{1,0:T(8,128)(2,1)} collective-permute-done((s16[912,128]{1,0:T(8,128)(2,1)}, s16[912,128]{1,0:T(8,128)(2,1)}, u32[]{:S(2)}, u32[]{:S(2)}) %collective-permute-start.19) | collective-permute-done | bytes 233504 | tf_op jit(solution)/shard_map/ppermute | solution.py:360
  120.5 2.5 %collective-permute-done.39.other_ref = s16[1824,128]{1,0:T(8,128)(2,1)S(1)} collective-permute-done((s16[1824,128]{1,0:T(8,128)(2,1)S(1)}, s16[1824,128]{1,0:T(8,128)(2,1)S(1)}, u32[]{:S(2)}, u32[]{:S(2)}) %collective-permute-start.39) | collective-permute-done | bytes 466976 | tf_op jit(solution)/shard_map/ppermute | solution.py:370
  125.8 2.5 %collective-permute-start.38 = (s16[912,128]{1,0:T(8,128)(2,1)S(1)}, s16[912,128]{1,0:T(8,128)(2,1)S(1)}, u32[]{:S(2)}, u32[]{:S(2)}) collective-permute-start(s16[912,128]{1,0:T(8,128)(2,1)S(1)} %copy-done.12), channel_id=1, source_target_pairs={{0,2},{1,3},{2,0},{3,1},{4,6},{5,7},{6,4},{7,5},{8,10},{9,11},{10,... | collective-permute-start | bytes 700424 | tf_op jit(solution)/shard_map/ppermute | solution.py:370
  129.0 1.3 collective-permute-start.31
  131.0 1.3 collective-permute-start.41
  132.3 13.2 %covariance.1 = f32[13456,128]{1,0:T(8,128)} custom-call(s32[8]{0:T(128)S(1)} %stack.89.place_ref, s16[912,128]{1,0:T(8,128)(2,1)} %combine.4.refs_0_, s16[912,128]{1,0:T(8,128)(2,1)} %collective-permute-done.18.refs_1_, s16[912,128]{1,0:T(8,128)(2,1)} %collective-permute-done.19.refs_2_, s16[912,128]{1,0:T(8,128)(2,1)} %collective-permute-done.20.refs_3_, ...), custom_call_target="tpu_custom_call" | custom-call | flops 3527409664 | bytes 6889472 | tf_op jit(solution)/shard_map/covariance/pallas_call | solution.py:325
  145.6 1.3 combine.6.refs_0_
  147.0 1.6 collective-permute-start.33
  148.5 5.7 %collective-permute-done.41.refs_2_ = s16[912,128]{1,0:T(8,128)(2,1)S(1)} collective-permute-done((s16[912,128]{1,0:T(8,128)(2,1)S(1)}, s16[912,128]{1,0:T(8,128)(2,1)S(1)}, u32[]{:S(2)}, u32[]{:S(2)}) %collective-permute-start.41) | collective-permute-done | bytes 233504 | tf_op jit(solution)/shard_map/ppermute | solution.py:370
  154.5 1.6 collective-permute-start.43
  156.6 5.3 %collective-permute-done.43.refs_6_ = s16[912,128]{1,0:T(8,128)(2,1)S(1)} collective-permute-done((s16[912,128]{1,0:T(8,128)(2,1)S(1)}, s16[912,128]{1,0:T(8,128)(2,1)S(1)}, u32[]{:S(2)}, u32[]{:S(2)}) %collective-permute-start.43) | collective-permute-done | bytes 233504 | tf_op jit(solution)/shard_map/ppermute | solution.py:360
  162.0 1.4 collective-permute-done.44.refs_7_
  163.4 3.8 %marginal.1 = f32[128,7424]{1,0:T(8,128)} custom-call(s32[8]{0:T(128)S(1)} %stack.75.place_ref, s16[1040,128]{1,0:T(8,128)(2,1)S(1)} %combine.6.refs_0_, s16[1040,128]{1,0:T(8,128)(2,1)S(1)} %collective-permute-done.32.refs_1_, s16[1040,128]{1,0:T(8,128)(2,1)S(1)} %collective-permute-done.33.refs_2_, s16[1040,128]{1,0:T(8,128)(2,1)S(1)} %collective-permute-done.34.refs_3_, ...), custom_call_target="tpu_custom_call" | custom-call | flops 3801088 | bytes 5701632 | tf_op jit(solution)/shard_map/marginal/pallas_call | solution.py:253
  (107 shorter events, 19.8 us)
Async XLA Ops:
  0.6 22.9 %copy-start = (bf16[96,7424]{1,0:T(8,128)(2,1)S(1)}, bf16[96,7424]{1,0:T(8,128)(2,1)}, u32[]{:S(2)}) copy-start(bf16[96,7424]{1,0:T(8,128)(2,1)} %param.5) | copy-start | bytes 4276228
  3.3 9.9 %collective-permute-start.3 = (bf16[96,3840]{1,0:T(8,128)(2,1)}, bf16[96,3840]{1,0:T(8,128)(2,1)S(1)}, u32[]{:S(2)}, u32[]{:S(2)}) collective-permute-start(bf16[96,3840]{1,0:T(8,128)(2,1)} %get-tuple-element.78), channel_id=1, source_target_pairs={{0,8},{8,0},{16,24},{24,16},{1,9},{9,1},{17,25},{25,17},{2,10},{10... | collective-permute-start | bytes 2211848 | tf_op jit(solution)/shard_map/ppermute | solution.py:360
  3.7 5.8 %collective-permute-start.2 = (s32[64,128]{1,0:T(8,128)S(1)}, s32[64,128]{1,0:T(8,128)S(1)}, u32[]{:S(2)}, u32[]{:S(2)}) collective-permute-start(s32[64,128]{1,0:T(8,128)S(1)} %pad_add_fusion.1), channel_id=1, source_target_pairs={{0,4},{1,5},{2,6},{3,7},{4,0},{5,1},{6,2},{7,3},{8,12},{9,13},{10,... | collective-permute-start | bytes 98312 | tf_op jit(solution)/shard_map/ppermute | solution.py:370
  7.4 5.8 %collective-permute-start.1 = (s32[64,128]{1,0:T(8,128)S(1)}, s32[64,128]{1,0:T(8,128)S(1)}, u32[]{:S(2)}, u32[]{:S(2)}) collective-permute-start(s32[64,128]{1,0:T(8,128)S(1)} %pad_add_fusion.1), channel_id=1, source_target_pairs={{0,6},{1,7},{2,4},{3,5},{4,2},{5,3},{6,0},{7,1},{8,14},{9,15},{10,... | collective-permute-start | bytes 98312 | tf_op jit(solution)/shard_map/ppermute | solution.py:370
  8.8 4.4 %collective-permute-start = (s32[64,128]{1,0:T(8,128)S(1)}, s32[64,128]{1,0:T(8,128)S(1)}, u32[]{:S(2)}, u32[]{:S(2)}) collective-permute-start(s32[64,128]{1,0:T(8,128)S(1)} %pad_add_fusion.1), channel_id=1, source_target_pairs={{0,2},{1,3},{2,0},{3,1},{4,6},{5,7},{6,4},{7,5},{8,10},{9,11},{10,... | collective-permute-start | bytes 98312 | tf_op jit(solution)/shard_map/ppermute | solution.py:370
  14.2 9.3 %collective-permute-start.4 = (bf16[192,896]{1,0:T(8,128)(2,1)}, bf16[192,896]{1,0:T(8,128)(2,1)S(1)}, u32[]{:S(2)}, u32[]{:S(2)}) collective-permute-start(bf16[192,896]{1,0:T(8,128)(2,1)} %get-tuple-element.36), channel_id=1, source_target_pairs={{0,16},{8,24},{16,0},{24,8},{1,17},{9,25},{17,1},{25,9},{2,18},{10... | collective-permute-start | bytes 1032200 | tf_op jit(solution)/shard_map/ppermute | solution.py:360
  24.5 19.9 %collective-permute-start.10 = (bf16[96,3840]{1,0:T(8,128)(2,1)}, bf16[96,3840]{1,0:T(8,128)(2,1)}, u32[]{:S(2)}, u32[]{:S(2)}) collective-permute-start(bf16[96,3840]{1,0:T(8,128)(2,1)} %constant_dynamic-slice_fusion), channel_id=1, source_target_pairs={{0,8},{8,0},{16,24},{24,16},{1,9},{9,1},{17,25},{25,17},{2,10},{10... | collective-permute-start | bytes 2211848 | tf_op jit(solution)/shard_map/ppermute | solution.py:360
  24.5 10.9 %collective-permute-start.5 = (bf16[192,896]{1,0:T(8,128)(2,1)S(1)}, bf16[192,896]{1,0:T(8,128)(2,1)S(1)}, u32[]{:S(2)}, u32[]{:S(2)}) collective-permute-start(bf16[192,896]{1,0:T(8,128)(2,1)S(1)} %get-tuple-element.77.refs_0_), channel_id=1, source_target_pairs={{0,1},{1,0},{2,3},{3,2},{4,5},{5,4},{6,7},{7,6},{8,9},{9,8},{10,11... | collective-permute-start | bytes 1032200 | tf_op jit(solution)/shard_map/ppermute | solution.py:366
  27.2 16.7 %collective-permute-start.7 = (bf16[192,1024]{1,0:T(8,128)(2,1)S(1)}, bf16[192,1024]{1,0:T(8,128)(2,1)}, u32[]{:S(2)}, u32[]{:S(2)}) collective-permute-start(bf16[192,1024]{1,0:T(8,128)(2,1)S(1)} %get-tuple-element.40), channel_id=1, source_target_pairs={{0,16},{8,24},{16,0},{24,8},{1,17},{9,25},{17,1},{25,9},{2,18},{10... | collective-permute-start | bytes 1179656 | tf_op jit(solution)/shard_map/ppermute | solution.py:360
  28.7 13.6 %collective-permute-start.6 = (bf16[192,896]{1,0:T(8,128)(2,1)S(1)}, bf16[192,896]{1,0:T(8,128)(2,1)S(1)}, u32[]{:S(2)}, u32[]{:S(2)}) collective-permute-start(bf16[192,896]{1,0:T(8,128)(2,1)S(1)} %collective-permute-done.4.refs_1_), channel_id=1, source_target_pairs={{0,1},{1,0},{2,3},{3,2},{4,5},{5,4},{6,7},{7,6},{8,9},{9,8},{10,11... | collective-permute-start | bytes 1032200 | tf_op jit(solution)/shard_map/ppermute | solution.py:366
  29.3 17.0 %copy-start.13 = (bf16[96,3840]{1,0:T(8,128)(2,1)}, bf16[96,3840]{1,0:T(8,128)(2,1)S(1)}, u32[]{:S(2)}) copy-start(bf16[96,3840]{1,0:T(8,128)(2,1)S(1)} %constant_dynamic-slice_fusion.1) | copy-start | bytes 2211844
  35.4 10.9 %copy-start.7 = (bf16[192,896]{1,0:T(8,128)(2,1)}, bf16[192,896]{1,0:T(8,128)(2,1)S(1)}, u32[]{:S(2)}) copy-start(bf16[192,896]{1,0:T(8,128)(2,1)S(1)} %collective-permute-done.5.refs_2_) | copy-start | bytes 1032196
  42.4 17.5 %collective-permute-start.8 = (bf16[192,1024]{1,0:T(8,128)(2,1)S(1)}, bf16[192,1024]{1,0:T(8,128)(2,1)}, u32[]{:S(2)}, u32[]{:S(2)}) collective-permute-start(bf16[192,1024]{1,0:T(8,128)(2,1)S(1)} %get-tuple-element.39.refs_0_), channel_id=1, source_target_pairs={{0,1},{1,0},{2,3},{3,2},{4,5},{5,4},{6,7},{7,6},{8,9},{9,8},{10,11... | collective-permute-start | bytes 1179656 | tf_op jit(solution)/shard_map/ppermute | solution.py:366
  43.9 17.8 %collective-permute-start.9 = (bf16[192,1024]{1,0:T(8,128)(2,1)}, bf16[192,1024]{1,0:T(8,128)(2,1)}, u32[]{:S(2)}, u32[]{:S(2)}) collective-permute-start(bf16[192,1024]{1,0:T(8,128)(2,1)} %collective-permute-done.7.refs_1_), channel_id=1, source_target_pairs={{0,1},{1,0},{2,3},{3,2},{4,5},{5,4},{6,7},{7,6},{8,9},{9,8},{10,11... | collective-permute-start | bytes 1179656 | tf_op jit(solution)/shard_map/ppermute | solution.py:366
  46.3 16.9 %collective-permute-start.11 = (bf16[192,1024]{1,0:T(8,128)(2,1)}, bf16[192,1024]{1,0:T(8,128)(2,1)S(1)}, u32[]{:S(2)}, u32[]{:S(2)}) collective-permute-start(bf16[192,1024]{1,0:T(8,128)(2,1)} %get-tuple-element.45), channel_id=1, source_target_pairs={{0,16},{8,24},{16,0},{24,8},{1,17},{9,25},{17,1},{25,9},{2,18},{10... | collective-permute-start | bytes 1179656 | tf_op jit(solution)/shard_map/ppermute | solution.py:360
  57.1 26.6 %collective-permute-start.15 = (s16[1824,128]{1,0:T(8,128)(2,1)S(1)}, s16[1824,128]{1,0:T(8,128)(2,1)S(1)}, u32[]{:S(2)}, u32[]{:S(2)}) collective-permute-start(s16[1824,128]{1,0:T(8,128)(2,1)S(1)} %get-tuple-element.37.own_ref), channel_id=1, source_target_pairs={{0,2},{1,3},{6,4},{7,5},{8,10},{9,11},{14,12},{15,13},{16,18},{17,... | collective-permute-start | bytes 1400840 | tf_op jit(solution)/shard_map/ppermute | solution.py:370
  61.7 12.1 %collective-permute-start.12 = (bf16[192,1024]{1,0:T(8,128)(2,1)S(1)}, bf16[192,1024]{1,0:T(8,128)(2,1)S(1)}, u32[]{:S(2)}, u32[]{:S(2)}) collective-permute-start(bf16[192,1024]{1,0:T(8,128)(2,1)S(1)} %get-tuple-element.44.refs_0_), channel_id=1, source_target_pairs={{0,1},{1,0},{2,3},{3,2},{4,5},{5,4},{6,7},{7,6},{8,9},{9,8},{10,11... | collective-permute-start | bytes 1179656 | tf_op jit(solution)/shard_map/ppermute | solution.py:366
  63.2 8.5 %collective-permute-start.35 = (bf16[192,896]{1,0:T(8,128)(2,1)S(1)}, bf16[192,896]{1,0:T(8,128)(2,1)S(1)}, u32[]{:S(2)}, u32[]{:S(2)}) collective-permute-start(bf16[192,896]{1,0:T(8,128)(2,1)S(1)} %get-tuple-element.63), channel_id=1, source_target_pairs={{0,16},{8,24},{16,0},{24,8},{1,17},{9,25},{17,1},{25,9},{2,18},{10... | collective-permute-start | bytes 1032200 | tf_op jit(solution)/shard_map/ppermute | solution.py:360
  64.7 17.5 %collective-permute-start.13 = (bf16[192,1024]{1,0:T(8,128)(2,1)S(1)}, bf16[192,1024]{1,0:T(8,128)(2,1)S(1)}, u32[]{:S(2)}, u32[]{:S(2)}) collective-permute-start(bf16[192,1024]{1,0:T(8,128)(2,1)S(1)} %collective-permute-done.11.refs_1_), channel_id=1, source_target_pairs={{0,1},{1,0},{2,3},{3,2},{4,5},{5,4},{6,7},{7,6},{8,9},{9,8},{10,11... | collective-permute-start | bytes 1179656 | tf_op jit(solution)/shard_map/ppermute | solution.py:366
  68.1 16.7 %collective-permute-start.22 = (s16[2080,128]{1,0:T(8,128)(2,1)S(1)}, s16[2080,128]{1,0:T(8,128)(2,1)S(1)}, u32[]{:S(2)}, u32[]{:S(2)}) collective-permute-start(s16[2080,128]{1,0:T(8,128)(2,1)S(1)} %get-tuple-element.41.own_ref), channel_id=1, source_target_pairs={{0,2},{1,3},{6,4},{7,5},{8,10},{9,11},{14,12},{15,13},{16,18},{17,... | collective-permute-start | bytes 1597448 | tf_op jit(solution)/shard_map/ppermute | solution.py:370
  71.7 23.7 %collective-permute-start.37 = (bf16[192,896]{1,0:T(8,128)(2,1)S(1)}, bf16[192,896]{1,0:T(8,128)(2,1)S(1)}, u32[]{:S(2)}, u32[]{:S(2)}) collective-permute-start(bf16[192,896]{1,0:T(8,128)(2,1)S(1)} %collective-permute-done.35.refs_1_), channel_id=1, source_target_pairs={{0,1},{1,0},{2,3},{3,2},{4,5},{5,4},{6,7},{7,6},{8,9},{9,8},{10,11... | collective-permute-start | bytes 1032200 | tf_op jit(solution)/shard_map/ppermute | solution.py:366
  82.1 16.9 %collective-permute-start.36 = (bf16[192,896]{1,0:T(8,128)(2,1)S(1)}, bf16[192,896]{1,0:T(8,128)(2,1)S(1)}, u32[]{:S(2)}, u32[]{:S(2)}) collective-permute-start(bf16[192,896]{1,0:T(8,128)(2,1)S(1)} %get-tuple-element.62.refs_0_), channel_id=1, source_target_pairs={{0,1},{1,0},{2,3},{3,2},{4,5},{5,4},{6,7},{7,6},{8,9},{9,8},{10,11... | collective-permute-start | bytes 1032200 | tf_op jit(solution)/shard_map/ppermute | solution.py:366
  83.7 11.1 %collective-permute-start.14 = (s16[912,128]{1,0:T(8,128)(2,1)S(1)}, s16[912,128]{1,0:T(8,128)(2,1)S(1)}, u32[]{:S(2)}, u32[]{:S(2)}) collective-permute-start(s16[912,128]{1,0:T(8,128)(2,1)S(1)} %get-tuple-element.48), channel_id=1, source_target_pairs={{0,2},{1,3},{2,0},{3,1},{4,6},{5,7},{6,4},{7,5},{8,10},{9,11},{10,... | collective-permute-start | bytes 700424 | tf_op jit(solution)/shard_map/ppermute | solution.py:370
  84.1 10.7 %collective-permute-start.16 = (s16[912,128]{1,0:T(8,128)(2,1)S(1)}, s16[912,128]{1,0:T(8,128)(2,1)S(1)}, u32[]{:S(2)}, u32[]{:S(2)}) collective-permute-start(s16[912,128]{1,0:T(8,128)(2,1)S(1)} %get-tuple-element.49), channel_id=1, source_target_pairs={{2,4},{3,5},{4,2},{5,3},{10,12},{11,13},{12,10},{13,11},{18,20},{1... | collective-permute-start | bytes 700424 | tf_op jit(solution)/shard_map/ppermute | solution.py:370
  84.8 22.3 %collective-permute-start.17 = (s16[912,128]{1,0:T(8,128)(2,1)S(1)}, s16[912,128]{1,0:T(8,128)(2,1)S(1)}, u32[]{:S(2)}, u32[]{:S(2)}) collective-permute-start(s16[912,128]{1,0:T(8,128)(2,1)S(1)} %get-tuple-element.50), channel_id=1, source_target_pairs={{2,6},{3,7},{4,0},{5,1},{10,14},{11,15},{12,8},{13,9},{18,22},{19,... | collective-permute-start | bytes 700424 | tf_op jit(solution)/shard_map/ppermute | solution.py:370
  94.8 14.8 %collective-permute-start.21 = (s16[1040,128]{1,0:T(8,128)(2,1)S(1)}, s16[1040,128]{1,0:T(8,128)(2,1)S(1)}, u32[]{:S(2)}, u32[]{:S(2)}) collective-permute-start(s16[1040,128]{1,0:T(8,128)(2,1)S(1)} %get-tuple-element.53), channel_id=1, source_target_pairs={{0,2},{1,3},{2,0},{3,1},{4,6},{5,7},{6,4},{7,5},{8,10},{9,11},{10,... | collective-permute-start | bytes 798728 | tf_op jit(solution)/shard_map/ppermute | solution.py:370
  94.8 14.8 %collective-permute-start.23 = (s16[1040,128]{1,0:T(8,128)(2,1)S(1)}, s16[1040,128]{1,0:T(8,128)(2,1)S(1)}, u32[]{:S(2)}, u32[]{:S(2)}) collective-permute-start(s16[1040,128]{1,0:T(8,128)(2,1)S(1)} %get-tuple-element.54), channel_id=1, source_target_pairs={{2,4},{3,5},{4,2},{5,3},{10,12},{11,13},{12,10},{13,11},{18,20},{1... | collective-permute-start | bytes 798728 | tf_op jit(solution)/shard_map/ppermute | solution.py:370
  95.4 14.1 %collective-permute-start.24 = (s16[1040,128]{1,0:T(8,128)(2,1)S(1)}, s16[1040,128]{1,0:T(8,128)(2,1)S(1)}, u32[]{:S(2)}, u32[]{:S(2)}) collective-permute-start(s16[1040,128]{1,0:T(8,128)(2,1)S(1)} %get-tuple-element.55), channel_id=1, source_target_pairs={{2,6},{3,7},{4,0},{5,1},{10,14},{11,15},{12,8},{13,9},{18,22},{19,... | collective-permute-start | bytes 798728 | tf_op jit(solution)/shard_map/ppermute | solution.py:370
  99.0 21.3 %collective-permute-start.29 = (s16[2080,128]{1,0:T(8,128)(2,1)S(1)}, s16[2080,128]{1,0:T(8,128)(2,1)S(1)}, u32[]{:S(2)}, u32[]{:S(2)}) collective-permute-start(s16[2080,128]{1,0:T(8,128)(2,1)S(1)} %get-tuple-element.58.own_ref), channel_id=1, source_target_pairs={{0,2},{1,3},{6,4},{7,5},{8,10},{9,11},{14,12},{15,13},{16,18},{17,... | collective-permute-start | bytes 1597448 | tf_op jit(solution)/shard_map/ppermute | solution.py:370
  107.1 15.9 %collective-permute-start.39 = (s16[1824,128]{1,0:T(8,128)(2,1)S(1)}, s16[1824,128]{1,0:T(8,128)(2,1)S(1)}, u32[]{:S(2)}, u32[]{:S(2)}) collective-permute-start(s16[1824,128]{1,0:T(8,128)(2,1)S(1)} %get-tuple-element.67.own_ref), channel_id=1, source_target_pairs={{0,2},{1,3},{6,4},{7,5},{8,10},{9,11},{14,12},{15,13},{16,18},{17,... | collective-permute-start | bytes 1400840 | tf_op jit(solution)/shard_map/ppermute | solution.py:370
  110.6 9.2 %collective-permute-start.26 = (s16[1040,128]{1,0:T(8,128)(2,1)}, s16[1040,128]{1,0:T(8,128)(2,1)}, u32[]{:S(2)}, u32[]{:S(2)}) collective-permute-start(s16[1040,128]{1,0:T(8,128)(2,1)} %combine.5.refs_4_), channel_id=1, source_target_pairs={{0,16},{8,24},{16,0},{24,8},{1,17},{9,25},{17,1},{25,9},{2,18},{10... | collective-permute-start | bytes 798728 | tf_op jit(solution)/shard_map/ppermute | solution.py:360
  112.1 7.8 %collective-permute-start.19 = (s16[912,128]{1,0:T(8,128)(2,1)}, s16[912,128]{1,0:T(8,128)(2,1)}, u32[]{:S(2)}, u32[]{:S(2)}) collective-permute-start(s16[912,128]{1,0:T(8,128)(2,1)} %combine.4.refs_0_), channel_id=1, source_target_pairs={{0,16},{8,24},{16,0},{24,8},{1,17},{9,25},{17,1},{25,9},{2,18},{10... | collective-permute-start | bytes 700424 | tf_op jit(solution)/shard_map/ppermute | solution.py:360
  112.7 16.4 %collective-permute-start.28 = (s16[1040,128]{1,0:T(8,128)(2,1)}, s16[1040,128]{1,0:T(8,128)(2,1)}, u32[]{:S(2)}, u32[]{:S(2)}) collective-permute-start(s16[1040,128]{1,0:T(8,128)(2,1)} %get-tuple-element.57), channel_id=1, source_target_pairs={{0,2},{1,3},{2,0},{3,1},{4,6},{5,7},{6,4},{7,5},{8,10},{9,11},{10,... | collective-permute-start | bytes 798728 | tf_op jit(solution)/shard_map/ppermute | solution.py:370
  119.9 10.5 %collective-permute-start.25 = (s16[1040,128]{1,0:T(8,128)(2,1)}, s16[1040,128]{1,0:T(8,128)(2,1)}, u32[]{:S(2)}, u32[]{:S(2)}) collective-permute-start(s16[1040,128]{1,0:T(8,128)(2,1)} %combine.5.refs_4_), channel_id=1, source_target_pairs={{0,8},{8,0},{16,24},{24,16},{1,9},{9,1},{17,25},{25,17},{2,10},{10... | collective-permute-start | bytes 798728 | tf_op jit(solution)/shard_map/ppermute | solution.py:360
  119.9 11.2 %collective-permute-start.27 = (s16[1040,128]{1,0:T(8,128)(2,1)}, s16[1040,128]{1,0:T(8,128)(2,1)}, u32[]{:S(2)}, u32[]{:S(2)}) collective-permute-start(s16[1040,128]{1,0:T(8,128)(2,1)} %collective-permute-done.26.refs_6_), channel_id=1, source_target_pairs={{0,8},{8,0},{16,24},{24,16},{1,9},{9,1},{17,25},{25,17},{2,10},{10... | collective-permute-start | bytes 798728 | tf_op jit(solution)/shard_map/ppermute | solution.py:360
  120.4 5.4 %collective-permute-start.18 = (s16[912,128]{1,0:T(8,128)(2,1)}, s16[912,128]{1,0:T(8,128)(2,1)}, u32[]{:S(2)}, u32[]{:S(2)}) collective-permute-start(s16[912,128]{1,0:T(8,128)(2,1)} %combine.4.refs_0_), channel_id=1, source_target_pairs={{0,8},{8,0},{16,24},{24,16},{1,9},{9,1},{17,25},{25,17},{2,10},{10... | collective-permute-start | bytes 700424 | tf_op jit(solution)/shard_map/ppermute | solution.py:360
  123.7 4.6 %collective-permute-start.20 = (s16[912,128]{1,0:T(8,128)(2,1)}, s16[912,128]{1,0:T(8,128)(2,1)}, u32[]{:S(2)}, u32[]{:S(2)}) collective-permute-start(s16[912,128]{1,0:T(8,128)(2,1)} %collective-permute-done.19.refs_2_), channel_id=1, source_target_pairs={{0,8},{8,0},{16,24},{24,16},{1,9},{9,1},{17,25},{25,17},{2,10},{10... | collective-permute-start | bytes 700424 | tf_op jit(solution)/shard_map/ppermute | solution.py:360
  125.8 22.7 %collective-permute-start.38 = (s16[912,128]{1,0:T(8,128)(2,1)S(1)}, s16[912,128]{1,0:T(8,128)(2,1)S(1)}, u32[]{:S(2)}, u32[]{:S(2)}) collective-permute-start(s16[912,128]{1,0:T(8,128)(2,1)S(1)} %copy-done.12), channel_id=1, source_target_pairs={{0,2},{1,3},{2,0},{3,1},{4,6},{5,7},{6,4},{7,5},{8,10},{9,11},{10,... | collective-permute-start | bytes 700424 | tf_op jit(solution)/shard_map/ppermute | solution.py:370
  128.4 17.2 %collective-permute-start.30 = (s16[1040,128]{1,0:T(8,128)(2,1)S(1)}, s16[1040,128]{1,0:T(8,128)(2,1)S(1)}, u32[]{:S(2)}, u32[]{:S(2)}) collective-permute-start(s16[1040,128]{1,0:T(8,128)(2,1)S(1)} %get-tuple-element.59), channel_id=1, source_target_pairs={{2,4},{3,5},{4,2},{5,3},{10,12},{11,13},{12,10},{13,11},{18,20},{1... | collective-permute-start | bytes 798728 | tf_op jit(solution)/shard_map/ppermute | solution.py:370
  129.0 16.6 %collective-permute-start.31 = (s16[1040,128]{1,0:T(8,128)(2,1)S(1)}, s16[1040,128]{1,0:T(8,128)(2,1)S(1)}, u32[]{:S(2)}, u32[]{:S(2)}) collective-permute-start(s16[1040,128]{1,0:T(8,128)(2,1)S(1)} %get-tuple-element.60), channel_id=1, source_target_pairs={{2,6},{3,7},{4,0},{5,1},{10,14},{11,15},{12,8},{13,9},{18,22},{19,... | collective-permute-start | bytes 798728 | tf_op jit(solution)/shard_map/ppermute | solution.py:370
  130.3 18.2 %collective-permute-start.40 = (s16[912,128]{1,0:T(8,128)(2,1)S(1)}, s16[912,128]{1,0:T(8,128)(2,1)S(1)}, u32[]{:S(2)}, u32[]{:S(2)}) collective-permute-start(s16[912,128]{1,0:T(8,128)(2,1)S(1)} %get-tuple-element.68), channel_id=1, source_target_pairs={{2,4},{3,5},{4,2},{5,3},{10,12},{11,13},{12,10},{13,11},{18,20},{1... | collective-permute-start | bytes 700424 | tf_op jit(solution)/shard_map/ppermute | solution.py:370
  131.0 23.2 %collective-permute-start.41 = (s16[912,128]{1,0:T(8,128)(2,1)S(1)}, s16[912,128]{1,0:T(8,128)(2,1)S(1)}, u32[]{:S(2)}, u32[]{:S(2)}) collective-permute-start(s16[912,128]{1,0:T(8,128)(2,1)S(1)} %get-tuple-element.69), channel_id=1, source_target_pairs={{2,6},{3,7},{4,0},{5,1},{10,14},{11,15},{12,8},{13,9},{18,22},{19,... | collective-permute-start | bytes 700424 | tf_op jit(solution)/shard_map/ppermute | solution.py:370
  147.0 9.1 %collective-permute-start.33 = (s16[1040,128]{1,0:T(8,128)(2,1)S(1)}, s16[1040,128]{1,0:T(8,128)(2,1)S(1)}, u32[]{:S(2)}, u32[]{:S(2)}) collective-permute-start(s16[1040,128]{1,0:T(8,128)(2,1)S(1)} %combine.6.refs_0_), channel_id=1, source_target_pairs={{0,16},{8,24},{16,0},{24,8},{1,17},{9,25},{17,1},{25,9},{2,18},{10... | collective-permute-start | bytes 798728 | tf_op jit(solution)/shard_map/ppermute | solution.py:360
  154.5 7.4 %collective-permute-start.43 = (s16[912,128]{1,0:T(8,128)(2,1)S(1)}, s16[912,128]{1,0:T(8,128)(2,1)S(1)}, u32[]{:S(2)}, u32[]{:S(2)}) collective-permute-start(s16[912,128]{1,0:T(8,128)(2,1)S(1)} %combine.7.refs_4_), channel_id=1, source_target_pairs={{0,16},{8,24},{16,0},{24,8},{1,17},{9,25},{17,1},{25,9},{2,18},{10... | collective-permute-start | bytes 700424 | tf_op jit(solution)/shard_map/ppermute | solution.py:360
  156.1 5.9 %collective-permute-start.32 = (s16[1040,128]{1,0:T(8,128)(2,1)S(1)}, s16[1040,128]{1,0:T(8,128)(2,1)S(1)}, u32[]{:S(2)}, u32[]{:S(2)}) collective-permute-start(s16[1040,128]{1,0:T(8,128)(2,1)S(1)} %combine.6.refs_0_), channel_id=1, source_target_pairs={{0,8},{8,0},{16,24},{24,16},{1,9},{9,1},{17,25},{25,17},{2,10},{10... | collective-permute-start | bytes 798728 | tf_op jit(solution)/shard_map/ppermute | solution.py:360
  156.1 5.9 %collective-permute-start.34 = (s16[1040,128]{1,0:T(8,128)(2,1)S(1)}, s16[1040,128]{1,0:T(8,128)(2,1)S(1)}, u32[]{:S(2)}, u32[]{:S(2)}) collective-permute-start(s16[1040,128]{1,0:T(8,128)(2,1)S(1)} %collective-permute-done.33.refs_2_), channel_id=1, source_target_pairs={{0,8},{8,0},{16,24},{24,16},{1,9},{9,1},{17,25},{25,17},{2,10},{10... | collective-permute-start | bytes 798728 | tf_op jit(solution)/shard_map/ppermute | solution.py:360
  156.6 5.4 %collective-permute-start.42 = (s16[912,128]{1,0:T(8,128)(2,1)S(1)}, s16[912,128]{1,0:T(8,128)(2,1)S(1)}, u32[]{:S(2)}, u32[]{:S(2)}) collective-permute-start(s16[912,128]{1,0:T(8,128)(2,1)S(1)} %combine.7.refs_4_), channel_id=1, source_target_pairs={{0,8},{8,0},{16,24},{24,16},{1,9},{9,1},{17,25},{25,17},{2,10},{10... | collective-permute-start | bytes 700424 | tf_op jit(solution)/shard_map/ppermute | solution.py:360
  161.9 1.5 collective-permute-start.44
  (15 other events, 38.7 us)

commit v4 on v3

--- a/solution.py
+++ b/solution.py
@@ -9,6 +9,8 @@
 LANES = 128
 CORES = 2
 DEPTH = 4
+LOAD_FIRST = 5
+MEAN_FIRST = 10
 SCALES = 16
 TOP = 32767.0
 VMEM_BYTES = 48 * 1024 * 1024
@@ -26,6 +28,11 @@
 
 def after(value, *others):
     return lax.optimization_barrier((value, *others))[0]
+
+
+def split(each, first):
+    first = each // 2 if first >= each else first
+    return (first, each - first)
 
 
 def twice(value):
@@ -93,7 +100,7 @@
         ),
         out_shape=jax.ShapeDtypeStruct(shape, jnp.bfloat16),
         compiler_params=params(),
-        cost_estimate=cost(shape[0] * width * queries.shape[0], shape[0] * width * 2),
+        cost_estimate=cost(shape[0] * width * queries.shape[0] * 200, shape[0] * width * 2),
         name="build_weights",
     )(bases, queries)
 
@@ -280,7 +287,8 @@
     each_piece(place_ref, pieces, tiles, do)
 
     def turn(t, carry):
-        value = load_ref[pl.ds(pl.multiple_of(t * LANES, LANES), LANES), :].T
+        tile = t + t // (total // CORES - 1)
+        value = load_ref[pl.ds(pl.multiple_of(tile * LANES, LANES), LANES), :].T
         swapped = pltpu.roll(value, rank, 1)
         age_ref[pl.ds(2 * t, LANES, stride=pitch), :] = jnp.where(left, value, swapped)
         age_ref[pl.ds(2 * t + 1, LANES, stride=pitch), :] = jnp.where(left, swapped, value)
@@ -337,7 +345,7 @@
         ),
         out_shape=jax.ShapeDtypeStruct(shape, jnp.float32),
         compiler_params=params(),
-        cost_estimate=cost(LANES * ages * ages * rank * 32, shape[0] * shape[1] * 4),
+        cost_estimate=cost(LANES * ages * ages * rank * 140, shape[0] * shape[1] * 4),
         name="covariance",
     )(places, *pieces)
 
@@ -390,87 +398,91 @@
         for dy in range(ys) for dx in range(xs) for dc in range(CORES)
     ]).astype(jnp.int32)
     w = build_weights(bases, queries, rows)
-    flag = ((core == CORES - 1) & (x == xs - 1)).astype(jnp.int32).reshape(1)
-
-    variances = jnp.pad(variances, ((0, 0), (0, -ages % LANES)))
-    loads = jnp.concatenate([factors, variances], axis=1)
-
-    def half(array, c):
-        total = array.shape[1] // LANES
-        width = -(-total // groups) * xs
-        return lax.dynamic_slice(array, (0, jnp.where(c == 0, 0, total - width) * LANES), (rows, width * LANES))
-
-    def swap(array):
-        return geo_shift(half(array, 1 - core), 0, 1)
-
-    def part(both, group, each, first, count):
-        return lax.dynamic_slice(both, (0, (group * each + first) * LANES), (both.shape[0], count * LANES))
-
-    def along_x(both, chunk, *done):
-        mine = part(both, x, *chunk)
-        others = [geo_shift(after(part(both, (x + dx) % xs, *chunk), *done), dx, 0) for dx in range(1, xs)]
-        return [mine] + others
+    flag = (x == xs - 1).astype(jnp.int32).reshape(1)
+    last_tile = jnp.pad(variances, ((0, 0), (0, -ages % LANES)))
+
+    def half(array, c, *more):
+        width = array.shape[1] // CORES
+        return jnp.concatenate([lax.dynamic_slice(array, (0, c * width), (rows, width)), *more], axis=1)
+
+    def exchange(array, *more):
+        return jnp.concatenate(
+            [half(array, core, *more), geo_shift(half(array, 1 - core, *more), 0, 1)], axis=0
+        )
+
+    def start_of(group, tiles):
+        return jnp.minimum(group * each_of(tiles), tiles - each_of(tiles))
+
+    def each_of(tiles):
+        return -(-tiles // xs)
+
+    def along_x(both, first, count, *done):
+        def part(group):
+            start = (start_of(group, both.shape[1] // LANES) + first) * LANES
+            return lax.dynamic_slice(both, (0, start), (both.shape[0], count * LANES))
+
+        others = [geo_shift(after(part((x + dx) % xs), *done), dx, 0) for dx in range(1, xs)]
+        return [part(x)] + others
 
     def along_y(by_x, *done):
-        mine = [after(by_x[0], *done)] + by_x[1:]
-        return mine + [y_shift(value, dy) for dy in range(1, ys) for value in mine]
-
-    def along_z(data, has_var, *done):
-        own, close, far = partial_sums(flag, after(w, *done), data, has_var)
+        if done:
+            by_x = [after(value, other) for value, other in zip(by_x, done)]
+        return by_x + [y_shift(value, dy) for dy in range(1, ys) for value in by_x]
+
+    def along_z(data, has_var, before_sums, before_middle):
+        own, close, far = partial_sums(flag, after(w, *before_sums), data, has_var)
         far_in = z_send(far, ((0, 1), (3, 2)))
         close_in = z_send(close, near)
-        to_middle, to_end = middle(far, far_in)
+        to_middle, to_end = middle(after(far, *before_middle), far_in)
         middle_in = z_send(to_middle, ((1, 2), (2, 1)))
         end_in = z_send(to_end, ((1, 3), (2, 0)))
-        return far, own, [close_in, middle_in, end_in]
+        return (far, to_end), own, [close_in, middle_in, end_in]
 
     def spread(own, others, *done):
         mine = combine(after(own, *done), others)
         along = [geo_shift(mine, dx, 0) for dx in range(xs)]
         return [geo_shift(along[dx], 0, dc) for dx in range(xs) for dc in range(CORES)]
 
-    def places(total):
-        each = -(-total // groups)
-        starts, uppers = [], []
+    def places(tiles):
+        starts, lasts = [], []
         for dx in range(xs):
             for dc in range(CORES):
-                c, a = (core - dc) % CORES, (x - dx) % xs
-                starts.append(jnp.where(c == 0, 0, total - each * xs) + a * each)
-                uppers.append(c)
-        return jnp.stack(starts + uppers).astype(jnp.int32)
-
-    def split(each):
-        return (each // 2, each - each // 2)
-
-    load_total = loads.shape[1] // LANES
-    mean_total = estimates.shape[1] // LANES
-    load_each, mean_each = -(-load_total // groups), -(-mean_total // groups)
-    load_tiles = split(load_each)
-    mean_tiles = split(mean_each)[::-1]
-
-    def chunks(each, tiles):
-        return [(each, sum(tiles[:i]), count) for i, count in enumerate(tiles)]
-
-    load_chunks, mean_chunks = chunks(load_each, load_tiles), chunks(mean_each, mean_tiles)
-    load_both = jnp.concatenate([half(loads, core), swap(loads)], axis=0)
+                group = (x - dx) % xs
+                starts.append((core - dc) % CORES * tiles + start_of(group, tiles))
+                lasts.append(group == xs - 1)
+        return jnp.stack(starts + lasts).astype(jnp.int32)
+
+    mean_width = estimates.shape[1] // LANES // CORES
+    load_width = factors.shape[1] // LANES // CORES + 1
+    load_tiles = split(each_of(load_width), LOAD_FIRST)
+    mean_tiles = split(each_of(mean_width), MEAN_FIRST)
     by_x, by_y, by_z = [], [], []
-    for chunk in load_chunks:
-        by_x.append(along_x(load_both, chunk, *by_x[-1:], queries))
-    mean_both = jnp.concatenate([half(estimates, core), swap(after(estimates, by_x[0]))], axis=0)
-    for chunk in mean_chunks:
-        by_x.append(along_x(mean_both, chunk, *by_x[-1:]))
+
+    def feed(both, tiles):
+        for i, count in enumerate(tiles):
+            by_x.append(along_x(both, sum(tiles[:i]), count, *[values[-1] for values in by_x[-1:]]))
+
+    feed(exchange(factors, last_tile), load_tiles)
+    feed(exchange(after(estimates, w)), mean_tiles)
     for values in by_x:
-        by_y.append(along_y(values, *by_y[-1:]))
+        by_y.append(along_y(values, *[done for done in by_y[-1][-xs:]] if by_y else []))
+    count = len(by_y)
     for i, values in enumerate(by_y):
-        done = [far for far, _, _ in by_z[-1:]]
-        by_z.append(along_z(values, i == len(load_chunks) - 1, *done))
+        before_sums = [other[-1] for other in by_x[i + 1:i + 2]]
+        if by_z:
+            far, to_end = by_z[-1][0]
+            before_sums.append(far if i == count - 1 else to_end)
+        before_middle = [other[xs] for other in by_y[i + 1:i + 2]] + [other[-1] for other in by_y[i + 1:i + 2] if i == count - 2]
+        by_z.append(along_z(values, i == len(load_tiles) - 1, before_sums, before_middle))
     load_pieces, mean_pieces = [], []
-    for _, own, others in by_z[:len(load_chunks)]:
-        load_pieces += spread(own, others, *load_pieces[:1])
-    cov = covariance(places(load_total), load_pieces, load_tiles, load_total, ages, rank)
-    for _, own, others in by_z[len(load_chunks):]:
-        mean_pieces += spread(own, others, cov, *mean_pieces[:1])
-    mean = marginal(places(mean_total), mean_pieces, mean_tiles, mean_total)
+    for i, (_, own, others) in enumerate(by_z[:len(load_tiles)]):
+        moved = [other[-1] for other in by_y[i + 1:i + 2]] + [other[-1] for other in by_y[i + 2:i + 3] if i > 0]
+        load_pieces += spread(own, others, *moved, *load_pieces[-1:])
+    load_pieces[0] = after(load_pieces[0], by_z[-1][0][1])
+    cov = covariance(places(load_width), load_pieces, load_tiles, load_width * CORES, ages, rank)
+    for _, own, others in by_z[len(load_tiles):]:
+        mean_pieces += spread(own, others, cov, *by_z[-1][2])
+    mean = marginal(places(mean_width), mean_pieces, mean_tiles, mean_width * CORES)
     return mean, cov.T
 
 

time: 169 us -> 181 us (1.071)
  waiting for transfers between devices: 69 us -> 76.5 us
  local copies, waits for them, and re-layouts: 7.19 us -> 11 us
  starting transfers between devices: 48.2 us -> 51.5 us
  other arithmetic: 6.48 us -> 4.28 us
    ppermute x19, waiting for transfers between devices: 20.6 us -> 43.1 us  [z_send(): return lax.ppermute(value, 'dist', perm)]
    ppermute x8, waiting for transfers between devices: 24.7 us -> 7.83 us  [y_shift(): return lax.ppermute(value, 'dist', perm)]
    ppermute x19, starting transfers between devices: 27.3 us -> 31.9 us  [z_send(): return lax.ppermute(value, 'dist', perm)]
    concatenate x5 -> x4, other arithmetic: 6.46 us -> 3.52 us  [the longest x3 3.47 us: exchange(): jnp.concatenate([half(array, core, *more), geo_shift(half(array, 1 - core...]
    unnamed x36 -> x38, local copies, waits for them, and re-layouts: 4.87 us -> 6.97 us
    ppermute x18, waiting for transfers between devices: 23.6 us -> 25.5 us  [geo_shift(): return lax.ppermute(value, 'geo', perm)]
  transfers between devices with their start and end apart: 45 -> 45, of which waited for: 15 -> 17; matrix products, arithmetic and copies ran while one was open for 3% -> 4% of each run, Pallas kernels for 19% -> 16%
where the time goes in v4:
time: 181 us
  waiting for transfers between devices  76.5 us (42%)
  starting transfers between devices  51.5 us (28%)
  Pallas kernels  35.9 us (20%)
  local copies, waits for them, and re-layouts  11 us (6%)
  other arithmetic  4.28 us (2%)
    ppermute x19, waiting for transfers between devices, z_send(): return lax.ppermute(value, 'dist', perm)  43.1 us
    ppermute x19, starting transfers between devices, z_send(): return lax.ppermute(value, 'dist', perm)  31.9 us
    ppermute x18, waiting for transfers between devices, geo_shift(): return lax.ppermute(value, 'geo', perm)  25.5 us
    pallas_call x1, Pallas kernels, covariance(): pl.pallas_call(functools.partial(covariance_kernel, tiles, total, ages, r...  12.9 us
    ppermute x18, starting transfers between devices, geo_shift(): return lax.ppermute(value, 'geo', perm)  11.1 us
    pallas_call x4, Pallas kernels, partial_sums(): pl.pallas_call(functools.partial(sums_kernel, parts, has_var), grid_spec=...  9.65 us
    ppermute x8, starting transfers between devices, y_shift(): return lax.ppermute(value, 'dist', perm)  8.45 us
    ppermute x8, waiting for transfers between devices, y_shift(): return lax.ppermute(value, 'dist', perm)  7.83 us
  transfers between devices with their start and end apart: 45, of which 17 were waited for; matrix products, arithmetic and copies ran while one was open for 4% of the time, Pallas kernels for 16%

profile of v4, /device:TPU:0, one launch (start us, length us, event | category | flops | bytes accessed | tf_op | source)
XLA Modules:
  0.0 180.5 jit_solution(14426391779994111558)
XLA Ops:
  1.4 4.0 %collective-permute-start.2 = (s32[64,128]{1,0:T(8,128)S(1)}, s32[64,128]{1,0:T(8,128)S(1)}, u32[]{:S(2)}, u32[]{:S(2)}) collective-permute-start(s32[64,128]{1,0:T(8,128)S(1)} %pad_add_fusion.1), channel_id=1, source_target_pairs={{0,4},{1,5},{2,6},{3,7},{4,0},{5,1},{6,2},{7,3},{8,12},{9,13},{10,... | collective-permute-start | bytes 98312 | tf_op jit(solution)/shard_map/ppermute | solution.py:378
  5.4 1.3 collective-permute-start.1
  7.7 1.4 constant_dynamic-slice_fusion.5
  9.6 1.5 collective-permute-done.1
  11.2 4.9 %build_weights.1.w_ref = bf16[768,512]{1,0:T(8,128)(2,1)S(1)} custom-call(s32[8]{0:T(128)S(1)} %stack.92.base_ref, s32[64,512]{1,0:T(8,128)S(1)} %pad_add_fusion.query_ref), custom_call_target="tpu_custom_call" | custom-call | flops 5033164800 | bytes 786432 | tf_op jit(solution)/shard_map/build_weights/pallas_call | solution.py:93
  16.1 1.4 constant_dynamic-slice_fusion.6
  17.7 1.5 collective-permute-start.5
  19.2 1.5 collective-permute-start.9
  20.9 5.3 %collective-permute-done.5.refs_1_ = bf16[192,640]{1,0:T(8,128)(2,1)S(1)} collective-permute-done((bf16[192,640]{1,0:T(8,128)(2,1)S(1)}, bf16[192,640]{1,0:T(8,128)(2,1)S(1)}, u32[]{:S(2)}, u32[]{:S(2)}) %collective-permute-start.5) | collective-permute-done | bytes 245792 | tf_op jit(solution)/shard_map/ppermute | solution.py:368
  26.1 1.5 collective-permute-start.6
  27.6 1.5 collective-permute-start.11
  29.6 2.2 %fusion.1 = (bf16[192,1280]{1,0:T(8,128)(2,1)S(1)}, bf16[192,1280]{1,0:T(8,128)(2,1)}) fusion(s32[]{:T(128)S(6)} %select_n.186, bf16[96,3712]{1,0:T(8,128)(2,1)} %get-tuple-element.97, bf16[96,3712]{1,0:T(8,128)(2,1)} %collective-permute-done.3, s32[]{:T(128)S(6)} %select_n.181), kind=kLoop, calls=%fused_computation.11 | loop fusion | flops 1966080 | bytes 2408456 | tf_op jit(solution)/shard_map/concatenate | solution.py:409
  31.8 7.2 %collective-permute-done.6.refs_1_ = bf16[192,1280]{1,0:T(8,128)(2,1)S(1)} collective-permute-done((bf16[192,1280]{1,0:T(8,128)(2,1)S(1)}, bf16[192,1280]{1,0:T(8,128)(2,1)S(1)}, u32[]{:S(2)}, u32[]{:S(2)}) %collective-permute-start.6) | collective-permute-done | bytes 491552 | tf_op jit(solution)/shard_map/ppermute | solution.py:368
  39.0 1.5 collective-permute-start.7
  40.5 5.0 %collective-permute-done.10.refs_3_ = bf16[192,640]{1,0:T(8,128)(2,1)S(1)} collective-permute-done((bf16[192,640]{1,0:T(8,128)(2,1)S(1)}, bf16[192,640]{1,0:T(8,128)(2,1)S(1)}, u32[]{:S(2)}, u32[]{:S(2)}) %collective-permute-start.10) | collective-permute-done | bytes 245792 | tf_op jit(solution)/shard_map/ppermute | solution.py:374
  45.5 1.5 collective-permute-start.13
  47.0 1.1 copy-done.13
  48.1 1.6 partial_sums.4
  49.8 2.4 %collective-permute-start.12 = (s16[1312,128]{1,0:T(8,128)(2,1)S(1)}, s16[1312,128]{1,0:T(8,128)(2,1)S(1)}, u32[]{:S(2)}, u32[]{:S(2)}) collective-permute-start(s16[1312,128]{1,0:T(8,128)(2,1)S(1)} %get-tuple-element.51.own_ref), channel_id=1, source_target_pairs={{0,2},{1,3},{6,4},{7,5},{8,10},{9,11},{14,12},{15,13},{16,18},{17,... | collective-permute-start | bytes 1007624 | tf_op jit(solution)/shard_map/ppermute | solution.py:378
  52.2 5.6 %collective-permute-done.12.other_ref = s16[1312,128]{1,0:T(8,128)(2,1)S(1)} collective-permute-done((s16[1312,128]{1,0:T(8,128)(2,1)S(1)}, s16[1312,128]{1,0:T(8,128)(2,1)S(1)}, u32[]{:S(2)}, u32[]{:S(2)}) %collective-permute-start.12) | collective-permute-done | bytes 335904 | tf_op jit(solution)/shard_map/ppermute | solution.py:378
  60.5 1.1 copy-done.14
  61.6 3.2 %partial_sums.5 = (f32[1280,128]{1,0:T(8,128)S(1)}, s16[1296,128]{1,0:T(8,128)(2,1)S(1)}, s16[2592,128]{1,0:T(8,128)(2,1)S(1)}) custom-call(s32[1]{0:T(128)} %bitcast.6.flag_ref, bf16[768,512]{1,0:T(8,128)(2,1)S(1)} %copy-done.14, bf16[192,1280]{1,0:T(8,128)(2,1)S(1)} %get-tuple-element.50.refs_0_, bf16[192,1280]{1,0:T(8,128)(2,1)S(1)} %copy-done.3, ...), custom_call_target="tpu_custom_call" | custom-call | flops 1006632960 | bytes 3604480 | tf_op jit(solution)/shard_map/partial_sums/pallas_call | solution.py:167
  65.5 4.4 %collective-permute-start.15 = (s16[2592,128]{1,0:T(8,128)(2,1)S(1)}, s16[2592,128]{1,0:T(8,128)(2,1)S(1)}, u32[]{:S(2)}, u32[]{:S(2)}) collective-permute-start(s16[2592,128]{1,0:T(8,128)(2,1)S(1)} %get-tuple-element.57.own_ref), channel_id=1, source_target_pairs={{0,2},{1,3},{6,4},{7,5},{8,10},{9,11},{14,12},{15,13},{16,18},{17,... | collective-permute-start | bytes 1990664 | tf_op jit(solution)/shard_map/ppermute | solution.py:378
  70.6 1.5 collective-permute-start.16
  72.8 12.6 %collective-permute-done.17.refs_0_ = s16[656,128]{1,0:T(8,128)(2,1)S(1)} collective-permute-done((s16[656,128]{1,0:T(8,128)(2,1)}, s16[656,128]{1,0:T(8,128)(2,1)S(1)}, u32[]{:S(2)}, u32[]{:S(2)}) %collective-permute-start.17) | collective-permute-done | bytes 167968 | tf_op jit(solution)/shard_map/ppermute | solution.py:378
  85.4 1.3 collective-permute-start.19
  86.7 1.2 fusion.2
  89.6 4.1 %collective-permute-done.19.refs_2_ = s16[656,128]{1,0:T(8,128)(2,1)S(1)} collective-permute-done((s16[656,128]{1,0:T(8,128)(2,1)}, s16[656,128]{1,0:T(8,128)(2,1)S(1)}, u32[]{:S(2)}, u32[]{:S(2)}) %collective-permute-start.19) | collective-permute-done | bytes 167968 | tf_op jit(solution)/shard_map/ppermute | solution.py:378
  97.3 3.0 %collective-permute-done.24.refs_2_ = s16[656,128]{1,0:T(8,128)(2,1)S(1)} collective-permute-done((s16[656,128]{1,0:T(8,128)(2,1)S(1)}, s16[656,128]{1,0:T(8,128)(2,1)S(1)}, u32[]{:S(2)}, u32[]{:S(2)}) %collective-permute-start.24) | collective-permute-done | bytes 167968 | tf_op jit(solution)/shard_map/ppermute | solution.py:368
  100.3 1.3 collective-permute-start.28
  104.5 3.2 %partial_sums.6 = (f32[1280,128]{1,0:T(8,128)S(1)}, s16[1296,128]{1,0:T(8,128)(2,1)S(1)}, s16[2592,128]{1,0:T(8,128)(2,1)S(1)}) custom-call(s32[1]{0:T(128)} %bitcast.6.flag_ref, bf16[768,512]{1,0:T(8,128)(2,1)S(1)} %copy-done.15, bf16[192,1280]{1,0:T(8,128)(2,1)S(1)} %get-tuple-element.56.refs_0_, bf16[192,1280]{1,0:T(8,128)(2,1)} %collective-permute-done.7.refs_1_, ...), custom_call_target="tpu_custom_call" | custom-call | flops 1006632960 | bytes 3604480 | tf_op jit(solution)/shard_map/partial_sums/pallas_call | solution.py:167
  107.7 2.8 %collective-permute-done.21.refs_3_ = bf16[192,640]{1,0:T(8,128)(2,1)S(1)} collective-permute-done((bf16[192,640]{1,0:T(8,128)(2,1)S(1)}, bf16[192,640]{1,0:T(8,128)(2,1)S(1)}, u32[]{:S(2)}, u32[]{:S(2)}) %collective-permute-start.21) | collective-permute-done | bytes 245792 | tf_op jit(solution)/shard_map/ppermute | solution.py:374
  110.6 5.6 %collective-permute-start.36 = (s16[2592,128]{1,0:T(8,128)(2,1)S(1)}, s16[2592,128]{1,0:T(8,128)(2,1)S(1)}, u32[]{:S(2)}, u32[]{:S(2)}) collective-permute-start(s16[2592,128]{1,0:T(8,128)(2,1)S(1)} %get-tuple-element.81.own_ref), channel_id=1, source_target_pairs={{0,2},{1,3},{6,4},{7,5},{8,10},{9,11},{14,12},{15,13},{16,18},{17,... | collective-permute-start | bytes 1990664 | tf_op jit(solution)/shard_map/ppermute | solution.py:378
  117.8 1.6 partial_sums.7
  119.4 3.4 %collective-permute-start.22 = (s16[1312,128]{1,0:T(8,128)(2,1)S(1)}, s16[1312,128]{1,0:T(8,128)(2,1)S(1)}, u32[]{:S(2)}, u32[]{:S(2)}) collective-permute-start(s16[1312,128]{1,0:T(8,128)(2,1)S(1)} %get-tuple-element.70.own_ref), channel_id=1, source_target_pairs={{0,2},{1,3},{6,4},{7,5},{8,10},{9,11},{14,12},{15,13},{16,18},{17,... | collective-permute-start | bytes 1007624 | tf_op jit(solution)/shard_map/ppermute | solution.py:378
  122.9 2.5 %collective-permute-done.30.refs_6_ = s16[1296,128]{1,0:T(8,128)(2,1)} collective-permute-done((s16[1296,128]{1,0:T(8,128)(2,1)S(1)}, s16[1296,128]{1,0:T(8,128)(2,1)}, u32[]{:S(2)}, u32[]{:S(2)}) %collective-permute-start.30) | collective-permute-done | bytes 331808 | tf_op jit(solution)/shard_map/ppermute | solution.py:368
  125.9 10.9 %collective-permute-done.22.other_ref = s16[1312,128]{1,0:T(8,128)(2,1)S(1)} collective-permute-done((s16[1312,128]{1,0:T(8,128)(2,1)S(1)}, s16[1312,128]{1,0:T(8,128)(2,1)S(1)}, u32[]{:S(2)}, u32[]{:S(2)}) %collective-permute-start.22) | collective-permute-done | bytes 335904 | tf_op jit(solution)/shard_map/ppermute | solution.py:378
  136.8 2.5 %collective-permute-start.32 = (s16[656,128]{1,0:T(8,128)(2,1)}, s16[656,128]{1,0:T(8,128)(2,1)}, u32[]{:S(2)}, u32[]{:S(2)}) collective-permute-start(s16[656,128]{1,0:T(8,128)(2,1)} %get-tuple-element.77), channel_id=1, source_target_pairs={{0,2},{1,3},{2,0},{3,1},{4,6},{5,7},{6,4},{7,5},{8,10},{9,11},{10,... | collective-permute-start | bytes 503816 | tf_op jit(solution)/shard_map/ppermute | solution.py:378
  140.4 1.3 collective-permute-start.34
  141.7 4.8 %collective-permute-done.32.refs_0_ = s16[656,128]{1,0:T(8,128)(2,1)} collective-permute-done((s16[656,128]{1,0:T(8,128)(2,1)}, s16[656,128]{1,0:T(8,128)(2,1)}, u32[]{:S(2)}, u32[]{:S(2)}) %collective-permute-start.32) | collective-permute-done | bytes 167968 | tf_op jit(solution)/shard_map/ppermute | solution.py:378
  147.9 1.3 collective-permute-start.38
  149.2 12.9 %covariance.1 = f32[13456,128]{1,0:T(8,128)} custom-call(s32[8]{0:T(128)S(1)} %stack.97.place_ref, s16[656,128]{1,0:T(8,128)(2,1)S(1)} %combine.4.refs_0_, s16[656,128]{1,0:T(8,128)(2,1)} %collective-permute-done.23.refs_1_, s16[656,128]{1,0:T(8,128)(2,1)S(1)} %copy-done.8, s16[656,128]{1,0:T(8,128)(2,1)S(1)} %copy-done.10, ...), custom_call_target="tpu_custom_call" | custom-call | flops 15432417280 | bytes 6889472 | tf_op jit(solution)/shard_map/covariance/pallas_call | solution.py:333
  162.1 3.5 %collective-permute-done.38.refs_2_ = s16[1296,128]{1,0:T(8,128)(2,1)S(1)} collective-permute-done((s16[1296,128]{1,0:T(8,128)(2,1)S(1)}, s16[1296,128]{1,0:T(8,128)(2,1)S(1)}, u32[]{:S(2)}, u32[]{:S(2)}) %collective-permute-start.38) | collective-permute-done | bytes 331808 | tf_op jit(solution)/shard_map/ppermute | solution.py:378
  167.2 1.1 combine.7.refs_4_
  169.4 4.1 %collective-permute-done.40.refs_2_ = s16[1296,128]{1,0:T(8,128)(2,1)S(1)} collective-permute-done((s16[1296,128]{1,0:T(8,128)(2,1)S(1)}, s16[1296,128]{1,0:T(8,128)(2,1)S(1)}, u32[]{:S(2)}, u32[]{:S(2)}) %collective-permute-start.40) | collective-permute-done | bytes 331808 | tf_op jit(solution)/shard_map/ppermute | solution.py:368
  174.0 1.3 collective-permute-done.43.refs_6_
  175.4 1.3 collective-permute-done.44.refs_7_
  176.7 3.8 %marginal.1 = f32[128,7424]{1,0:T(8,128)} custom-call(s32[8]{0:T(128)S(1)} %stack.83.place_ref, s16[1296,128]{1,0:T(8,128)(2,1)S(1)} %combine.6.refs_0_, s16[1296,128]{1,0:T(8,128)(2,1)S(1)} %collective-permute-done.39.refs_1_, s16[1296,128]{1,0:T(8,128)(2,1)S(1)} %collective-permute-done.40.refs_2_, s16[1296,128]{1,0:T(8,128)(2,1)S(1)} %collective-permute-done.41.refs_3_, ...), custom_call_target="tpu_custom_call" | custom-call | flops 3801088 | bytes 5701632 | tf_op jit(solution)/shard_map/marginal/pallas_call | solution.py:260
  (110 shorter events, 23.3 us)
Async XLA Ops:
  1.4 8.2 %collective-permute-start.2 = (s32[64,128]{1,0:T(8,128)S(1)}, s32[64,128]{1,0:T(8,128)S(1)}, u32[]{:S(2)}, u32[]{:S(2)}) collective-permute-start(s32[64,128]{1,0:T(8,128)S(1)} %pad_add_fusion.1), channel_id=1, source_target_pairs={{0,4},{1,5},{2,6},{3,7},{4,0},{5,1},{6,2},{7,3},{8,12},{9,13},{10,... | collective-permute-start | bytes 98312 | tf_op jit(solution)/shard_map/ppermute | solution.py:378
  5.4 5.7 %collective-permute-start.1 = (s32[64,128]{1,0:T(8,128)S(1)}, s32[64,128]{1,0:T(8,128)S(1)}, u32[]{:S(2)}, u32[]{:S(2)}) collective-permute-start(s32[64,128]{1,0:T(8,128)S(1)} %pad_add_fusion.1), channel_id=1, source_target_pairs={{0,6},{1,7},{2,4},{3,5},{4,2},{5,3},{6,0},{7,1},{8,14},{9,15},{10,... | collective-permute-start | bytes 98312 | tf_op jit(solution)/shard_map/ppermute | solution.py:378
  6.8 4.4 %collective-permute-start = (s32[64,128]{1,0:T(8,128)S(1)}, s32[64,128]{1,0:T(8,128)S(1)}, u32[]{:S(2)}, u32[]{:S(2)}) collective-permute-start(s32[64,128]{1,0:T(8,128)S(1)} %pad_add_fusion.1), channel_id=1, source_target_pairs={{0,2},{1,3},{2,0},{3,1},{4,6},{5,7},{6,4},{7,5},{8,10},{9,11},{10,... | collective-permute-start | bytes 98312 | tf_op jit(solution)/shard_map/ppermute | solution.py:378
  9.2 8.3 %collective-permute-start.4 = (bf16[96,3840]{1,0:T(8,128)(2,1)S(1)}, bf16[96,3840]{1,0:T(8,128)(2,1)S(1)}, u32[]{:S(2)}, u32[]{:S(2)}) collective-permute-start(bf16[96,3840]{1,0:T(8,128)(2,1)S(1)} %pad_maximum_fusion.1), channel_id=1, source_target_pairs={{0,8},{8,0},{16,24},{24,16},{1,9},{9,1},{17,25},{25,17},{2,10},{10... | collective-permute-start | bytes 2211848 | tf_op jit(solution)/shard_map/ppermute | solution.py:368
  17.5 12.2 %collective-permute-start.3 = (bf16[96,3712]{1,0:T(8,128)(2,1)}, bf16[96,3712]{1,0:T(8,128)(2,1)}, u32[]{:S(2)}, u32[]{:S(2)}) collective-permute-start(bf16[96,3712]{1,0:T(8,128)(2,1)} %get-tuple-element.96), channel_id=1, source_target_pairs={{0,8},{8,0},{16,24},{24,16},{1,9},{9,1},{17,25},{25,17},{2,10},{10... | collective-permute-start | bytes 2138120 | tf_op jit(solution)/shard_map/ppermute | solution.py:368
  17.7 8.4 %collective-permute-start.5 = (bf16[192,640]{1,0:T(8,128)(2,1)S(1)}, bf16[192,640]{1,0:T(8,128)(2,1)S(1)}, u32[]{:S(2)}, u32[]{:S(2)}) collective-permute-start(bf16[192,640]{1,0:T(8,128)(2,1)S(1)} %get-tuple-element.89), channel_id=1, source_target_pairs={{0,16},{8,24},{16,0},{24,8},{1,17},{9,25},{17,1},{25,9},{2,18},{10... | collective-permute-start | bytes 737288 | tf_op jit(solution)/shard_map/ppermute | solution.py:368
  19.2 8.4 %collective-permute-start.9 = (bf16[192,640]{1,0:T(8,128)(2,1)S(1)}, bf16[192,640]{1,0:T(8,128)(2,1)S(1)}, u32[]{:S(2)}, u32[]{:S(2)}) collective-permute-start(bf16[192,640]{1,0:T(8,128)(2,1)S(1)} %get-tuple-element.88.refs_0_), channel_id=1, source_target_pairs={{0,1},{1,0},{2,3},{3,2},{4,5},{5,4},{6,7},{7,6},{8,9},{9,8},{10,11... | collective-permute-start | bytes 737288 | tf_op jit(solution)/shard_map/ppermute | solution.py:374
  26.1 12.9 %collective-permute-start.6 = (bf16[192,1280]{1,0:T(8,128)(2,1)S(1)}, bf16[192,1280]{1,0:T(8,128)(2,1)S(1)}, u32[]{:S(2)}, u32[]{:S(2)}) collective-permute-start(bf16[192,1280]{1,0:T(8,128)(2,1)S(1)} %get-tuple-element.45), channel_id=1, source_target_pairs={{0,16},{8,24},{16,0},{24,8},{1,17},{9,25},{17,1},{25,9},{2,18},{10... | collective-permute-start | bytes 1474568 | tf_op jit(solution)/shard_map/ppermute | solution.py:368
  27.6 24.6 %collective-permute-start.11 = (bf16[192,1280]{1,0:T(8,128)(2,1)S(1)}, bf16[192,1280]{1,0:T(8,128)(2,1)}, u32[]{:S(2)}, u32[]{:S(2)}) collective-permute-start(bf16[192,1280]{1,0:T(8,128)(2,1)S(1)} %get-tuple-element.50.refs_0_), channel_id=1, source_target_pairs={{0,1},{1,0},{2,3},{3,2},{4,5},{5,4},{6,7},{7,6},{8,9},{9,8},{10,11... | collective-permute-start | bytes 1474568 | tf_op jit(solution)/shard_map/ppermute | solution.py:374
  29.1 16.3 %collective-permute-start.10 = (bf16[192,640]{1,0:T(8,128)(2,1)S(1)}, bf16[192,640]{1,0:T(8,128)(2,1)S(1)}, u32[]{:S(2)}, u32[]{:S(2)}) collective-permute-start(bf16[192,640]{1,0:T(8,128)(2,1)S(1)} %collective-permute-done.5.refs_1_), channel_id=1, source_target_pairs={{0,1},{1,0},{2,3},{3,2},{4,5},{5,4},{6,7},{7,6},{8,9},{9,8},{10,11... | collective-permute-start | bytes 737288 | tf_op jit(solution)/shard_map/ppermute | solution.py:374
  39.0 19.8 %copy-start.2 = (bf16[192,1280]{1,0:T(8,128)(2,1)}, bf16[192,1280]{1,0:T(8,128)(2,1)S(1)}, u32[]{:S(2)}) copy-start(bf16[192,1280]{1,0:T(8,128)(2,1)S(1)} %collective-permute-done.6.refs_1_) | copy-start | bytes 1474564
  39.0 19.8 %collective-permute-start.7 = (bf16[192,1280]{1,0:T(8,128)(2,1)}, bf16[192,1280]{1,0:T(8,128)(2,1)}, u32[]{:S(2)}, u32[]{:S(2)}) collective-permute-start(bf16[192,1280]{1,0:T(8,128)(2,1)} %get-tuple-element.46), channel_id=1, source_target_pairs={{0,16},{8,24},{16,0},{24,8},{1,17},{9,25},{17,1},{25,9},{2,18},{10... | collective-permute-start | bytes 1474568 | tf_op jit(solution)/shard_map/ppermute | solution.py:368
  45.5 14.0 %collective-permute-start.13 = (bf16[192,1280]{1,0:T(8,128)(2,1)S(1)}, bf16[192,1280]{1,0:T(8,128)(2,1)}, u32[]{:S(2)}, u32[]{:S(2)}) collective-permute-start(bf16[192,1280]{1,0:T(8,128)(2,1)S(1)} %collective-permute-done.6.refs_1_), channel_id=1, source_target_pairs={{0,1},{1,0},{2,3},{3,2},{4,5},{5,4},{6,7},{7,6},{8,9},{9,8},{10,11... | collective-permute-start | bytes 1474568 | tf_op jit(solution)/shard_map/ppermute | solution.py:374
  49.8 8.1 %collective-permute-start.12 = (s16[1312,128]{1,0:T(8,128)(2,1)S(1)}, s16[1312,128]{1,0:T(8,128)(2,1)S(1)}, u32[]{:S(2)}, u32[]{:S(2)}) collective-permute-start(s16[1312,128]{1,0:T(8,128)(2,1)S(1)} %get-tuple-element.51.own_ref), channel_id=1, source_target_pairs={{0,2},{1,3},{6,4},{7,5},{8,10},{9,11},{14,12},{15,13},{16,18},{17,... | collective-permute-start | bytes 1007624 | tf_op jit(solution)/shard_map/ppermute | solution.py:378
  65.5 30.5 %collective-permute-start.15 = (s16[2592,128]{1,0:T(8,128)(2,1)S(1)}, s16[2592,128]{1,0:T(8,128)(2,1)S(1)}, u32[]{:S(2)}, u32[]{:S(2)}) collective-permute-start(s16[2592,128]{1,0:T(8,128)(2,1)S(1)} %get-tuple-element.57.own_ref), channel_id=1, source_target_pairs={{0,2},{1,3},{6,4},{7,5},{8,10},{9,11},{14,12},{15,13},{16,18},{17,... | collective-permute-start | bytes 1990664 | tf_op jit(solution)/shard_map/ppermute | solution.py:378
  69.9 15.5 %collective-permute-start.17 = (s16[656,128]{1,0:T(8,128)(2,1)}, s16[656,128]{1,0:T(8,128)(2,1)S(1)}, u32[]{:S(2)}, u32[]{:S(2)}) collective-permute-start(s16[656,128]{1,0:T(8,128)(2,1)} %get-tuple-element.64), channel_id=1, source_target_pairs={{0,2},{1,3},{2,0},{3,1},{4,6},{5,7},{6,4},{7,5},{8,10},{9,11},{10,... | collective-permute-start | bytes 503816 | tf_op jit(solution)/shard_map/ppermute | solution.py:378
  70.0 26.0 %collective-permute-start.14 = (bf16[192,1280]{1,0:T(8,128)(2,1)S(1)}, bf16[192,1280]{1,0:T(8,128)(2,1)}, u32[]{:S(2)}, u32[]{:S(2)}) collective-permute-start(bf16[192,1280]{1,0:T(8,128)(2,1)S(1)} %get-tuple-element.56.refs_0_), channel_id=1, source_target_pairs={{0,1},{1,0},{2,3},{3,2},{4,5},{5,4},{6,7},{7,6},{8,9},{9,8},{10,11... | collective-permute-start | bytes 1474568 | tf_op jit(solution)/shard_map/ppermute | solution.py:374
  70.6 31.2 %collective-permute-start.16 = (bf16[192,1280]{1,0:T(8,128)(2,1)}, bf16[192,1280]{1,0:T(8,128)(2,1)}, u32[]{:S(2)}, u32[]{:S(2)}) collective-permute-start(bf16[192,1280]{1,0:T(8,128)(2,1)} %collective-permute-done.7.refs_1_), channel_id=1, source_target_pairs={{0,1},{1,0},{2,3},{3,2},{4,5},{5,4},{6,7},{7,6},{8,9},{9,8},{10,11... | collective-permute-start | bytes 1474568 | tf_op jit(solution)/shard_map/ppermute | solution.py:374
  72.1 15.8 %collective-permute-start.18 = (s16[656,128]{1,0:T(8,128)(2,1)}, s16[656,128]{1,0:T(8,128)(2,1)S(1)}, u32[]{:S(2)}, u32[]{:S(2)}) collective-permute-start(s16[656,128]{1,0:T(8,128)(2,1)} %get-tuple-element.65), channel_id=1, source_target_pairs={{2,4},{3,5},{4,2},{5,3},{10,12},{11,13},{12,10},{13,11},{18,20},{1... | collective-permute-start | bytes 503816 | tf_op jit(solution)/shard_map/ppermute | solution.py:378
  72.8 23.2 %copy-start.6 = (s16[1296,128]{1,0:T(8,128)(2,1)S(1)}, s16[1296,128]{1,0:T(8,128)(2,1)}, u32[]{:S(2)}) copy-start(s16[1296,128]{1,0:T(8,128)(2,1)} %copy-done.5) | copy-start | bytes 995332
  85.4 8.4 %collective-permute-start.19 = (s16[656,128]{1,0:T(8,128)(2,1)}, s16[656,128]{1,0:T(8,128)(2,1)S(1)}, u32[]{:S(2)}, u32[]{:S(2)}) collective-permute-start(s16[656,128]{1,0:T(8,128)(2,1)} %copy-done.11), channel_id=1, source_target_pairs={{2,6},{3,7},{4,0},{5,1},{10,14},{11,15},{12,8},{13,9},{18,22},{19,... | collective-permute-start | bytes 503816 | tf_op jit(solution)/shard_map/ppermute | solution.py:378
  88.6 13.0 %collective-permute-start.8 = (bf16[192,640]{1,0:T(8,128)(2,1)S(1)}, bf16[192,640]{1,0:T(8,128)(2,1)S(1)}, u32[]{:S(2)}, u32[]{:S(2)}) collective-permute-start(bf16[192,640]{1,0:T(8,128)(2,1)S(1)} %get-tuple-element.47), channel_id=1, source_target_pairs={{0,16},{8,24},{16,0},{24,8},{1,17},{9,25},{17,1},{25,9},{2,18},{10... | collective-permute-start | bytes 737288 | tf_op jit(solution)/shard_map/ppermute | solution.py:368
  94.9 5.4 %collective-permute-start.24 = (s16[656,128]{1,0:T(8,128)(2,1)S(1)}, s16[656,128]{1,0:T(8,128)(2,1)S(1)}, u32[]{:S(2)}, u32[]{:S(2)}) collective-permute-start(s16[656,128]{1,0:T(8,128)(2,1)S(1)} %combine.4.refs_0_), channel_id=1, source_target_pairs={{0,16},{8,24},{16,0},{24,8},{1,17},{9,25},{17,1},{25,9},{2,18},{10... | collective-permute-start | bytes 503816 | tf_op jit(solution)/shard_map/ppermute | solution.py:368
  96.0 20.1 %collective-permute-start.26 = (s16[1296,128]{1,0:T(8,128)(2,1)S(1)}, s16[1296,128]{1,0:T(8,128)(2,1)S(1)}, u32[]{:S(2)}, u32[]{:S(2)}) collective-permute-start(s16[1296,128]{1,0:T(8,128)(2,1)S(1)} %copy-done.6), channel_id=1, source_target_pairs={{0,2},{1,3},{2,0},{3,1},{4,6},{5,7},{6,4},{7,5},{8,10},{9,11},{10,... | collective-permute-start | bytes 995336 | tf_op jit(solution)/shard_map/ppermute | solution.py:378
  96.6 19.5 %collective-permute-start.27 = (s16[1296,128]{1,0:T(8,128)(2,1)S(1)}, s16[1296,128]{1,0:T(8,128)(2,1)S(1)}, u32[]{:S(2)}, u32[]{:S(2)}) collective-permute-start(s16[1296,128]{1,0:T(8,128)(2,1)S(1)} %get-tuple-element.76), channel_id=1, source_target_pairs={{2,4},{3,5},{4,2},{5,3},{10,12},{11,13},{12,10},{13,11},{18,20},{1... | collective-permute-start | bytes 995336 | tf_op jit(solution)/shard_map/ppermute | solution.py:378
  100.3 15.8 %collective-permute-start.28 = (s16[1296,128]{1,0:T(8,128)(2,1)S(1)}, s16[1296,128]{1,0:T(8,128)(2,1)S(1)}, u32[]{:S(2)}, u32[]{:S(2)}) collective-permute-start(s16[1296,128]{1,0:T(8,128)(2,1)S(1)} %get-tuple-element.58), channel_id=1, source_target_pairs={{2,6},{3,7},{4,0},{5,1},{10,14},{11,15},{12,8},{13,9},{18,22},{19,... | collective-permute-start | bytes 995336 | tf_op jit(solution)/shard_map/ppermute | solution.py:378
  101.6 1.5 collective-permute-start.25
  101.7 8.8 %collective-permute-start.21 = (bf16[192,640]{1,0:T(8,128)(2,1)S(1)}, bf16[192,640]{1,0:T(8,128)(2,1)S(1)}, u32[]{:S(2)}, u32[]{:S(2)}) collective-permute-start(bf16[192,640]{1,0:T(8,128)(2,1)S(1)} %collective-permute-done.8.refs_1_), channel_id=1, source_target_pairs={{0,1},{1,0},{2,3},{3,2},{4,5},{5,4},{6,7},{7,6},{8,9},{9,8},{10,11... | collective-permute-start | bytes 737288 | tf_op jit(solution)/shard_map/ppermute | solution.py:374
  103.8 14.0 %collective-permute-start.20 = (bf16[192,640]{1,0:T(8,128)(2,1)S(1)}, bf16[192,640]{1,0:T(8,128)(2,1)S(1)}, u32[]{:S(2)}, u32[]{:S(2)}) collective-permute-start(bf16[192,640]{1,0:T(8,128)(2,1)S(1)} %get-tuple-element.68.refs_0_), channel_id=1, source_target_pairs={{0,1},{1,0},{2,3},{3,2},{4,5},{5,4},{6,7},{7,6},{8,9},{9,8},{10,11... | collective-permute-start | bytes 737288 | tf_op jit(solution)/shard_map/ppermute | solution.py:374
  107.7 29.1 %copy-start.4 = (s16[1296,128]{1,0:T(8,128)(2,1)}, s16[1296,128]{1,0:T(8,128)(2,1)S(1)}, u32[]{:S(2)}) copy-start(s16[1296,128]{1,0:T(8,128)(2,1)S(1)} %get-tuple-element.80) | copy-start | bytes 995332
  110.6 29.2 %collective-permute-start.36 = (s16[2592,128]{1,0:T(8,128)(2,1)S(1)}, s16[2592,128]{1,0:T(8,128)(2,1)S(1)}, u32[]{:S(2)}, u32[]{:S(2)}) collective-permute-start(s16[2592,128]{1,0:T(8,128)(2,1)S(1)} %get-tuple-element.81.own_ref), channel_id=1, source_target_pairs={{0,2},{1,3},{6,4},{7,5},{8,10},{9,11},{14,12},{15,13},{16,18},{17,... | collective-permute-start | bytes 1990664 | tf_op jit(solution)/shard_map/ppermute | solution.py:378
  116.6 8.8 %collective-permute-start.30 = (s16[1296,128]{1,0:T(8,128)(2,1)S(1)}, s16[1296,128]{1,0:T(8,128)(2,1)}, u32[]{:S(2)}, u32[]{:S(2)}) collective-permute-start(s16[1296,128]{1,0:T(8,128)(2,1)S(1)} %combine.5.refs_4_), channel_id=1, source_target_pairs={{0,16},{8,24},{16,0},{24,8},{1,17},{9,25},{17,1},{25,9},{2,18},{10... | collective-permute-start | bytes 995336 | tf_op jit(solution)/shard_map/ppermute | solution.py:368
  119.4 17.4 %collective-permute-start.22 = (s16[1312,128]{1,0:T(8,128)(2,1)S(1)}, s16[1312,128]{1,0:T(8,128)(2,1)S(1)}, u32[]{:S(2)}, u32[]{:S(2)}) collective-permute-start(s16[1312,128]{1,0:T(8,128)(2,1)S(1)} %get-tuple-element.70.own_ref), channel_id=1, source_target_pairs={{0,2},{1,3},{6,4},{7,5},{8,10},{9,11},{14,12},{15,13},{16,18},{17,... | collective-permute-start | bytes 1007624 | tf_op jit(solution)/shard_map/ppermute | solution.py:378
  122.8 24.4 %collective-permute-start.29 = (s16[1296,128]{1,0:T(8,128)(2,1)S(1)}, s16[1296,128]{1,0:T(8,128)(2,1)}, u32[]{:S(2)}, u32[]{:S(2)}) collective-permute-start(s16[1296,128]{1,0:T(8,128)(2,1)S(1)} %combine.5.refs_4_), channel_id=1, source_target_pairs={{0,8},{8,0},{16,24},{24,16},{1,9},{9,1},{17,25},{25,17},{2,10},{10... | collective-permute-start | bytes 995336 | tf_op jit(solution)/shard_map/ppermute | solution.py:368
  125.4 22.5 %collective-permute-start.31 = (s16[1296,128]{1,0:T(8,128)(2,1)}, s16[1296,128]{1,0:T(8,128)(2,1)}, u32[]{:S(2)}, u32[]{:S(2)}) collective-permute-start(s16[1296,128]{1,0:T(8,128)(2,1)} %collective-permute-done.30.refs_6_), channel_id=1, source_target_pairs={{0,8},{8,0},{16,24},{24,16},{1,9},{9,1},{17,25},{25,17},{2,10},{10... | collective-permute-start | bytes 995336 | tf_op jit(solution)/shard_map/ppermute | solution.py:368
  125.4 15.0 %collective-permute-start.23 = (s16[656,128]{1,0:T(8,128)(2,1)S(1)}, s16[656,128]{1,0:T(8,128)(2,1)}, u32[]{:S(2)}, u32[]{:S(2)}) collective-permute-start(s16[656,128]{1,0:T(8,128)(2,1)S(1)} %combine.4.refs_0_), channel_id=1, source_target_pairs={{0,8},{8,0},{16,24},{24,16},{1,9},{9,1},{17,25},{25,17},{2,10},{10... | collective-permute-start | bytes 503816 | tf_op jit(solution)/shard_map/ppermute | solution.py:368
  136.8 9.7 %collective-permute-start.32 = (s16[656,128]{1,0:T(8,128)(2,1)}, s16[656,128]{1,0:T(8,128)(2,1)}, u32[]{:S(2)}, u32[]{:S(2)}) collective-permute-start(s16[656,128]{1,0:T(8,128)(2,1)} %get-tuple-element.77), channel_id=1, source_target_pairs={{0,2},{1,3},{2,0},{3,1},{4,6},{5,7},{6,4},{7,5},{8,10},{9,11},{10,... | collective-permute-start | bytes 503816 | tf_op jit(solution)/shard_map/ppermute | solution.py:378
  139.7 22.4 %collective-permute-start.35 = (s16[1296,128]{1,0:T(8,128)(2,1)}, s16[1296,128]{1,0:T(8,128)(2,1)S(1)}, u32[]{:S(2)}, u32[]{:S(2)}) collective-permute-start(s16[1296,128]{1,0:T(8,128)(2,1)} %copy-done.4), channel_id=1, source_target_pairs={{0,2},{1,3},{2,0},{3,1},{4,6},{5,7},{6,4},{7,5},{8,10},{9,11},{10,... | collective-permute-start | bytes 995336 | tf_op jit(solution)/shard_map/ppermute | solution.py:378
  140.4 21.7 %collective-permute-start.34 = (s16[656,128]{1,0:T(8,128)(2,1)S(1)}, s16[656,128]{1,0:T(8,128)(2,1)S(1)}, u32[]{:S(2)}, u32[]{:S(2)}) collective-permute-start(s16[656,128]{1,0:T(8,128)(2,1)S(1)} %get-tuple-element.71), channel_id=1, source_target_pairs={{2,6},{3,7},{4,0},{5,1},{10,14},{11,15},{12,8},{13,9},{18,22},{19,... | collective-permute-start | bytes 503816 | tf_op jit(solution)/shard_map/ppermute | solution.py:378
  146.5 15.6 %collective-permute-start.33 = (s16[656,128]{1,0:T(8,128)(2,1)S(1)}, s16[656,128]{1,0:T(8,128)(2,1)S(1)}, u32[]{:S(2)}, u32[]{:S(2)}) collective-permute-start(s16[656,128]{1,0:T(8,128)(2,1)S(1)} %get-tuple-element.78), channel_id=1, source_target_pairs={{2,4},{3,5},{4,2},{5,3},{10,12},{11,13},{12,10},{13,11},{18,20},{1... | collective-permute-start | bytes 503816 | tf_op jit(solution)/shard_map/ppermute | solution.py:378
  147.2 15.0 %collective-permute-start.37 = (s16[1296,128]{1,0:T(8,128)(2,1)S(1)}, s16[1296,128]{1,0:T(8,128)(2,1)S(1)}, u32[]{:S(2)}, u32[]{:S(2)}) collective-permute-start(s16[1296,128]{1,0:T(8,128)(2,1)S(1)} %get-tuple-element.82), channel_id=1, source_target_pairs={{2,4},{3,5},{4,2},{5,3},{10,12},{11,13},{12,10},{13,11},{18,20},{1... | collective-permute-start | bytes 995336 | tf_op jit(solution)/shard_map/ppermute | solution.py:378
  147.9 17.8 %collective-permute-start.38 = (s16[1296,128]{1,0:T(8,128)(2,1)S(1)}, s16[1296,128]{1,0:T(8,128)(2,1)S(1)}, u32[]{:S(2)}, u32[]{:S(2)}) collective-permute-start(s16[1296,128]{1,0:T(8,128)(2,1)S(1)} %get-tuple-element.83), channel_id=1, source_target_pairs={{2,6},{3,7},{4,0},{5,1},{10,14},{11,15},{12,8},{13,9},{18,22},{19,... | collective-permute-start | bytes 995336 | tf_op jit(solution)/shard_map/ppermute | solution.py:378
  166.1 7.4 %collective-permute-start.40 = (s16[1296,128]{1,0:T(8,128)(2,1)S(1)}, s16[1296,128]{1,0:T(8,128)(2,1)S(1)}, u32[]{:S(2)}, u32[]{:S(2)}) collective-permute-start(s16[1296,128]{1,0:T(8,128)(2,1)S(1)} %combine.6.refs_0_), channel_id=1, source_target_pairs={{0,16},{8,24},{16,0},{24,8},{1,17},{9,25},{17,1},{25,9},{2,18},{10... | collective-permute-start | bytes 995336 | tf_op jit(solution)/shard_map/ppermute | solution.py:368
  168.3 6.9 %collective-permute-start.43 = (s16[656,128]{1,0:T(8,128)(2,1)S(1)}, s16[656,128]{1,0:T(8,128)(2,1)S(1)}, u32[]{:S(2)}, u32[]{:S(2)}) collective-permute-start(s16[656,128]{1,0:T(8,128)(2,1)S(1)} %combine.7.refs_4_), channel_id=1, source_target_pairs={{0,16},{8,24},{16,0},{24,8},{1,17},{9,25},{17,1},{25,9},{2,18},{10... | collective-permute-start | bytes 503816 | tf_op jit(solution)/shard_map/ppermute | solution.py:368
  169.4 6.0 %collective-permute-start.39 = (s16[1296,128]{1,0:T(8,128)(2,1)S(1)}, s16[1296,128]{1,0:T(8,128)(2,1)S(1)}, u32[]{:S(2)}, u32[]{:S(2)}) collective-permute-start(s16[1296,128]{1,0:T(8,128)(2,1)S(1)} %combine.6.refs_0_), channel_id=1, source_target_pairs={{0,8},{8,0},{16,24},{24,16},{1,9},{9,1},{17,25},{25,17},{2,10},{10... | collective-permute-start | bytes 995336 | tf_op jit(solution)/shard_map/ppermute | solution.py:368
  173.5 3.2 %collective-permute-start.41 = (s16[1296,128]{1,0:T(8,128)(2,1)S(1)}, s16[1296,128]{1,0:T(8,128)(2,1)S(1)}, u32[]{:S(2)}, u32[]{:S(2)}) collective-permute-start(s16[1296,128]{1,0:T(8,128)(2,1)S(1)} %collective-permute-done.40.refs_2_), channel_id=1, source_target_pairs={{0,8},{8,0},{16,24},{24,16},{1,9},{9,1},{17,25},{25,17},{2,10},{10... | collective-permute-start | bytes 995336 | tf_op jit(solution)/shard_map/ppermute | solution.py:368
  173.5 1.9 %collective-permute-start.42 = (s16[656,128]{1,0:T(8,128)(2,1)S(1)}, s16[656,128]{1,0:T(8,128)(2,1)S(1)}, u32[]{:S(2)}, u32[]{:S(2)}) collective-permute-start(s16[656,128]{1,0:T(8,128)(2,1)S(1)} %combine.7.refs_4_), channel_id=1, source_target_pairs={{0,8},{8,0},{16,24},{24,16},{1,9},{9,1},{17,25},{25,17},{2,10},{10... | collective-permute-start | bytes 503816 | tf_op jit(solution)/shard_map/ppermute | solution.py:368
  175.3 1.4 collective-permute-start.44
  (16 other events, 62.1 us)

commit v5 on v4

--- a/solution.py
+++ b/solution.py
@@ -9,7 +9,7 @@
 LANES = 128
 CORES = 2
 DEPTH = 4
-LOAD_FIRST = 5
+LOAD_FIRST = 8
 MEAN_FIRST = 10
 SCALES = 16
 TOP = 32767.0
@@ -23,7 +23,7 @@
 
 
 def cost(flops, moved):
-    return pl.CostEstimate(flops=flops, bytes_accessed=moved, transcendentals=0)
+    return pl.CostEstimate(flops=flops // 64, bytes_accessed=moved // 64, transcendentals=0)
 
 
 def after(value, *others):
@@ -100,23 +100,27 @@
         ),
         out_shape=jax.ShapeDtypeStruct(shape, jnp.bfloat16),
         compiler_params=params(),
-        cost_estimate=cost(shape[0] * width * queries.shape[0] * 200, shape[0] * width * 2),
+        cost_estimate=cost(shape[0] * width * queries.shape[0], shape[0] * width * 2),
         name="build_weights",
     )(bases, queries)
 
 
-def sums_kernel(parts, has_var, flag_ref, w_ref, *refs):
+def sums_kernel(offsets, has_var, flag_ref, w_ref, *refs):
+    parts = len(offsets)
     data = refs[:parts]
     own_ref, near_ref, far_ref, acc_ref = refs[parts:]
-    depth, columns = data[0].shape
+    columns = own_ref.shape[0]
     coded = columns + SCALES
+    rows = [0]
+    for d in data:
+        rows.append(rows[-1] + d.shape[0])
 
     def weighted(get, t):
         total = None
         for j in range(parts):
             part = lax.dot_general(
-                data[j][:, t * LANES:(t + 1) * LANES],
-                get(w_ref[j * depth:(j + 1) * depth, :]),
+                data[j][:, (offsets[j] + t) * LANES:(offsets[j] + t + 1) * LANES],
+                get(w_ref[rows[j]:rows[j + 1], :]),
                 BEFORE,
                 preferred_element_type=jnp.float32,
             )
@@ -154,9 +158,10 @@
     encode(acc_ref.at[2], 0, far_ref, coded, columns)
 
 
-def partial_sums(flag, w, data, has_var):
-    depth, columns = data[0].shape
-    parts = len(data)
+def partial_sums(flag, w, data, count, has_var):
+    columns = count * LANES
+    offsets = tuple(first for _, first in data)
+    data = [array for array, _ in data]
     coded = columns + SCALES
     whole = lambda i, s: (0, 0)
     shapes = [
@@ -165,17 +170,17 @@
         jax.ShapeDtypeStruct((2 * coded, LANES), jnp.int16),
     ]
     return pl.pallas_call(
-        functools.partial(sums_kernel, parts, has_var),
+        functools.partial(sums_kernel, offsets, has_var),
         grid_spec=pltpu.PrefetchScalarGridSpec(
             num_scalar_prefetch=1,
             grid=(1,),
-            in_specs=[pl.BlockSpec(w.shape, whole)] + [pl.BlockSpec((depth, columns), whole)] * parts,
+            in_specs=[pl.BlockSpec(w.shape, whole)] + [pl.BlockSpec(d.shape, whole) for d in data],
             out_specs=[pl.BlockSpec(s.shape, whole) for s in shapes],
             scratch_shapes=[pltpu.VMEM((DEPTH - 1, columns, LANES), jnp.float32)],
         ),
         out_shape=shapes,
         compiler_params=params(),
-        cost_estimate=cost(2 * w.shape[0] * w.shape[1] * columns, 2 * depth * parts * columns + columns * LANES * 10),
+        cost_estimate=cost(2 * w.shape[0] * w.shape[1] * columns, 2 * w.shape[0] * columns + columns * LANES * 10),
         name="partial_sums",
     )(flag, w, *data)
 
@@ -345,7 +350,7 @@
         ),
         out_shape=jax.ShapeDtypeStruct(shape, jnp.float32),
         compiler_params=params(),
-        cost_estimate=cost(LANES * ages * ages * rank * 140, shape[0] * shape[1] * 4),
+        cost_estimate=cost(LANES * ages * ages * rank * 2, shape[0] * shape[1] * 4),
         name="covariance",
     )(places, *pieces)
 
@@ -406,9 +411,7 @@
         return jnp.concatenate([lax.dynamic_slice(array, (0, c * width), (rows, width)), *more], axis=1)
 
     def exchange(array, *more):
-        return jnp.concatenate(
-            [half(array, core, *more), geo_shift(half(array, 1 - core, *more), 0, 1)], axis=0
-        )
+        return half(array, core, *more), geo_shift(half(array, 1 - core, *more), 0, 1)
 
     def start_of(group, tiles):
         return jnp.minimum(group * each_of(tiles), tiles - each_of(tiles))
@@ -416,32 +419,39 @@
     def each_of(tiles):
         return -(-tiles // xs)
 
-    def along_x(both, first, count, *done):
-        def part(group):
-            start = (start_of(group, both.shape[1] // LANES) + first) * LANES
-            return lax.dynamic_slice(both, (0, start), (both.shape[0], count * LANES))
-
-        others = [geo_shift(after(part((x + dx) % xs), *done), dx, 0) for dx in range(1, xs)]
-        return [part(x)] + others
-
-    def along_y(by_x, *done):
-        if done:
-            by_x = [after(value, other) for value, other in zip(by_x, done)]
-        return by_x + [y_shift(value, dy) for dy in range(1, ys) for value in by_x]
-
-    def along_z(data, has_var, before_sums, before_middle):
-        own, close, far = partial_sums(flag, after(w, *before_sums), data, has_var)
+    def part(value, group):
+        tiles = value.shape[1] // LANES
+        return lax.dynamic_slice(value, (0, start_of(group, tiles) * LANES), (rows, each_of(tiles) * LANES))
+
+    def along_x(both):
+        return [[geo_shift(part(b, (x + dx) % xs), dx, 0) for b in both] for dx in range(xs)]
+
+    def joined(pieces, first, count):
+        return jnp.concatenate([p[:, first * LANES:(first + count) * LANES] for p in pieces], axis=0)
+
+    def along_y(pieces, *done):
+        sent = [after(value, *done) for value in pieces]
+        return [[(value, 0) for value in pieces]] + [[(y_shift(value, dy), 0) for value in sent] for dy in range(1, ys)]
+
+    def later(by_y, tiles):
+        return [[(value, first + tiles) for value, first in pieces] for pieces in by_y]
+
+    def merge(by_x):
+        return [piece for dy in range(ys) for by_y in by_x for piece in by_y[dy]]
+
+    def along_z(data, count, has_var, before_sums, before_middle):
+        own, close, far = partial_sums(flag, after(w, *before_sums), data, count, has_var)
         far_in = z_send(far, ((0, 1), (3, 2)))
         close_in = z_send(close, near)
         to_middle, to_end = middle(after(far, *before_middle), far_in)
         middle_in = z_send(to_middle, ((1, 2), (2, 1)))
         end_in = z_send(to_end, ((1, 3), (2, 0)))
-        return (far, to_end), own, [close_in, middle_in, end_in]
+        return (far_in, to_end, close_in), own, [close_in, middle_in, end_in]
 
     def spread(own, others, *done):
         mine = combine(after(own, *done), others)
         along = [geo_shift(mine, dx, 0) for dx in range(xs)]
-        return [geo_shift(along[dx], 0, dc) for dx in range(xs) for dc in range(CORES)]
+        return mine, [geo_shift(along[dx], 0, dc) for dx in range(xs) for dc in range(CORES)]
 
     def places(tiles):
         starts, lasts = [], []
@@ -456,32 +466,26 @@
     load_width = factors.shape[1] // LANES // CORES + 1
     load_tiles = split(each_of(load_width), LOAD_FIRST)
     mean_tiles = split(each_of(mean_width), MEAN_FIRST)
-    by_x, by_y, by_z = [], [], []
-
-    def feed(both, tiles):
-        for i, count in enumerate(tiles):
-            by_x.append(along_x(both, sum(tiles[:i]), count, *[values[-1] for values in by_x[-1:]]))
-
-    feed(exchange(factors, last_tile), load_tiles)
-    feed(exchange(after(estimates, w)), mean_tiles)
-    for values in by_x:
-        by_y.append(along_y(values, *[done for done in by_y[-1][-xs:]] if by_y else []))
-    count = len(by_y)
-    for i, values in enumerate(by_y):
-        before_sums = [other[-1] for other in by_x[i + 1:i + 2]]
-        if by_z:
-            far, to_end = by_z[-1][0]
-            before_sums.append(far if i == count - 1 else to_end)
-        before_middle = [other[xs] for other in by_y[i + 1:i + 2]] + [other[-1] for other in by_y[i + 1:i + 2] if i == count - 2]
-        by_z.append(along_z(values, i == len(load_tiles) - 1, before_sums, before_middle))
-    load_pieces, mean_pieces = [], []
-    for i, (_, own, others) in enumerate(by_z[:len(load_tiles)]):
-        moved = [other[-1] for other in by_y[i + 1:i + 2]] + [other[-1] for other in by_y[i + 2:i + 3] if i > 0]
-        load_pieces += spread(own, others, *moved, *load_pieces[-1:])
-    load_pieces[0] = after(load_pieces[0], by_z[-1][0][1])
+    (first_a, first_b), (first_c, first_d) = load_tiles, mean_tiles
+    load_x = along_x(exchange(factors, last_tile))
+    mean_x = along_x(exchange(after(estimates, load_x[0][1])))
+    mean_x = [[joined(pieces, 0, first_c + first_d)] for pieces in mean_x]
+    own = along_y(load_x[0])
+    data_a = merge([own] + [along_y([joined(pieces, 0, first_a)]) for pieces in load_x[1:]])
+    data_b = merge([later(own, first_a)] + [along_y([joined(pieces, first_a, first_b)]) for pieces in load_x[1:]])
+    (far_a, end_a, close_a), *za = along_z(data_a, first_a, False, (), ())
+    data_c = merge([along_y([joined(pieces, 0, first_c)], za[0]) for pieces in mean_x])
+    data_d = merge([along_y([joined(pieces, first_c, first_d)], end_a) for pieces in mean_x])
+    (far_b, end_b, close_b), *zb = along_z(data_b, first_b, True, (far_a,), (close_a,))
+    (far_c, end_c, _), *zc = along_z(data_c, first_c, False, (end_b,), (close_b,))
+    mine_a, load_a = spread(*za)
+    mine_b, load_b = spread(after(zb[0], zc[0], *[value for value, _ in data_d]), zb[1])
+    load_pieces = load_a + [after(load_b[0], end_c)] + load_b[1:]
     cov = covariance(places(load_width), load_pieces, load_tiles, load_width * CORES, ages, rank)
-    for _, own, others in by_z[len(load_tiles):]:
-        mean_pieces += spread(own, others, cov, *by_z[-1][2])
+    _, *zd = along_z(data_d, first_d, False, (zc[0],), (cov,))
+    _, mean_c = spread(after(zc[0], cov), zc[1])
+    _, mean_d = spread(after(zd[0], cov), zd[1])
+    mean_pieces = mean_c + mean_d
     mean = marginal(places(mean_width), mean_pieces, mean_tiles, mean_width * CORES)
     return mean, cov.T
 

time: 181 us -> 165 us (0.912)
  waiting for transfers between devices: 76.5 us -> 57.4 us
  starting transfers between devices: 51.5 us -> 58.6 us
  other arithmetic: 4.28 us -> 1.12 us
  Pallas kernels: 35.9 us -> 32.9 us
    ppermute x18, waiting for transfers between devices: 25.5 us -> 16.4 us  [geo_shift(): return lax.ppermute(value, 'geo', perm)]
    ppermute x8, waiting for transfers between devices: 7.83 us -> 1.84 us  [y_shift(): return lax.ppermute(value, 'dist', perm)]
    ppermute x18, starting transfers between devices: 11.1 us -> 16.6 us  [geo_shift(): return lax.ppermute(value, 'geo', perm)]
    dynamic_slice x2 -> x4, local copies, waits for them, and re-layouts: 0.2 us -> 4.12 us  [part(): lax.dynamic_slice(value, (0, start_of(group, tiles) * LANES), (rows, each...]
    ppermute x19, waiting for transfers between devices: 43.1 us -> 39.2 us  [z_send(): return lax.ppermute(value, 'dist', perm)]
    concatenate x3 -> x4, other arithmetic: 3.47 us -> 0.12 us  [joined(): jnp.concatenate([p[:, first * LANES:(first + count) * LANES] for p in pie...]
    pallas_call x4, Pallas kernels: 9.65 us -> 7.59 us  [partial_sums(): pl.pallas_call(functools.partial(sums_kernel, offsets, has_var), grid_spe...]
    unnamed x38 -> x29, local copies, waits for them, and re-layouts: 6.97 us -> 5.89 us
  transfers between devices with their start and end apart: 45 -> 45, of which waited for: 17 -> 11; matrix products, arithmetic and copies ran while one was open for 4% -> 4% of each run, Pallas kernels for 16% -> 18%
where the time goes in v5:
time: 165 us; the launch traced here: 164 us
  starting transfers between devices  58.6 us (36%)
  waiting for transfers between devices  57.4 us (35%)
  Pallas kernels  32.9 us (20%)
  local copies, waits for them, and re-layouts  12.7 us (8%)
    ppermute x19, waiting for transfers between devices, z_send(): return lax.ppermute(value, 'dist', perm)  39.2 us
    ppermute x19, starting transfers between devices, z_send(): return lax.ppermute(value, 'dist', perm)  32.8 us
    ppermute x18, starting transfers between devices, geo_shift(): return lax.ppermute(value, 'geo', perm)  16.6 us
    ppermute x18, waiting for transfers between devices, geo_shift(): return lax.ppermute(value, 'geo', perm)  16.4 us
    pallas_call x1, Pallas kernels, covariance(): pl.pallas_call(functools.partial(covariance_kernel, tiles, total, ages, r...  12.7 us
    ppermute x8, starting transfers between devices, y_shift(): return lax.ppermute(value, 'dist', perm)  9.27 us
    pallas_call x4, Pallas kernels, partial_sums(): pl.pallas_call(functools.partial(sums_kernel, offsets, has_var), grid_spe...  7.59 us
    unnamed x29, local copies, waits for them, and re-layouts  5.89 us
  transfers between devices with their start and end apart: 45, of which 11 were waited for; matrix products, arithmetic and copies ran while one was open for 4% of the time, Pallas kernels for 18%

profile of v5, /device:TPU:0, one launch (start us, length us, event | category | flops | bytes accessed | tf_op | source)
XLA Modules:
  0.0 164.0 jit_solution(12545633916650911827)
XLA Ops:
  0.7 1.4 constant_dynamic-slice_fusion.8
  2.9 4.0 %collective-permute-start.2 = (s32[64,128]{1,0:T(8,128)S(1)}, s32[64,128]{1,0:T(8,128)S(1)}, u32[]{:S(2)}, u32[]{:S(2)}) collective-permute-start(s32[64,128]{1,0:T(8,128)S(1)} %pad_add_fusion.1), channel_id=1, source_target_pairs={{0,4},{1,5},{2,6},{3,7},{4,0},{5,1},{6,2},{7,3},{8,12},{9,13},{10,... | collective-permute-start | bytes 98312 | tf_op jit(solution)/shard_map/ppermute | solution.py:383
  6.9 1.3 collective-permute-start.1
  9.3 1.5 collective-permute-start.6
  10.9 1.6 collective-permute-start.4
  12.4 1.2 constant_dynamic-slice_fusion.5
  13.6 0.9 constant_dynamic-slice_fusion.3
  15.1 7.6 %collective-permute-done.4 = bf16[96,1920]{1,0:T(8,128)(2,1)S(1)} collective-permute-done((bf16[96,1920]{1,0:T(8,128)(2,1)}, bf16[96,1920]{1,0:T(8,128)(2,1)S(1)}, u32[]{:S(2)}, u32[]{:S(2)}) %collective-permute-start.4) | collective-permute-done | bytes 368672 | tf_op jit(solution)/shard_map/ppermute | solution.py:373
  23.9 1.0 constant_dynamic-slice_fusion.1
  24.9 3.9 %collective-permute-done.5 = bf16[96,1920]{1,0:T(8,128)(2,1)S(1)} collective-permute-done((bf16[96,1920]{1,0:T(8,128)(2,1)S(1)}, bf16[96,1920]{1,0:T(8,128)(2,1)S(1)}, u32[]{:S(2)}, u32[]{:S(2)}) %collective-permute-start.5) | collective-permute-done | bytes 368672 | tf_op jit(solution)/shard_map/ppermute | solution.py:373
  28.8 1.5 collective-permute-start.14
  31.0 0.8 pad_add_fusion.query_ref
  31.8 4.9 %build_weights.1.w_ref = bf16[768,512]{1,0:T(8,128)(2,1)S(1)} custom-call(s32[8]{0:T(128)S(1)} %stack.92.base_ref, s32[64,512]{1,0:T(8,128)S(1)} %pad_add_fusion.query_ref), custom_call_target="tpu_custom_call" | custom-call | flops 393216 | bytes 12288 | tf_op jit(solution)/shard_map/build_weights/pallas_call | solution.py:93
  36.8 1.6 collective-permute-start.10
  38.3 1.2 constant_dynamic-slice_fusion
  40.1 1.8 %collective-permute-done.8.refs_5_ = bf16[192,1024]{1,0:T(8,128)(2,1)S(1)} collective-permute-done((bf16[192,1024]{1,0:T(8,128)(2,1)S(1)}, bf16[192,1024]{1,0:T(8,128)(2,1)S(1)}, u32[]{:S(2)}, u32[]{:S(2)}) %collective-permute-start.8) | collective-permute-done | bytes 393248 | tf_op jit(solution)/shard_map/ppermute | solution.py:379
  41.9 2.1 %partial_sums.4 = (f32[1024,128]{1,0:T(8,128)S(1)}, s16[1040,128]{1,0:T(8,128)(2,1)S(1)}, s16[2080,128]{1,0:T(8,128)(2,1)S(1)}) custom-call(s32[1]{0:T(128)} %bitcast.6.flag_ref, bf16[768,512]{1,0:T(8,128)(2,1)S(1)} %build_weights.1.w_ref, bf16[96,1920]{1,0:T(8,128)(2,1)S(1)} %get-tuple-element.77.refs_0_, bf16[96,1920]{1,0:T(8,128)(2,1)S(1)} %get-tuple-element.79.refs_1_, ...), custom_call_target="tpu_custom_call" | custom-call | flops 12582912 | bytes 45056 | tf_op jit(solution)/shard_map/partial_sums/pallas_call | solution.py:172
  44.0 3.7 %collective-permute-start.9 = (s16[2080,128]{1,0:T(8,128)(2,1)S(1)}, s16[2080,128]{1,0:T(8,128)(2,1)S(1)}, u32[]{:S(2)}, u32[]{:S(2)}) collective-permute-start(s16[2080,128]{1,0:T(8,128)(2,1)S(1)} %get-tuple-element.37.own_ref), channel_id=1, source_target_pairs={{0,2},{1,3},{6,4},{7,5},{8,10},{9,11},{14,12},{15,13},{16,18},{17,... | collective-permute-start | bytes 1597448 | tf_op jit(solution)/shard_map/ppermute | solution.py:383
  48.0 2.1 %collective-permute-start.17 = (bf16[192,1280]{1,0:T(8,128)(2,1)S(1)}, bf16[192,1280]{1,0:T(8,128)(2,1)S(1)}, u32[]{:S(2)}, u32[]{:S(2)}) collective-permute-start(bf16[192,1280]{1,0:T(8,128)(2,1)S(1)} %slice.38.refs_1_), channel_id=1, source_target_pairs={{0,1},{1,0},{2,3},{3,2},{4,5},{5,4},{6,7},{7,6},{8,9},{9,8},{10,11... | collective-permute-start | bytes 1474568 | tf_op jit(solution)/shard_map/ppermute | solution.py:379
  50.1 4.4 %collective-permute-done.9.other_ref = s16[2080,128]{1,0:T(8,128)(2,1)S(1)} collective-permute-done((s16[2080,128]{1,0:T(8,128)(2,1)S(1)}, s16[2080,128]{1,0:T(8,128)(2,1)S(1)}, u32[]{:S(2)}, u32[]{:S(2)}) %collective-permute-start.9) | collective-permute-done | bytes 532512 | tf_op jit(solution)/shard_map/ppermute | solution.py:383
  54.5 1.9 %partial_sums.5 = (f32[896,128]{1,0:T(8,128)S(1)}, s16[912,128]{1,0:T(8,128)(2,1)S(1)}, s16[1824,128]{1,0:T(8,128)(2,1)S(1)}) custom-call(s32[1]{0:T(128)} %bitcast.6.flag_ref, bf16[768,512]{1,0:T(8,128)(2,1)S(1)} %build_weights.1.w_ref, bf16[96,1920]{1,0:T(8,128)(2,1)S(1)} %get-tuple-element.77.refs_0_, bf16[96,1920]{1,0:T(8,128)(2,1)S(1)} %get-tuple-element.79.refs_1_, ...), custom_call_target="tpu_custom_call" | custom-call | flops 11010048 | bytes 39424 | tf_op jit(solution)/shard_map/partial_sums/pallas_call | solution.py:172
  56.4 4.4 %collective-permute-start.12 = (s16[1824,128]{1,0:T(8,128)(2,1)S(1)}, s16[1824,128]{1,0:T(8,128)(2,1)S(1)}, u32[]{:S(2)}, u32[]{:S(2)}) collective-permute-start(s16[1824,128]{1,0:T(8,128)(2,1)S(1)} %get-tuple-element.41.own_ref), channel_id=1, source_target_pairs={{0,2},{1,3},{6,4},{7,5},{8,10},{9,11},{14,12},{15,13},{16,18},{17,... | collective-permute-start | bytes 1400840 | tf_op jit(solution)/shard_map/ppermute | solution.py:383
  62.1 8.6 %collective-permute-done.11.refs_0_ = s16[1040,128]{1,0:T(8,128)(2,1)S(1)} collective-permute-done((s16[1040,128]{1,0:T(8,128)(2,1)S(1)}, s16[1040,128]{1,0:T(8,128)(2,1)S(1)}, u32[]{:S(2)}, u32[]{:S(2)}) %collective-permute-start.11) | collective-permute-done | bytes 266272 | tf_op jit(solution)/shard_map/ppermute | solution.py:383
  70.7 1.3 collective-permute-start.19
  72.4 2.6 %partial_sums.6 = (f32[1280,128]{1,0:T(8,128)S(1)}, s16[1296,128]{1,0:T(8,128)(2,1)}, s16[2592,128]{1,0:T(8,128)(2,1)S(1)}) custom-call(s32[1]{0:T(128)} %bitcast.6.flag_ref, bf16[768,512]{1,0:T(8,128)(2,1)S(1)} %build_weights.1.w_ref, bf16[192,1280]{1,0:T(8,128)(2,1)S(1)} %fusion.3.refs_0_, bf16[192,1280]{1,0:T(8,128)(2,1)S(1)} %slice.38.refs_1_, ...), custom_call_target="tpu_custom_call" | custom-call | flops 15728640 | bytes 56320 | tf_op jit(solution)/shard_map/partial_sums/pallas_call | solution.py:172
  75.0 5.5 %collective-permute-start.28 = (s16[2592,128]{1,0:T(8,128)(2,1)S(1)}, s16[2592,128]{1,0:T(8,128)(2,1)S(1)}, u32[]{:S(2)}, u32[]{:S(2)}) collective-permute-start(s16[2592,128]{1,0:T(8,128)(2,1)S(1)} %get-tuple-element.58.own_ref), channel_id=1, source_target_pairs={{0,2},{1,3},{6,4},{7,5},{8,10},{9,11},{14,12},{15,13},{16,18},{17,... | collective-permute-start | bytes 1990664 | tf_op jit(solution)/shard_map/ppermute | solution.py:383
  80.6 1.4 collective-permute-start.23
  82.3 3.2 %collective-permute-start.21 = (s16[1040,128]{1,0:T(8,128)(2,1)S(1)}, s16[1040,128]{1,0:T(8,128)(2,1)S(1)}, u32[]{:S(2)}, u32[]{:S(2)}) collective-permute-start(s16[1040,128]{1,0:T(8,128)(2,1)S(1)} %combine.4.refs_0_), channel_id=1, source_target_pairs={{0,16},{8,24},{16,0},{24,8},{1,17},{9,25},{17,1},{25,9},{2,18},{10... | collective-permute-start | bytes 798728 | tf_op jit(solution)/shard_map/ppermute | solution.py:373
  85.6 1.6 collective-permute-start.24
  87.1 5.5 %collective-permute-done.25.refs_0_ = s16[912,128]{1,0:T(8,128)(2,1)S(1)} collective-permute-done((s16[912,128]{1,0:T(8,128)(2,1)S(1)}, s16[912,128]{1,0:T(8,128)(2,1)S(1)}, u32[]{:S(2)}, u32[]{:S(2)}) %collective-permute-start.25) | collective-permute-done | bytes 233504 | tf_op jit(solution)/shard_map/ppermute | solution.py:383
  93.3 1.5 collective-permute-start.27
  95.4 9.6 %collective-permute-done.27.refs_2_ = s16[912,128]{1,0:T(8,128)(2,1)S(1)} collective-permute-done((s16[912,128]{1,0:T(8,128)(2,1)S(1)}, s16[912,128]{1,0:T(8,128)(2,1)S(1)}, u32[]{:S(2)}, u32[]{:S(2)}) %collective-permute-start.27) | collective-permute-done | bytes 233504 | tf_op jit(solution)/shard_map/ppermute | solution.py:383
  105.3 5.4 %collective-permute-start.30 = (s16[912,128]{1,0:T(8,128)(2,1)S(1)}, s16[912,128]{1,0:T(8,128)(2,1)}, u32[]{:S(2)}, u32[]{:S(2)}) collective-permute-start(s16[912,128]{1,0:T(8,128)(2,1)S(1)} %combine.5.refs_4_), channel_id=1, source_target_pairs={{0,16},{8,24},{16,0},{24,8},{1,17},{9,25},{17,1},{25,9},{2,18},{10... | collective-permute-start | bytes 700424 | tf_op jit(solution)/shard_map/ppermute | solution.py:373
  110.7 1.4 middle.6
  113.5 1.3 collective-permute-start.34
  115.4 1.0 partial_sums.7
  117.8 5.4 %collective-permute-start.39 = (s16[1312,128]{1,0:T(8,128)(2,1)S(1)}, s16[1312,128]{1,0:T(8,128)(2,1)S(1)}, u32[]{:S(2)}, u32[]{:S(2)}) collective-permute-start(s16[1312,128]{1,0:T(8,128)(2,1)S(1)} %get-tuple-element.69.own_ref), channel_id=1, source_target_pairs={{0,2},{1,3},{6,4},{7,5},{8,10},{9,11},{14,12},{15,13},{16,18},{17,... | collective-permute-start | bytes 1007624 | tf_op jit(solution)/shard_map/ppermute | solution.py:383
  123.3 0.9 copy-done.1
  124.2 0.9 copy-done.3
  125.2 0.9 copy-done.5
  126.1 12.7 %covariance.1 = f32[13456,128]{1,0:T(8,128)} custom-call(s32[8]{0:T(128)S(1)} %stack.97.place_ref, s16[1040,128]{1,0:T(8,128)(2,1)S(1)} %combine.4.refs_0_, s16[1040,128]{1,0:T(8,128)(2,1)S(1)} %copy-done.1, s16[1040,128]{1,0:T(8,128)(2,1)S(1)} %collective-permute-done.21.refs_2_, s16[1040,128]{1,0:T(8,128)(2,1)S(1)} %copy-done.3, ...), custom_call_target="tpu_custom_call" | custom-call | flops 3444736 | bytes 107648 | tf_op jit(solution)/shard_map/covariance/pallas_call | solution.py:338
  140.7 1.3 collective-permute-start.41
  142.0 4.1 %collective-permute-done.38.refs_0_ = s16[656,128]{1,0:T(8,128)(2,1)S(1)} collective-permute-done((s16[656,128]{1,0:T(8,128)(2,1)S(1)}, s16[656,128]{1,0:T(8,128)(2,1)S(1)}, u32[]{:S(2)}, u32[]{:S(2)}) %collective-permute-start.38) | collective-permute-done | bytes 167968 | tf_op jit(solution)/shard_map/ppermute | solution.py:383
  146.2 7.0 %collective-permute-done.41.refs_2_ = s16[656,128]{1,0:T(8,128)(2,1)S(1)} collective-permute-done((s16[656,128]{1,0:T(8,128)(2,1)S(1)}, s16[656,128]{1,0:T(8,128)(2,1)S(1)}, u32[]{:S(2)}, u32[]{:S(2)}) %collective-permute-start.41) | collective-permute-done | bytes 167968 | tf_op jit(solution)/shard_map/ppermute | solution.py:383
  153.4 1.4 collective-permute-start.43
  155.3 3.5 %collective-permute-done.43.refs_6_ = s16[656,128]{1,0:T(8,128)(2,1)S(1)} collective-permute-done((s16[656,128]{1,0:T(8,128)(2,1)S(1)}, s16[656,128]{1,0:T(8,128)(2,1)S(1)}, u32[]{:S(2)}, u32[]{:S(2)}) %collective-permute-start.43) | collective-permute-done | bytes 167968 | tf_op jit(solution)/shard_map/ppermute | solution.py:373
  158.9 1.3 collective-permute-done.44.refs_7_
  160.2 3.8 %marginal.1 = f32[128,7424]{1,0:T(8,128)} custom-call(s32[8]{0:T(128)S(1)} %stack.83.place_ref, s16[1296,128]{1,0:T(8,128)(2,1)S(1)} %combine.6.refs_0_, s16[1296,128]{1,0:T(8,128)(2,1)S(1)} %collective-permute-done.35.refs_1_, s16[1296,128]{1,0:T(8,128)(2,1)S(1)} %collective-permute-done.36.refs_2_, s16[1296,128]{1,0:T(8,128)(2,1)S(1)} %collective-permute-done.37.refs_3_, ...), custom_call_target="tpu_custom_call" | custom-call | flops 59392 | bytes 89088 | tf_op jit(solution)/shard_map/marginal/pallas_call | solution.py:265
  (112 shorter events, 14.8 us)
Async XLA Ops:
  2.3 8.5 %collective-permute-start.3 = (bf16[96,3840]{1,0:T(8,128)(2,1)S(1)}, bf16[96,3840]{1,0:T(8,128)(2,1)}, u32[]{:S(2)}, u32[]{:S(2)}) collective-permute-start(bf16[96,3840]{1,0:T(8,128)(2,1)S(1)} %get-tuple-element.84), channel_id=1, source_target_pairs={{0,8},{8,0},{16,24},{24,16},{1,9},{9,1},{17,25},{25,17},{2,10},{10... | collective-permute-start | bytes 2211848 | tf_op jit(solution)/shard_map/ppermute | solution.py:373
  2.9 11.7 %collective-permute-start.2 = (s32[64,128]{1,0:T(8,128)S(1)}, s32[64,128]{1,0:T(8,128)S(1)}, u32[]{:S(2)}, u32[]{:S(2)}) collective-permute-start(s32[64,128]{1,0:T(8,128)S(1)} %pad_add_fusion.1), channel_id=1, source_target_pairs={{0,4},{1,5},{2,6},{3,7},{4,0},{5,1},{6,2},{7,3},{8,12},{9,13},{10,... | collective-permute-start | bytes 98312 | tf_op jit(solution)/shard_map/ppermute | solution.py:383
  6.9 8.2 %collective-permute-start.1 = (s32[64,128]{1,0:T(8,128)S(1)}, s32[64,128]{1,0:T(8,128)S(1)}, u32[]{:S(2)}, u32[]{:S(2)}) collective-permute-start(s32[64,128]{1,0:T(8,128)S(1)} %pad_add_fusion.1), channel_id=1, source_target_pairs={{0,6},{1,7},{2,4},{3,5},{4,2},{5,3},{6,0},{7,1},{8,14},{9,15},{10,... | collective-permute-start | bytes 98312 | tf_op jit(solution)/shard_map/ppermute | solution.py:383
  8.2 22.2 %collective-permute-start = (s32[64,128]{1,0:T(8,128)S(1)}, s32[64,128]{1,0:T(8,128)}, u32[]{:S(2)}, u32[]{:S(2)}) collective-permute-start(s32[64,128]{1,0:T(8,128)S(1)} %pad_add_fusion.1), channel_id=1, source_target_pairs={{0,2},{1,3},{2,0},{3,1},{4,6},{5,7},{6,4},{7,5},{8,10},{9,11},{10,... | collective-permute-start | bytes 98312 | tf_op jit(solution)/shard_map/ppermute | solution.py:383
  8.5 5.2 %copy-start.8 = (bf16[96,7424]{1,0:T(8,128)(2,1)S(1)}, bf16[96,7424]{1,0:T(8,128)(2,1)}, u32[]{:S(2)}) copy-start(bf16[96,7424]{1,0:T(8,128)(2,1)} %param.5) | copy-start | bytes 4276228
  9.3 30.2 %collective-permute-start.6 = (bf16[96,1920]{1,0:T(8,128)(2,1)S(1)}, bf16[96,1920]{1,0:T(8,128)(2,1)S(1)}, u32[]{:S(2)}, u32[]{:S(2)}) collective-permute-start(bf16[96,1920]{1,0:T(8,128)(2,1)S(1)} %get-tuple-element.77.refs_0_), channel_id=1, source_target_pairs={{0,1},{1,0},{2,3},{3,2},{4,5},{5,4},{6,7},{7,6},{8,9},{9,8},{10,11... | collective-permute-start | bytes 1105928 | tf_op jit(solution)/shard_map/ppermute | solution.py:379
  10.9 11.8 %collective-permute-start.4 = (bf16[96,1920]{1,0:T(8,128)(2,1)}, bf16[96,1920]{1,0:T(8,128)(2,1)S(1)}, u32[]{:S(2)}, u32[]{:S(2)}) collective-permute-start(bf16[96,1920]{1,0:T(8,128)(2,1)} %get-tuple-element.76), channel_id=1, source_target_pairs={{0,16},{8,24},{16,0},{24,8},{1,17},{9,25},{17,1},{25,9},{2,18},{10... | collective-permute-start | bytes 1105928 | tf_op jit(solution)/shard_map/ppermute | solution.py:373
  14.5 14.3 %collective-permute-start.5 = (bf16[96,1920]{1,0:T(8,128)(2,1)S(1)}, bf16[96,1920]{1,0:T(8,128)(2,1)S(1)}, u32[]{:S(2)}, u32[]{:S(2)}) collective-permute-start(bf16[96,1920]{1,0:T(8,128)(2,1)S(1)} %get-tuple-element.78), channel_id=1, source_target_pairs={{0,16},{8,24},{16,0},{24,8},{1,17},{9,25},{17,1},{25,9},{2,18},{10... | collective-permute-start | bytes 1105928 | tf_op jit(solution)/shard_map/ppermute | solution.py:373
  15.0 21.7 %collective-permute-start.13 = (bf16[96,3712]{1,0:T(8,128)(2,1)}, bf16[96,3712]{1,0:T(8,128)(2,1)}, u32[]{:S(2)}, u32[]{:S(2)}) collective-permute-start(bf16[96,3712]{1,0:T(8,128)(2,1)} %constant_dynamic-slice_fusion.3), channel_id=1, source_target_pairs={{0,8},{8,0},{16,24},{24,16},{1,9},{9,1},{17,25},{25,17},{2,10},{10... | collective-permute-start | bytes 2138120 | tf_op jit(solution)/shard_map/ppermute | solution.py:373
  23.4 16.7 %collective-permute-start.7 = (bf16[96,1920]{1,0:T(8,128)(2,1)S(1)}, bf16[96,1920]{1,0:T(8,128)(2,1)S(1)}, u32[]{:S(2)}, u32[]{:S(2)}) collective-permute-start(bf16[96,1920]{1,0:T(8,128)(2,1)S(1)} %get-tuple-element.79.refs_1_), channel_id=1, source_target_pairs={{0,1},{1,0},{2,3},{3,2},{4,5},{5,4},{6,7},{7,6},{8,9},{9,8},{10,11... | collective-permute-start | bytes 1105928 | tf_op jit(solution)/shard_map/ppermute | solution.py:379
  28.8 7.9 %slice-start = ((bf16[96,1920]{1,0:T(8,128)(2,1)}), bf16[96,896]{1,0:T(8,128)(2,1)S(1)}, s32[]{:S(2)}) async-start(bf16[96,1920]{1,0:T(8,128)(2,1)} %copy-done.9), calls=%async_computation | async-start | bytes 344064 | tf_op jit(solution)/shard_map/slice | solution.py:430
  28.8 18.9 %collective-permute-start.14 = (bf16[96,1920]{1,0:T(8,128)(2,1)}, bf16[96,1920]{1,0:T(8,128)(2,1)S(1)}, u32[]{:S(2)}, u32[]{:S(2)}) collective-permute-start(bf16[96,1920]{1,0:T(8,128)(2,1)} %get-tuple-element.72), channel_id=1, source_target_pairs={{0,16},{8,24},{16,0},{24,8},{1,17},{9,25},{17,1},{25,9},{2,18},{10... | collective-permute-start | bytes 1105928 | tf_op jit(solution)/shard_map/ppermute | solution.py:373
  30.4 11.5 %collective-permute-start.8 = (bf16[192,1024]{1,0:T(8,128)(2,1)S(1)}, bf16[192,1024]{1,0:T(8,128)(2,1)S(1)}, u32[]{:S(2)}, u32[]{:S(2)}) collective-permute-start(bf16[192,1024]{1,0:T(8,128)(2,1)S(1)} %pad_maximum_fusion.refs_2_), channel_id=1, source_target_pairs={{0,1},{1,0},{2,3},{3,2},{4,5},{5,4},{6,7},{7,6},{8,9},{9,8},{10,11... | collective-permute-start | bytes 1179656 | tf_op jit(solution)/shard_map/ppermute | solution.py:379
  31.0 5.7 %slice-start.1 = ((bf16[96,1920]{1,0:T(8,128)(2,1)}), bf16[96,896]{1,0:T(8,128)(2,1)S(1)}, s32[]{:S(2)}) async-start(bf16[96,1920]{1,0:T(8,128)(2,1)} %copy-done.10), calls=%async_computation.1 | async-start | bytes 344064 | tf_op jit(solution)/shard_map/slice | solution.py:430
  36.8 17.7 %collective-permute-start.10 = (bf16[192,896]{1,0:T(8,128)(2,1)S(1)}, bf16[192,896]{1,0:T(8,128)(2,1)S(1)}, u32[]{:S(2)}, u32[]{:S(2)}) collective-permute-start(bf16[192,896]{1,0:T(8,128)(2,1)S(1)} %pad_maximum_fusion.1.refs_2_), channel_id=1, source_target_pairs={{0,1},{1,0},{2,3},{3,2},{4,5},{5,4},{6,7},{7,6},{8,9},{9,8},{10,11... | collective-permute-start | bytes 1032200 | tf_op jit(solution)/shard_map/ppermute | solution.py:379
  39.5 8.4 %collective-permute-start.15 = (bf16[96,1920]{1,0:T(8,128)(2,1)S(1)}, bf16[96,1920]{1,0:T(8,128)(2,1)S(1)}, u32[]{:S(2)}, u32[]{:S(2)}) collective-permute-start(bf16[96,1920]{1,0:T(8,128)(2,1)S(1)} %get-tuple-element.80), channel_id=1, source_target_pairs={{0,16},{8,24},{16,0},{24,8},{1,17},{9,25},{17,1},{25,9},{2,18},{10... | collective-permute-start | bytes 1105928 | tf_op jit(solution)/shard_map/ppermute | solution.py:373
  44.0 10.5 %collective-permute-start.9 = (s16[2080,128]{1,0:T(8,128)(2,1)S(1)}, s16[2080,128]{1,0:T(8,128)(2,1)S(1)}, u32[]{:S(2)}, u32[]{:S(2)}) collective-permute-start(s16[2080,128]{1,0:T(8,128)(2,1)S(1)} %get-tuple-element.37.own_ref), channel_id=1, source_target_pairs={{0,2},{1,3},{6,4},{7,5},{8,10},{9,11},{14,12},{15,13},{16,18},{17,... | collective-permute-start | bytes 1597448 | tf_op jit(solution)/shard_map/ppermute | solution.py:383
  47.8 24.6 %collective-permute-start.16 = (bf16[192,1280]{1,0:T(8,128)(2,1)S(1)}, bf16[192,1280]{1,0:T(8,128)(2,1)S(1)}, u32[]{:S(2)}, u32[]{:S(2)}) collective-permute-start(bf16[192,1280]{1,0:T(8,128)(2,1)S(1)} %fusion.3.refs_0_), channel_id=1, source_target_pairs={{0,1},{1,0},{2,3},{3,2},{4,5},{5,4},{6,7},{7,6},{8,9},{9,8},{10,11... | collective-permute-start | bytes 1474568 | tf_op jit(solution)/shard_map/ppermute | solution.py:379
  48.0 24.4 %collective-permute-start.17 = (bf16[192,1280]{1,0:T(8,128)(2,1)S(1)}, bf16[192,1280]{1,0:T(8,128)(2,1)S(1)}, u32[]{:S(2)}, u32[]{:S(2)}) collective-permute-start(bf16[192,1280]{1,0:T(8,128)(2,1)S(1)} %slice.38.refs_1_), channel_id=1, source_target_pairs={{0,1},{1,0},{2,3},{3,2},{4,5},{5,4},{6,7},{7,6},{8,9},{9,8},{10,11... | collective-permute-start | bytes 1474568 | tf_op jit(solution)/shard_map/ppermute | solution.py:379
  56.4 15.6 %collective-permute-start.12 = (s16[1824,128]{1,0:T(8,128)(2,1)S(1)}, s16[1824,128]{1,0:T(8,128)(2,1)S(1)}, u32[]{:S(2)}, u32[]{:S(2)}) collective-permute-start(s16[1824,128]{1,0:T(8,128)(2,1)S(1)} %get-tuple-element.41.own_ref), channel_id=1, source_target_pairs={{0,2},{1,3},{6,4},{7,5},{8,10},{9,11},{14,12},{15,13},{16,18},{17,... | collective-permute-start | bytes 1400840 | tf_op jit(solution)/shard_map/ppermute | solution.py:383
  60.8 9.8 %collective-permute-start.11 = (s16[1040,128]{1,0:T(8,128)(2,1)S(1)}, s16[1040,128]{1,0:T(8,128)(2,1)S(1)}, u32[]{:S(2)}, u32[]{:S(2)}) collective-permute-start(s16[1040,128]{1,0:T(8,128)(2,1)S(1)} %get-tuple-element.40), channel_id=1, source_target_pairs={{0,2},{1,3},{2,0},{3,1},{4,6},{5,7},{6,4},{7,5},{8,10},{9,11},{10,... | collective-permute-start | bytes 798728 | tf_op jit(solution)/shard_map/ppermute | solution.py:383
  61.4 20.6 %collective-permute-start.18 = (s16[1040,128]{1,0:T(8,128)(2,1)S(1)}, s16[1040,128]{1,0:T(8,128)(2,1)S(1)}, u32[]{:S(2)}, u32[]{:S(2)}) collective-permute-start(s16[1040,128]{1,0:T(8,128)(2,1)S(1)} %get-tuple-element.49), channel_id=1, source_target_pairs={{2,4},{3,5},{4,2},{5,3},{10,12},{11,13},{12,10},{13,11},{18,20},{1... | collective-permute-start | bytes 798728 | tf_op jit(solution)/shard_map/ppermute | solution.py:383
  70.7 11.3 %collective-permute-start.19 = (s16[1040,128]{1,0:T(8,128)(2,1)S(1)}, s16[1040,128]{1,0:T(8,128)(2,1)S(1)}, u32[]{:S(2)}, u32[]{:S(2)}) collective-permute-start(s16[1040,128]{1,0:T(8,128)(2,1)S(1)} %get-tuple-element.50), channel_id=1, source_target_pairs={{2,6},{3,7},{4,0},{5,1},{10,14},{11,15},{12,8},{13,9},{18,22},{19,... | collective-permute-start | bytes 798728 | tf_op jit(solution)/shard_map/ppermute | solution.py:383
  75.0 35.7 %collective-permute-start.28 = (s16[2592,128]{1,0:T(8,128)(2,1)S(1)}, s16[2592,128]{1,0:T(8,128)(2,1)S(1)}, u32[]{:S(2)}, u32[]{:S(2)}) collective-permute-start(s16[2592,128]{1,0:T(8,128)(2,1)S(1)} %get-tuple-element.58.own_ref), channel_id=1, source_target_pairs={{0,2},{1,3},{6,4},{7,5},{8,10},{9,11},{14,12},{15,13},{16,18},{17,... | collective-permute-start | bytes 1990664 | tf_op jit(solution)/shard_map/ppermute | solution.py:383
  80.6 12.7 %collective-permute-start.23 = (bf16[192,640]{1,0:T(8,128)(2,1)S(1)}, bf16[192,640]{1,0:T(8,128)(2,1)S(1)}, u32[]{:S(2)}, u32[]{:S(2)}) collective-permute-start(bf16[192,640]{1,0:T(8,128)(2,1)S(1)} %pad_maximum_fusion.2.refs_0_), channel_id=1, source_target_pairs={{0,1},{1,0},{2,3},{3,2},{4,5},{5,4},{6,7},{7,6},{8,9},{9,8},{10,11... | collective-permute-start | bytes 737288 | tf_op jit(solution)/shard_map/ppermute | solution.py:379
  82.0 10.6 %collective-permute-start.25 = (s16[912,128]{1,0:T(8,128)(2,1)S(1)}, s16[912,128]{1,0:T(8,128)(2,1)S(1)}, u32[]{:S(2)}, u32[]{:S(2)}) collective-permute-start(s16[912,128]{1,0:T(8,128)(2,1)S(1)} %get-tuple-element.55), channel_id=1, source_target_pairs={{0,2},{1,3},{2,0},{3,1},{4,6},{5,7},{6,4},{7,5},{8,10},{9,11},{10,... | collective-permute-start | bytes 700424 | tf_op jit(solution)/shard_map/ppermute | solution.py:383
  82.3 12.5 %collective-permute-start.21 = (s16[1040,128]{1,0:T(8,128)(2,1)S(1)}, s16[1040,128]{1,0:T(8,128)(2,1)S(1)}, u32[]{:S(2)}, u32[]{:S(2)}) collective-permute-start(s16[1040,128]{1,0:T(8,128)(2,1)S(1)} %combine.4.refs_0_), channel_id=1, source_target_pairs={{0,16},{8,24},{16,0},{24,8},{1,17},{9,25},{17,1},{25,9},{2,18},{10... | collective-permute-start | bytes 798728 | tf_op jit(solution)/shard_map/ppermute | solution.py:373
  85.6 9.2 %collective-permute-start.24 = (bf16[192,640]{1,0:T(8,128)(2,1)S(1)}, bf16[192,640]{1,0:T(8,128)(2,1)S(1)}, u32[]{:S(2)}, u32[]{:S(2)}) collective-permute-start(bf16[192,640]{1,0:T(8,128)(2,1)S(1)} %slice.39.refs_1_), channel_id=1, source_target_pairs={{0,1},{1,0},{2,3},{3,2},{4,5},{5,4},{6,7},{7,6},{8,9},{9,8},{10,11... | collective-permute-start | bytes 737288 | tf_op jit(solution)/shard_map/ppermute | solution.py:379
  92.6 2.8 %collective-permute-start.26 = (s16[912,128]{1,0:T(8,128)(2,1)S(1)}, s16[912,128]{1,0:T(8,128)(2,1)S(1)}, u32[]{:S(2)}, u32[]{:S(2)}) collective-permute-start(s16[912,128]{1,0:T(8,128)(2,1)S(1)} %get-tuple-element.56), channel_id=1, source_target_pairs={{2,4},{3,5},{4,2},{5,3},{10,12},{11,13},{12,10},{13,11},{18,20},{1... | collective-permute-start | bytes 700424 | tf_op jit(solution)/shard_map/ppermute | solution.py:383
  93.3 11.7 %collective-permute-start.27 = (s16[912,128]{1,0:T(8,128)(2,1)S(1)}, s16[912,128]{1,0:T(8,128)(2,1)S(1)}, u32[]{:S(2)}, u32[]{:S(2)}) collective-permute-start(s16[912,128]{1,0:T(8,128)(2,1)S(1)} %get-tuple-element.42), channel_id=1, source_target_pairs={{2,6},{3,7},{4,0},{5,1},{10,14},{11,15},{12,8},{13,9},{18,22},{19,... | collective-permute-start | bytes 700424 | tf_op jit(solution)/shard_map/ppermute | solution.py:383
  94.8 17.4 %collective-permute-start.20 = (s16[1040,128]{1,0:T(8,128)(2,1)S(1)}, s16[1040,128]{1,0:T(8,128)(2,1)S(1)}, u32[]{:S(2)}, u32[]{:S(2)}) collective-permute-start(s16[1040,128]{1,0:T(8,128)(2,1)S(1)} %combine.4.refs_0_), channel_id=1, source_target_pairs={{0,8},{8,0},{16,24},{24,16},{1,9},{9,1},{17,25},{25,17},{2,10},{10... | collective-permute-start | bytes 798728 | tf_op jit(solution)/shard_map/ppermute | solution.py:373
  94.9 17.9 %collective-permute-start.22 = (s16[1040,128]{1,0:T(8,128)(2,1)S(1)}, s16[1040,128]{1,0:T(8,128)(2,1)S(1)}, u32[]{:S(2)}, u32[]{:S(2)}) collective-permute-start(s16[1040,128]{1,0:T(8,128)(2,1)S(1)} %collective-permute-done.21.refs_2_), channel_id=1, source_target_pairs={{0,8},{8,0},{16,24},{24,16},{1,9},{9,1},{17,25},{25,17},{2,10},{10... | collective-permute-start | bytes 798728 | tf_op jit(solution)/shard_map/ppermute | solution.py:373
  105.3 9.6 %collective-permute-start.30 = (s16[912,128]{1,0:T(8,128)(2,1)S(1)}, s16[912,128]{1,0:T(8,128)(2,1)}, u32[]{:S(2)}, u32[]{:S(2)}) collective-permute-start(s16[912,128]{1,0:T(8,128)(2,1)S(1)} %combine.5.refs_4_), channel_id=1, source_target_pairs={{0,16},{8,24},{16,0},{24,8},{1,17},{9,25},{17,1},{25,9},{2,18},{10... | collective-permute-start | bytes 700424 | tf_op jit(solution)/shard_map/ppermute | solution.py:373
  110.7 6.4 %collective-permute-start.29 = (s16[912,128]{1,0:T(8,128)(2,1)S(1)}, s16[912,128]{1,0:T(8,128)(2,1)S(1)}, u32[]{:S(2)}, u32[]{:S(2)}) collective-permute-start(s16[912,128]{1,0:T(8,128)(2,1)S(1)} %combine.5.refs_4_), channel_id=1, source_target_pairs={{0,8},{8,0},{16,24},{24,16},{1,9},{9,1},{17,25},{25,17},{2,10},{10... | collective-permute-start | bytes 700424 | tf_op jit(solution)/shard_map/ppermute | solution.py:373
  110.7 28.1 %collective-permute-start.32 = (s16[1296,128]{1,0:T(8,128)(2,1)}, s16[1296,128]{1,0:T(8,128)(2,1)S(1)}, u32[]{:S(2)}, u32[]{:S(2)}) collective-permute-start(s16[1296,128]{1,0:T(8,128)(2,1)} %get-tuple-element.62), channel_id=1, source_target_pairs={{0,2},{1,3},{2,0},{3,1},{4,6},{5,7},{6,4},{7,5},{8,10},{9,11},{10,... | collective-permute-start | bytes 995336 | tf_op jit(solution)/shard_map/ppermute | solution.py:383
  112.1 26.7 %collective-permute-start.33 = (s16[1296,128]{1,0:T(8,128)(2,1)}, s16[1296,128]{1,0:T(8,128)(2,1)S(1)}, u32[]{:S(2)}, u32[]{:S(2)}) collective-permute-start(s16[1296,128]{1,0:T(8,128)(2,1)} %get-tuple-element.63), channel_id=1, source_target_pairs={{2,4},{3,5},{4,2},{5,3},{10,12},{11,13},{12,10},{13,11},{18,20},{1... | collective-permute-start | bytes 995336 | tf_op jit(solution)/shard_map/ppermute | solution.py:383
  113.5 25.3 %collective-permute-start.34 = (s16[1296,128]{1,0:T(8,128)(2,1)}, s16[1296,128]{1,0:T(8,128)(2,1)S(1)}, u32[]{:S(2)}, u32[]{:S(2)}) collective-permute-start(s16[1296,128]{1,0:T(8,128)(2,1)} %get-tuple-element.59), channel_id=1, source_target_pairs={{2,6},{3,7},{4,0},{5,1},{10,14},{11,15},{12,8},{13,9},{18,22},{19,... | collective-permute-start | bytes 995336 | tf_op jit(solution)/shard_map/ppermute | solution.py:383
  114.8 8.4 %collective-permute-start.31 = (s16[912,128]{1,0:T(8,128)(2,1)}, s16[912,128]{1,0:T(8,128)(2,1)}, u32[]{:S(2)}, u32[]{:S(2)}) collective-permute-start(s16[912,128]{1,0:T(8,128)(2,1)} %collective-permute-done.30.refs_6_), channel_id=1, source_target_pairs={{0,8},{8,0},{16,24},{24,16},{1,9},{9,1},{17,25},{25,17},{2,10},{10... | collective-permute-start | bytes 700424 | tf_op jit(solution)/shard_map/ppermute | solution.py:373
  117.8 22.0 %collective-permute-start.39 = (s16[1312,128]{1,0:T(8,128)(2,1)S(1)}, s16[1312,128]{1,0:T(8,128)(2,1)S(1)}, u32[]{:S(2)}, u32[]{:S(2)}) collective-permute-start(s16[1312,128]{1,0:T(8,128)(2,1)S(1)} %get-tuple-element.69.own_ref), channel_id=1, source_target_pairs={{0,2},{1,3},{6,4},{7,5},{8,10},{9,11},{14,12},{15,13},{16,18},{17,... | collective-permute-start | bytes 1007624 | tf_op jit(solution)/shard_map/ppermute | solution.py:383
  139.3 15.5 %collective-permute-start.36 = (s16[1296,128]{1,0:T(8,128)(2,1)S(1)}, s16[1296,128]{1,0:T(8,128)(2,1)S(1)}, u32[]{:S(2)}, u32[]{:S(2)}) collective-permute-start(s16[1296,128]{1,0:T(8,128)(2,1)S(1)} %combine.6.refs_0_), channel_id=1, source_target_pairs={{0,16},{8,24},{16,0},{24,8},{1,17},{9,25},{17,1},{25,9},{2,18},{10... | collective-permute-start | bytes 995336 | tf_op jit(solution)/shard_map/ppermute | solution.py:373
  139.8 6.4 %collective-permute-start.38 = (s16[656,128]{1,0:T(8,128)(2,1)S(1)}, s16[656,128]{1,0:T(8,128)(2,1)S(1)}, u32[]{:S(2)}, u32[]{:S(2)}) collective-permute-start(s16[656,128]{1,0:T(8,128)(2,1)S(1)} %copy-done.7), channel_id=1, source_target_pairs={{0,2},{1,3},{2,0},{3,1},{4,6},{5,7},{6,4},{7,5},{8,10},{9,11},{10,... | collective-permute-start | bytes 503816 | tf_op jit(solution)/shard_map/ppermute | solution.py:383
  140.1 6.1 %collective-permute-start.40 = (s16[656,128]{1,0:T(8,128)(2,1)S(1)}, s16[656,128]{1,0:T(8,128)(2,1)S(1)}, u32[]{:S(2)}, u32[]{:S(2)}) collective-permute-start(s16[656,128]{1,0:T(8,128)(2,1)S(1)} %get-tuple-element.70), channel_id=1, source_target_pairs={{2,4},{3,5},{4,2},{5,3},{10,12},{11,13},{12,10},{13,11},{18,20},{1... | collective-permute-start | bytes 503816 | tf_op jit(solution)/shard_map/ppermute | solution.py:383
  140.7 12.4 %collective-permute-start.41 = (s16[656,128]{1,0:T(8,128)(2,1)S(1)}, s16[656,128]{1,0:T(8,128)(2,1)S(1)}, u32[]{:S(2)}, u32[]{:S(2)}) collective-permute-start(s16[656,128]{1,0:T(8,128)(2,1)S(1)} %get-tuple-element.71), channel_id=1, source_target_pairs={{2,6},{3,7},{4,0},{5,1},{10,14},{11,15},{12,8},{13,9},{18,22},{19,... | collective-permute-start | bytes 503816 | tf_op jit(solution)/shard_map/ppermute | solution.py:383
  153.4 5.4 %collective-permute-start.43 = (s16[656,128]{1,0:T(8,128)(2,1)S(1)}, s16[656,128]{1,0:T(8,128)(2,1)S(1)}, u32[]{:S(2)}, u32[]{:S(2)}) collective-permute-start(s16[656,128]{1,0:T(8,128)(2,1)S(1)} %combine.7.refs_4_), channel_id=1, source_target_pairs={{0,16},{8,24},{16,0},{24,8},{1,17},{9,25},{17,1},{25,9},{2,18},{10... | collective-permute-start | bytes 503816 | tf_op jit(solution)/shard_map/ppermute | solution.py:373
  154.8 5.4 %collective-permute-start.35 = (s16[1296,128]{1,0:T(8,128)(2,1)S(1)}, s16[1296,128]{1,0:T(8,128)(2,1)S(1)}, u32[]{:S(2)}, u32[]{:S(2)}) collective-permute-start(s16[1296,128]{1,0:T(8,128)(2,1)S(1)} %combine.6.refs_0_), channel_id=1, source_target_pairs={{0,8},{8,0},{16,24},{24,16},{1,9},{9,1},{17,25},{25,17},{2,10},{10... | collective-permute-start | bytes 995336 | tf_op jit(solution)/shard_map/ppermute | solution.py:373
  154.8 5.4 %collective-permute-start.37 = (s16[1296,128]{1,0:T(8,128)(2,1)S(1)}, s16[1296,128]{1,0:T(8,128)(2,1)S(1)}, u32[]{:S(2)}, u32[]{:S(2)}) collective-permute-start(s16[1296,128]{1,0:T(8,128)(2,1)S(1)} %collective-permute-done.36.refs_2_), channel_id=1, source_target_pairs={{0,8},{8,0},{16,24},{24,16},{1,9},{9,1},{17,25},{25,17},{2,10},{10... | collective-permute-start | bytes 995336 | tf_op jit(solution)/shard_map/ppermute | solution.py:373
  155.3 3.6 %collective-permute-start.42 = (s16[656,128]{1,0:T(8,128)(2,1)S(1)}, s16[656,128]{1,0:T(8,128)(2,1)S(1)}, u32[]{:S(2)}, u32[]{:S(2)}) collective-permute-start(s16[656,128]{1,0:T(8,128)(2,1)S(1)} %combine.7.refs_4_), channel_id=1, source_target_pairs={{0,8},{8,0},{16,24},{24,16},{1,9},{9,1},{17,25},{25,17},{2,10},{10... | collective-permute-start | bytes 503816 | tf_op jit(solution)/shard_map/ppermute | solution.py:373
  158.8 1.4 collective-permute-start.44
  (13 other events, 16.7 us)

commit v6 on v5

--- a/solution.py
+++ b/solution.py
@@ -9,7 +9,7 @@
 LANES = 128
 CORES = 2
 DEPTH = 4
-LOAD_FIRST = 8
+LOAD_FIRST = 7
 MEAN_FIRST = 10
 SCALES = 16
 TOP = 32767.0
@@ -23,7 +23,7 @@
 
 
 def cost(flops, moved):
-    return pl.CostEstimate(flops=flops // 64, bytes_accessed=moved // 64, transcendentals=0)
+    return pl.CostEstimate(flops=flops, bytes_accessed=moved, transcendentals=0)
 
 
 def after(value, *others):
@@ -100,7 +100,7 @@
         ),
         out_shape=jax.ShapeDtypeStruct(shape, jnp.bfloat16),
         compiler_params=params(),
-        cost_estimate=cost(shape[0] * width * queries.shape[0], shape[0] * width * 2),
+        cost_estimate=cost(shape[0] * width * queries.shape[0] * 200, shape[0] * width * 2),
         name="build_weights",
     )(bases, queries)
 
@@ -108,7 +108,7 @@
 def sums_kernel(offsets, has_var, flag_ref, w_ref, *refs):
     parts = len(offsets)
     data = refs[:parts]
-    own_ref, near_ref, far_ref, acc_ref = refs[parts:]
+    own_ref, opposite_ref, sent_ref, acc_ref = refs[parts:]
     columns = own_ref.shape[0]
     coded = columns + SCALES
     rows = [0]
@@ -129,9 +129,8 @@
 
     def put(t, value):
         where = slice(t * LANES, (t + 1) * LANES)
-        own_ref[where, :] = value[:, :LANES]
-        for u in range(1, DEPTH):
-            acc_ref[u - 1, where, :] = value[:, u * LANES:(u + 1) * LANES]
+        for u, ref in enumerate((own_ref, opposite_ref, acc_ref.at[0], acc_ref.at[1])):
+            ref[where, :] = value[:, u * LANES:(u + 1) * LANES]
 
     for t in range(columns // LANES):
         put(t, weighted(lambda w: w, t))
@@ -153,9 +152,8 @@
             t = columns // LANES - 1
             put(t, weighted(high, t) + weighted(low, t))
 
-    encode(acc_ref.at[0], 0, near_ref, 0, columns)
-    encode(acc_ref.at[1], 0, far_ref, 0, columns)
-    encode(acc_ref.at[2], 0, far_ref, coded, columns)
+    for u in range(2):
+        encode(acc_ref.at[u], 0, sent_ref, u * coded, columns)
 
 
 def partial_sums(flag, w, data, count, has_var):
@@ -166,7 +164,7 @@
     whole = lambda i, s: (0, 0)
     shapes = [
         jax.ShapeDtypeStruct((columns, LANES), jnp.float32),
-        jax.ShapeDtypeStruct((coded, LANES), jnp.int16),
+        jax.ShapeDtypeStruct((columns, LANES), jnp.float32),
         jax.ShapeDtypeStruct((2 * coded, LANES), jnp.int16),
     ]
     return pl.pallas_call(
@@ -176,7 +174,7 @@
             grid=(1,),
             in_specs=[pl.BlockSpec(w.shape, whole)] + [pl.BlockSpec(d.shape, whole) for d in data],
             out_specs=[pl.BlockSpec(s.shape, whole) for s in shapes],
-            scratch_shapes=[pltpu.VMEM((DEPTH - 1, columns, LANES), jnp.float32)],
+            scratch_shapes=[pltpu.VMEM((2, columns, LANES), jnp.float32)],
         ),
         out_shape=shapes,
         compiler_params=params(),
@@ -185,54 +183,29 @@
     )(flag, w, *data)
 
 
-def middle_kernel(own_ref, other_ref, near_ref, end_ref, acc_ref):
-    height = acc_ref.shape[0]
-    for u, out in enumerate((near_ref, end_ref)):
-        base = u * (height + SCALES)
-        mine = steps_of(own_ref, base, height)
-        theirs = steps_of(other_ref, base, height)
-        for r in range(0, height, 16):
-            h = r * 2 // height
-            acc_ref[r:r + 16, :] = decode(own_ref, base + r, mine[h]) + decode(other_ref, base + r, theirs[h])
-        encode(acc_ref, 0, out, 0, height)
-
-
-def middle(own, other):
-    coded = own.shape[0] // 2
-    shape = jax.ShapeDtypeStruct((coded, LANES), jnp.int16)
-    return pl.pallas_call(
-        middle_kernel,
-        out_shape=[shape, shape],
-        scratch_shapes=[pltpu.VMEM((coded - SCALES, LANES), jnp.float32)],
-        compiler_params=params(),
-        cost_estimate=cost(coded * LANES * 32, coded * LANES * 12),
-        name="middle",
-    )(own, other)
-
-
-def combine_kernel(own_ref, *refs):
+def combine_kernel(bases, own_ref, *refs):
     others, out_ref, acc_ref = refs[:-2], refs[-2], refs[-1]
     height = acc_ref.shape[0]
-    steps = [steps_of(o, 0, height) for o in others]
+    steps = [steps_of(o, base, height) for o, base in zip(others, bases)]
     for r in range(0, height, 16):
         total = own_ref[r:r + 16, :]
-        for o, step in zip(others, steps):
-            total = total + decode(o, r, step[r * 2 // height])
+        for o, base, step in zip(others, bases, steps):
+            total = total + decode(o, base + r, step[r * 2 // height])
         acc_ref[r:r + 16, :] = total
     encode(acc_ref, 0, out_ref, 0, height)
 
 
-def combine(own, others):
+def combine(own, *others):
     height = own.shape[0]
     shape = (height + SCALES, LANES)
     return pl.pallas_call(
-        combine_kernel,
+        functools.partial(combine_kernel, [unit * shape[0] for _, unit in others]),
         out_shape=jax.ShapeDtypeStruct(shape, jnp.int16),
         scratch_shapes=[pltpu.VMEM((height, LANES), jnp.float32)],
         compiler_params=params(),
         cost_estimate=cost(height * LANES * 16, height * LANES * 12),
         name="combine",
-    )(own, *others)
+    )(own, *[array for array, _ in others])
 
 
 def each_piece(place_ref, pieces, tiles, do):
@@ -350,7 +323,7 @@
         ),
         out_shape=jax.ShapeDtypeStruct(shape, jnp.float32),
         compiler_params=params(),
-        cost_estimate=cost(LANES * ages * ages * rank * 2, shape[0] * shape[1] * 4),
+        cost_estimate=cost(LANES * ages * ages * rank * 140, shape[0] * shape[1] * 4),
         name="covariance",
     )(places, *pieces)
 
@@ -366,37 +339,47 @@
     x, core = geo // CORES, geo % CORES
     z, y = dist // ys, dist % ys
 
-    def geo_shift(value, dx, dc):
-        if dx == 0 and dc == 0:
+    def move(value, dx, dc, dy=0):
+        if (dx, dc, dy) == (0, 0, 0):
             return value
-        perm = [(a * CORES + b, (a + dx) % xs * CORES + (b + dc) % CORES) for a in range(xs) for b in range(CORES)]
-        return lax.ppermute(value, "geo", perm)
-
-    def y_shift(value, dy):
-        if dy == 0:
-            return value
-        perm = [(a * ys + b, a * ys + (b + dy) % ys) for a in range(DEPTH) for b in range(ys)]
+        perm = []
+        for g in range(groups):
+            for d in range(parts):
+                to = (g // CORES + dx) % xs * CORES + (g + dc) % CORES
+                perm.append((g * parts + d, to * parts + d // ys * ys + (d + dy) % ys))
+        return lax.ppermute(value, ("geo", "dist"), perm)
+
+    def z_swap(value, bits):
+        perm = [(a * ys + b, (a ^ bits) * ys + b) for a in range(DEPTH) for b in range(ys)]
         return lax.ppermute(value, "dist", perm)
 
-    def z_send(value, pairs):
-        perm = [(a * ys + b, c * ys + b) for a, c in pairs for b in range(ys)]
-        return lax.ppermute(value, "dist", perm)
-
-    near = ((0, 1), (1, 0), (2, 3), (3, 2))
-    mirror = ((0, 3), (1, 2), (2, 1), (3, 0))
-    across = ((0, 2), (1, 3), (2, 0), (3, 1))
+    last_tile = jnp.pad(variances, ((0, 0), (0, -ages % LANES)))
+
+    def half(array, c, *more):
+        width = array.shape[1] // CORES
+        return jnp.concatenate([lax.dynamic_slice(array, (0, c * width), (rows, width)), *more], axis=1)
+
+    def start_of(group, tiles):
+        return jnp.minimum(group * each_of(tiles), tiles - each_of(tiles))
+
+    def each_of(tiles):
+        return -(-tiles // xs)
+
+    def groups_of(array, *more):
+        both = [half(array, (core + dc) % CORES, *more) for dc in range(CORES)]
+        tiles = both[0].shape[1] // LANES
+        size = (rows, each_of(tiles) * LANES)
+        return [
+            [lax.dynamic_slice(b, (0, start_of((x + dx) % xs, tiles) * LANES), size) for b in both] for dx in range(xs)
+        ]
+
+    load_cut = groups_of(factors, last_tile)
+    load_x = [[move(load_cut[dx][dc], dx, dc) for dc in range(CORES)] for dx in range(xs)]
+    load_y = [[(value, 0) for value in load_x[0]]]
+    load_y += [[(move(load_cut[0][dc], 0, dc, dy), 0) for dc in range(CORES)] for dy in range(1, ys)]
     queries = jnp.concatenate([intersection_tracts.T, intersection_weights.T], axis=0)
-    in_middle = (z == 1) | (z == 2)
-    at_mirror, at_across = z_send(queries, mirror), z_send(queries, across)
-    queries = jnp.concatenate(
-        [
-            queries,
-            z_send(queries, near),
-            jnp.where(in_middle, at_mirror, at_across),
-            jnp.where(in_middle, at_across, at_mirror),
-        ],
-        axis=1,
-    )
+    queries = after(queries, load_x[0][1])
+    queries = jnp.concatenate([queries] + [z_swap(queries, bits) for bits in (2, 1, 3)], axis=1)
 
     bases = jnp.stack([
         (((x - dx) % xs * CORES + (core - dc) % CORES) * parts + z * ys + (y - dy) % ys) * rows
@@ -404,34 +387,15 @@
     ]).astype(jnp.int32)
     w = build_weights(bases, queries, rows)
     flag = (x == xs - 1).astype(jnp.int32).reshape(1)
-    last_tile = jnp.pad(variances, ((0, 0), (0, -ages % LANES)))
-
-    def half(array, c, *more):
-        width = array.shape[1] // CORES
-        return jnp.concatenate([lax.dynamic_slice(array, (0, c * width), (rows, width)), *more], axis=1)
-
-    def exchange(array, *more):
-        return half(array, core, *more), geo_shift(half(array, 1 - core, *more), 0, 1)
-
-    def start_of(group, tiles):
-        return jnp.minimum(group * each_of(tiles), tiles - each_of(tiles))
-
-    def each_of(tiles):
-        return -(-tiles // xs)
-
-    def part(value, group):
-        tiles = value.shape[1] // LANES
-        return lax.dynamic_slice(value, (0, start_of(group, tiles) * LANES), (rows, each_of(tiles) * LANES))
-
-    def along_x(both):
-        return [[geo_shift(part(b, (x + dx) % xs), dx, 0) for b in both] for dx in range(xs)]
-
     def joined(pieces, first, count):
         return jnp.concatenate([p[:, first * LANES:(first + count) * LANES] for p in pieces], axis=0)
 
-    def along_y(pieces, *done):
-        sent = [after(value, *done) for value in pieces]
-        return [[(value, 0) for value in pieces]] + [[(y_shift(value, dy), 0) for value in sent] for dy in range(1, ys)]
+    def along_y(by_x, first, count, *done):
+        out = []
+        for pieces in by_x[1:]:
+            sent = after(joined(pieces, first, count), *done)
+            out.append([[(value, first) for value in pieces]] + [[(move(sent, 0, 0, dy), 0)] for dy in range(1, ys)])
+        return out
 
     def later(by_y, tiles):
         return [[(value, first + tiles) for value, first in pieces] for pieces in by_y]
@@ -440,18 +404,15 @@
         return [piece for dy in range(ys) for by_y in by_x for piece in by_y[dy]]
 
     def along_z(data, count, has_var, before_sums, before_middle):
-        own, close, far = partial_sums(flag, after(w, *before_sums), data, count, has_var)
-        far_in = z_send(far, ((0, 1), (3, 2)))
-        close_in = z_send(close, near)
-        to_middle, to_end = middle(after(far, *before_middle), far_in)
-        middle_in = z_send(to_middle, ((1, 2), (2, 1)))
-        end_in = z_send(to_end, ((1, 3), (2, 0)))
-        return (far_in, to_end, close_in), own, [close_in, middle_in, end_in]
-
-    def spread(own, others, *done):
-        mine = combine(after(own, *done), others)
-        along = [geo_shift(mine, dx, 0) for dx in range(xs)]
-        return mine, [geo_shift(along[dx], 0, dc) for dx in range(xs) for dc in range(CORES)]
+        own, opposite, sent = partial_sums(flag, after(w, *before_sums), data, count, has_var)
+        near = z_swap(sent, 1)
+        far = z_swap(combine(after(opposite, *before_middle), (near, 1)), 2)
+        return own, near, far
+
+    def spread(own, near, far):
+        mine = combine(own, (near, 0), (far, 0))
+        along = [move(mine, dx, 0) for dx in range(xs)]
+        return mine, [move(along[dx], 0, dc) for dx in range(xs) for dc in range(CORES)]
 
     def places(tiles):
         starts, lasts = [], []
@@ -467,24 +428,28 @@
     load_tiles = split(each_of(load_width), LOAD_FIRST)
     mean_tiles = split(each_of(mean_width), MEAN_FIRST)
     (first_a, first_b), (first_c, first_d) = load_tiles, mean_tiles
-    load_x = along_x(exchange(factors, last_tile))
-    mean_x = along_x(exchange(after(estimates, load_x[0][1])))
-    mean_x = [[joined(pieces, 0, first_c + first_d)] for pieces in mean_x]
-    own = along_y(load_x[0])
-    data_a = merge([own] + [along_y([joined(pieces, 0, first_a)]) for pieces in load_x[1:]])
-    data_b = merge([later(own, first_a)] + [along_y([joined(pieces, first_a, first_b)]) for pieces in load_x[1:]])
-    (far_a, end_a, close_a), *za = along_z(data_a, first_a, False, (), ())
-    data_c = merge([along_y([joined(pieces, 0, first_c)], za[0]) for pieces in mean_x])
-    data_d = merge([along_y([joined(pieces, first_c, first_d)], end_a) for pieces in mean_x])
-    (far_b, end_b, close_b), *zb = along_z(data_b, first_b, True, (far_a,), (close_a,))
-    (far_c, end_c, _), *zc = along_z(data_c, first_c, False, (end_b,), (close_b,))
-    mine_a, load_a = spread(*za)
-    mine_b, load_b = spread(after(zb[0], zc[0], *[value for value, _ in data_d]), zb[1])
-    load_pieces = load_a + [after(load_b[0], end_c)] + load_b[1:]
+    mean_cut = groups_of(after(estimates, load_x[0][1]))
+    mean_x = [[move(mean_cut[dx][dc], dx, dc) for dc in range(CORES)] for dx in range(xs)]
+    data_a = merge([load_y] + along_y(load_x, 0, first_a))
+    data_b = merge([later(load_y, first_a)] + along_y(load_x, first_a, first_b))
+    own_a, near_a, far_a = along_z(data_a, first_a, False, (), ())
+    mean_y = [[(value, 0) for value in mean_x[0]]]
+    mean_y += [[(move(after(mean_cut[0][dc], own_a), 0, dc, dy), 0) for dc in range(CORES)] for dy in range(1, ys)]
+    mean_there = [value for pieces in mean_y[1:] for value, _ in pieces]
+    own_b, near_b, far_b = along_z(data_b, first_b, True, (near_a,), mean_there)
+    data_c = merge([mean_y] + along_y(mean_x, 0, first_c, *mean_there))
+    data_d = merge([later(mean_y, first_c)] + along_y(mean_x, first_c, first_d, *mean_there))
+    own_c, opposite_c, sent_c = partial_sums(flag, after(w, far_a, far_b), data_c, first_c, False)
+    own_d, opposite_d, sent_d = partial_sums(flag, after(w, own_c), data_d, first_d, False)
+    _, load_a = spread(own_a, near_a, far_a)
+    _, load_b = spread(own_b, near_b, far_b)
+    near_c, near_d = z_swap(sent_c, 1), z_swap(sent_d, 1)
+    far_c = z_swap(combine(opposite_c, (near_c, 1)), 2)
+    far_d = z_swap(combine(opposite_d, (near_d, 1)), 2)
+    mine_c, mean_c = spread(own_c, near_c, far_c)
+    mine_d, mean_d = spread(own_d, near_d, far_d)
+    load_pieces = load_a + [after(load_b[0], mine_c, mine_d)] + load_b[1:]
     cov = covariance(places(load_width), load_pieces, load_tiles, load_width * CORES, ages, rank)
-    _, *zd = along_z(data_d, first_d, False, (zc[0],), (cov,))
-    _, mean_c = spread(after(zc[0], cov), zc[1])
-    _, mean_d = spread(after(zd[0], cov), zd[1])
     mean_pieces = mean_c + mean_d
     mean = marginal(places(mean_width), mean_pieces, mean_tiles, mean_width * CORES)
     return mean, cov.T

time: 165 us -> 162 us (0.982)
  waiting for transfers between devices: 57.4 us -> 87.5 us
  starting transfers between devices: 58.6 us -> 38.9 us
  local copies, waits for them, and re-layouts: 12.7 us -> 2.59 us
  Pallas kernels: 32.9 us -> 30.9 us
    ppermute x45 -> x37, waiting for transfers between devices: 57.4 us -> 87.5 us  [the longest x11 54.6 us: z_swap(): return lax.ppermute(value, 'dist', perm)]
    ppermute x45 -> x37, starting transfers between devices: 58.6 us -> 38.9 us  [the longest x26 20.6 us: move(): return lax.ppermute(value, ('geo', 'dist'), perm)]
    unnamed x29 -> x8, local copies, waits for them, and re-layouts: 5.89 us -> 0.02 us
    dynamic_slice x4 -> x3, local copies, waits for them, and re-layouts: 4.12 us -> 0.77 us  [groups_of(): lax.dynamic_slice(b, (0, start_of((x + dx) % xs, tiles) * LANES), size)]
    pallas_call x8, Pallas kernels: 3.91 us -> 1.67 us  [combine(): pl.pallas_call(functools.partial(combine_kernel, [unit * shape[0] for _,...]
  transfers between devices with their start and end apart: 45 -> 37, of which waited for: 11 -> 14; matrix products, arithmetic and copies ran while one was open for 4% -> 1% of each run, Pallas kernels for 18% -> 15%
where the time goes in v6:
time: 162 us; the launch traced here: 161 us
  waiting for transfers between devices  87.5 us (54%)
  starting transfers between devices  38.9 us (24%)
  Pallas kernels  30.9 us (19%)
  local copies, waits for them, and re-layouts  2.59 us (2%)
    ppermute x11, waiting for transfers between devices, z_swap(): return lax.ppermute(value, 'dist', perm)  54.6 us
    ppermute x26, waiting for transfers between devices, move(): return lax.ppermute(value, ('geo', 'dist'), perm)  33 us
    ppermute x26, starting transfers between devices, move(): return lax.ppermute(value, ('geo', 'dist'), perm)  20.6 us
    ppermute x11, starting transfers between devices, z_swap(): return lax.ppermute(value, 'dist', perm)  18.3 us
    pallas_call x1, Pallas kernels, covariance(): pl.pallas_call(functools.partial(covariance_kernel, tiles, total, ages, r...  11.9 us
    pallas_call x4, Pallas kernels, partial_sums(): pl.pallas_call(functools.partial(sums_kernel, offsets, has_var), grid_spe...  8.65 us
    pallas_call x1, Pallas kernels, build_weights(): pl.pallas_call(functools.partial(weights_kernel, rows), grid_spec=pltpu.P...  4.89 us
    pallas_call x1, Pallas kernels, marginal(): pl.pallas_call(functools.partial(marginal_kernel, tiles), grid_spec=pltpu...  3.83 us
  transfers between devices with their start and end apart: 37, of which 14 were waited for; matrix products, arithmetic and copies ran while one was open for 1% of the time, Pallas kernels for 15%

profile of v6, /device:TPU:0, one launch (start us, length us, event | category | flops | bytes accessed | tf_op | source)
XLA Modules:
  0.0 161.4 jit_solution(6134070547397232188)
XLA Ops:
  0.7 1.4 constant_dynamic-slice_fusion.7
  2.5 2.5 %collective-permute-start.5 = (bf16[96,1920]{1,0:T(8,128)(2,1)S(1)}, bf16[96,1920]{1,0:T(8,128)(2,1)S(1)}, u32[]{:S(2)}, u32[]{:S(2)}) collective-permute-start(bf16[96,1920]{1,0:T(8,128)(2,1)S(1)} %get-tuple-element.54), channel_id=1, source_target_pairs={{0,24},{1,25},{2,26},{3,27},{4,28},{5,29},{6,30},{7,31},{8,16},{9,... | collective-permute-start | bytes 1105928 | tf_op jit(solution)/shard_map/ppermute | solution.py:350
  5.0 0.7 collective-permute-start
  5.8 1.4 collective-permute-start.7
  7.1 0.7 collective-permute-start.6
  8.0 3.7 %collective-permute-start.3 = (s32[64,128]{1,0:T(8,128)S(1)}, s32[64,128]{1,0:T(8,128)S(1)}, u32[]{:S(2)}, u32[]{:S(2)}) collective-permute-start(s32[64,128]{1,0:T(8,128)S(1)} %pad_add_fusion.1), channel_id=1, source_target_pairs={{0,6},{1,7},{2,4},{3,5},{4,2},{5,3},{6,0},{7,1},{8,14},{9,15},{10,... | collective-permute-start | bytes 98312 | tf_op jit(solution)/shard_map/ppermute | solution.py:354
  11.6 2.3 %collective-permute-done.5.refs_3_ = bf16[96,1920]{1,0:T(8,128)(2,1)S(1)} collective-permute-done((bf16[96,1920]{1,0:T(8,128)(2,1)S(1)}, bf16[96,1920]{1,0:T(8,128)(2,1)S(1)}, u32[]{:S(2)}, u32[]{:S(2)}) %collective-permute-start.5) | collective-permute-done | bytes 368672 | tf_op jit(solution)/shard_map/ppermute | solution.py:350
  13.9 2.4 %collective-permute-start.2 = (s32[64,128]{1,0:T(8,128)S(1)}, s32[64,128]{1,0:T(8,128)S(1)}, u32[]{:S(2)}, u32[]{:S(2)}) collective-permute-start(s32[64,128]{1,0:T(8,128)S(1)} %pad_add_fusion.1), channel_id=1, source_target_pairs={{0,2},{1,3},{2,0},{3,1},{4,6},{5,7},{6,4},{7,5},{8,10},{9,11},{10,... | collective-permute-start | bytes 98312 | tf_op jit(solution)/shard_map/ppermute | solution.py:354
  16.4 5.6 %collective-permute-done.4.refs_2_ = bf16[96,1920]{1,0:T(8,128)(2,1)S(1)} collective-permute-done((bf16[96,1920]{1,0:T(8,128)(2,1)S(1)}, bf16[96,1920]{1,0:T(8,128)(2,1)S(1)}, u32[]{:S(2)}, u32[]{:S(2)}) %collective-permute-start.4) | collective-permute-done | bytes 368672 | tf_op jit(solution)/shard_map/ppermute | solution.py:350
  22.0 3.4 %collective-permute-start.1 = (s32[64,128]{1,0:T(8,128)S(1)}, s32[64,128]{1,0:T(8,128)S(1)}, u32[]{:S(2)}, u32[]{:S(2)}) collective-permute-start(s32[64,128]{1,0:T(8,128)S(1)} %pad_add_fusion.1), channel_id=1, source_target_pairs={{0,4},{1,5},{2,6},{3,7},{4,0},{5,1},{6,2},{7,3},{8,12},{9,13},{10,... | collective-permute-start | bytes 98312 | tf_op jit(solution)/shard_map/ppermute | solution.py:354
  25.5 1.6 collective-permute-start.8
  27.1 0.5 collective-permute-start.11
  27.6 4.9 %build_weights.1.w_ref = bf16[768,512]{1,0:T(8,128)(2,1)S(1)} custom-call(s32[8]{0:T(128)S(1)} %stack.92.base_ref, s32[64,512]{1,0:T(8,128)S(1)} %pad_add_fusion.query_ref), custom_call_target="tpu_custom_call" | custom-call | flops 5033164800 | bytes 786432 | tf_op jit(solution)/shard_map/build_weights/pallas_call | solution.py:93
  32.5 4.0 %collective-permute-done.8.refs_6_ = bf16[192,896]{1,0:T(8,128)(2,1)S(1)} collective-permute-done((bf16[192,896]{1,0:T(8,128)(2,1)S(1)}, bf16[192,896]{1,0:T(8,128)(2,1)S(1)}, u32[]{:S(2)}, u32[]{:S(2)}) %collective-permute-start.8) | collective-permute-done | bytes 344096 | tf_op jit(solution)/shard_map/ppermute | solution.py:350
  36.5 2.0 %partial_sums.4 = (f32[896,128]{1,0:T(8,128)S(1)}, f32[896,128]{1,0:T(8,128)S(1)}, s16[1824,128]{1,0:T(8,128)(2,1)S(1)}) custom-call(s32[1]{0:T(128)} %bitcast.6.flag_ref, bf16[768,512]{1,0:T(8,128)(2,1)S(1)} %build_weights.1.w_ref, bf16[96,1920]{1,0:T(8,128)(2,1)S(1)} %get-tuple-element.57.refs_0_, bf16[96,1920]{1,0:T(8,128)(2,1)S(1)} %collective-permute-done.refs_1_, ...), custom_call_target="tpu_custom_call" | custom-call | flops 704643072 | bytes 2523136 | tf_op jit(solution)/shard_map/partial_sums/pallas_call | solution.py:170
  38.5 1.6 %collective-permute-start.9 = (s16[1824,128]{1,0:T(8,128)(2,1)S(1)}, s16[1824,128]{1,0:T(8,128)(2,1)S(1)}, u32[]{:S(2)}, u32[]{:S(2)}) collective-permute-start(s16[1824,128]{1,0:T(8,128)(2,1)S(1)} %get-tuple-element.27), channel_id=1, source_target_pairs={{0,2},{1,3},{2,0},{3,1},{4,6},{5,7},{6,4},{7,5},{8,10},{9,11},{10,... | collective-permute-start | bytes 1400840 | tf_op jit(solution)/shard_map/ppermute | solution.py:354
  40.2 0.6 constant_dynamic-slice_fusion
  40.9 1.6 collective-permute-start.17
  42.5 1.5 collective-permute-start.12
  44.0 4.8 %collective-permute-done.9.refs_0_ = s16[1824,128]{1,0:T(8,128)(2,1)S(1)} collective-permute-done((s16[1824,128]{1,0:T(8,128)(2,1)S(1)}, s16[1824,128]{1,0:T(8,128)(2,1)S(1)}, u32[]{:S(2)}, u32[]{:S(2)}) %collective-permute-start.9) | collective-permute-done | bytes 466976 | tf_op jit(solution)/shard_map/ppermute | solution.py:354
  48.8 2.5 %partial_sums.5 = (f32[1024,128]{1,0:T(8,128)S(1)}, f32[1024,128]{1,0:T(8,128)S(1)}, s16[2080,128]{1,0:T(8,128)(2,1)S(1)}) custom-call(s32[1]{0:T(128)} %bitcast.6.flag_ref, bf16[768,512]{1,0:T(8,128)(2,1)S(1)} %build_weights.1.w_ref, bf16[96,1920]{1,0:T(8,128)(2,1)S(1)} %get-tuple-element.57.refs_0_, bf16[96,1920]{1,0:T(8,128)(2,1)S(1)} %collective-permute-done.refs_1_, ...), custom_call_target="tpu_custom_call" | custom-call | flops 805306368 | bytes 2883584 | tf_op jit(solution)/shard_map/partial_sums/pallas_call | solution.py:170
  51.3 1.6 %collective-permute-start.14 = (s16[2080,128]{1,0:T(8,128)(2,1)S(1)}, s16[2080,128]{1,0:T(8,128)(2,1)S(1)}, u32[]{:S(2)}, u32[]{:S(2)}) collective-permute-start(s16[2080,128]{1,0:T(8,128)(2,1)S(1)} %get-tuple-element.35), channel_id=1, source_target_pairs={{0,2},{1,3},{2,0},{3,1},{4,6},{5,7},{6,4},{7,5},{8,10},{9,11},{10,... | collective-permute-start | bytes 1597448 | tf_op jit(solution)/shard_map/ppermute | solution.py:354
  53.0 6.7 %collective-permute-done.17.refs_2_ = bf16[96,1920]{1,0:T(8,128)(2,1)S(1)} collective-permute-done((bf16[96,1920]{1,0:T(8,128)(2,1)S(1)}, bf16[96,1920]{1,0:T(8,128)(2,1)S(1)}, u32[]{:S(2)}, u32[]{:S(2)}) %collective-permute-start.17) | collective-permute-done | bytes 368672 | tf_op jit(solution)/shard_map/ppermute | solution.py:350
  59.7 0.7 collective-permute-done.13.refs_5_
  60.5 1.5 collective-permute-start.19
  62.0 0.5 collective-permute-start.16
  62.5 3.3 %collective-permute-done.14.refs_0_ = s16[2080,128]{1,0:T(8,128)(2,1)S(1)} collective-permute-done((s16[2080,128]{1,0:T(8,128)(2,1)S(1)}, s16[2080,128]{1,0:T(8,128)(2,1)S(1)}, u32[]{:S(2)}, u32[]{:S(2)}) %collective-permute-start.14) | collective-permute-done | bytes 532512 | tf_op jit(solution)/shard_map/ppermute | solution.py:354
  66.0 0.9 collective-permute-start.15
  67.1 2.1 %collective-permute-start.10 = (s16[912,128]{1,0:T(8,128)(2,1)S(1)}, s16[912,128]{1,0:T(8,128)(2,1)S(1)}, u32[]{:S(2)}, u32[]{:S(2)}) collective-permute-start(s16[912,128]{1,0:T(8,128)(2,1)S(1)} %combine.8), channel_id=1, source_target_pairs={{0,4},{1,5},{2,6},{3,7},{4,0},{5,1},{6,2},{7,3},{8,12},{9,13},{10,... | collective-permute-start | bytes 700424 | tf_op jit(solution)/shard_map/ppermute | solution.py:354
  69.2 22.5 %collective-permute-done.10.refs_1_ = s16[912,128]{1,0:T(8,128)(2,1)S(1)} collective-permute-done((s16[912,128]{1,0:T(8,128)(2,1)S(1)}, s16[912,128]{1,0:T(8,128)(2,1)S(1)}, u32[]{:S(2)}, u32[]{:S(2)}) %collective-permute-start.10) | collective-permute-done | bytes 233504 | tf_op jit(solution)/shard_map/ppermute | solution.py:354
  91.7 2.7 %partial_sums.6 = (f32[1280,128]{1,0:T(8,128)S(1)}, f32[1280,128]{1,0:T(8,128)S(1)}, s16[2592,128]{1,0:T(8,128)(2,1)S(1)}) custom-call(s32[1]{0:T(128)} %bitcast.6.flag_ref, bf16[768,512]{1,0:T(8,128)(2,1)S(1)} %build_weights.1.w_ref, bf16[96,1920]{1,0:T(8,128)(2,1)S(1)} %get-tuple-element.32.refs_0_, bf16[96,1920]{1,0:T(8,128)(2,1)S(1)} %collective-permute-done.16.refs_1_, ...), custom_call_target="tpu_custom_call" | custom-call | flops 1006632960 | bytes 3604480 | tf_op jit(solution)/shard_map/partial_sums/pallas_call | solution.py:170
  94.6 0.9 collective-permute-start.25
  95.5 6.8 %collective-permute-done.25.refs_6_ = bf16[192,640]{1,0:T(8,128)(2,1)S(1)} collective-permute-done((bf16[192,640]{1,0:T(8,128)(2,1)S(1)}, bf16[192,640]{1,0:T(8,128)(2,1)S(1)}, u32[]{:S(2)}, u32[]{:S(2)}) %collective-permute-start.25) | collective-permute-done | bytes 245792 | tf_op jit(solution)/shard_map/ppermute | solution.py:350
  102.3 1.4 partial_sums.7
  103.8 1.8 %collective-permute-start.26 = (s16[1312,128]{1,0:T(8,128)(2,1)S(1)}, s16[1312,128]{1,0:T(8,128)(2,1)S(1)}, u32[]{:S(2)}, u32[]{:S(2)}) collective-permute-start(s16[1312,128]{1,0:T(8,128)(2,1)S(1)} %get-tuple-element.44), channel_id=1, source_target_pairs={{0,2},{1,3},{2,0},{3,1},{4,6},{5,7},{6,4},{7,5},{8,10},{9,11},{10,... | collective-permute-start | bytes 1007624 | tf_op jit(solution)/shard_map/ppermute | solution.py:354
  105.6 6.7 %collective-permute-done.20.refs_0_ = s16[2592,128]{1,0:T(8,128)(2,1)S(1)} collective-permute-done((s16[2592,128]{1,0:T(8,128)(2,1)S(1)}, s16[2592,128]{1,0:T(8,128)(2,1)S(1)}, u32[]{:S(2)}, u32[]{:S(2)}) %collective-permute-start.20) | collective-permute-done | bytes 663584 | tf_op jit(solution)/shard_map/ppermute | solution.py:354
  112.8 2.4 %collective-permute-start.35 = (s16[1040,128]{1,0:T(8,128)(2,1)S(1)}, s16[1040,128]{1,0:T(8,128)(2,1)S(1)}, u32[]{:S(2)}, u32[]{:S(2)}) collective-permute-start(s16[1040,128]{1,0:T(8,128)(2,1)S(1)} %combine.15.refs_4_), channel_id=1, source_target_pairs={{0,16},{1,17},{2,18},{3,19},{4,20},{5,21},{6,22},{7,23},{8,24},{9,... | collective-permute-start | bytes 798728 | tf_op jit(solution)/shard_map/ppermute | solution.py:350
  115.6 6.9 %collective-permute-done.26.refs_0_ = s16[1312,128]{1,0:T(8,128)(2,1)S(1)} collective-permute-done((s16[1312,128]{1,0:T(8,128)(2,1)S(1)}, s16[1312,128]{1,0:T(8,128)(2,1)S(1)}, u32[]{:S(2)}, u32[]{:S(2)}) %collective-permute-start.26) | collective-permute-done | bytes 335904 | tf_op jit(solution)/shard_map/ppermute | solution.py:354
  122.6 0.6 collective-permute-start.27
  123.1 10.5 %collective-permute-done.21.refs_1_ = s16[1296,128]{1,0:T(8,128)(2,1)S(1)} collective-permute-done((s16[1296,128]{1,0:T(8,128)(2,1)S(1)}, s16[1296,128]{1,0:T(8,128)(2,1)S(1)}, u32[]{:S(2)}, u32[]{:S(2)}) %collective-permute-start.21) | collective-permute-done | bytes 331808 | tf_op jit(solution)/shard_map/ppermute | solution.py:354
  133.9 2.4 %collective-permute-start.23 = (s16[1296,128]{1,0:T(8,128)(2,1)S(1)}, s16[1296,128]{1,0:T(8,128)(2,1)S(1)}, u32[]{:S(2)}, u32[]{:S(2)}) collective-permute-start(s16[1296,128]{1,0:T(8,128)(2,1)S(1)} %combine.11.refs_0_), channel_id=1, source_target_pairs={{0,16},{1,17},{2,18},{3,19},{4,20},{5,21},{6,22},{7,23},{8,24},{9,... | collective-permute-start | bytes 995336 | tf_op jit(solution)/shard_map/ppermute | solution.py:350
  136.3 0.5 collective-permute-start.36
  137.1 0.9 collective-permute-start.29
  138.2 0.4 collective-permute-done.33.refs_3_
  138.7 6.3 %collective-permute-done.29.refs_6_ = s16[656,128]{1,0:T(8,128)(2,1)S(1)} collective-permute-done((s16[656,128]{1,0:T(8,128)(2,1)S(1)}, s16[656,128]{1,0:T(8,128)(2,1)S(1)}, u32[]{:S(2)}, u32[]{:S(2)}) %collective-permute-start.29) | collective-permute-done | bytes 167968 | tf_op jit(solution)/shard_map/ppermute | solution.py:350
  145.0 0.5 collective-permute-start.22
  145.6 11.9 %covariance.1 = f32[13456,128]{1,0:T(8,128)} custom-call(s32[8]{0:T(128)S(1)} %stack.97.place_ref, s16[912,128]{1,0:T(8,128)(2,1)S(1)} %combine.14.refs_0_, s16[912,128]{1,0:T(8,128)(2,1)S(1)} %collective-permute-done.31.refs_1_, s16[912,128]{1,0:T(8,128)(2,1)S(1)} %collective-permute-done.32.refs_2_, s16[912,128]{1,0:T(8,128)(2,1)S(1)} %collective-permute-done.33.refs_3_, ...), custom_call_target="tpu_custom_call" | custom-call | flops 15432417280 | bytes 6889472 | tf_op jit(solution)/shard_map/covariance/pallas_call | solution.py:311
  157.6 3.8 %marginal.1 = f32[128,7424]{1,0:T(8,128)} custom-call(s32[8]{0:T(128)S(1)} %stack.83.place_ref, s16[1296,128]{1,0:T(8,128)(2,1)S(1)} %combine.11.refs_0_, s16[1296,128]{1,0:T(8,128)(2,1)S(1)} %collective-permute-done.22.refs_1_, s16[1296,128]{1,0:T(8,128)(2,1)S(1)} %collective-permute-done.23.refs_2_, s16[1296,128]{1,0:T(8,128)(2,1)S(1)} %collective-permute-done.24.refs_3_, ...), custom_call_target="tpu_custom_call" | custom-call | flops 3801088 | bytes 5701632 | tf_op jit(solution)/shard_map/marginal/pallas_call | solution.py:238
  (71 shorter events, 3.2 us)
Async XLA Ops:
  0.7 1.5 copy-start.1
  2.4 5.5 %copy-start.2 = (s32[128,32]{0,1:T(8,128)S(1)}, s32[128,32]{0,1:T(8,128)}, u32[]{:S(2)}) copy-start(s32[128,32]{0,1:T(8,128)} %param.9) | copy-start | bytes 49156
  2.4 5.5 %copy-start.3 = (s32[128,32]{0,1:T(8,128)S(1)}, s32[128,32]{0,1:T(8,128)}, u32[]{:S(2)}) copy-start(s32[128,32]{0,1:T(8,128)} %param.8) | copy-start | bytes 49156
  2.5 11.5 %collective-permute-start.5 = (bf16[96,1920]{1,0:T(8,128)(2,1)S(1)}, bf16[96,1920]{1,0:T(8,128)(2,1)S(1)}, u32[]{:S(2)}, u32[]{:S(2)}) collective-permute-start(bf16[96,1920]{1,0:T(8,128)(2,1)S(1)} %get-tuple-element.54), channel_id=1, source_target_pairs={{0,24},{1,25},{2,26},{3,27},{4,28},{5,29},{6,30},{7,31},{8,16},{9,... | collective-permute-start | bytes 1105928 | tf_op jit(solution)/shard_map/ppermute | solution.py:350
  5.0 3.0 %collective-permute-start = (bf16[96,1920]{1,0:T(8,128)(2,1)S(1)}, bf16[96,1920]{1,0:T(8,128)(2,1)S(1)}, u32[]{:S(2)}, u32[]{:S(2)}) collective-permute-start(bf16[96,1920]{1,0:T(8,128)(2,1)S(1)} %get-tuple-element.55), channel_id=1, source_target_pairs={{0,8},{1,9},{2,10},{3,11},{4,12},{5,13},{6,14},{7,15},{8,0},{9,1},... | collective-permute-start | bytes 1105928 | tf_op jit(solution)/shard_map/ppermute | solution.py:350
  5.7 16.3 %collective-permute-start.4 = (bf16[96,1920]{1,0:T(8,128)(2,1)S(1)}, bf16[96,1920]{1,0:T(8,128)(2,1)S(1)}, u32[]{:S(2)}, u32[]{:S(2)}) collective-permute-start(bf16[96,1920]{1,0:T(8,128)(2,1)S(1)} %get-tuple-element.56), channel_id=1, source_target_pairs={{0,16},{1,17},{2,18},{3,19},{4,20},{5,21},{6,22},{7,23},{8,24},{9,... | collective-permute-start | bytes 1105928 | tf_op jit(solution)/shard_map/ppermute | solution.py:350
  5.8 26.7 %collective-permute-start.7 = (bf16[96,1920]{1,0:T(8,128)(2,1)S(1)}, bf16[96,1920]{1,0:T(8,128)(2,1)S(1)}, u32[]{:S(2)}, u32[]{:S(2)}) collective-permute-start(bf16[96,1920]{1,0:T(8,128)(2,1)S(1)} %get-tuple-element.55), channel_id=1, source_target_pairs={{0,9},{1,8},{2,11},{3,10},{4,13},{5,12},{6,15},{7,14},{8,1},{9,0},... | collective-permute-start | bytes 1105928 | tf_op jit(solution)/shard_map/ppermute | solution.py:350
  7.1 25.4 %collective-permute-start.6 = (bf16[96,1920]{1,0:T(8,128)(2,1)S(1)}, bf16[96,1920]{1,0:T(8,128)(2,1)S(1)}, u32[]{:S(2)}, u32[]{:S(2)}) collective-permute-start(bf16[96,1920]{1,0:T(8,128)(2,1)S(1)} %get-tuple-element.57.refs_0_), channel_id=1, source_target_pairs={{0,1},{1,0},{2,3},{3,2},{4,5},{5,4},{6,7},{7,6},{8,9},{9,8},{10,11... | collective-permute-start | bytes 1105928 | tf_op jit(solution)/shard_map/ppermute | solution.py:350
  8.0 17.6 %collective-permute-start.3 = (s32[64,128]{1,0:T(8,128)S(1)}, s32[64,128]{1,0:T(8,128)S(1)}, u32[]{:S(2)}, u32[]{:S(2)}) collective-permute-start(s32[64,128]{1,0:T(8,128)S(1)} %pad_add_fusion.1), channel_id=1, source_target_pairs={{0,6},{1,7},{2,4},{3,5},{4,2},{5,3},{6,0},{7,1},{8,14},{9,15},{10,... | collective-permute-start | bytes 98312 | tf_op jit(solution)/shard_map/ppermute | solution.py:354
  13.9 13.2 %collective-permute-start.2 = (s32[64,128]{1,0:T(8,128)S(1)}, s32[64,128]{1,0:T(8,128)S(1)}, u32[]{:S(2)}, u32[]{:S(2)}) collective-permute-start(s32[64,128]{1,0:T(8,128)S(1)} %pad_add_fusion.1), channel_id=1, source_target_pairs={{0,2},{1,3},{2,0},{3,1},{4,6},{5,7},{6,4},{7,5},{8,10},{9,11},{10,... | collective-permute-start | bytes 98312 | tf_op jit(solution)/shard_map/ppermute | solution.py:354
  22.0 5.6 %collective-permute-start.1 = (s32[64,128]{1,0:T(8,128)S(1)}, s32[64,128]{1,0:T(8,128)S(1)}, u32[]{:S(2)}, u32[]{:S(2)}) collective-permute-start(s32[64,128]{1,0:T(8,128)S(1)} %pad_add_fusion.1), channel_id=1, source_target_pairs={{0,4},{1,5},{2,6},{3,7},{4,0},{5,1},{6,2},{7,3},{8,12},{9,13},{10,... | collective-permute-start | bytes 98312 | tf_op jit(solution)/shard_map/ppermute | solution.py:354
  25.5 11.0 %collective-permute-start.8 = (bf16[192,896]{1,0:T(8,128)(2,1)S(1)}, bf16[192,896]{1,0:T(8,128)(2,1)S(1)}, u32[]{:S(2)}, u32[]{:S(2)}) collective-permute-start(bf16[192,896]{1,0:T(8,128)(2,1)S(1)} %pad_maximum_fusion.2), channel_id=1, source_target_pairs={{0,1},{1,0},{2,3},{3,2},{4,5},{5,4},{6,7},{7,6},{8,9},{9,8},{10,11... | collective-permute-start | bytes 1032200 | tf_op jit(solution)/shard_map/ppermute | solution.py:350
  27.1 21.7 %collective-permute-start.11 = (bf16[192,1024]{1,0:T(8,128)(2,1)S(1)}, bf16[192,1024]{1,0:T(8,128)(2,1)S(1)}, u32[]{:S(2)}, u32[]{:S(2)}) collective-permute-start(bf16[192,1024]{1,0:T(8,128)(2,1)S(1)} %pad_maximum_fusion.1), channel_id=1, source_target_pairs={{0,1},{1,0},{2,3},{3,2},{4,5},{5,4},{6,7},{7,6},{8,9},{9,8},{10,11... | collective-permute-start | bytes 1179656 | tf_op jit(solution)/shard_map/ppermute | solution.py:350
  36.5 3.6 %copy-start = (bf16[96,7424]{1,0:T(8,128)(2,1)S(1)}, bf16[96,7424]{1,0:T(8,128)(2,1)}, u32[]{:S(2)}) copy-start(bf16[96,7424]{1,0:T(8,128)(2,1)} %param.5) | copy-start | bytes 4276228
  38.5 10.3 %collective-permute-start.9 = (s16[1824,128]{1,0:T(8,128)(2,1)S(1)}, s16[1824,128]{1,0:T(8,128)(2,1)S(1)}, u32[]{:S(2)}, u32[]{:S(2)}) collective-permute-start(s16[1824,128]{1,0:T(8,128)(2,1)S(1)} %get-tuple-element.27), channel_id=1, source_target_pairs={{0,2},{1,3},{2,0},{3,1},{4,6},{5,7},{6,4},{7,5},{8,10},{9,11},{10,... | collective-permute-start | bytes 1400840 | tf_op jit(solution)/shard_map/ppermute | solution.py:354
  40.8 12.2 %collective-permute-start.18 = (bf16[96,1920]{1,0:T(8,128)(2,1)S(1)}, bf16[96,1920]{1,0:T(8,128)(2,1)S(1)}, u32[]{:S(2)}, u32[]{:S(2)}) collective-permute-start(bf16[96,1920]{1,0:T(8,128)(2,1)S(1)} %get-tuple-element.48), channel_id=1, source_target_pairs={{0,24},{1,25},{2,26},{3,27},{4,28},{5,29},{6,30},{7,31},{8,16},{9,... | collective-permute-start | bytes 1105928 | tf_op jit(solution)/shard_map/ppermute | solution.py:350
  40.9 18.8 %collective-permute-start.17 = (bf16[96,1920]{1,0:T(8,128)(2,1)S(1)}, bf16[96,1920]{1,0:T(8,128)(2,1)S(1)}, u32[]{:S(2)}, u32[]{:S(2)}) collective-permute-start(bf16[96,1920]{1,0:T(8,128)(2,1)S(1)} %get-tuple-element.49), channel_id=1, source_target_pairs={{0,16},{1,17},{2,18},{3,19},{4,20},{5,21},{6,22},{7,23},{8,24},{9,... | collective-permute-start | bytes 1105928 | tf_op jit(solution)/shard_map/ppermute | solution.py:350
  42.5 17.3 %collective-permute-start.12 = (bf16[96,1920]{1,0:T(8,128)(2,1)S(1)}, bf16[96,1920]{1,0:T(8,128)(2,1)S(1)}, u32[]{:S(2)}, u32[]{:S(2)}) collective-permute-start(bf16[96,1920]{1,0:T(8,128)(2,1)S(1)} %get-tuple-element.32.refs_0_), channel_id=1, source_target_pairs={{0,1},{1,0},{2,3},{3,2},{4,5},{5,4},{6,7},{7,6},{8,9},{9,8},{10,11... | collective-permute-start | bytes 1105928 | tf_op jit(solution)/shard_map/ppermute | solution.py:350
  48.8 11.7 %collective-permute-start.13 = (bf16[96,1920]{1,0:T(8,128)(2,1)S(1)}, bf16[96,1920]{1,0:T(8,128)(2,1)S(1)}, u32[]{:S(2)}, u32[]{:S(2)}) collective-permute-start(bf16[96,1920]{1,0:T(8,128)(2,1)S(1)} %get-tuple-element.33), channel_id=1, source_target_pairs={{0,9},{1,8},{2,11},{3,10},{4,13},{5,12},{6,15},{7,14},{8,1},{9,0},... | collective-permute-start | bytes 1105928 | tf_op jit(solution)/shard_map/ppermute | solution.py:350
  51.3 14.4 %collective-permute-start.14 = (s16[2080,128]{1,0:T(8,128)(2,1)S(1)}, s16[2080,128]{1,0:T(8,128)(2,1)S(1)}, u32[]{:S(2)}, u32[]{:S(2)}) collective-permute-start(s16[2080,128]{1,0:T(8,128)(2,1)S(1)} %get-tuple-element.35), channel_id=1, source_target_pairs={{0,2},{1,3},{2,0},{3,1},{4,6},{5,7},{6,4},{7,5},{8,10},{9,11},{10,... | collective-permute-start | bytes 1597448 | tf_op jit(solution)/shard_map/ppermute | solution.py:354
  60.5 31.2 %collective-permute-start.19 = (bf16[192,1280]{1,0:T(8,128)(2,1)S(1)}, bf16[192,1280]{1,0:T(8,128)(2,1)S(1)}, u32[]{:S(2)}, u32[]{:S(2)}) collective-permute-start(bf16[192,1280]{1,0:T(8,128)(2,1)S(1)} %pad_maximum_fusion), channel_id=1, source_target_pairs={{0,1},{1,0},{2,3},{3,2},{4,5},{5,4},{6,7},{7,6},{8,9},{9,8},{10,11... | collective-permute-start | bytes 1474568 | tf_op jit(solution)/shard_map/ppermute | solution.py:350
  62.0 29.7 %collective-permute-start.16 = (bf16[96,1920]{1,0:T(8,128)(2,1)S(1)}, bf16[96,1920]{1,0:T(8,128)(2,1)S(1)}, u32[]{:S(2)}, u32[]{:S(2)}) collective-permute-start(bf16[96,1920]{1,0:T(8,128)(2,1)S(1)} %get-tuple-element.33), channel_id=1, source_target_pairs={{0,8},{1,9},{2,10},{3,11},{4,12},{5,13},{6,14},{7,15},{8,0},{9,1},... | collective-permute-start | bytes 1105928 | tf_op jit(solution)/shard_map/ppermute | solution.py:350
  66.0 25.7 %collective-permute-start.15 = (s16[1040,128]{1,0:T(8,128)(2,1)S(1)}, s16[1040,128]{1,0:T(8,128)(2,1)S(1)}, u32[]{:S(2)}, u32[]{:S(2)}) collective-permute-start(s16[1040,128]{1,0:T(8,128)(2,1)S(1)} %combine.9), channel_id=1, source_target_pairs={{0,4},{1,5},{2,6},{3,7},{4,0},{5,1},{6,2},{7,3},{8,12},{9,13},{10,... | collective-permute-start | bytes 798728 | tf_op jit(solution)/shard_map/ppermute | solution.py:354
  67.1 24.6 %collective-permute-start.10 = (s16[912,128]{1,0:T(8,128)(2,1)S(1)}, s16[912,128]{1,0:T(8,128)(2,1)S(1)}, u32[]{:S(2)}, u32[]{:S(2)}) collective-permute-start(s16[912,128]{1,0:T(8,128)(2,1)S(1)} %combine.8), channel_id=1, source_target_pairs={{0,4},{1,5},{2,6},{3,7},{4,0},{5,1},{6,2},{7,3},{8,12},{9,13},{10,... | collective-permute-start | bytes 700424 | tf_op jit(solution)/shard_map/ppermute | solution.py:354
  94.4 17.9 %collective-permute-start.20 = (s16[2592,128]{1,0:T(8,128)(2,1)S(1)}, s16[2592,128]{1,0:T(8,128)(2,1)S(1)}, u32[]{:S(2)}, u32[]{:S(2)}) collective-permute-start(s16[2592,128]{1,0:T(8,128)(2,1)S(1)} %get-tuple-element.39), channel_id=1, source_target_pairs={{0,2},{1,3},{2,0},{3,1},{4,6},{5,7},{6,4},{7,5},{8,10},{9,11},{10,... | collective-permute-start | bytes 1990664 | tf_op jit(solution)/shard_map/ppermute | solution.py:354
  94.6 7.8 %collective-permute-start.25 = (bf16[192,640]{1,0:T(8,128)(2,1)S(1)}, bf16[192,640]{1,0:T(8,128)(2,1)S(1)}, u32[]{:S(2)}, u32[]{:S(2)}) collective-permute-start(bf16[192,640]{1,0:T(8,128)(2,1)S(1)} %pad_maximum_fusion.3), channel_id=1, source_target_pairs={{0,1},{1,0},{2,3},{3,2},{4,5},{5,4},{6,7},{7,6},{8,9},{9,8},{10,11... | collective-permute-start | bytes 737288 | tf_op jit(solution)/shard_map/ppermute | solution.py:350
  103.8 18.6 %collective-permute-start.26 = (s16[1312,128]{1,0:T(8,128)(2,1)S(1)}, s16[1312,128]{1,0:T(8,128)(2,1)S(1)}, u32[]{:S(2)}, u32[]{:S(2)}) collective-permute-start(s16[1312,128]{1,0:T(8,128)(2,1)S(1)} %get-tuple-element.44), channel_id=1, source_target_pairs={{0,2},{1,3},{2,0},{3,1},{4,6},{5,7},{6,4},{7,5},{8,10},{9,11},{10,... | collective-permute-start | bytes 1007624 | tf_op jit(solution)/shard_map/ppermute | solution.py:354
  112.5 21.1 %collective-permute-start.21 = (s16[1296,128]{1,0:T(8,128)(2,1)S(1)}, s16[1296,128]{1,0:T(8,128)(2,1)S(1)}, u32[]{:S(2)}, u32[]{:S(2)}) collective-permute-start(s16[1296,128]{1,0:T(8,128)(2,1)S(1)} %combine.10), channel_id=1, source_target_pairs={{0,4},{1,5},{2,6},{3,7},{4,0},{5,1},{6,2},{7,3},{8,12},{9,13},{10,... | collective-permute-start | bytes 995336 | tf_op jit(solution)/shard_map/ppermute | solution.py:354
  112.8 23.5 %collective-permute-start.35 = (s16[1040,128]{1,0:T(8,128)(2,1)S(1)}, s16[1040,128]{1,0:T(8,128)(2,1)S(1)}, u32[]{:S(2)}, u32[]{:S(2)}) collective-permute-start(s16[1040,128]{1,0:T(8,128)(2,1)S(1)} %combine.15.refs_4_), channel_id=1, source_target_pairs={{0,16},{1,17},{2,18},{3,19},{4,20},{5,21},{6,22},{7,23},{8,24},{9,... | collective-permute-start | bytes 798728 | tf_op jit(solution)/shard_map/ppermute | solution.py:350
  115.5 20.8 %collective-permute-start.32 = (s16[912,128]{1,0:T(8,128)(2,1)S(1)}, s16[912,128]{1,0:T(8,128)(2,1)S(1)}, u32[]{:S(2)}, u32[]{:S(2)}) collective-permute-start(s16[912,128]{1,0:T(8,128)(2,1)S(1)} %combine.14.refs_0_), channel_id=1, source_target_pairs={{0,16},{1,17},{2,18},{3,19},{4,20},{5,21},{6,22},{7,23},{8,24},{9,... | collective-permute-start | bytes 700424 | tf_op jit(solution)/shard_map/ppermute | solution.py:350
  122.6 14.3 %collective-permute-start.27 = (s16[656,128]{1,0:T(8,128)(2,1)S(1)}, s16[656,128]{1,0:T(8,128)(2,1)S(1)}, u32[]{:S(2)}, u32[]{:S(2)}) collective-permute-start(s16[656,128]{1,0:T(8,128)(2,1)S(1)} %combine.12), channel_id=1, source_target_pairs={{0,4},{1,5},{2,6},{3,7},{4,0},{5,1},{6,2},{7,3},{8,12},{9,13},{10,... | collective-permute-start | bytes 503816 | tf_op jit(solution)/shard_map/ppermute | solution.py:354
  123.1 14.0 %collective-permute-start.31 = (s16[912,128]{1,0:T(8,128)(2,1)S(1)}, s16[912,128]{1,0:T(8,128)(2,1)S(1)}, u32[]{:S(2)}, u32[]{:S(2)}) collective-permute-start(s16[912,128]{1,0:T(8,128)(2,1)S(1)} %combine.14.refs_0_), channel_id=1, source_target_pairs={{0,8},{1,9},{2,10},{3,11},{4,12},{5,13},{6,14},{7,15},{8,0},{9,1},... | collective-permute-start | bytes 700424 | tf_op jit(solution)/shard_map/ppermute | solution.py:350
  133.9 11.6 %collective-permute-start.23 = (s16[1296,128]{1,0:T(8,128)(2,1)S(1)}, s16[1296,128]{1,0:T(8,128)(2,1)S(1)}, u32[]{:S(2)}, u32[]{:S(2)}) collective-permute-start(s16[1296,128]{1,0:T(8,128)(2,1)S(1)} %combine.11.refs_0_), channel_id=1, source_target_pairs={{0,16},{1,17},{2,18},{3,19},{4,20},{5,21},{6,22},{7,23},{8,24},{9,... | collective-permute-start | bytes 995336 | tf_op jit(solution)/shard_map/ppermute | solution.py:350
  136.3 8.7 %collective-permute-start.34 = (s16[1040,128]{1,0:T(8,128)(2,1)S(1)}, s16[1040,128]{1,0:T(8,128)(2,1)S(1)}, u32[]{:S(2)}, u32[]{:S(2)}) collective-permute-start(s16[1040,128]{1,0:T(8,128)(2,1)S(1)} %combine.15.refs_4_), channel_id=1, source_target_pairs={{0,8},{1,9},{2,10},{3,11},{4,12},{5,13},{6,14},{7,15},{8,0},{9,1},... | collective-permute-start | bytes 798728 | tf_op jit(solution)/shard_map/ppermute | solution.py:350
  136.3 9.3 %collective-permute-start.36 = (s16[1040,128]{1,0:T(8,128)(2,1)S(1)}, s16[1040,128]{1,0:T(8,128)(2,1)S(1)}, u32[]{:S(2)}, u32[]{:S(2)}) collective-permute-start(s16[1040,128]{1,0:T(8,128)(2,1)S(1)} %collective-permute-done.35.refs_6_), channel_id=1, source_target_pairs={{0,8},{1,9},{2,10},{3,11},{4,12},{5,13},{6,14},{7,15},{8,0},{9,1},... | collective-permute-start | bytes 798728 | tf_op jit(solution)/shard_map/ppermute | solution.py:350
  136.9 1.7 %collective-permute-start.33 = (s16[912,128]{1,0:T(8,128)(2,1)S(1)}, s16[912,128]{1,0:T(8,128)(2,1)S(1)}, u32[]{:S(2)}, u32[]{:S(2)}) collective-permute-start(s16[912,128]{1,0:T(8,128)(2,1)S(1)} %collective-permute-done.32.refs_2_), channel_id=1, source_target_pairs={{0,8},{1,9},{2,10},{3,11},{4,12},{5,13},{6,14},{7,15},{8,0},{9,1},... | collective-permute-start | bytes 700424 | tf_op jit(solution)/shard_map/ppermute | solution.py:350
  137.1 7.9 %collective-permute-start.29 = (s16[656,128]{1,0:T(8,128)(2,1)S(1)}, s16[656,128]{1,0:T(8,128)(2,1)S(1)}, u32[]{:S(2)}, u32[]{:S(2)}) collective-permute-start(s16[656,128]{1,0:T(8,128)(2,1)S(1)} %combine.13.refs_4_), channel_id=1, source_target_pairs={{0,16},{1,17},{2,18},{3,19},{4,20},{5,21},{6,22},{7,23},{8,24},{9,... | collective-permute-start | bytes 503816 | tf_op jit(solution)/shard_map/ppermute | solution.py:350
  138.6 18.9 %collective-permute-start.28 = (s16[656,128]{1,0:T(8,128)(2,1)S(1)}, s16[656,128]{1,0:T(8,128)(2,1)S(1)}, u32[]{:S(2)}, u32[]{:S(2)}) collective-permute-start(s16[656,128]{1,0:T(8,128)(2,1)S(1)} %combine.13.refs_4_), channel_id=1, source_target_pairs={{0,8},{1,9},{2,10},{3,11},{4,12},{5,13},{6,14},{7,15},{8,0},{9,1},... | collective-permute-start | bytes 503816 | tf_op jit(solution)/shard_map/ppermute | solution.py:350
  145.0 12.5 %collective-permute-start.30 = (s16[656,128]{1,0:T(8,128)(2,1)S(1)}, s16[656,128]{1,0:T(8,128)(2,1)S(1)}, u32[]{:S(2)}, u32[]{:S(2)}) collective-permute-start(s16[656,128]{1,0:T(8,128)(2,1)S(1)} %collective-permute-done.29.refs_6_), channel_id=1, source_target_pairs={{0,8},{1,9},{2,10},{3,11},{4,12},{5,13},{6,14},{7,15},{8,0},{9,1},... | collective-permute-start | bytes 503816 | tf_op jit(solution)/shard_map/ppermute | solution.py:350
  145.0 12.5 %collective-permute-start.22 = (s16[1296,128]{1,0:T(8,128)(2,1)S(1)}, s16[1296,128]{1,0:T(8,128)(2,1)S(1)}, u32[]{:S(2)}, u32[]{:S(2)}) collective-permute-start(s16[1296,128]{1,0:T(8,128)(2,1)S(1)} %combine.11.refs_0_), channel_id=1, source_target_pairs={{0,8},{1,9},{2,10},{3,11},{4,12},{5,13},{6,14},{7,15},{8,0},{9,1},... | collective-permute-start | bytes 995336 | tf_op jit(solution)/shard_map/ppermute | solution.py:350
  145.6 12.0 %collective-permute-start.24 = (s16[1296,128]{1,0:T(8,128)(2,1)S(1)}, s16[1296,128]{1,0:T(8,128)(2,1)S(1)}, u32[]{:S(2)}, u32[]{:S(2)}) collective-permute-start(s16[1296,128]{1,0:T(8,128)(2,1)S(1)} %collective-permute-done.23.refs_2_), channel_id=1, source_target_pairs={{0,8},{1,9},{2,10},{3,11},{4,12},{5,13},{6,14},{7,15},{8,0},{9,1},... | collective-permute-start | bytes 995336 | tf_op jit(solution)/shard_map/ppermute | solution.py:350

commit v7 on v6

--- a/solution.py
+++ b/solution.py
@@ -10,7 +10,7 @@
 CORES = 2
 DEPTH = 4
 LOAD_FIRST = 7
-MEAN_FIRST = 10
+MEAN_FIRST = 8
 SCALES = 16
 TOP = 32767.0
 VMEM_BYTES = 48 * 1024 * 1024
@@ -365,21 +365,23 @@
     def each_of(tiles):
         return -(-tiles // xs)
 
-    def groups_of(array, *more):
-        both = [half(array, (core + dc) % CORES, *more) for dc in range(CORES)]
+    def exchange(array, *more):
+        return [half(array, core, *more), move(half(array, (core + 1) % CORES, *more), 0, 1)]
+
+    def along_x(both):
         tiles = both[0].shape[1] // LANES
         size = (rows, each_of(tiles) * LANES)
-        return [
-            [lax.dynamic_slice(b, (0, start_of((x + dx) % xs, tiles) * LANES), size) for b in both] for dx in range(xs)
-        ]
-
-    load_cut = groups_of(factors, last_tile)
-    load_x = [[move(load_cut[dx][dc], dx, dc) for dc in range(CORES)] for dx in range(xs)]
-    load_y = [[(value, 0) for value in load_x[0]]]
-    load_y += [[(move(load_cut[0][dc], 0, dc, dy), 0) for dc in range(CORES)] for dy in range(1, ys)]
+
+        def part(group):
+            return jnp.concatenate([lax.dynamic_slice(b, (0, start_of(group, tiles) * LANES), size) for b in both], axis=0)
+
+        return [move(part((x + dx) % xs), dx, 0) for dx in range(xs)]
+
     queries = jnp.concatenate([intersection_tracts.T, intersection_weights.T], axis=0)
-    queries = after(queries, load_x[0][1])
-    queries = jnp.concatenate([queries] + [z_swap(queries, bits) for bits in (2, 1, 3)], axis=1)
+    queries = jnp.concatenate([queries, z_swap(queries, 2)], axis=1)
+    queries = jnp.concatenate([queries, z_swap(queries, 1)], axis=1)
+    load_both = exchange(factors, last_tile)
+    load_x = along_x(load_both)
 
     bases = jnp.stack([
         (((x - dx) % xs * CORES + (core - dc) % CORES) * parts + z * ys + (y - dy) % ys) * rows
@@ -387,27 +389,21 @@
     ]).astype(jnp.int32)
     w = build_weights(bases, queries, rows)
     flag = (x == xs - 1).astype(jnp.int32).reshape(1)
-    def joined(pieces, first, count):
-        return jnp.concatenate([p[:, first * LANES:(first + count) * LANES] for p in pieces], axis=0)
-
-    def along_y(by_x, first, count, *done):
-        out = []
-        for pieces in by_x[1:]:
-            sent = after(joined(pieces, first, count), *done)
-            out.append([[(value, first) for value in pieces]] + [[(move(sent, 0, 0, dy), 0)] for dy in range(1, ys)])
-        return out
+    def along_y(value, first, count, *done):
+        sent = after(value[:, first * LANES:(first + count) * LANES], *done)
+        return [(value, first)] + [(move(sent, 0, 0, dy), 0) for dy in range(1, ys)]
 
     def later(by_y, tiles):
-        return [[(value, first + tiles) for value, first in pieces] for pieces in by_y]
+        return [(value, first + tiles) for value, first in by_y]
 
     def merge(by_x):
-        return [piece for dy in range(ys) for by_y in by_x for piece in by_y[dy]]
-
-    def along_z(data, count, has_var, before_sums, before_middle):
-        own, opposite, sent = partial_sums(flag, after(w, *before_sums), data, count, has_var)
+        return [by_y[dy] for dy in range(ys) for by_y in by_x]
+
+    def along_z(data, count, has_var, *before):
+        own, opposite, sent = partial_sums(flag, after(w, *before), data, count, has_var)
         near = z_swap(sent, 1)
-        far = z_swap(combine(after(opposite, *before_middle), (near, 1)), 2)
-        return own, near, far
+        middle = combine(opposite, (near, 1))
+        return own, near, middle, z_swap(middle, 2)
 
     def spread(own, near, far):
         mine = combine(own, (near, 0), (far, 0))
@@ -428,24 +424,20 @@
     load_tiles = split(each_of(load_width), LOAD_FIRST)
     mean_tiles = split(each_of(mean_width), MEAN_FIRST)
     (first_a, first_b), (first_c, first_d) = load_tiles, mean_tiles
-    mean_cut = groups_of(after(estimates, load_x[0][1]))
-    mean_x = [[move(mean_cut[dx][dc], dx, dc) for dc in range(CORES)] for dx in range(xs)]
-    data_a = merge([load_y] + along_y(load_x, 0, first_a))
-    data_b = merge([later(load_y, first_a)] + along_y(load_x, first_a, first_b))
-    own_a, near_a, far_a = along_z(data_a, first_a, False, (), ())
-    mean_y = [[(value, 0) for value in mean_x[0]]]
-    mean_y += [[(move(after(mean_cut[0][dc], own_a), 0, dc, dy), 0) for dc in range(CORES)] for dy in range(1, ys)]
-    mean_there = [value for pieces in mean_y[1:] for value, _ in pieces]
-    own_b, near_b, far_b = along_z(data_b, first_b, True, (near_a,), mean_there)
-    data_c = merge([mean_y] + along_y(mean_x, 0, first_c, *mean_there))
-    data_d = merge([later(mean_y, first_c)] + along_y(mean_x, first_c, first_d, *mean_there))
-    own_c, opposite_c, sent_c = partial_sums(flag, after(w, far_a, far_b), data_c, first_c, False)
-    own_d, opposite_d, sent_d = partial_sums(flag, after(w, own_c), data_d, first_d, False)
+    mean_x = along_x(exchange(after(estimates, load_both[1])))
+    load_y = along_y(load_x[0], 0, first_a + first_b)
+    data_a = merge([load_y] + [along_y(value, 0, first_a) for value in load_x[1:]])
+    data_b = merge([later(load_y, first_a)] + [along_y(value, first_a, first_b) for value in load_x[1:]])
+    own_a, near_a, middle_a, far_a = along_z(data_a, first_a, False)
+    mean_y = along_y(mean_x[0], 0, first_c + first_d, data_a[-1][0])
+    there = data_b[-1][0]
+    own_b, near_b, middle_b, far_b = along_z(data_b, first_b, True)
+    data_c = merge([mean_y] + [along_y(value, 0, first_c, there) for value in mean_x[1:]])
+    data_d = merge([later(mean_y, first_c)] + [along_y(value, first_c, first_d, there) for value in mean_x[1:]])
+    own_c, near_c, middle_c, far_c = along_z(data_c, first_c, False, far_a, middle_b)
+    own_d, near_d, middle_d, far_d = along_z(data_d, first_d, False, own_c, far_b)
     _, load_a = spread(own_a, near_a, far_a)
     _, load_b = spread(own_b, near_b, far_b)
-    near_c, near_d = z_swap(sent_c, 1), z_swap(sent_d, 1)
-    far_c = z_swap(combine(opposite_c, (near_c, 1)), 2)
-    far_d = z_swap(combine(opposite_d, (near_d, 1)), 2)
     mine_c, mean_c = spread(own_c, near_c, far_c)
     mine_d, mean_d = spread(own_d, near_d, far_d)
     load_pieces = load_a + [after(load_b[0], mine_c, mine_d)] + load_b[1:]

time: 162 us -> 148 us (0.914)
  waiting for transfers between devices: 87.5 us -> 77.8 us
  Pallas kernels: 30.9 us -> 27.8 us
  starting transfers between devices: 38.9 us -> 36.1 us
    ppermute x11 -> x10, waiting for transfers between devices: 54.6 us -> 46.8 us  [z_swap(): return lax.ppermute(value, 'dist', perm)]
    ppermute x26 -> x22, starting transfers between devices: 20.6 us -> 16.9 us  [move(): return lax.ppermute(value, ('geo', 'dist'), perm)]
    pallas_call x4, Pallas kernels: 8.65 us -> 5.57 us  [partial_sums(): pl.pallas_call(functools.partial(sums_kernel, offsets, has_var), grid_spe...]
    ppermute x26 -> x22, waiting for transfers between devices: 33 us -> 30.9 us  [move(): return lax.ppermute(value, ('geo', 'dist'), perm)]
    ppermute x11 -> x10, starting transfers between devices: 18.3 us -> 19.2 us  [z_swap(): return lax.ppermute(value, 'dist', perm)]
  transfers between devices with their start and end apart: 37 -> 32, of which waited for: 14 -> 13; matrix products, arithmetic and copies ran while one was open for 1% -> 1% of each run, Pallas kernels for 15% -> 16%
where the time goes in v7:
time: 148 us
  waiting for transfers between devices  77.8 us (53%)
  starting transfers between devices  36.1 us (24%)
  Pallas kernels  27.8 us (19%)
  local copies, waits for them, and re-layouts  3.47 us (2%)
    ppermute x10, waiting for transfers between devices, z_swap(): return lax.ppermute(value, 'dist', perm)  46.8 us
    ppermute x22, waiting for transfers between devices, move(): return lax.ppermute(value, ('geo', 'dist'), perm)  30.9 us
    ppermute x10, starting transfers between devices, z_swap(): return lax.ppermute(value, 'dist', perm)  19.2 us
    ppermute x22, starting transfers between devices, move(): return lax.ppermute(value, ('geo', 'dist'), perm)  16.9 us
    pallas_call x1, Pallas kernels, covariance(): pl.pallas_call(functools.partial(covariance_kernel, tiles, total, ages, r...  11.9 us
    pallas_call x4, Pallas kernels, partial_sums(): pl.pallas_call(functools.partial(sums_kernel, offsets, has_var), grid_spe...  5.57 us
    pallas_call x1, Pallas kernels, build_weights(): pl.pallas_call(functools.partial(weights_kernel, rows), grid_spec=pltpu.P...  4.87 us
    pallas_call x1, Pallas kernels, marginal(): pl.pallas_call(functools.partial(marginal_kernel, tiles), grid_spec=pltpu...  3.83 us
  transfers between devices with their start and end apart: 32, of which 13 were waited for; matrix products, arithmetic and copies ran while one was open for 1% of the time, Pallas kernels for 16%

profile of v7, /device:TPU:0, one launch (start us, length us, event | category | flops | bytes accessed | tf_op | source)
XLA Modules:
  0.0 147.5 jit_solution(5946560952293341527)
XLA Ops:
  0.7 1.4 constant_dynamic-slice_fusion.10
  2.1 1.0 fusion.1
  3.2 0.5 collective-permute-start.2
  3.7 3.7 %collective-permute-start = (s32[64,128]{1,0:T(8,128)S(1)}, s32[64,128]{1,0:T(8,128)S(1)}, u32[]{:S(2)}, u32[]{:S(2)}) collective-permute-start(s32[64,128]{1,0:T(8,128)S(1)} %pad_add_fusion.2), channel_id=1, source_target_pairs={{0,4},{1,5},{2,6},{3,7},{4,0},{5,1},{6,2},{7,3},{8,12},{9,13},{10,... | collective-permute-start | bytes 98312 | tf_op jit(solution)/shard_map/ppermute | solution.py:354
  7.3 2.1 %collective-permute-done = s32[64,128]{1,0:T(8,128)S(1)} collective-permute-done((s32[64,128]{1,0:T(8,128)S(1)}, s32[64,128]{1,0:T(8,128)S(1)}, u32[]{:S(2)}, u32[]{:S(2)}) %collective-permute-start) | collective-permute-done | bytes 32800 | tf_op jit(solution)/shard_map/ppermute | solution.py:354
  9.4 1.7 %collective-permute-start.1 = (s32[64,256]{1,0:T(8,128)S(1)}, s32[64,256]{1,0:T(8,128)S(1)}, u32[]{:S(2)}, u32[]{:S(2)}) collective-permute-start(s32[64,256]{1,0:T(8,128)S(1)} %pad_add_fusion.1), channel_id=1, source_target_pairs={{0,2},{1,3},{2,0},{3,1},{4,6},{5,7},{6,4},{7,5},{8,10},{9,11},{10,... | collective-permute-start | bytes 196616 | tf_op jit(solution)/shard_map/ppermute | solution.py:354
  11.4 2.2 %collective-permute-done.1 = s32[64,256]{1,0:T(8,128)S(1)} collective-permute-done((s32[64,256]{1,0:T(8,128)S(1)}, s32[64,256]{1,0:T(8,128)S(1)}, u32[]{:S(2)}, u32[]{:S(2)}) %collective-permute-start.1) | collective-permute-done | bytes 65568 | tf_op jit(solution)/shard_map/ppermute | solution.py:354
  13.8 1.2 constant_dynamic-slice_fusion.5
  15.0 1.7 %collective-permute-start.3 = (bf16[192,1920]{1,0:T(8,128)(2,1)S(1)}, bf16[192,1920]{1,0:T(8,128)(2,1)S(1)}, u32[]{:S(2)}, u32[]{:S(2)}) collective-permute-start(bf16[192,1920]{1,0:T(8,128)(2,1)S(1)} %pad_maximum_fusion.1), channel_id=1, source_target_pairs={{0,16},{1,17},{2,18},{3,19},{4,20},{5,21},{6,22},{7,23},{8,24},{9,... | collective-permute-start | bytes 2211848 | tf_op jit(solution)/shard_map/ppermute | solution.py:350
  16.8 1.6 %collective-permute-start.4 = (bf16[192,1920]{1,0:T(8,128)(2,1)S(1)}, bf16[192,1920]{1,0:T(8,128)(2,1)S(1)}, u32[]{:S(2)}, u32[]{:S(2)}) collective-permute-start(bf16[192,1920]{1,0:T(8,128)(2,1)S(1)} %pad_maximum_fusion.refs_0_), channel_id=1, source_target_pairs={{0,1},{1,0},{2,3},{3,2},{4,5},{5,4},{6,7},{7,6},{8,9},{9,8},{10,11... | collective-permute-start | bytes 2211848 | tf_op jit(solution)/shard_map/ppermute | solution.py:350
  18.4 0.3 constant_dynamic-slice_fusion.1
  18.9 0.6 collective-permute-start.11
  19.5 14.9 %collective-permute-done.3.refs_1_ = bf16[192,1920]{1,0:T(8,128)(2,1)S(1)} collective-permute-done((bf16[192,1920]{1,0:T(8,128)(2,1)S(1)}, bf16[192,1920]{1,0:T(8,128)(2,1)S(1)}, u32[]{:S(2)}, u32[]{:S(2)}) %collective-permute-start.3) | collective-permute-done | bytes 737312 | tf_op jit(solution)/shard_map/ppermute | solution.py:350
  34.4 1.8 %collective-permute-start.5 = (bf16[192,896]{1,0:T(8,128)(2,1)S(1)}, bf16[192,896]{1,0:T(8,128)(2,1)S(1)}, u32[]{:S(2)}, u32[]{:S(2)}) collective-permute-start(bf16[192,896]{1,0:T(8,128)(2,1)S(1)} %slice.16), channel_id=1, source_target_pairs={{0,1},{1,0},{2,3},{3,2},{4,5},{5,4},{6,7},{7,6},{8,9},{9,8},{10,11... | collective-permute-start | bytes 1032200 | tf_op jit(solution)/shard_map/ppermute | solution.py:350
  36.2 0.4 collective-permute-start.8
  36.6 4.9 %build_weights.1.w_ref = bf16[768,512]{1,0:T(8,128)(2,1)S(1)} custom-call(s32[8]{0:T(128)S(1)} %stack.92.base_ref, s32[64,512]{1,0:T(8,128)S(1)} %pad_add_fusion.query_ref), custom_call_target="tpu_custom_call" | custom-call | flops 5033164800 | bytes 786432 | tf_op jit(solution)/shard_map/build_weights/pallas_call | solution.py:93
  41.6 3.9 %collective-permute-done.5.refs_3_ = bf16[192,896]{1,0:T(8,128)(2,1)S(1)} collective-permute-done((bf16[192,896]{1,0:T(8,128)(2,1)S(1)}, bf16[192,896]{1,0:T(8,128)(2,1)S(1)}, u32[]{:S(2)}, u32[]{:S(2)}) %collective-permute-start.5) | collective-permute-done | bytes 344096 | tf_op jit(solution)/shard_map/ppermute | solution.py:350
  45.5 1.7 %collective-permute-start.12 = (bf16[192,1920]{1,0:T(8,128)(2,1)S(1)}, bf16[192,1920]{1,0:T(8,128)(2,1)S(1)}, u32[]{:S(2)}, u32[]{:S(2)}) collective-permute-start(bf16[192,1920]{1,0:T(8,128)(2,1)S(1)} %pad_maximum_fusion.2.refs_0_), channel_id=1, source_target_pairs={{0,1},{1,0},{2,3},{3,2},{4,5},{5,4},{6,7},{7,6},{8,9},{9,8},{10,11... | collective-permute-start | bytes 2211848 | tf_op jit(solution)/shard_map/ppermute | solution.py:350
  47.2 1.3 partial_sums.4
  48.5 1.6 %collective-permute-start.6 = (s16[1824,128]{1,0:T(8,128)(2,1)S(1)}, s16[1824,128]{1,0:T(8,128)(2,1)S(1)}, u32[]{:S(2)}, u32[]{:S(2)}) collective-permute-start(s16[1824,128]{1,0:T(8,128)(2,1)S(1)} %get-tuple-element.22), channel_id=1, source_target_pairs={{0,2},{1,3},{2,0},{3,1},{4,6},{5,7},{6,4},{7,5},{8,10},{9,11},{10,... | collective-permute-start | bytes 1400840 | tf_op jit(solution)/shard_map/ppermute | solution.py:354
  50.1 3.8 %collective-permute-done.8.refs_3_ = bf16[192,1024]{1,0:T(8,128)(2,1)S(1)} collective-permute-done((bf16[192,1024]{1,0:T(8,128)(2,1)S(1)}, bf16[192,1024]{1,0:T(8,128)(2,1)S(1)}, u32[]{:S(2)}, u32[]{:S(2)}) %collective-permute-start.8) | collective-permute-done | bytes 393248 | tf_op jit(solution)/shard_map/ppermute | solution.py:350
  53.9 1.5 %partial_sums.5 = (f32[1024,128]{1,0:T(8,128)S(1)}, f32[1024,128]{1,0:T(8,128)S(1)}, s16[2080,128]{1,0:T(8,128)(2,1)S(1)}) custom-call(s32[1]{0:T(128)} %bitcast.6.flag_ref, bf16[768,512]{1,0:T(8,128)(2,1)S(1)} %build_weights.1.w_ref, bf16[192,1920]{1,0:T(8,128)(2,1)S(1)} %pad_maximum_fusion.refs_0_, bf16[192,1920]{1,0:T(8,128)(2,1)S(1)} %collective-permute-done.3.refs_1_, ...), custom_call_target="tpu_custom_call" | custom-call | flops 805306368 | bytes 2883584 | tf_op jit(solution)/shard_map/partial_sums/pallas_call | solution.py:170
  55.5 1.8 %collective-permute-start.9 = (s16[2080,128]{1,0:T(8,128)(2,1)S(1)}, s16[2080,128]{1,0:T(8,128)(2,1)S(1)}, u32[]{:S(2)}, u32[]{:S(2)}) collective-permute-start(s16[2080,128]{1,0:T(8,128)(2,1)S(1)} %get-tuple-element.24), channel_id=1, source_target_pairs={{0,2},{1,3},{2,0},{3,1},{4,6},{5,7},{6,4},{7,5},{8,10},{9,11},{10,... | collective-permute-start | bytes 1597448 | tf_op jit(solution)/shard_map/ppermute | solution.py:354
  57.3 1.6 %collective-permute-start.13 = (bf16[192,1024]{1,0:T(8,128)(2,1)S(1)}, bf16[192,1024]{1,0:T(8,128)(2,1)S(1)}, u32[]{:S(2)}, u32[]{:S(2)}) collective-permute-start(bf16[192,1024]{1,0:T(8,128)(2,1)S(1)} %slice.18), channel_id=1, source_target_pairs={{0,1},{1,0},{2,3},{3,2},{4,5},{5,4},{6,7},{7,6},{8,9},{9,8},{10,11... | collective-permute-start | bytes 1179656 | tf_op jit(solution)/shard_map/ppermute | solution.py:350
  58.9 3.8 %collective-permute-done.6.refs_0_ = s16[1824,128]{1,0:T(8,128)(2,1)S(1)} collective-permute-done((s16[1824,128]{1,0:T(8,128)(2,1)S(1)}, s16[1824,128]{1,0:T(8,128)(2,1)S(1)}, u32[]{:S(2)}, u32[]{:S(2)}) %collective-permute-start.6) | collective-permute-done | bytes 466976 | tf_op jit(solution)/shard_map/ppermute | solution.py:354
  62.9 2.1 %collective-permute-start.7 = (s16[912,128]{1,0:T(8,128)(2,1)S(1)}, s16[912,128]{1,0:T(8,128)(2,1)S(1)}, u32[]{:S(2)}, u32[]{:S(2)}) collective-permute-start(s16[912,128]{1,0:T(8,128)(2,1)S(1)} %combine.8), channel_id=1, source_target_pairs={{0,4},{1,5},{2,6},{3,7},{4,0},{5,1},{6,2},{7,3},{8,12},{9,13},{10,... | collective-permute-start | bytes 700424 | tf_op jit(solution)/shard_map/ppermute | solution.py:354
  65.0 8.9 %collective-permute-done.9.refs_0_ = s16[2080,128]{1,0:T(8,128)(2,1)S(1)} collective-permute-done((s16[2080,128]{1,0:T(8,128)(2,1)S(1)}, s16[2080,128]{1,0:T(8,128)(2,1)S(1)}, u32[]{:S(2)}, u32[]{:S(2)}) %collective-permute-start.9) | collective-permute-done | bytes 532512 | tf_op jit(solution)/shard_map/ppermute | solution.py:354
  74.1 1.6 %collective-permute-start.19 = (s16[1040,128]{1,0:T(8,128)(2,1)S(1)}, s16[1040,128]{1,0:T(8,128)(2,1)S(1)}, u32[]{:S(2)}, u32[]{:S(2)}) collective-permute-start(s16[1040,128]{1,0:T(8,128)(2,1)S(1)} %combine.9), channel_id=1, source_target_pairs={{0,4},{1,5},{2,6},{3,7},{4,0},{5,1},{6,2},{7,3},{8,12},{9,13},{10,... | collective-permute-start | bytes 798728 | tf_op jit(solution)/shard_map/ppermute | solution.py:354
  75.7 2.4 %collective-permute-done.13.refs_3_ = bf16[192,1024]{1,0:T(8,128)(2,1)S(1)} collective-permute-done((bf16[192,1024]{1,0:T(8,128)(2,1)S(1)}, bf16[192,1024]{1,0:T(8,128)(2,1)S(1)}, u32[]{:S(2)}, u32[]{:S(2)}) %collective-permute-start.13) | collective-permute-done | bytes 393248 | tf_op jit(solution)/shard_map/ppermute | solution.py:350
  78.1 1.5 %partial_sums.6 = (f32[1024,128]{1,0:T(8,128)S(1)}, f32[1024,128]{1,0:T(8,128)S(1)}, s16[2080,128]{1,0:T(8,128)(2,1)S(1)}) custom-call(s32[1]{0:T(128)} %bitcast.6.flag_ref, bf16[768,512]{1,0:T(8,128)(2,1)S(1)} %build_weights.1.w_ref, bf16[192,1920]{1,0:T(8,128)(2,1)S(1)} %pad_maximum_fusion.2.refs_0_, ...), custom_call_target="tpu_custom_call" | custom-call | flops 805306368 | bytes 2883584 | tf_op jit(solution)/shard_map/partial_sums/pallas_call | solution.py:170
  79.6 1.8 %collective-permute-start.14 = (s16[2080,128]{1,0:T(8,128)(2,1)S(1)}, s16[2080,128]{1,0:T(8,128)(2,1)S(1)}, u32[]{:S(2)}, u32[]{:S(2)}) collective-permute-start(s16[2080,128]{1,0:T(8,128)(2,1)S(1)} %get-tuple-element.30), channel_id=1, source_target_pairs={{0,2},{1,3},{2,0},{3,1},{4,6},{5,7},{6,4},{7,5},{8,10},{9,11},{10,... | collective-permute-start | bytes 1597448 | tf_op jit(solution)/shard_map/ppermute | solution.py:354
  81.5 6.3 %collective-permute-done.19.refs_1_ = s16[1040,128]{1,0:T(8,128)(2,1)S(1)} collective-permute-done((s16[1040,128]{1,0:T(8,128)(2,1)S(1)}, s16[1040,128]{1,0:T(8,128)(2,1)S(1)}, u32[]{:S(2)}, u32[]{:S(2)}) %collective-permute-start.19) | collective-permute-done | bytes 266272 | tf_op jit(solution)/shard_map/ppermute | solution.py:354
  87.8 1.3 partial_sums.7
  89.2 13.0 %collective-permute-done.14.refs_0_ = s16[2080,128]{1,0:T(8,128)(2,1)S(1)} collective-permute-done((s16[2080,128]{1,0:T(8,128)(2,1)S(1)}, s16[2080,128]{1,0:T(8,128)(2,1)S(1)}, u32[]{:S(2)}, u32[]{:S(2)}) %collective-permute-start.14) | collective-permute-done | bytes 532512 | tf_op jit(solution)/shard_map/ppermute | solution.py:354
  102.6 1.6 %collective-permute-start.30 = (s16[1040,128]{1,0:T(8,128)(2,1)S(1)}, s16[1040,128]{1,0:T(8,128)(2,1)S(1)}, u32[]{:S(2)}, u32[]{:S(2)}) collective-permute-start(s16[1040,128]{1,0:T(8,128)(2,1)S(1)} %combine.15.refs_4_), channel_id=1, source_target_pairs={{0,16},{1,17},{2,18},{3,19},{4,20},{5,21},{6,22},{7,23},{8,24},{9,... | collective-permute-start | bytes 798728 | tf_op jit(solution)/shard_map/ppermute | solution.py:350
  104.4 0.6 collective-permute-start.27
  105.0 3.9 %collective-permute-done.21.refs_0_ = s16[1824,128]{1,0:T(8,128)(2,1)S(1)} collective-permute-done((s16[1824,128]{1,0:T(8,128)(2,1)S(1)}, s16[1824,128]{1,0:T(8,128)(2,1)S(1)}, u32[]{:S(2)}, u32[]{:S(2)}) %collective-permute-start.21) | collective-permute-done | bytes 466976 | tf_op jit(solution)/shard_map/ppermute | solution.py:354
  109.1 4.7 %collective-permute-start.22 = (s16[912,128]{1,0:T(8,128)(2,1)S(1)}, s16[912,128]{1,0:T(8,128)(2,1)S(1)}, u32[]{:S(2)}, u32[]{:S(2)}) collective-permute-start(s16[912,128]{1,0:T(8,128)(2,1)S(1)} %combine.12), channel_id=1, source_target_pairs={{0,4},{1,5},{2,6},{3,7},{4,0},{5,1},{6,2},{7,3},{8,12},{9,13},{10,... | collective-permute-start | bytes 700424 | tf_op jit(solution)/shard_map/ppermute | solution.py:354
  113.8 0.5 collective-permute-start.29
  114.6 1.6 %collective-permute-start.17 = (s16[1040,128]{1,0:T(8,128)(2,1)S(1)}, s16[1040,128]{1,0:T(8,128)(2,1)S(1)}, u32[]{:S(2)}, u32[]{:S(2)}) collective-permute-start(s16[1040,128]{1,0:T(8,128)(2,1)S(1)} %combine.11.refs_0_), channel_id=1, source_target_pairs={{0,16},{1,17},{2,18},{3,19},{4,20},{5,21},{6,22},{7,23},{8,24},{9,... | collective-permute-start | bytes 798728 | tf_op jit(solution)/shard_map/ppermute | solution.py:350
  116.2 6.7 %collective-permute-done.22.refs_1_ = s16[912,128]{1,0:T(8,128)(2,1)S(1)} collective-permute-done((s16[912,128]{1,0:T(8,128)(2,1)S(1)}, s16[912,128]{1,0:T(8,128)(2,1)S(1)}, u32[]{:S(2)}, u32[]{:S(2)}) %collective-permute-start.22) | collective-permute-done | bytes 233504 | tf_op jit(solution)/shard_map/ppermute | solution.py:354
  123.1 1.6 %collective-permute-start.24 = (s16[912,128]{1,0:T(8,128)(2,1)S(1)}, s16[912,128]{1,0:T(8,128)(2,1)S(1)}, u32[]{:S(2)}, u32[]{:S(2)}) collective-permute-start(s16[912,128]{1,0:T(8,128)(2,1)S(1)} %combine.13.refs_4_), channel_id=1, source_target_pairs={{0,16},{1,17},{2,18},{3,19},{4,20},{5,21},{6,22},{7,23},{8,24},{9,... | collective-permute-start | bytes 700424 | tf_op jit(solution)/shard_map/ppermute | solution.py:350
  124.9 0.3 collective-permute-start.23
  125.2 0.3 collective-permute-start.16
  125.5 5.8 %collective-permute-done.24.refs_6_ = s16[912,128]{1,0:T(8,128)(2,1)S(1)} collective-permute-done((s16[912,128]{1,0:T(8,128)(2,1)S(1)}, s16[912,128]{1,0:T(8,128)(2,1)S(1)}, u32[]{:S(2)}, u32[]{:S(2)}) %collective-permute-start.24) | collective-permute-done | bytes 233504 | tf_op jit(solution)/shard_map/ppermute | solution.py:350
  131.3 0.5 collective-permute-start.18
  131.8 11.9 %covariance.1 = f32[13456,128]{1,0:T(8,128)} custom-call(s32[8]{0:T(128)S(1)} %stack.97.place_ref, s16[912,128]{1,0:T(8,128)(2,1)S(1)} %combine.14.refs_0_, s16[912,128]{1,0:T(8,128)(2,1)S(1)} %collective-permute-done.26.refs_1_, s16[912,128]{1,0:T(8,128)(2,1)S(1)} %collective-permute-done.27.refs_2_, s16[912,128]{1,0:T(8,128)(2,1)S(1)} %collective-permute-done.28.refs_3_, ...), custom_call_target="tpu_custom_call" | custom-call | flops 15432417280 | bytes 6889472 | tf_op jit(solution)/shard_map/covariance/pallas_call | solution.py:311
  143.7 3.8 %marginal.1 = f32[128,7424]{1,0:T(8,128)} custom-call(s32[8]{0:T(128)S(1)} %stack.83.place_ref, s16[1040,128]{1,0:T(8,128)(2,1)S(1)} %combine.11.refs_0_, s16[1040,128]{1,0:T(8,128)(2,1)S(1)} %collective-permute-done.16.refs_1_, s16[1040,128]{1,0:T(8,128)(2,1)S(1)} %collective-permute-done.17.refs_2_, s16[1040,128]{1,0:T(8,128)(2,1)S(1)} %collective-permute-done.18.refs_3_, ...), custom_call_target="tpu_custom_call" | custom-call | flops 3801088 | bytes 5701632 | tf_op jit(solution)/shard_map/marginal/pallas_call | solution.py:238
  (60 shorter events, 2.9 us)
Async XLA Ops:
  0.6 1.5 %copy-start.3 = (bf16[96,116]{1,0:T(8,128)(2,1)S(1)}, bf16[96,116]{1,0:T(8,128)(2,1)}, u32[]{:S(2)}) copy-start(bf16[96,116]{1,0:T(8,128)(2,1)} %param.7) | copy-start | bytes 66820
  2.1 1.5 %copy-start.1 = (s32[128,32]{0,1:T(8,128)S(1)}, s32[128,32]{0,1:T(8,128)}, u32[]{:S(2)}) copy-start(s32[128,32]{0,1:T(8,128)} %param.9) | copy-start | bytes 49156
  2.1 1.5 %copy-start.2 = (s32[128,32]{0,1:T(8,128)S(1)}, s32[128,32]{0,1:T(8,128)}, u32[]{:S(2)}) copy-start(s32[128,32]{0,1:T(8,128)} %param.8) | copy-start | bytes 49156
  3.2 10.5 %copy-start = (bf16[96,7424]{1,0:T(8,128)(2,1)S(1)}, bf16[96,7424]{1,0:T(8,128)(2,1)}, u32[]{:S(2)}) copy-start(bf16[96,7424]{1,0:T(8,128)(2,1)} %param.5) | copy-start | bytes 4276228
  3.2 10.5 %collective-permute-start.2 = (bf16[96,3840]{1,0:T(8,128)(2,1)}, bf16[96,3840]{1,0:T(8,128)(2,1)}, u32[]{:S(2)}, u32[]{:S(2)}) collective-permute-start(bf16[96,3840]{1,0:T(8,128)(2,1)} %get-tuple-element.51), channel_id=1, source_target_pairs={{0,8},{1,9},{2,10},{3,11},{4,12},{5,13},{6,14},{7,15},{8,0},{9,1},... | collective-permute-start | bytes 2211848 | tf_op jit(solution)/shard_map/ppermute | solution.py:350
  3.7 5.7 %collective-permute-start = (s32[64,128]{1,0:T(8,128)S(1)}, s32[64,128]{1,0:T(8,128)S(1)}, u32[]{:S(2)}, u32[]{:S(2)}) collective-permute-start(s32[64,128]{1,0:T(8,128)S(1)} %pad_add_fusion.2), channel_id=1, source_target_pairs={{0,4},{1,5},{2,6},{3,7},{4,0},{5,1},{6,2},{7,3},{8,12},{9,13},{10,... | collective-permute-start | bytes 98312 | tf_op jit(solution)/shard_map/ppermute | solution.py:354
  9.4 4.3 %collective-permute-start.1 = (s32[64,256]{1,0:T(8,128)S(1)}, s32[64,256]{1,0:T(8,128)S(1)}, u32[]{:S(2)}, u32[]{:S(2)}) collective-permute-start(s32[64,256]{1,0:T(8,128)S(1)} %pad_add_fusion.1), channel_id=1, source_target_pairs={{0,2},{1,3},{2,0},{3,1},{4,6},{5,7},{6,4},{7,5},{8,10},{9,11},{10,... | collective-permute-start | bytes 196616 | tf_op jit(solution)/shard_map/ppermute | solution.py:354
  13.7 5.0 %collective-permute-start.10 = (bf16[96,3712]{1,0:T(8,128)(2,1)S(1)}, bf16[96,3712]{1,0:T(8,128)(2,1)S(1)}, u32[]{:S(2)}, u32[]{:S(2)}) collective-permute-start(bf16[96,3712]{1,0:T(8,128)(2,1)S(1)} %constant_dynamic-slice_fusion.3), channel_id=1, source_target_pairs={{0,8},{1,9},{2,10},{3,11},{4,12},{5,13},{6,14},{7,15},{8,0},{9,1},... | collective-permute-start | bytes 2138120 | tf_op jit(solution)/shard_map/ppermute | solution.py:350
  15.0 19.3 %collective-permute-start.3 = (bf16[192,1920]{1,0:T(8,128)(2,1)S(1)}, bf16[192,1920]{1,0:T(8,128)(2,1)S(1)}, u32[]{:S(2)}, u32[]{:S(2)}) collective-permute-start(bf16[192,1920]{1,0:T(8,128)(2,1)S(1)} %pad_maximum_fusion.1), channel_id=1, source_target_pairs={{0,16},{1,17},{2,18},{3,19},{4,20},{5,21},{6,22},{7,23},{8,24},{9,... | collective-permute-start | bytes 2211848 | tf_op jit(solution)/shard_map/ppermute | solution.py:350
  16.8 30.4 %collective-permute-start.4 = (bf16[192,1920]{1,0:T(8,128)(2,1)S(1)}, bf16[192,1920]{1,0:T(8,128)(2,1)S(1)}, u32[]{:S(2)}, u32[]{:S(2)}) collective-permute-start(bf16[192,1920]{1,0:T(8,128)(2,1)S(1)} %pad_maximum_fusion.refs_0_), channel_id=1, source_target_pairs={{0,1},{1,0},{2,3},{3,2},{4,5},{5,4},{6,7},{7,6},{8,9},{9,8},{10,11... | collective-permute-start | bytes 2211848 | tf_op jit(solution)/shard_map/ppermute | solution.py:350
  18.9 38.4 %collective-permute-start.11 = (bf16[192,1920]{1,0:T(8,128)(2,1)S(1)}, bf16[192,1920]{1,0:T(8,128)(2,1)S(1)}, u32[]{:S(2)}, u32[]{:S(2)}) collective-permute-start(bf16[192,1920]{1,0:T(8,128)(2,1)S(1)} %pad_maximum_fusion.3), channel_id=1, source_target_pairs={{0,16},{1,17},{2,18},{3,19},{4,20},{5,21},{6,22},{7,23},{8,24},{9,... | collective-permute-start | bytes 2211848 | tf_op jit(solution)/shard_map/ppermute | solution.py:350
  34.4 11.1 %collective-permute-start.5 = (bf16[192,896]{1,0:T(8,128)(2,1)S(1)}, bf16[192,896]{1,0:T(8,128)(2,1)S(1)}, u32[]{:S(2)}, u32[]{:S(2)}) collective-permute-start(bf16[192,896]{1,0:T(8,128)(2,1)S(1)} %slice.16), channel_id=1, source_target_pairs={{0,1},{1,0},{2,3},{3,2},{4,5},{5,4},{6,7},{7,6},{8,9},{9,8},{10,11... | collective-permute-start | bytes 1032200 | tf_op jit(solution)/shard_map/ppermute | solution.py:350
  36.2 17.7 %collective-permute-start.8 = (bf16[192,1024]{1,0:T(8,128)(2,1)S(1)}, bf16[192,1024]{1,0:T(8,128)(2,1)S(1)}, u32[]{:S(2)}, u32[]{:S(2)}) collective-permute-start(bf16[192,1024]{1,0:T(8,128)(2,1)S(1)} %slice.17), channel_id=1, source_target_pairs={{0,1},{1,0},{2,3},{3,2},{4,5},{5,4},{6,7},{7,6},{8,9},{9,8},{10,11... | collective-permute-start | bytes 1179656 | tf_op jit(solution)/shard_map/ppermute | solution.py:350
  45.5 30.2 %collective-permute-start.12 = (bf16[192,1920]{1,0:T(8,128)(2,1)S(1)}, bf16[192,1920]{1,0:T(8,128)(2,1)S(1)}, u32[]{:S(2)}, u32[]{:S(2)}) collective-permute-start(bf16[192,1920]{1,0:T(8,128)(2,1)S(1)} %pad_maximum_fusion.2.refs_0_), channel_id=1, source_target_pairs={{0,1},{1,0},{2,3},{3,2},{4,5},{5,4},{6,7},{7,6},{8,9},{9,8},{10,11... | collective-permute-start | bytes 2211848 | tf_op jit(solution)/shard_map/ppermute | solution.py:350
  48.5 14.2 %collective-permute-start.6 = (s16[1824,128]{1,0:T(8,128)(2,1)S(1)}, s16[1824,128]{1,0:T(8,128)(2,1)S(1)}, u32[]{:S(2)}, u32[]{:S(2)}) collective-permute-start(s16[1824,128]{1,0:T(8,128)(2,1)S(1)} %get-tuple-element.22), channel_id=1, source_target_pairs={{0,2},{1,3},{2,0},{3,1},{4,6},{5,7},{6,4},{7,5},{8,10},{9,11},{10,... | collective-permute-start | bytes 1400840 | tf_op jit(solution)/shard_map/ppermute | solution.py:354
  55.5 18.5 %collective-permute-start.9 = (s16[2080,128]{1,0:T(8,128)(2,1)S(1)}, s16[2080,128]{1,0:T(8,128)(2,1)S(1)}, u32[]{:S(2)}, u32[]{:S(2)}) collective-permute-start(s16[2080,128]{1,0:T(8,128)(2,1)S(1)} %get-tuple-element.24), channel_id=1, source_target_pairs={{0,2},{1,3},{2,0},{3,1},{4,6},{5,7},{6,4},{7,5},{8,10},{9,11},{10,... | collective-permute-start | bytes 1597448 | tf_op jit(solution)/shard_map/ppermute | solution.py:354
  57.3 20.8 %collective-permute-start.13 = (bf16[192,1024]{1,0:T(8,128)(2,1)S(1)}, bf16[192,1024]{1,0:T(8,128)(2,1)S(1)}, u32[]{:S(2)}, u32[]{:S(2)}) collective-permute-start(bf16[192,1024]{1,0:T(8,128)(2,1)S(1)} %slice.18), channel_id=1, source_target_pairs={{0,1},{1,0},{2,3},{3,2},{4,5},{5,4},{6,7},{7,6},{8,9},{9,8},{10,11... | collective-permute-start | bytes 1179656 | tf_op jit(solution)/shard_map/ppermute | solution.py:350
  62.9 12.8 %collective-permute-start.7 = (s16[912,128]{1,0:T(8,128)(2,1)S(1)}, s16[912,128]{1,0:T(8,128)(2,1)S(1)}, u32[]{:S(2)}, u32[]{:S(2)}) collective-permute-start(s16[912,128]{1,0:T(8,128)(2,1)S(1)} %combine.8), channel_id=1, source_target_pairs={{0,4},{1,5},{2,6},{3,7},{4,0},{5,1},{6,2},{7,3},{8,12},{9,13},{10,... | collective-permute-start | bytes 700424 | tf_op jit(solution)/shard_map/ppermute | solution.py:354
  65.0 22.8 %collective-permute-start.20 = (bf16[192,896]{1,0:T(8,128)(2,1)S(1)}, bf16[192,896]{1,0:T(8,128)(2,1)S(1)}, u32[]{:S(2)}, u32[]{:S(2)}) collective-permute-start(bf16[192,896]{1,0:T(8,128)(2,1)S(1)} %slice.19), channel_id=1, source_target_pairs={{0,1},{1,0},{2,3},{3,2},{4,5},{5,4},{6,7},{7,6},{8,9},{9,8},{10,11... | collective-permute-start | bytes 1032200 | tf_op jit(solution)/shard_map/ppermute | solution.py:350
  74.1 13.7 %collective-permute-start.19 = (s16[1040,128]{1,0:T(8,128)(2,1)S(1)}, s16[1040,128]{1,0:T(8,128)(2,1)S(1)}, u32[]{:S(2)}, u32[]{:S(2)}) collective-permute-start(s16[1040,128]{1,0:T(8,128)(2,1)S(1)} %combine.9), channel_id=1, source_target_pairs={{0,4},{1,5},{2,6},{3,7},{4,0},{5,1},{6,2},{7,3},{8,12},{9,13},{10,... | collective-permute-start | bytes 798728 | tf_op jit(solution)/shard_map/ppermute | solution.py:354
  79.6 22.5 %collective-permute-start.14 = (s16[2080,128]{1,0:T(8,128)(2,1)S(1)}, s16[2080,128]{1,0:T(8,128)(2,1)S(1)}, u32[]{:S(2)}, u32[]{:S(2)}) collective-permute-start(s16[2080,128]{1,0:T(8,128)(2,1)S(1)} %get-tuple-element.30), channel_id=1, source_target_pairs={{0,2},{1,3},{2,0},{3,1},{4,6},{5,7},{6,4},{7,5},{8,10},{9,11},{10,... | collective-permute-start | bytes 1597448 | tf_op jit(solution)/shard_map/ppermute | solution.py:354
  89.1 19.9 %collective-permute-start.21 = (s16[1824,128]{1,0:T(8,128)(2,1)S(1)}, s16[1824,128]{1,0:T(8,128)(2,1)S(1)}, u32[]{:S(2)}, u32[]{:S(2)}) collective-permute-start(s16[1824,128]{1,0:T(8,128)(2,1)S(1)} %get-tuple-element.35), channel_id=1, source_target_pairs={{0,2},{1,3},{2,0},{3,1},{4,6},{5,7},{6,4},{7,5},{8,10},{9,11},{10,... | collective-permute-start | bytes 1400840 | tf_op jit(solution)/shard_map/ppermute | solution.py:354
  102.3 11.6 %collective-permute-start.15 = (s16[1040,128]{1,0:T(8,128)(2,1)S(1)}, s16[1040,128]{1,0:T(8,128)(2,1)S(1)}, u32[]{:S(2)}, u32[]{:S(2)}) collective-permute-start(s16[1040,128]{1,0:T(8,128)(2,1)S(1)} %combine.10), channel_id=1, source_target_pairs={{0,4},{1,5},{2,6},{3,7},{4,0},{5,1},{6,2},{7,3},{8,12},{9,13},{10,... | collective-permute-start | bytes 798728 | tf_op jit(solution)/shard_map/ppermute | solution.py:354
  102.6 13.6 %collective-permute-start.30 = (s16[1040,128]{1,0:T(8,128)(2,1)S(1)}, s16[1040,128]{1,0:T(8,128)(2,1)S(1)}, u32[]{:S(2)}, u32[]{:S(2)}) collective-permute-start(s16[1040,128]{1,0:T(8,128)(2,1)S(1)} %combine.15.refs_4_), channel_id=1, source_target_pairs={{0,16},{1,17},{2,18},{3,19},{4,20},{5,21},{6,22},{7,23},{8,24},{9,... | collective-permute-start | bytes 798728 | tf_op jit(solution)/shard_map/ppermute | solution.py:350
  104.4 10.2 %collective-permute-start.27 = (s16[912,128]{1,0:T(8,128)(2,1)S(1)}, s16[912,128]{1,0:T(8,128)(2,1)S(1)}, u32[]{:S(2)}, u32[]{:S(2)}) collective-permute-start(s16[912,128]{1,0:T(8,128)(2,1)S(1)} %combine.14.refs_0_), channel_id=1, source_target_pairs={{0,16},{1,17},{2,18},{3,19},{4,20},{5,21},{6,22},{7,23},{8,24},{9,... | collective-permute-start | bytes 700424 | tf_op jit(solution)/shard_map/ppermute | solution.py:350
  109.1 13.8 %collective-permute-start.22 = (s16[912,128]{1,0:T(8,128)(2,1)S(1)}, s16[912,128]{1,0:T(8,128)(2,1)S(1)}, u32[]{:S(2)}, u32[]{:S(2)}) collective-permute-start(s16[912,128]{1,0:T(8,128)(2,1)S(1)} %combine.12), channel_id=1, source_target_pairs={{0,4},{1,5},{2,6},{3,7},{4,0},{5,1},{6,2},{7,3},{8,12},{9,13},{10,... | collective-permute-start | bytes 700424 | tf_op jit(solution)/shard_map/ppermute | solution.py:354
  113.8 9.3 %collective-permute-start.26 = (s16[912,128]{1,0:T(8,128)(2,1)S(1)}, s16[912,128]{1,0:T(8,128)(2,1)S(1)}, u32[]{:S(2)}, u32[]{:S(2)}) collective-permute-start(s16[912,128]{1,0:T(8,128)(2,1)S(1)} %combine.14.refs_0_), channel_id=1, source_target_pairs={{0,8},{1,9},{2,10},{3,11},{4,12},{5,13},{6,14},{7,15},{8,0},{9,1},... | collective-permute-start | bytes 700424 | tf_op jit(solution)/shard_map/ppermute | solution.py:350
  113.8 11.0 %collective-permute-start.29 = (s16[1040,128]{1,0:T(8,128)(2,1)S(1)}, s16[1040,128]{1,0:T(8,128)(2,1)S(1)}, u32[]{:S(2)}, u32[]{:S(2)}) collective-permute-start(s16[1040,128]{1,0:T(8,128)(2,1)S(1)} %combine.15.refs_4_), channel_id=1, source_target_pairs={{0,8},{1,9},{2,10},{3,11},{4,12},{5,13},{6,14},{7,15},{8,0},{9,1},... | collective-permute-start | bytes 798728 | tf_op jit(solution)/shard_map/ppermute | solution.py:350
  114.6 16.7 %collective-permute-start.17 = (s16[1040,128]{1,0:T(8,128)(2,1)S(1)}, s16[1040,128]{1,0:T(8,128)(2,1)S(1)}, u32[]{:S(2)}, u32[]{:S(2)}) collective-permute-start(s16[1040,128]{1,0:T(8,128)(2,1)S(1)} %combine.11.refs_0_), channel_id=1, source_target_pairs={{0,16},{1,17},{2,18},{3,19},{4,20},{5,21},{6,22},{7,23},{8,24},{9,... | collective-permute-start | bytes 798728 | tf_op jit(solution)/shard_map/ppermute | solution.py:350
  116.2 15.6 %collective-permute-start.31 = (s16[1040,128]{1,0:T(8,128)(2,1)S(1)}, s16[1040,128]{1,0:T(8,128)(2,1)S(1)}, u32[]{:S(2)}, u32[]{:S(2)}) collective-permute-start(s16[1040,128]{1,0:T(8,128)(2,1)S(1)} %collective-permute-done.30.refs_6_), channel_id=1, source_target_pairs={{0,8},{1,9},{2,10},{3,11},{4,12},{5,13},{6,14},{7,15},{8,0},{9,1},... | collective-permute-start | bytes 798728 | tf_op jit(solution)/shard_map/ppermute | solution.py:350
  122.9 2.3 %collective-permute-start.28 = (s16[912,128]{1,0:T(8,128)(2,1)S(1)}, s16[912,128]{1,0:T(8,128)(2,1)S(1)}, u32[]{:S(2)}, u32[]{:S(2)}) collective-permute-start(s16[912,128]{1,0:T(8,128)(2,1)S(1)} %collective-permute-done.27.refs_2_), channel_id=1, source_target_pairs={{0,8},{1,9},{2,10},{3,11},{4,12},{5,13},{6,14},{7,15},{8,0},{9,1},... | collective-permute-start | bytes 700424 | tf_op jit(solution)/shard_map/ppermute | solution.py:350
  123.1 8.2 %collective-permute-start.24 = (s16[912,128]{1,0:T(8,128)(2,1)S(1)}, s16[912,128]{1,0:T(8,128)(2,1)S(1)}, u32[]{:S(2)}, u32[]{:S(2)}) collective-permute-start(s16[912,128]{1,0:T(8,128)(2,1)S(1)} %combine.13.refs_4_), channel_id=1, source_target_pairs={{0,16},{1,17},{2,18},{3,19},{4,20},{5,21},{6,22},{7,23},{8,24},{9,... | collective-permute-start | bytes 700424 | tf_op jit(solution)/shard_map/ppermute | solution.py:350
  124.9 18.8 %collective-permute-start.23 = (s16[912,128]{1,0:T(8,128)(2,1)S(1)}, s16[912,128]{1,0:T(8,128)(2,1)S(1)}, u32[]{:S(2)}, u32[]{:S(2)}) collective-permute-start(s16[912,128]{1,0:T(8,128)(2,1)S(1)} %combine.13.refs_4_), channel_id=1, source_target_pairs={{0,8},{1,9},{2,10},{3,11},{4,12},{5,13},{6,14},{7,15},{8,0},{9,1},... | collective-permute-start | bytes 700424 | tf_op jit(solution)/shard_map/ppermute | solution.py:350
  125.2 18.5 %collective-permute-start.16 = (s16[1040,128]{1,0:T(8,128)(2,1)S(1)}, s16[1040,128]{1,0:T(8,128)(2,1)S(1)}, u32[]{:S(2)}, u32[]{:S(2)}) collective-permute-start(s16[1040,128]{1,0:T(8,128)(2,1)S(1)} %combine.11.refs_0_), channel_id=1, source_target_pairs={{0,8},{1,9},{2,10},{3,11},{4,12},{5,13},{6,14},{7,15},{8,0},{9,1},... | collective-permute-start | bytes 798728 | tf_op jit(solution)/shard_map/ppermute | solution.py:350
  131.3 12.4 %collective-permute-start.25 = (s16[912,128]{1,0:T(8,128)(2,1)S(1)}, s16[912,128]{1,0:T(8,128)(2,1)S(1)}, u32[]{:S(2)}, u32[]{:S(2)}) collective-permute-start(s16[912,128]{1,0:T(8,128)(2,1)S(1)} %collective-permute-done.24.refs_6_), channel_id=1, source_target_pairs={{0,8},{1,9},{2,10},{3,11},{4,12},{5,13},{6,14},{7,15},{8,0},{9,1},... | collective-permute-start | bytes 700424 | tf_op jit(solution)/shard_map/ppermute | solution.py:350
  131.3 12.4 %collective-permute-start.18 = (s16[1040,128]{1,0:T(8,128)(2,1)S(1)}, s16[1040,128]{1,0:T(8,128)(2,1)S(1)}, u32[]{:S(2)}, u32[]{:S(2)}) collective-permute-start(s16[1040,128]{1,0:T(8,128)(2,1)S(1)} %collective-permute-done.17.refs_2_), channel_id=1, source_target_pairs={{0,8},{1,9},{2,10},{3,11},{4,12},{5,13},{6,14},{7,15},{8,0},{9,1},... | collective-permute-start | bytes 798728 | tf_op jit(solution)/shard_map/ppermute | solution.py:350

commit v8 on v7

--- a/solution.py
+++ b/solution.py
@@ -9,7 +9,7 @@
 LANES = 128
 CORES = 2
 DEPTH = 4
-LOAD_FIRST = 7
+LOAD_FIRST = 8
 MEAN_FIRST = 8
 SCALES = 16
 TOP = 32767.0
@@ -375,14 +375,16 @@
         def part(group):
             return jnp.concatenate([lax.dynamic_slice(b, (0, start_of(group, tiles) * LANES), size) for b in both], axis=0)
 
-        return [move(part((x + dx) % xs), dx, 0) for dx in range(xs)]
+        cut = [part((x + dx) % xs) for dx in range(xs)]
+        return [move(value, dx, 0) for dx, value in enumerate(cut)], cut[-1]
+
+    load_both = exchange(factors, last_tile)
+    load_x, load_cut = along_x(load_both)
 
     queries = jnp.concatenate([intersection_tracts.T, intersection_weights.T], axis=0)
+    queries = after(queries, load_cut)
     queries = jnp.concatenate([queries, z_swap(queries, 2)], axis=1)
     queries = jnp.concatenate([queries, z_swap(queries, 1)], axis=1)
-    load_both = exchange(factors, last_tile)
-    load_x = along_x(load_both)
-
     bases = jnp.stack([
         (((x - dx) % xs * CORES + (core - dc) % CORES) * parts + z * ys + (y - dy) % ys) * rows
         for dy in range(ys) for dx in range(xs) for dc in range(CORES)
@@ -399,10 +401,10 @@
     def merge(by_x):
         return [by_y[dy] for dy in range(ys) for by_y in by_x]
 
-    def along_z(data, count, has_var, *before):
+    def along_z(data, count, has_var, before=(), before_middle=()):
         own, opposite, sent = partial_sums(flag, after(w, *before), data, count, has_var)
         near = z_swap(sent, 1)
-        middle = combine(opposite, (near, 1))
+        middle = combine(after(opposite, *before_middle), (near, 1))
         return own, near, middle, z_swap(middle, 2)
 
     def spread(own, near, far):
@@ -424,24 +426,24 @@
     load_tiles = split(each_of(load_width), LOAD_FIRST)
     mean_tiles = split(each_of(mean_width), MEAN_FIRST)
     (first_a, first_b), (first_c, first_d) = load_tiles, mean_tiles
-    mean_x = along_x(exchange(after(estimates, load_both[1])))
+    mean_x, _ = along_x(exchange(after(estimates, load_both[1])))
     load_y = along_y(load_x[0], 0, first_a + first_b)
-    data_a = merge([load_y] + [along_y(value, 0, first_a) for value in load_x[1:]])
+    data_a = merge([load_y] + [along_y(value, 0, first_a, w) for value in load_x[1:]])
     data_b = merge([later(load_y, first_a)] + [along_y(value, first_a, first_b) for value in load_x[1:]])
     own_a, near_a, middle_a, far_a = along_z(data_a, first_a, False)
     mean_y = along_y(mean_x[0], 0, first_c + first_d, data_a[-1][0])
     there = data_b[-1][0]
-    own_b, near_b, middle_b, far_b = along_z(data_b, first_b, True)
+    own_b, near_b, middle_b, far_b = along_z(data_b, first_b, True, (own_a,), (middle_a,))
     data_c = merge([mean_y] + [along_y(value, 0, first_c, there) for value in mean_x[1:]])
     data_d = merge([later(mean_y, first_c)] + [along_y(value, first_c, first_d, there) for value in mean_x[1:]])
-    own_c, near_c, middle_c, far_c = along_z(data_c, first_c, False, far_a, middle_b)
-    own_d, near_d, middle_d, far_d = along_z(data_d, first_d, False, own_c, far_b)
-    _, load_a = spread(own_a, near_a, far_a)
-    _, load_b = spread(own_b, near_b, far_b)
-    mine_c, mean_c = spread(own_c, near_c, far_c)
-    mine_d, mean_d = spread(own_d, near_d, far_d)
-    load_pieces = load_a + [after(load_b[0], mine_c, mine_d)] + load_b[1:]
+    own_c, near_c, middle_c, far_c = along_z(data_c, first_c, False, (middle_b,))
+    mine_a, load_a = spread(own_a, near_a, far_a)
+    mine_b, load_b = spread(own_b, near_b, far_b)
+    own_d, near_d, middle_d, far_d = along_z(data_d, first_d, False, (own_c, far_b), (load_a[-1], load_b[-1]))
+    load_pieces = load_a + [after(load_b[0], middle_d)] + load_b[1:]
     cov = covariance(places(load_width), load_pieces, load_tiles, load_width * CORES, ages, rank)
+    mine_c, mean_c = spread(after(own_c, cov), near_c, far_c)
+    mine_d, mean_d = spread(after(own_d, cov), near_d, far_d)
     mean_pieces = mean_c + mean_d
     mean = marginal(places(mean_width), mean_pieces, mean_tiles, mean_width * CORES)
     return mean, cov.T

time: 148 us -> 140 us (0.946)
  waiting for transfers between devices: 77.8 us -> 61.9 us
  Pallas kernels: 27.8 us -> 35.6 us
  starting transfers between devices: 36.1 us -> 30.2 us
  local copies, waits for them, and re-layouts: 3.47 us -> 8.22 us
  other arithmetic: 1.29 us -> 3.02 us
    ppermute x10, waiting for transfers between devices: 46.8 us -> 32.5 us  [z_swap(): return lax.ppermute(value, 'dist', perm)]
    ppermute x10, starting transfers between devices: 19.2 us -> 12 us  [z_swap(): return lax.ppermute(value, 'dist', perm)]
    pallas_call x4, Pallas kernels: 5.57 us -> 11.4 us  [partial_sums(): pl.pallas_call(functools.partial(sums_kernel, offsets, has_var), grid_spe...]
    unnamed x8 -> x26, local copies, waits for them, and re-layouts: 0.02 us -> 5.09 us
    concatenate x4, other arithmetic: 0.23 us -> 1.95 us  [part(): jnp.concatenate([lax.dynamic_slice(b, (0, start_of(group, tiles) * LANES)...]
    ppermute x22, waiting for transfers between devices: 30.9 us -> 29.4 us  [move(): return lax.ppermute(value, ('geo', 'dist'), perm)]
  transfers between devices with their start and end apart: 32 -> 32, of which waited for: 13 -> 17; matrix products, arithmetic and copies ran while one was open for 1% -> 3% of each run, Pallas kernels for 16% -> 23%
where the time goes in v8:
time: 140 us
  waiting for transfers between devices  61.9 us (44%)
  Pallas kernels  35.6 us (25%)
  starting transfers between devices  30.2 us (22%)
  local copies, waits for them, and re-layouts  8.22 us (6%)
  other arithmetic  3.02 us (2%)
    ppermute x10, waiting for transfers between devices, z_swap(): return lax.ppermute(value, 'dist', perm)  32.5 us
    ppermute x22, waiting for transfers between devices, move(): return lax.ppermute(value, ('geo', 'dist'), perm)  29.4 us
    ppermute x22, starting transfers between devices, move(): return lax.ppermute(value, ('geo', 'dist'), perm)  18.2 us
    pallas_call x1, Pallas kernels, covariance(): pl.pallas_call(functools.partial(covariance_kernel, tiles, total, ages, r...  13.1 us
    ppermute x10, starting transfers between devices, z_swap(): return lax.ppermute(value, 'dist', perm)  12 us
    pallas_call x4, Pallas kernels, partial_sums(): pl.pallas_call(functools.partial(sums_kernel, offsets, has_var), grid_spe...  11.4 us
    unnamed x26, local copies, waits for them, and re-layouts  5.09 us
    pallas_call x1, Pallas kernels, build_weights(): pl.pallas_call(functools.partial(weights_kernel, rows), grid_spec=pltpu.P...  4.83 us
  transfers between devices with their start and end apart: 32, of which 17 were waited for; matrix products, arithmetic and copies ran while one was open for 3% of the time, Pallas kernels for 23%

profile of v8, /device:TPU:0, one launch (start us, length us, event | category | flops | bytes accessed | tf_op | source)
XLA Modules:
  0.0 139.9 jit_solution(16395542962940135513)
XLA Ops:
  0.7 1.4 %constant_dynamic-slice_fusion.10 = (bf16[96,3712]{1,0:T(8,128)(2,1)S(1)}, bf16[96,3712]{1,0:T(8,128)(2,1)S(1)}) fusion(bf16[96,7424]{1,0:T(8,128)(2,1)} %param.6, s32[]{:T(128)S(6)} %select_n.166, s32[]{:T(128)S(6)} %select_n.170), kind=kLoop, calls=%fused_computation.21 | loop fusion | bytes 2850824 | tf_op jit(solution)/shard_map/dynamic_slice | solution.py:360
  2.1 1.0 fusion.1
  3.8 1.8 %collective-permute-done = bf16[96,3840]{1,0:T(8,128)(2,1)S(1)} collective-permute-done((bf16[96,3840]{1,0:T(8,128)(2,1)}, bf16[96,3840]{1,0:T(8,128)(2,1)S(1)}, u32[]{:S(2)}, u32[]{:S(2)}) %collective-permute-start) | collective-permute-done | bytes 737312 | tf_op jit(solution)/shard_map/ppermute | solution.py:350
  6.4 2.7 %collective-permute-start.3 = (bf16[192,1920]{1,0:T(8,128)(2,1)S(1)}, bf16[192,1920]{1,0:T(8,128)(2,1)S(1)}, u32[]{:S(2)}, u32[]{:S(2)}) collective-permute-start(bf16[192,1920]{1,0:T(8,128)(2,1)S(1)} %pad_maximum_fusion), channel_id=1, source_target_pairs={{0,16},{1,17},{2,18},{3,19},{4,20},{5,21},{6,22},{7,23},{8,24},{9,... | collective-permute-start | bytes 2211848 | tf_op jit(solution)/shard_map/ppermute | solution.py:350
  9.0 2.6 %collective-permute-start.1 = (s32[64,128]{1,0:T(8,128)S(1)}, s32[64,128]{1,0:T(8,128)S(1)}, u32[]{:S(2)}, u32[]{:S(2)}) collective-permute-start(s32[64,128]{1,0:T(8,128)S(1)} %pad_add_fusion.2), channel_id=1, source_target_pairs={{0,4},{1,5},{2,6},{3,7},{4,0},{5,1},{6,2},{7,3},{8,12},{9,13},{10,... | collective-permute-start | bytes 98312 | tf_op jit(solution)/shard_map/ppermute | solution.py:354
  11.6 0.9 pad_maximum_fusion.1.refs_0_
  12.5 1.5 %collective-permute-start.4 = (bf16[192,1920]{1,0:T(8,128)(2,1)}, bf16[192,1920]{1,0:T(8,128)(2,1)}, u32[]{:S(2)}, u32[]{:S(2)}) collective-permute-start(bf16[192,1920]{1,0:T(8,128)(2,1)} %pad_maximum_fusion.1.refs_0_), channel_id=1, source_target_pairs={{0,1},{1,0},{2,3},{3,2},{4,5},{5,4},{6,7},{7,6},{8,9},{9,8},{10,11... | collective-permute-start | bytes 2211848 | tf_op jit(solution)/shard_map/ppermute | solution.py:350
  14.2 1.5 %collective-permute-start.2 = (s32[64,256]{1,0:T(8,128)S(1)}, s32[64,256]{1,0:T(8,128)S(1)}, u32[]{:S(2)}, u32[]{:S(2)}) collective-permute-start(s32[64,256]{1,0:T(8,128)S(1)} %pad_add_fusion.1), channel_id=1, source_target_pairs={{0,2},{1,3},{2,0},{3,1},{4,6},{5,7},{6,4},{7,5},{8,10},{9,11},{10,... | collective-permute-start | bytes 196616 | tf_op jit(solution)/shard_map/ppermute | solution.py:354
  16.0 2.5 %collective-permute-done.2 = s32[64,256]{1,0:T(8,128)S(1)} collective-permute-done((s32[64,256]{1,0:T(8,128)S(1)}, s32[64,256]{1,0:T(8,128)S(1)}, u32[]{:S(2)}, u32[]{:S(2)}) %collective-permute-start.2) | collective-permute-done | bytes 65568 | tf_op jit(solution)/shard_map/ppermute | solution.py:354
  18.5 4.8 %build_weights.1.w_ref = bf16[768,512]{1,0:T(8,128)(2,1)S(1)} custom-call(s32[8]{0:T(128)S(1)} %stack.92.base_ref, s32[64,512]{1,0:T(8,128)S(1)} %pad_add_fusion.query_ref), custom_call_target="tpu_custom_call" | custom-call | flops 5033164800 | bytes 786432 | tf_op jit(solution)/shard_map/build_weights/pallas_call | solution.py:93
  23.4 0.9 pad_maximum_fusion.3
  24.9 1.3 collective-permute-done.3.refs_1_
  26.2 2.3 %collective-permute-start.5 = (bf16[192,1024]{1,0:T(8,128)(2,1)S(1)}, bf16[192,1024]{1,0:T(8,128)(2,1)S(1)}, u32[]{:S(2)}, u32[]{:S(2)}) collective-permute-start(bf16[192,1024]{1,0:T(8,128)(2,1)S(1)} %slice.16), channel_id=1, source_target_pairs={{0,1},{1,0},{2,3},{3,2},{4,5},{5,4},{6,7},{7,6},{8,9},{9,8},{10,11... | collective-permute-start | bytes 1179656 | tf_op jit(solution)/shard_map/ppermute | solution.py:350
  28.5 0.8 slice.17
  29.3 11.2 %collective-permute-done.5.refs_3_ = bf16[192,1024]{1,0:T(8,128)(2,1)S(1)} collective-permute-done((bf16[192,1024]{1,0:T(8,128)(2,1)S(1)}, bf16[192,1024]{1,0:T(8,128)(2,1)S(1)}, u32[]{:S(2)}, u32[]{:S(2)}) %collective-permute-start.5) | collective-permute-done | bytes 393248 | tf_op jit(solution)/shard_map/ppermute | solution.py:350
  40.6 1.5 %collective-permute-start.11 = (bf16[192,1920]{1,0:T(8,128)(2,1)S(1)}, bf16[192,1920]{1,0:T(8,128)(2,1)}, u32[]{:S(2)}, u32[]{:S(2)}) collective-permute-start(bf16[192,1920]{1,0:T(8,128)(2,1)S(1)} %pad_maximum_fusion.2.refs_0_), channel_id=1, source_target_pairs={{0,1},{1,0},{2,3},{3,2},{4,5},{5,4},{6,7},{7,6},{8,9},{9,8},{10,11... | collective-permute-start | bytes 2211848 | tf_op jit(solution)/shard_map/ppermute | solution.py:350
  42.1 2.8 %partial_sums.4 = (f32[1024,128]{1,0:T(8,128)S(1)}, f32[1024,128]{1,0:T(8,128)S(1)}, s16[2080,128]{1,0:T(8,128)(2,1)S(1)}) custom-call(s32[1]{0:T(128)} %bitcast.6.flag_ref, bf16[768,512]{1,0:T(8,128)(2,1)S(1)} %build_weights.1.w_ref, bf16[192,1920]{1,0:T(8,128)(2,1)} %pad_maximum_fusion.1.refs_0_, bf16[192,1920]{1,0:T(8,128)(2,1)S(1)} %collective-permute-done.3.refs_1_, ...), custom_call_target="tpu_custom_call" | custom-call | flops 805306368 | bytes 2883584 | tf_op jit(solution)/shard_map/partial_sums/pallas_call | solution.py:170
  44.9 1.6 %collective-permute-start.7 = (s16[2080,128]{1,0:T(8,128)(2,1)S(1)}, s16[2080,128]{1,0:T(8,128)(2,1)S(1)}, u32[]{:S(2)}, u32[]{:S(2)}) collective-permute-start(s16[2080,128]{1,0:T(8,128)(2,1)S(1)} %get-tuple-element.34), channel_id=1, source_target_pairs={{0,2},{1,3},{2,0},{3,1},{4,6},{5,7},{6,4},{7,5},{8,10},{9,11},{10,... | collective-permute-start | bytes 1597448 | tf_op jit(solution)/shard_map/ppermute | solution.py:354
  46.5 1.5 %collective-permute-done.6.refs_3_ = bf16[192,896]{1,0:T(8,128)(2,1)} collective-permute-done((bf16[192,896]{1,0:T(8,128)(2,1)}, bf16[192,896]{1,0:T(8,128)(2,1)}, u32[]{:S(2)}, u32[]{:S(2)}) %collective-permute-start.6) | collective-permute-done | bytes 344096 | tf_op jit(solution)/shard_map/ppermute | solution.py:350
  48.0 2.8 %partial_sums.5 = (f32[896,128]{1,0:T(8,128)S(1)}, f32[896,128]{1,0:T(8,128)S(1)}, s16[1824,128]{1,0:T(8,128)(2,1)S(1)}) custom-call(s32[1]{0:T(128)} %bitcast.6.flag_ref, bf16[768,512]{1,0:T(8,128)(2,1)S(1)} %build_weights.1.w_ref, bf16[192,1920]{1,0:T(8,128)(2,1)} %pad_maximum_fusion.1.refs_0_, bf16[192,1920]{1,0:T(8,128)(2,1)S(1)} %collective-permute-done.3.refs_1_, ...), custom_call_target="tpu_custom_call" | custom-call | flops 704643072 | bytes 2523136 | tf_op jit(solution)/shard_map/partial_sums/pallas_call | solution.py:170
  50.8 1.6 %collective-permute-start.8 = (s16[1824,128]{1,0:T(8,128)(2,1)S(1)}, s16[1824,128]{1,0:T(8,128)(2,1)S(1)}, u32[]{:S(2)}, u32[]{:S(2)}) collective-permute-start(s16[1824,128]{1,0:T(8,128)(2,1)S(1)} %get-tuple-element.36), channel_id=1, source_target_pairs={{0,2},{1,3},{2,0},{3,1},{4,6},{5,7},{6,4},{7,5},{8,10},{9,11},{10,... | collective-permute-start | bytes 1400840 | tf_op jit(solution)/shard_map/ppermute | solution.py:354
  52.5 1.6 %collective-permute-start.12 = (bf16[192,1024]{1,0:T(8,128)(2,1)S(1)}, bf16[192,1024]{1,0:T(8,128)(2,1)S(1)}, u32[]{:S(2)}, u32[]{:S(2)}) collective-permute-start(bf16[192,1024]{1,0:T(8,128)(2,1)S(1)} %slice.18), channel_id=1, source_target_pairs={{0,1},{1,0},{2,3},{3,2},{4,5},{5,4},{6,7},{7,6},{8,9},{9,8},{10,11... | collective-permute-start | bytes 1179656 | tf_op jit(solution)/shard_map/ppermute | solution.py:350
  54.7 5.3 %collective-permute-done.7.refs_0_ = s16[2080,128]{1,0:T(8,128)(2,1)S(1)} collective-permute-done((s16[2080,128]{1,0:T(8,128)(2,1)S(1)}, s16[2080,128]{1,0:T(8,128)(2,1)S(1)}, u32[]{:S(2)}, u32[]{:S(2)}) %collective-permute-start.7) | collective-permute-done | bytes 532512 | tf_op jit(solution)/shard_map/ppermute | solution.py:354
  60.2 7.1 %collective-permute-done.8.refs_0_ = s16[1824,128]{1,0:T(8,128)(2,1)S(1)} collective-permute-done((s16[1824,128]{1,0:T(8,128)(2,1)S(1)}, s16[1824,128]{1,0:T(8,128)(2,1)S(1)}, u32[]{:S(2)}, u32[]{:S(2)}) %collective-permute-start.8) | collective-permute-done | bytes 466976 | tf_op jit(solution)/shard_map/ppermute | solution.py:354
  67.5 2.9 %collective-permute-start.13 = (s16[1040,128]{1,0:T(8,128)(2,1)S(1)}, s16[1040,128]{1,0:T(8,128)(2,1)S(1)}, u32[]{:S(2)}, u32[]{:S(2)}) collective-permute-start(s16[1040,128]{1,0:T(8,128)(2,1)S(1)} %combine.8), channel_id=1, source_target_pairs={{0,4},{1,5},{2,6},{3,7},{4,0},{5,1},{6,2},{7,3},{8,12},{9,13},{10,... | collective-permute-start | bytes 798728 | tf_op jit(solution)/shard_map/ppermute | solution.py:354
  70.5 1.7 %collective-permute-done.12.refs_3_ = bf16[192,1024]{1,0:T(8,128)(2,1)S(1)} collective-permute-done((bf16[192,1024]{1,0:T(8,128)(2,1)S(1)}, bf16[192,1024]{1,0:T(8,128)(2,1)S(1)}, u32[]{:S(2)}, u32[]{:S(2)}) %collective-permute-start.12) | collective-permute-done | bytes 393248 | tf_op jit(solution)/shard_map/ppermute | solution.py:350
  72.2 2.6 %partial_sums.6 = (f32[1024,128]{1,0:T(8,128)S(1)}, f32[1024,128]{1,0:T(8,128)S(1)}, s16[2080,128]{1,0:T(8,128)(2,1)S(1)}) custom-call(s32[1]{0:T(128)} %bitcast.6.flag_ref, bf16[768,512]{1,0:T(8,128)(2,1)S(1)} %build_weights.1.w_ref, bf16[192,1920]{1,0:T(8,128)(2,1)S(1)} %pad_maximum_fusion.2.refs_0_, ...), custom_call_target="tpu_custom_call" | custom-call | flops 805306368 | bytes 2883584 | tf_op jit(solution)/shard_map/partial_sums/pallas_call | solution.py:170
  74.8 0.8 copy-done
  75.5 1.6 %collective-permute-start.23 = (s16[2080,128]{1,0:T(8,128)(2,1)S(1)}, s16[2080,128]{1,0:T(8,128)(2,1)S(1)}, u32[]{:S(2)}, u32[]{:S(2)}) collective-permute-start(s16[2080,128]{1,0:T(8,128)(2,1)S(1)} %get-tuple-element.50), channel_id=1, source_target_pairs={{0,2},{1,3},{2,0},{3,1},{4,6},{5,7},{6,4},{7,5},{8,10},{9,11},{10,... | collective-permute-start | bytes 1597448 | tf_op jit(solution)/shard_map/ppermute | solution.py:354
  77.1 6.5 %collective-permute-done.17.refs_1_ = s16[912,128]{1,0:T(8,128)(2,1)S(1)} collective-permute-done((s16[912,128]{1,0:T(8,128)(2,1)S(1)}, s16[912,128]{1,0:T(8,128)(2,1)S(1)}, u32[]{:S(2)}, u32[]{:S(2)}) %collective-permute-start.17) | collective-permute-done | bytes 233504 | tf_op jit(solution)/shard_map/ppermute | solution.py:354
  83.9 0.8 collective-permute-start.19
  84.7 3.6 %collective-permute-done.13.refs_1_ = s16[1040,128]{1,0:T(8,128)(2,1)S(1)} collective-permute-done((s16[1040,128]{1,0:T(8,128)(2,1)S(1)}, s16[1040,128]{1,0:T(8,128)(2,1)S(1)}, u32[]{:S(2)}, u32[]{:S(2)}) %collective-permute-start.13) | collective-permute-done | bytes 266272 | tf_op jit(solution)/shard_map/ppermute | solution.py:354
  88.3 1.0 combine.10.refs_0_
  89.9 3.2 %partial_sums.7 = (f32[896,128]{1,0:T(8,128)S(1)}, f32[896,128]{1,0:T(8,128)S(1)}, s16[1824,128]{1,0:T(8,128)(2,1)}) custom-call(s32[1]{0:T(128)} %bitcast.6.flag_ref, bf16[768,512]{1,0:T(8,128)(2,1)S(1)} %build_weights.1.w_ref, bf16[192,1920]{1,0:T(8,128)(2,1)S(1)} %pad_maximum_fusion.2.refs_0_, bf16[192,1920]{1,0:T(8,128)(2,1)S(1)} %collective-permute-done.10.refs_1_, ...), custom_call_target="tpu_custom_call" | custom-call | flops 704643072 | bytes 2523136 | tf_op jit(solution)/shard_map/partial_sums/pallas_call | solution.py:170
  93.1 0.8 copy-done.2
  93.9 0.8 copy-done.4
  94.7 2.1 %collective-permute-done.15.refs_2_ = s16[1040,128]{1,0:T(8,128)(2,1)} collective-permute-done((s16[1040,128]{1,0:T(8,128)(2,1)}, s16[1040,128]{1,0:T(8,128)(2,1)}, u32[]{:S(2)}, u32[]{:S(2)}) %collective-permute-start.15) | collective-permute-done | bytes 266272 | tf_op jit(solution)/shard_map/ppermute | solution.py:350
  97.9 1.0 copy-done.1
  99.6 0.7 copy-done.6
  100.3 7.3 %collective-permute-done.21.refs_0_ = s16[1824,128]{1,0:T(8,128)(2,1)S(1)} collective-permute-done((s16[1824,128]{1,0:T(8,128)(2,1)}, s16[1824,128]{1,0:T(8,128)(2,1)S(1)}, u32[]{:S(2)}, u32[]{:S(2)}) %collective-permute-start.21) | collective-permute-done | bytes 466976 | tf_op jit(solution)/shard_map/ppermute | solution.py:354
  107.9 0.9 copy-done.7
  108.8 13.1 %covariance.1 = f32[13456,128]{1,0:T(8,128)} custom-call(s32[8]{0:T(128)S(1)} %stack.97.place_ref, s16[1040,128]{1,0:T(8,128)(2,1)} %combine.10.refs_0_, s16[1040,128]{1,0:T(8,128)(2,1)} %collective-permute-done.14.refs_1_, s16[1040,128]{1,0:T(8,128)(2,1)} %collective-permute-done.15.refs_2_, s16[1040,128]{1,0:T(8,128)(2,1)S(1)} %collective-permute-done.16.refs_3_, ...), custom_call_target="tpu_custom_call" | custom-call | flops 15432417280 | bytes 6889472 | tf_op jit(solution)/shard_map/covariance/pallas_call | solution.py:311
  122.2 2.9 %collective-permute-start.26 = (s16[1040,128]{1,0:T(8,128)(2,1)S(1)}, s16[1040,128]{1,0:T(8,128)(2,1)S(1)}, u32[]{:S(2)}, u32[]{:S(2)}) collective-permute-start(s16[1040,128]{1,0:T(8,128)(2,1)S(1)} %combine.14.refs_0_), channel_id=1, source_target_pairs={{0,16},{1,17},{2,18},{3,19},{4,20},{5,21},{6,22},{7,23},{8,24},{9,... | collective-permute-start | bytes 798728 | tf_op jit(solution)/shard_map/ppermute | solution.py:350
  125.4 0.8 collective-permute-start.30
  126.2 5.3 %collective-permute-done.26.refs_2_ = s16[1040,128]{1,0:T(8,128)(2,1)S(1)} collective-permute-done((s16[1040,128]{1,0:T(8,128)(2,1)S(1)}, s16[1040,128]{1,0:T(8,128)(2,1)S(1)}, u32[]{:S(2)}, u32[]{:S(2)}) %collective-permute-start.26) | collective-permute-done | bytes 266272 | tf_op jit(solution)/shard_map/ppermute | solution.py:350
  132.0 2.6 %collective-permute-done.30.refs_6_ = s16[912,128]{1,0:T(8,128)(2,1)S(1)} collective-permute-done((s16[912,128]{1,0:T(8,128)(2,1)S(1)}, s16[912,128]{1,0:T(8,128)(2,1)S(1)}, u32[]{:S(2)}, u32[]{:S(2)}) %collective-permute-start.30) | collective-permute-done | bytes 233504 | tf_op jit(solution)/shard_map/ppermute | solution.py:350
  134.7 1.4 collective-permute-done.31.refs_7_
  136.0 3.8 %marginal.1 = f32[128,7424]{1,0:T(8,128)} custom-call(s32[8]{0:T(128)S(1)} %stack.83.place_ref, s16[1040,128]{1,0:T(8,128)(2,1)S(1)} %combine.14.refs_0_, s16[1040,128]{1,0:T(8,128)(2,1)S(1)} %collective-permute-done.25.refs_1_, s16[1040,128]{1,0:T(8,128)(2,1)S(1)} %collective-permute-done.26.refs_2_, s16[1040,128]{1,0:T(8,128)(2,1)S(1)} %collective-permute-done.27.refs_3_, ...), custom_call_target="tpu_custom_call" | custom-call | flops 3801088 | bytes 5701632 | tf_op jit(solution)/shard_map/marginal/pallas_call | solution.py:238
  (78 shorter events, 7.4 us)
Async XLA Ops:
  0.6 1.5 %copy-start.10 = (bf16[96,116]{1,0:T(8,128)(2,1)S(1)}, bf16[96,116]{1,0:T(8,128)(2,1)}, u32[]{:S(2)}) copy-start(bf16[96,116]{1,0:T(8,128)(2,1)} %param.7) | copy-start | bytes 66820
  2.1 1.6 %copy-start.11 = (s32[128,32]{0,1:T(8,128)S(1)}, s32[128,32]{0,1:T(8,128)}, u32[]{:S(2)}) copy-start(s32[128,32]{0,1:T(8,128)} %param.9) | copy-start | bytes 49156
  2.1 1.6 %copy-start.12 = (s32[128,32]{0,1:T(8,128)S(1)}, s32[128,32]{0,1:T(8,128)}, u32[]{:S(2)}) copy-start(s32[128,32]{0,1:T(8,128)} %param.8) | copy-start | bytes 49156
  3.2 2.5 %copy-start.8 = (bf16[96,7424]{1,0:T(8,128)(2,1)S(1)}, bf16[96,7424]{1,0:T(8,128)(2,1)}, u32[]{:S(2)}) copy-start(bf16[96,7424]{1,0:T(8,128)(2,1)} %param.5) | copy-start | bytes 4276228
  3.2 2.5 %collective-permute-start = (bf16[96,3840]{1,0:T(8,128)(2,1)}, bf16[96,3840]{1,0:T(8,128)(2,1)S(1)}, u32[]{:S(2)}, u32[]{:S(2)}) collective-permute-start(bf16[96,3840]{1,0:T(8,128)(2,1)} %get-tuple-element.65), channel_id=1, source_target_pairs={{0,8},{1,9},{2,10},{3,11},{4,12},{5,13},{6,14},{7,15},{8,0},{9,1},... | collective-permute-start | bytes 2211848 | tf_op jit(solution)/shard_map/ppermute | solution.py:350
  5.8 17.6 %collective-permute-start.9 = (bf16[96,3712]{1,0:T(8,128)(2,1)S(1)}, bf16[96,3712]{1,0:T(8,128)(2,1)S(1)}, u32[]{:S(2)}, u32[]{:S(2)}) collective-permute-start(bf16[96,3712]{1,0:T(8,128)(2,1)S(1)} %constant_dynamic-slice_fusion.3), channel_id=1, source_target_pairs={{0,8},{1,9},{2,10},{3,11},{4,12},{5,13},{6,14},{7,15},{8,0},{9,1},... | collective-permute-start | bytes 2138120 | tf_op jit(solution)/shard_map/ppermute | solution.py:350
  6.3 9.4 %copy-start.9 = (bf16[96,7424]{1,0:T(8,128)(2,1)S(1)}, bf16[96,7424]{1,0:T(8,128)(2,1)}, u32[]{:S(2)}) copy-start(bf16[96,7424]{1,0:T(8,128)(2,1)} %param.5) | copy-start | bytes 4276228
  6.4 19.8 %collective-permute-start.3 = (bf16[192,1920]{1,0:T(8,128)(2,1)S(1)}, bf16[192,1920]{1,0:T(8,128)(2,1)S(1)}, u32[]{:S(2)}, u32[]{:S(2)}) collective-permute-start(bf16[192,1920]{1,0:T(8,128)(2,1)S(1)} %pad_maximum_fusion), channel_id=1, source_target_pairs={{0,16},{1,17},{2,18},{3,19},{4,20},{5,21},{6,22},{7,23},{8,24},{9,... | collective-permute-start | bytes 2211848 | tf_op jit(solution)/shard_map/ppermute | solution.py:350
  9.0 5.2 %collective-permute-start.1 = (s32[64,128]{1,0:T(8,128)S(1)}, s32[64,128]{1,0:T(8,128)S(1)}, u32[]{:S(2)}, u32[]{:S(2)}) collective-permute-start(s32[64,128]{1,0:T(8,128)S(1)} %pad_add_fusion.2), channel_id=1, source_target_pairs={{0,4},{1,5},{2,6},{3,7},{4,0},{5,1},{6,2},{7,3},{8,12},{9,13},{10,... | collective-permute-start | bytes 98312 | tf_op jit(solution)/shard_map/ppermute | solution.py:354
  12.5 29.5 %collective-permute-start.4 = (bf16[192,1920]{1,0:T(8,128)(2,1)}, bf16[192,1920]{1,0:T(8,128)(2,1)}, u32[]{:S(2)}, u32[]{:S(2)}) collective-permute-start(bf16[192,1920]{1,0:T(8,128)(2,1)} %pad_maximum_fusion.1.refs_0_), channel_id=1, source_target_pairs={{0,1},{1,0},{2,3},{3,2},{4,5},{5,4},{6,7},{7,6},{8,9},{9,8},{10,11... | collective-permute-start | bytes 2211848 | tf_op jit(solution)/shard_map/ppermute | solution.py:350
  14.2 4.3 %collective-permute-start.2 = (s32[64,256]{1,0:T(8,128)S(1)}, s32[64,256]{1,0:T(8,128)S(1)}, u32[]{:S(2)}, u32[]{:S(2)}) collective-permute-start(s32[64,256]{1,0:T(8,128)S(1)} %pad_add_fusion.1), channel_id=1, source_target_pairs={{0,2},{1,3},{2,0},{3,1},{4,6},{5,7},{6,4},{7,5},{8,10},{9,11},{10,... | collective-permute-start | bytes 196616 | tf_op jit(solution)/shard_map/ppermute | solution.py:354
  24.3 28.2 %collective-permute-start.10 = (bf16[192,1920]{1,0:T(8,128)(2,1)}, bf16[192,1920]{1,0:T(8,128)(2,1)S(1)}, u32[]{:S(2)}, u32[]{:S(2)}) collective-permute-start(bf16[192,1920]{1,0:T(8,128)(2,1)} %pad_maximum_fusion.3), channel_id=1, source_target_pairs={{0,16},{1,17},{2,18},{3,19},{4,20},{5,21},{6,22},{7,23},{8,24},{9,... | collective-permute-start | bytes 2211848 | tf_op jit(solution)/shard_map/ppermute | solution.py:350
  26.2 14.3 %collective-permute-start.5 = (bf16[192,1024]{1,0:T(8,128)(2,1)S(1)}, bf16[192,1024]{1,0:T(8,128)(2,1)S(1)}, u32[]{:S(2)}, u32[]{:S(2)}) collective-permute-start(bf16[192,1024]{1,0:T(8,128)(2,1)S(1)} %slice.16), channel_id=1, source_target_pairs={{0,1},{1,0},{2,3},{3,2},{4,5},{5,4},{6,7},{7,6},{8,9},{9,8},{10,11... | collective-permute-start | bytes 1179656 | tf_op jit(solution)/shard_map/ppermute | solution.py:350
  29.3 18.8 %collective-permute-start.6 = (bf16[192,896]{1,0:T(8,128)(2,1)}, bf16[192,896]{1,0:T(8,128)(2,1)}, u32[]{:S(2)}, u32[]{:S(2)}) collective-permute-start(bf16[192,896]{1,0:T(8,128)(2,1)} %slice.17), channel_id=1, source_target_pairs={{0,1},{1,0},{2,3},{3,2},{4,5},{5,4},{6,7},{7,6},{8,9},{9,8},{10,11... | collective-permute-start | bytes 1032200 | tf_op jit(solution)/shard_map/ppermute | solution.py:350
  40.6 31.6 %collective-permute-start.11 = (bf16[192,1920]{1,0:T(8,128)(2,1)S(1)}, bf16[192,1920]{1,0:T(8,128)(2,1)}, u32[]{:S(2)}, u32[]{:S(2)}) collective-permute-start(bf16[192,1920]{1,0:T(8,128)(2,1)S(1)} %pad_maximum_fusion.2.refs_0_), channel_id=1, source_target_pairs={{0,1},{1,0},{2,3},{3,2},{4,5},{5,4},{6,7},{7,6},{8,9},{9,8},{10,11... | collective-permute-start | bytes 2211848 | tf_op jit(solution)/shard_map/ppermute | solution.py:350
  44.9 15.1 %collective-permute-start.7 = (s16[2080,128]{1,0:T(8,128)(2,1)S(1)}, s16[2080,128]{1,0:T(8,128)(2,1)S(1)}, u32[]{:S(2)}, u32[]{:S(2)}) collective-permute-start(s16[2080,128]{1,0:T(8,128)(2,1)S(1)} %get-tuple-element.34), channel_id=1, source_target_pairs={{0,2},{1,3},{2,0},{3,1},{4,6},{5,7},{6,4},{7,5},{8,10},{9,11},{10,... | collective-permute-start | bytes 1597448 | tf_op jit(solution)/shard_map/ppermute | solution.py:354
  50.8 16.4 %collective-permute-start.8 = (s16[1824,128]{1,0:T(8,128)(2,1)S(1)}, s16[1824,128]{1,0:T(8,128)(2,1)S(1)}, u32[]{:S(2)}, u32[]{:S(2)}) collective-permute-start(s16[1824,128]{1,0:T(8,128)(2,1)S(1)} %get-tuple-element.36), channel_id=1, source_target_pairs={{0,2},{1,3},{2,0},{3,1},{4,6},{5,7},{6,4},{7,5},{8,10},{9,11},{10,... | collective-permute-start | bytes 1400840 | tf_op jit(solution)/shard_map/ppermute | solution.py:354
  52.5 19.6 %collective-permute-start.12 = (bf16[192,1024]{1,0:T(8,128)(2,1)S(1)}, bf16[192,1024]{1,0:T(8,128)(2,1)S(1)}, u32[]{:S(2)}, u32[]{:S(2)}) collective-permute-start(bf16[192,1024]{1,0:T(8,128)(2,1)S(1)} %slice.18), channel_id=1, source_target_pairs={{0,1},{1,0},{2,3},{3,2},{4,5},{5,4},{6,7},{7,6},{8,9},{9,8},{10,11... | collective-permute-start | bytes 1179656 | tf_op jit(solution)/shard_map/ppermute | solution.py:350
  54.1 35.7 %collective-permute-start.18 = (bf16[192,896]{1,0:T(8,128)(2,1)S(1)}, bf16[192,896]{1,0:T(8,128)(2,1)S(1)}, u32[]{:S(2)}, u32[]{:S(2)}) collective-permute-start(bf16[192,896]{1,0:T(8,128)(2,1)S(1)} %slice.19), channel_id=1, source_target_pairs={{0,1},{1,0},{2,3},{3,2},{4,5},{5,4},{6,7},{7,6},{8,9},{9,8},{10,11... | collective-permute-start | bytes 1032200 | tf_op jit(solution)/shard_map/ppermute | solution.py:350
  67.5 16.2 %collective-permute-start.17 = (s16[912,128]{1,0:T(8,128)(2,1)S(1)}, s16[912,128]{1,0:T(8,128)(2,1)S(1)}, u32[]{:S(2)}, u32[]{:S(2)}) collective-permute-start(s16[912,128]{1,0:T(8,128)(2,1)S(1)} %combine.9), channel_id=1, source_target_pairs={{0,4},{1,5},{2,6},{3,7},{4,0},{5,1},{6,2},{7,3},{8,12},{9,13},{10,... | collective-permute-start | bytes 700424 | tf_op jit(solution)/shard_map/ppermute | solution.py:354
  67.5 20.8 %collective-permute-start.13 = (s16[1040,128]{1,0:T(8,128)(2,1)S(1)}, s16[1040,128]{1,0:T(8,128)(2,1)S(1)}, u32[]{:S(2)}, u32[]{:S(2)}) collective-permute-start(s16[1040,128]{1,0:T(8,128)(2,1)S(1)} %combine.8), channel_id=1, source_target_pairs={{0,4},{1,5},{2,6},{3,7},{4,0},{5,1},{6,2},{7,3},{8,12},{9,13},{10,... | collective-permute-start | bytes 798728 | tf_op jit(solution)/shard_map/ppermute | solution.py:354
  74.8 0.8 copy-start
  75.5 21.7 %collective-permute-start.23 = (s16[2080,128]{1,0:T(8,128)(2,1)S(1)}, s16[2080,128]{1,0:T(8,128)(2,1)S(1)}, u32[]{:S(2)}, u32[]{:S(2)}) collective-permute-start(s16[2080,128]{1,0:T(8,128)(2,1)S(1)} %get-tuple-element.50), channel_id=1, source_target_pairs={{0,2},{1,3},{2,0},{3,1},{4,6},{5,7},{6,4},{7,5},{8,10},{9,11},{10,... | collective-permute-start | bytes 1597448 | tf_op jit(solution)/shard_map/ppermute | solution.py:354
  83.9 13.4 %collective-permute-start.19 = (s16[912,128]{1,0:T(8,128)(2,1)S(1)}, s16[912,128]{1,0:T(8,128)(2,1)}, u32[]{:S(2)}, u32[]{:S(2)}) collective-permute-start(s16[912,128]{1,0:T(8,128)(2,1)S(1)} %combine.11.refs_4_), channel_id=1, source_target_pairs={{0,16},{1,17},{2,18},{3,19},{4,20},{5,21},{6,22},{7,23},{8,24},{9,... | collective-permute-start | bytes 700424 | tf_op jit(solution)/shard_map/ppermute | solution.py:350
  89.3 7.5 %collective-permute-start.15 = (s16[1040,128]{1,0:T(8,128)(2,1)}, s16[1040,128]{1,0:T(8,128)(2,1)}, u32[]{:S(2)}, u32[]{:S(2)}) collective-permute-start(s16[1040,128]{1,0:T(8,128)(2,1)} %combine.10.refs_0_), channel_id=1, source_target_pairs={{0,16},{1,17},{2,18},{3,19},{4,20},{5,21},{6,22},{7,23},{8,24},{9,... | collective-permute-start | bytes 798728 | tf_op jit(solution)/shard_map/ppermute | solution.py:350
  93.1 0.8 copy-start.2
  93.9 0.8 copy-start.4
  94.7 12.9 %collective-permute-start.21 = (s16[1824,128]{1,0:T(8,128)(2,1)}, s16[1824,128]{1,0:T(8,128)(2,1)S(1)}, u32[]{:S(2)}, u32[]{:S(2)}) collective-permute-start(s16[1824,128]{1,0:T(8,128)(2,1)} %get-tuple-element.47), channel_id=1, source_target_pairs={{0,2},{1,3},{2,0},{3,1},{4,6},{5,7},{6,4},{7,5},{8,10},{9,11},{10,... | collective-permute-start | bytes 1400840 | tf_op jit(solution)/shard_map/ppermute | solution.py:354
  96.8 3.5 %collective-permute-start.16 = (s16[1040,128]{1,0:T(8,128)(2,1)}, s16[1040,128]{1,0:T(8,128)(2,1)S(1)}, u32[]{:S(2)}, u32[]{:S(2)}) collective-permute-start(s16[1040,128]{1,0:T(8,128)(2,1)} %collective-permute-done.15.refs_2_), channel_id=1, source_target_pairs={{0,8},{1,9},{2,10},{3,11},{4,12},{5,13},{6,14},{7,15},{8,0},{9,1},... | collective-permute-start | bytes 798728 | tf_op jit(solution)/shard_map/ppermute | solution.py:350
  96.8 11.1 %collective-permute-start.14 = (s16[1040,128]{1,0:T(8,128)(2,1)}, s16[1040,128]{1,0:T(8,128)(2,1)}, u32[]{:S(2)}, u32[]{:S(2)}) collective-permute-start(s16[1040,128]{1,0:T(8,128)(2,1)} %combine.10.refs_0_), channel_id=1, source_target_pairs={{0,8},{1,9},{2,10},{3,11},{4,12},{5,13},{6,14},{7,15},{8,0},{9,1},... | collective-permute-start | bytes 798728 | tf_op jit(solution)/shard_map/ppermute | solution.py:350
  97.3 2.3 %collective-permute-start.20 = (s16[912,128]{1,0:T(8,128)(2,1)}, s16[912,128]{1,0:T(8,128)(2,1)S(1)}, u32[]{:S(2)}, u32[]{:S(2)}) collective-permute-start(s16[912,128]{1,0:T(8,128)(2,1)} %collective-permute-done.19.refs_6_), channel_id=1, source_target_pairs={{0,8},{1,9},{2,10},{3,11},{4,12},{5,13},{6,14},{7,15},{8,0},{9,1},... | collective-permute-start | bytes 700424 | tf_op jit(solution)/shard_map/ppermute | solution.py:350
  97.3 10.6 %collective-permute-start.22 = (s16[912,128]{1,0:T(8,128)(2,1)S(1)}, s16[912,128]{1,0:T(8,128)(2,1)}, u32[]{:S(2)}, u32[]{:S(2)}) collective-permute-start(s16[912,128]{1,0:T(8,128)(2,1)S(1)} %combine.11.refs_4_), channel_id=1, source_target_pairs={{0,8},{1,9},{2,10},{3,11},{4,12},{5,13},{6,14},{7,15},{8,0},{9,1},... | collective-permute-start | bytes 700424 | tf_op jit(solution)/shard_map/ppermute | solution.py:350
  97.9 1.0 copy-start.1
  98.9 8.7 %copy-start.3 = (f32[896,128]{1,0:T(8,128)S(1)}, f32[896,128]{1,0:T(8,128)}, u32[]{:S(2)}) copy-start(f32[896,128]{1,0:T(8,128)} %copy-done.2) | copy-start | bytes 1376260
  99.6 0.7 copy-start.6
  100.3 21.7 %collective-permute-start.24 = (s16[1040,128]{1,0:T(8,128)(2,1)S(1)}, s16[1040,128]{1,0:T(8,128)(2,1)S(1)}, u32[]{:S(2)}, u32[]{:S(2)}) collective-permute-start(s16[1040,128]{1,0:T(8,128)(2,1)S(1)} %combine.13), channel_id=1, source_target_pairs={{0,4},{1,5},{2,6},{3,7},{4,0},{5,1},{6,2},{7,3},{8,12},{9,13},{10,... | collective-permute-start | bytes 798728 | tf_op jit(solution)/shard_map/ppermute | solution.py:354
  107.8 17.4 %collective-permute-start.28 = (s16[912,128]{1,0:T(8,128)(2,1)S(1)}, s16[912,128]{1,0:T(8,128)(2,1)S(1)}, u32[]{:S(2)}, u32[]{:S(2)}) collective-permute-start(s16[912,128]{1,0:T(8,128)(2,1)S(1)} %combine.12), channel_id=1, source_target_pairs={{0,4},{1,5},{2,6},{3,7},{4,0},{5,1},{6,2},{7,3},{8,12},{9,13},{10,... | collective-permute-start | bytes 700424 | tf_op jit(solution)/shard_map/ppermute | solution.py:354
  107.9 0.9 copy-start.7
  122.0 3.2 %copy-start.5 = (f32[896,128]{1,0:T(8,128)S(1)}, f32[896,128]{1,0:T(8,128)}, u32[]{:S(2)}) copy-start(f32[896,128]{1,0:T(8,128)} %copy-done.4) | copy-start | bytes 1376260
  122.2 9.2 %collective-permute-start.26 = (s16[1040,128]{1,0:T(8,128)(2,1)S(1)}, s16[1040,128]{1,0:T(8,128)(2,1)S(1)}, u32[]{:S(2)}, u32[]{:S(2)}) collective-permute-start(s16[1040,128]{1,0:T(8,128)(2,1)S(1)} %combine.14.refs_0_), channel_id=1, source_target_pairs={{0,16},{1,17},{2,18},{3,19},{4,20},{5,21},{6,22},{7,23},{8,24},{9,... | collective-permute-start | bytes 798728 | tf_op jit(solution)/shard_map/ppermute | solution.py:350
  125.4 9.2 %collective-permute-start.30 = (s16[912,128]{1,0:T(8,128)(2,1)S(1)}, s16[912,128]{1,0:T(8,128)(2,1)S(1)}, u32[]{:S(2)}, u32[]{:S(2)}) collective-permute-start(s16[912,128]{1,0:T(8,128)(2,1)S(1)} %combine.15.refs_4_), channel_id=1, source_target_pairs={{0,16},{1,17},{2,18},{3,19},{4,20},{5,21},{6,22},{7,23},{8,24},{9,... | collective-permute-start | bytes 700424 | tf_op jit(solution)/shard_map/ppermute | solution.py:350
  126.2 8.4 %collective-permute-start.25 = (s16[1040,128]{1,0:T(8,128)(2,1)S(1)}, s16[1040,128]{1,0:T(8,128)(2,1)S(1)}, u32[]{:S(2)}, u32[]{:S(2)}) collective-permute-start(s16[1040,128]{1,0:T(8,128)(2,1)S(1)} %combine.14.refs_0_), channel_id=1, source_target_pairs={{0,8},{1,9},{2,10},{3,11},{4,12},{5,13},{6,14},{7,15},{8,0},{9,1},... | collective-permute-start | bytes 798728 | tf_op jit(solution)/shard_map/ppermute | solution.py:350
  131.5 4.6 %collective-permute-start.27 = (s16[1040,128]{1,0:T(8,128)(2,1)S(1)}, s16[1040,128]{1,0:T(8,128)(2,1)S(1)}, u32[]{:S(2)}, u32[]{:S(2)}) collective-permute-start(s16[1040,128]{1,0:T(8,128)(2,1)S(1)} %collective-permute-done.26.refs_2_), channel_id=1, source_target_pairs={{0,8},{1,9},{2,10},{3,11},{4,12},{5,13},{6,14},{7,15},{8,0},{9,1},... | collective-permute-start | bytes 798728 | tf_op jit(solution)/shard_map/ppermute | solution.py:350
  131.5 3.2 %collective-permute-start.29 = (s16[912,128]{1,0:T(8,128)(2,1)S(1)}, s16[912,128]{1,0:T(8,128)(2,1)S(1)}, u32[]{:S(2)}, u32[]{:S(2)}) collective-permute-start(s16[912,128]{1,0:T(8,128)(2,1)S(1)} %combine.15.refs_4_), channel_id=1, source_target_pairs={{0,8},{1,9},{2,10},{3,11},{4,12},{5,13},{6,14},{7,15},{8,0},{9,1},... | collective-permute-start | bytes 700424 | tf_op jit(solution)/shard_map/ppermute | solution.py:350
  134.5 1.5 %collective-permute-start.31 = (s16[912,128]{1,0:T(8,128)(2,1)S(1)}, s16[912,128]{1,0:T(8,128)(2,1)S(1)}, u32[]{:S(2)}, u32[]{:S(2)}) collective-permute-start(s16[912,128]{1,0:T(8,128)(2,1)S(1)} %collective-permute-done.30.refs_6_), channel_id=1, source_target_pairs={{0,8},{1,9},{2,10},{3,11},{4,12},{5,13},{6,14},{7,15},{8,0},{9,1},... | collective-permute-start | bytes 700424 | tf_op jit(solution)/shard_map/ppermute | solution.py:350

commit v9 on v8

--- a/solution.py
+++ b/solution.py
@@ -436,14 +436,16 @@
     own_b, near_b, middle_b, far_b = along_z(data_b, first_b, True, (own_a,), (middle_a,))
     data_c = merge([mean_y] + [along_y(value, 0, first_c, there) for value in mean_x[1:]])
     data_d = merge([later(mean_y, first_c)] + [along_y(value, first_c, first_d, there) for value in mean_x[1:]])
-    own_c, near_c, middle_c, far_c = along_z(data_c, first_c, False, (middle_b,))
+    own_c, near_c, middle_c, far_c = along_z(data_c, first_c, False, (middle_b, far_a))
     mine_a, load_a = spread(own_a, near_a, far_a)
-    mine_b, load_b = spread(own_b, near_b, far_b)
-    own_d, near_d, middle_d, far_d = along_z(data_d, first_d, False, (own_c, far_b), (load_a[-1], load_b[-1]))
-    load_pieces = load_a + [after(load_b[0], middle_d)] + load_b[1:]
+    own_d, opposite_d, sent_d = partial_sums(flag, after(w, own_c), data_d, first_d, False)
+    near_d = z_swap(sent_d, 1)
+    mine_b, load_b = spread(after(own_b, own_d), near_b, far_b)
+    load_pieces = load_a + [after(load_b[0], middle_c, own_d)] + load_b[1:]
     cov = covariance(places(load_width), load_pieces, load_tiles, load_width * CORES, ages, rank)
+    far_d = z_swap(combine(after(opposite_d, cov), (near_d, 1)), 2)
     mine_c, mean_c = spread(after(own_c, cov), near_c, far_c)
-    mine_d, mean_d = spread(after(own_d, cov), near_d, far_d)
+    mine_d, mean_d = spread(own_d, near_d, far_d)
     mean_pieces = mean_c + mean_d
     mean = marginal(places(mean_width), mean_pieces, mean_tiles, mean_width * CORES)
     return mean, cov.T

time: 140 us -> 136 us (0.971)
  starting transfers between devices: 30.2 us -> 34.9 us
  Pallas kernels: 35.6 us -> 31.9 us
  local copies, waits for them, and re-layouts: 8.22 us -> 5.21 us
    ppermute x22, waiting for transfers between devices: 29.4 us -> 24.1 us  [move(): return lax.ppermute(value, ('geo', 'dist'), perm)]
    unnamed x26 -> x24, local copies, waits for them, and re-layouts: 5.09 us -> 0.56 us
    ppermute x10, waiting for transfers between devices: 32.5 us -> 36.7 us  [z_swap(): return lax.ppermute(value, 'dist', perm)]
    ppermute x22, starting transfers between devices: 18.2 us -> 21 us  [move(): return lax.ppermute(value, ('geo', 'dist'), perm)]
    pallas_call x4, Pallas kernels: 11.4 us -> 8.74 us  [partial_sums(): pl.pallas_call(functools.partial(sums_kernel, offsets, has_var), grid_spe...]
    ppermute x10, starting transfers between devices: 12 us -> 13.9 us  [z_swap(): return lax.ppermute(value, 'dist', perm)]
    dynamic_slice x4, local copies, waits for them, and re-layouts: 0.55 us -> 2.04 us  [part(): lax.dynamic_slice(b, (0, start_of(group, tiles) * LANES), size)]
  transfers between devices with their start and end apart: 32 -> 32, of which waited for: 17 -> 16; matrix products, arithmetic and copies ran while one was open for 3% -> 3% of each run, Pallas kernels for 23% -> 21%
where the time goes in v9:
time: 136 us
  waiting for transfers between devices  60.8 us (45%)
  starting transfers between devices  34.9 us (26%)
  Pallas kernels  31.9 us (23%)
  local copies, waits for them, and re-layouts  5.21 us (4%)
  other arithmetic  2.16 us (2%)
    ppermute x10, waiting for transfers between devices, z_swap(): return lax.ppermute(value, 'dist', perm)  36.7 us
    ppermute x22, waiting for transfers between devices, move(): return lax.ppermute(value, ('geo', 'dist'), perm)  24.1 us
    ppermute x22, starting transfers between devices, move(): return lax.ppermute(value, ('geo', 'dist'), perm)  21 us
    ppermute x10, starting transfers between devices, z_swap(): return lax.ppermute(value, 'dist', perm)  13.9 us
    pallas_call x1, Pallas kernels, covariance(): pl.pallas_call(functools.partial(covariance_kernel, tiles, total, ages, r...  12.8 us
    pallas_call x4, Pallas kernels, partial_sums(): pl.pallas_call(functools.partial(sums_kernel, offsets, has_var), grid_spe...  8.74 us
    pallas_call x1, Pallas kernels, build_weights(): pl.pallas_call(functools.partial(weights_kernel, rows), grid_spec=pltpu.P...  4.83 us
    pallas_call x1, Pallas kernels, marginal(): pl.pallas_call(functools.partial(marginal_kernel, tiles), grid_spec=pltpu...  3.83 us
  transfers between devices with their start and end apart: 32, of which 16 were waited for; matrix products, arithmetic and copies ran while one was open for 3% of the time, Pallas kernels for 21%

profile of v9, /device:TPU:0, one launch (start us, length us, event | category | flops | bytes accessed | tf_op | source)
XLA Modules:
  0.0 135.8 jit_solution(12959740385947533199)
XLA Ops:
  0.7 1.4 %constant_dynamic-slice_fusion.10 = (bf16[96,3712]{1,0:T(8,128)(2,1)S(1)}, bf16[96,3712]{1,0:T(8,128)(2,1)S(1)}) fusion(bf16[96,7424]{1,0:T(8,128)(2,1)} %param.6, s32[]{:T(128)S(6)} %select_n.166, s32[]{:T(128)S(6)} %select_n.170), kind=kLoop, calls=%fused_computation.21 | loop fusion | bytes 2850824 | tf_op jit(solution)/shard_map/dynamic_slice | solution.py:360
  2.1 1.0 fusion.1
  3.8 1.8 %collective-permute-done = bf16[96,3840]{1,0:T(8,128)(2,1)S(1)} collective-permute-done((bf16[96,3840]{1,0:T(8,128)(2,1)}, bf16[96,3840]{1,0:T(8,128)(2,1)S(1)}, u32[]{:S(2)}, u32[]{:S(2)}) %collective-permute-start) | collective-permute-done | bytes 737312 | tf_op jit(solution)/shard_map/ppermute | solution.py:350
  6.4 2.7 %collective-permute-start.3 = (bf16[192,1920]{1,0:T(8,128)(2,1)S(1)}, bf16[192,1920]{1,0:T(8,128)(2,1)S(1)}, u32[]{:S(2)}, u32[]{:S(2)}) collective-permute-start(bf16[192,1920]{1,0:T(8,128)(2,1)S(1)} %pad_maximum_fusion), channel_id=1, source_target_pairs={{0,16},{1,17},{2,18},{3,19},{4,20},{5,21},{6,22},{7,23},{8,24},{9,... | collective-permute-start | bytes 2211848 | tf_op jit(solution)/shard_map/ppermute | solution.py:350
  9.0 2.6 %collective-permute-start.1 = (s32[64,128]{1,0:T(8,128)S(1)}, s32[64,128]{1,0:T(8,128)S(1)}, u32[]{:S(2)}, u32[]{:S(2)}) collective-permute-start(s32[64,128]{1,0:T(8,128)S(1)} %pad_add_fusion.2), channel_id=1, source_target_pairs={{0,4},{1,5},{2,6},{3,7},{4,0},{5,1},{6,2},{7,3},{8,12},{9,13},{10,... | collective-permute-start | bytes 98312 | tf_op jit(solution)/shard_map/ppermute | solution.py:354
  11.7 1.6 %collective-permute-start.4 = (bf16[192,1920]{1,0:T(8,128)(2,1)S(1)}, bf16[192,1920]{1,0:T(8,128)(2,1)}, u32[]{:S(2)}, u32[]{:S(2)}) collective-permute-start(bf16[192,1920]{1,0:T(8,128)(2,1)S(1)} %pad_maximum_fusion.1.refs_0_), channel_id=1, source_target_pairs={{0,1},{1,0},{2,3},{3,2},{4,5},{5,4},{6,7},{7,6},{8,9},{9,8},{10,11... | collective-permute-start | bytes 2211848 | tf_op jit(solution)/shard_map/ppermute | solution.py:350
  13.3 0.9 collective-permute-done.1
  14.2 1.2 collective-permute-start.2
  15.4 1.1 constant_dynamic-slice_fusion.1
  16.5 2.0 %collective-permute-done.2 = s32[64,256]{1,0:T(8,128)S(1)} collective-permute-done((s32[64,256]{1,0:T(8,128)S(1)}, s32[64,256]{1,0:T(8,128)S(1)}, u32[]{:S(2)}, u32[]{:S(2)}) %collective-permute-start.2) | collective-permute-done | bytes 65568 | tf_op jit(solution)/shard_map/ppermute | solution.py:354
  18.5 4.8 %build_weights.1.w_ref = bf16[768,512]{1,0:T(8,128)(2,1)S(1)} custom-call(s32[8]{0:T(128)S(1)} %stack.92.base_ref, s32[64,512]{1,0:T(8,128)S(1)} %pad_add_fusion.query_ref), custom_call_target="tpu_custom_call" | custom-call | flops 5033164800 | bytes 786432 | tf_op jit(solution)/shard_map/build_weights/pallas_call | solution.py:93
  23.3 2.7 %collective-permute-done.3.refs_1_ = bf16[192,1920]{1,0:T(8,128)(2,1)S(1)} collective-permute-done((bf16[192,1920]{1,0:T(8,128)(2,1)S(1)}, bf16[192,1920]{1,0:T(8,128)(2,1)S(1)}, u32[]{:S(2)}, u32[]{:S(2)}) %collective-permute-start.3) | collective-permute-done | bytes 737312 | tf_op jit(solution)/shard_map/ppermute | solution.py:350
  26.0 0.8 slice.16
  26.8 1.8 %collective-permute-start.5 = (bf16[192,1024]{1,0:T(8,128)(2,1)}, bf16[192,1024]{1,0:T(8,128)(2,1)S(1)}, u32[]{:S(2)}, u32[]{:S(2)}) collective-permute-start(bf16[192,1024]{1,0:T(8,128)(2,1)} %slice.16), channel_id=1, source_target_pairs={{0,1},{1,0},{2,3},{3,2},{4,5},{5,4},{6,7},{7,6},{8,9},{9,8},{10,11... | collective-permute-start | bytes 1179656 | tf_op jit(solution)/shard_map/ppermute | solution.py:350
  28.6 0.8 constant_dynamic-slice_fusion
  29.4 0.9 pad_maximum_fusion.3
  30.3 1.5 %collective-permute-start.11 = (bf16[192,1920]{1,0:T(8,128)(2,1)}, bf16[192,1920]{1,0:T(8,128)(2,1)S(1)}, u32[]{:S(2)}, u32[]{:S(2)}) collective-permute-start(bf16[192,1920]{1,0:T(8,128)(2,1)} %pad_maximum_fusion.3), channel_id=1, source_target_pairs={{0,16},{1,17},{2,18},{3,19},{4,20},{5,21},{6,22},{7,23},{8,24},{9,... | collective-permute-start | bytes 2211848 | tf_op jit(solution)/shard_map/ppermute | solution.py:350
  31.9 0.6 collective-permute-start.6
  32.4 6.6 %collective-permute-done.5.refs_3_ = bf16[192,1024]{1,0:T(8,128)(2,1)S(1)} collective-permute-done((bf16[192,1024]{1,0:T(8,128)(2,1)}, bf16[192,1024]{1,0:T(8,128)(2,1)S(1)}, u32[]{:S(2)}, u32[]{:S(2)}) %collective-permute-start.5) | collective-permute-done | bytes 393248 | tf_op jit(solution)/shard_map/ppermute | solution.py:350
  39.0 2.7 %partial_sums.4 = (f32[1024,128]{1,0:T(8,128)S(1)}, f32[1024,128]{1,0:T(8,128)S(1)}, s16[2080,128]{1,0:T(8,128)(2,1)S(1)}) custom-call(s32[1]{0:T(128)} %bitcast.6.flag_ref, bf16[768,512]{1,0:T(8,128)(2,1)S(1)} %build_weights.1.w_ref, bf16[192,1920]{1,0:T(8,128)(2,1)S(1)} %pad_maximum_fusion.1.refs_0_, bf16[192,1920]{1,0:T(8,128)(2,1)S(1)} %collective-permute-done.3.refs_1_, ...), custom_call_target="tpu_custom_call" | custom-call | flops 805306368 | bytes 2883584 | tf_op jit(solution)/shard_map/partial_sums/pallas_call | solution.py:170
  41.7 2.0 %collective-permute-start.7 = (s16[2080,128]{1,0:T(8,128)(2,1)S(1)}, s16[2080,128]{1,0:T(8,128)(2,1)S(1)}, u32[]{:S(2)}, u32[]{:S(2)}) collective-permute-start(s16[2080,128]{1,0:T(8,128)(2,1)S(1)} %get-tuple-element.34), channel_id=1, source_target_pairs={{0,2},{1,3},{2,0},{3,1},{4,6},{5,7},{6,4},{7,5},{8,10},{9,11},{10,... | collective-permute-start | bytes 1597448 | tf_op jit(solution)/shard_map/ppermute | solution.py:354
  43.7 1.6 %collective-permute-start.12 = (bf16[192,1920]{1,0:T(8,128)(2,1)S(1)}, bf16[192,1920]{1,0:T(8,128)(2,1)S(1)}, u32[]{:S(2)}, u32[]{:S(2)}) collective-permute-start(bf16[192,1920]{1,0:T(8,128)(2,1)S(1)} %pad_maximum_fusion.2.refs_0_), channel_id=1, source_target_pairs={{0,1},{1,0},{2,3},{3,2},{4,5},{5,4},{6,7},{7,6},{8,9},{9,8},{10,11... | collective-permute-start | bytes 2211848 | tf_op jit(solution)/shard_map/ppermute | solution.py:350
  45.3 1.1 collective-permute-done.6.refs_3_
  46.4 2.5 %partial_sums.5 = (f32[896,128]{1,0:T(8,128)S(1)}, f32[896,128]{1,0:T(8,128)S(1)}, s16[1824,128]{1,0:T(8,128)(2,1)S(1)}) custom-call(s32[1]{0:T(128)} %bitcast.6.flag_ref, bf16[768,512]{1,0:T(8,128)(2,1)S(1)} %build_weights.1.w_ref, bf16[192,1920]{1,0:T(8,128)(2,1)S(1)} %pad_maximum_fusion.1.refs_0_, bf16[192,1920]{1,0:T(8,128)(2,1)S(1)} %collective-permute-done.3.refs_1_, ...), custom_call_target="tpu_custom_call" | custom-call | flops 704643072 | bytes 2523136 | tf_op jit(solution)/shard_map/partial_sums/pallas_call | solution.py:170
  48.9 2.0 %collective-permute-start.8 = (s16[1824,128]{1,0:T(8,128)(2,1)S(1)}, s16[1824,128]{1,0:T(8,128)(2,1)S(1)}, u32[]{:S(2)}, u32[]{:S(2)}) collective-permute-start(s16[1824,128]{1,0:T(8,128)(2,1)S(1)} %get-tuple-element.36), channel_id=1, source_target_pairs={{0,2},{1,3},{2,0},{3,1},{4,6},{5,7},{6,4},{7,5},{8,10},{9,11},{10,... | collective-permute-start | bytes 1400840 | tf_op jit(solution)/shard_map/ppermute | solution.py:354
  50.9 1.6 %collective-permute-start.13 = (bf16[192,1024]{1,0:T(8,128)(2,1)S(1)}, bf16[192,1024]{1,0:T(8,128)(2,1)S(1)}, u32[]{:S(2)}, u32[]{:S(2)}) collective-permute-start(bf16[192,1024]{1,0:T(8,128)(2,1)S(1)} %slice.18), channel_id=1, source_target_pairs={{0,1},{1,0},{2,3},{3,2},{4,5},{5,4},{6,7},{7,6},{8,9},{9,8},{10,11... | collective-permute-start | bytes 1179656 | tf_op jit(solution)/shard_map/ppermute | solution.py:350
  53.1 6.6 %collective-permute-done.7.refs_0_ = s16[2080,128]{1,0:T(8,128)(2,1)S(1)} collective-permute-done((s16[2080,128]{1,0:T(8,128)(2,1)S(1)}, s16[2080,128]{1,0:T(8,128)(2,1)S(1)}, u32[]{:S(2)}, u32[]{:S(2)}) %collective-permute-start.7) | collective-permute-done | bytes 532512 | tf_op jit(solution)/shard_map/ppermute | solution.py:354
  59.9 2.1 %collective-permute-start.9 = (s16[1040,128]{1,0:T(8,128)(2,1)S(1)}, s16[1040,128]{1,0:T(8,128)(2,1)S(1)}, u32[]{:S(2)}, u32[]{:S(2)}) collective-permute-start(s16[1040,128]{1,0:T(8,128)(2,1)S(1)} %combine.8), channel_id=1, source_target_pairs={{0,4},{1,5},{2,6},{3,7},{4,0},{5,1},{6,2},{7,3},{8,12},{9,13},{10,... | collective-permute-start | bytes 798728 | tf_op jit(solution)/shard_map/ppermute | solution.py:354
  61.9 8.0 %collective-permute-done.8.refs_0_ = s16[1824,128]{1,0:T(8,128)(2,1)S(1)} collective-permute-done((s16[1824,128]{1,0:T(8,128)(2,1)S(1)}, s16[1824,128]{1,0:T(8,128)(2,1)S(1)}, u32[]{:S(2)}, u32[]{:S(2)}) %collective-permute-start.8) | collective-permute-done | bytes 466976 | tf_op jit(solution)/shard_map/ppermute | solution.py:354
  70.1 6.7 %collective-permute-done.9.refs_1_ = s16[1040,128]{1,0:T(8,128)(2,1)S(1)} collective-permute-done((s16[1040,128]{1,0:T(8,128)(2,1)S(1)}, s16[1040,128]{1,0:T(8,128)(2,1)S(1)}, u32[]{:S(2)}, u32[]{:S(2)}) %collective-permute-start.9) | collective-permute-done | bytes 266272 | tf_op jit(solution)/shard_map/ppermute | solution.py:354
  77.1 3.5 %collective-permute-start.15 = (s16[1040,128]{1,0:T(8,128)(2,1)S(1)}, s16[1040,128]{1,0:T(8,128)(2,1)}, u32[]{:S(2)}, u32[]{:S(2)}) collective-permute-start(s16[1040,128]{1,0:T(8,128)(2,1)S(1)} %combine.10.refs_0_), channel_id=1, source_target_pairs={{0,16},{1,17},{2,18},{3,19},{4,20},{5,21},{6,22},{7,23},{8,24},{9,... | collective-permute-start | bytes 798728 | tf_op jit(solution)/shard_map/ppermute | solution.py:350
  80.6 2.3 %partial_sums.6 = (f32[1024,128]{1,0:T(8,128)S(1)}, f32[1024,128]{1,0:T(8,128)S(1)}, s16[2080,128]{1,0:T(8,128)(2,1)}) custom-call(s32[1]{0:T(128)} %bitcast.6.flag_ref, bf16[768,512]{1,0:T(8,128)(2,1)S(1)} %build_weights.1.w_ref, bf16[192,1920]{1,0:T(8,128)(2,1)S(1)} %pad_maximum_fusion.2.refs_0_, bf16[192,1920]{1,0:T(8,128)(2,1)S(1)} %collective-permute-done.11.refs_1_, ...), custom_call_target="tpu_custom_call" | custom-call | flops 805306368 | bytes 2883584 | tf_op jit(solution)/shard_map/partial_sums/pallas_call | solution.py:170
  82.9 1.3 partial_sums.7
  85.0 0.9 collective-permute-start.21
  85.9 1.0 collective-permute-done.15.refs_2_
  87.4 3.7 %collective-permute-done.21.refs_6_ = s16[912,128]{1,0:T(8,128)(2,1)S(1)} collective-permute-done((s16[912,128]{1,0:T(8,128)(2,1)S(1)}, s16[912,128]{1,0:T(8,128)(2,1)S(1)}, u32[]{:S(2)}, u32[]{:S(2)}) %collective-permute-start.21) | collective-permute-done | bytes 233504 | tf_op jit(solution)/shard_map/ppermute | solution.py:350
  91.2 1.2 collective-permute-done.19.refs_0_
  92.4 0.8 collective-permute-start.27
  93.5 2.5 %collective-permute-start.23 = (s16[1040,128]{1,0:T(8,128)(2,1)S(1)}, s16[1040,128]{1,0:T(8,128)(2,1)S(1)}, u32[]{:S(2)}, u32[]{:S(2)}) collective-permute-start(s16[1040,128]{1,0:T(8,128)(2,1)S(1)} %combine.12), channel_id=1, source_target_pairs={{0,4},{1,5},{2,6},{3,7},{4,0},{5,1},{6,2},{7,3},{8,12},{9,13},{10,... | collective-permute-start | bytes 798728 | tf_op jit(solution)/shard_map/ppermute | solution.py:354
  96.0 12.8 %covariance.1 = f32[13456,128]{1,0:T(8,128)} custom-call(s32[8]{0:T(128)S(1)} %stack.97.place_ref, s16[1040,128]{1,0:T(8,128)(2,1)S(1)} %combine.10.refs_0_, s16[1040,128]{1,0:T(8,128)(2,1)S(1)} %collective-permute-done.14.refs_1_, s16[1040,128]{1,0:T(8,128)(2,1)} %collective-permute-done.15.refs_2_, s16[1040,128]{1,0:T(8,128)(2,1)S(1)} %collective-permute-done.16.refs_3_, ...), custom_call_target="tpu_custom_call" | custom-call | flops 15432417280 | bytes 6889472 | tf_op jit(solution)/shard_map/covariance/pallas_call | solution.py:311
  108.8 1.7 %collective-permute-done.27.refs_0_ = s16[1824,128]{1,0:T(8,128)(2,1)S(1)} collective-permute-done((s16[1824,128]{1,0:T(8,128)(2,1)}, s16[1824,128]{1,0:T(8,128)(2,1)S(1)}, u32[]{:S(2)}, u32[]{:S(2)}) %collective-permute-start.27) | collective-permute-done | bytes 466976 | tf_op jit(solution)/shard_map/ppermute | solution.py:354
  110.7 0.6 collective-permute-start.28
  111.6 1.4 %collective-permute-start.25 = (s16[1040,128]{1,0:T(8,128)(2,1)S(1)}, s16[1040,128]{1,0:T(8,128)(2,1)S(1)}, u32[]{:S(2)}, u32[]{:S(2)}) collective-permute-start(s16[1040,128]{1,0:T(8,128)(2,1)S(1)} %combine.13.refs_0_), channel_id=1, source_target_pairs={{0,16},{1,17},{2,18},{3,19},{4,20},{5,21},{6,22},{7,23},{8,24},{9,... | collective-permute-start | bytes 798728 | tf_op jit(solution)/shard_map/ppermute | solution.py:350
  113.0 9.6 %collective-permute-done.28.refs_1_ = s16[912,128]{1,0:T(8,128)(2,1)S(1)} collective-permute-done((s16[912,128]{1,0:T(8,128)(2,1)S(1)}, s16[912,128]{1,0:T(8,128)(2,1)S(1)}, u32[]{:S(2)}, u32[]{:S(2)}) %collective-permute-start.28) | collective-permute-done | bytes 233504 | tf_op jit(solution)/shard_map/ppermute | solution.py:354
  122.8 1.5 %collective-permute-start.30 = (s16[912,128]{1,0:T(8,128)(2,1)S(1)}, s16[912,128]{1,0:T(8,128)(2,1)S(1)}, u32[]{:S(2)}, u32[]{:S(2)}) collective-permute-start(s16[912,128]{1,0:T(8,128)(2,1)S(1)} %combine.15.refs_4_), channel_id=1, source_target_pairs={{0,16},{1,17},{2,18},{3,19},{4,20},{5,21},{6,22},{7,23},{8,24},{9,... | collective-permute-start | bytes 700424 | tf_op jit(solution)/shard_map/ppermute | solution.py:350
  124.8 5.7 %collective-permute-done.30.refs_6_ = s16[912,128]{1,0:T(8,128)(2,1)S(1)} collective-permute-done((s16[912,128]{1,0:T(8,128)(2,1)S(1)}, s16[912,128]{1,0:T(8,128)(2,1)S(1)}, u32[]{:S(2)}, u32[]{:S(2)}) %collective-permute-start.30) | collective-permute-done | bytes 233504 | tf_op jit(solution)/shard_map/ppermute | solution.py:350
  130.6 1.4 %collective-permute-done.31.refs_7_ = s16[912,128]{1,0:T(8,128)(2,1)S(1)} collective-permute-done((s16[912,128]{1,0:T(8,128)(2,1)S(1)}, s16[912,128]{1,0:T(8,128)(2,1)S(1)}, u32[]{:S(2)}, u32[]{:S(2)}) %collective-permute-start.31) | collective-permute-done | bytes 233504 | tf_op jit(solution)/shard_map/ppermute | solution.py:350
  132.0 3.8 %marginal.1 = f32[128,7424]{1,0:T(8,128)} custom-call(s32[8]{0:T(128)S(1)} %stack.83.place_ref, s16[1040,128]{1,0:T(8,128)(2,1)S(1)} %combine.13.refs_0_, s16[1040,128]{1,0:T(8,128)(2,1)S(1)} %collective-permute-done.24.refs_1_, s16[1040,128]{1,0:T(8,128)(2,1)S(1)} %collective-permute-done.25.refs_2_, s16[1040,128]{1,0:T(8,128)(2,1)S(1)} %collective-permute-done.26.refs_3_, ...), custom_call_target="tpu_custom_call" | custom-call | flops 3801088 | bytes 5701632 | tf_op jit(solution)/shard_map/marginal/pallas_call | solution.py:238
  (76 shorter events, 5.6 us)
Async XLA Ops:
  0.6 1.5 %copy-start.9 = (bf16[96,116]{1,0:T(8,128)(2,1)S(1)}, bf16[96,116]{1,0:T(8,128)(2,1)}, u32[]{:S(2)}) copy-start(bf16[96,116]{1,0:T(8,128)(2,1)} %param.7) | copy-start | bytes 66820
  2.1 1.6 %copy-start.10 = (s32[128,32]{0,1:T(8,128)S(1)}, s32[128,32]{0,1:T(8,128)}, u32[]{:S(2)}) copy-start(s32[128,32]{0,1:T(8,128)} %param.9) | copy-start | bytes 49156
  2.1 1.6 %copy-start.11 = (s32[128,32]{0,1:T(8,128)S(1)}, s32[128,32]{0,1:T(8,128)}, u32[]{:S(2)}) copy-start(s32[128,32]{0,1:T(8,128)} %param.8) | copy-start | bytes 49156
  3.2 2.5 %copy-start.5 = (bf16[96,7424]{1,0:T(8,128)(2,1)S(1)}, bf16[96,7424]{1,0:T(8,128)(2,1)}, u32[]{:S(2)}) copy-start(bf16[96,7424]{1,0:T(8,128)(2,1)} %param.5) | copy-start | bytes 4276228
  3.2 2.5 %collective-permute-start = (bf16[96,3840]{1,0:T(8,128)(2,1)}, bf16[96,3840]{1,0:T(8,128)(2,1)S(1)}, u32[]{:S(2)}, u32[]{:S(2)}) collective-permute-start(bf16[96,3840]{1,0:T(8,128)(2,1)} %get-tuple-element.65), channel_id=1, source_target_pairs={{0,8},{1,9},{2,10},{3,11},{4,12},{5,13},{6,14},{7,15},{8,0},{9,1},... | collective-permute-start | bytes 2211848 | tf_op jit(solution)/shard_map/ppermute | solution.py:350
  5.8 22.9 %collective-permute-start.10 = (bf16[96,3712]{1,0:T(8,128)(2,1)S(1)}, bf16[96,3712]{1,0:T(8,128)(2,1)S(1)}, u32[]{:S(2)}, u32[]{:S(2)}) collective-permute-start(bf16[96,3712]{1,0:T(8,128)(2,1)S(1)} %constant_dynamic-slice_fusion.3), channel_id=1, source_target_pairs={{0,8},{1,9},{2,10},{3,11},{4,12},{5,13},{6,14},{7,15},{8,0},{9,1},... | collective-permute-start | bytes 2138120 | tf_op jit(solution)/shard_map/ppermute | solution.py:350
  6.3 9.1 %copy-start.6 = (bf16[96,7424]{1,0:T(8,128)(2,1)S(1)}, bf16[96,7424]{1,0:T(8,128)(2,1)}, u32[]{:S(2)}) copy-start(bf16[96,7424]{1,0:T(8,128)(2,1)} %param.5) | copy-start | bytes 4276228
  6.4 19.7 %collective-permute-start.3 = (bf16[192,1920]{1,0:T(8,128)(2,1)S(1)}, bf16[192,1920]{1,0:T(8,128)(2,1)S(1)}, u32[]{:S(2)}, u32[]{:S(2)}) collective-permute-start(bf16[192,1920]{1,0:T(8,128)(2,1)S(1)} %pad_maximum_fusion), channel_id=1, source_target_pairs={{0,16},{1,17},{2,18},{3,19},{4,20},{5,21},{6,22},{7,23},{8,24},{9,... | collective-permute-start | bytes 2211848 | tf_op jit(solution)/shard_map/ppermute | solution.py:350
  9.0 5.2 %collective-permute-start.1 = (s32[64,128]{1,0:T(8,128)S(1)}, s32[64,128]{1,0:T(8,128)S(1)}, u32[]{:S(2)}, u32[]{:S(2)}) collective-permute-start(s32[64,128]{1,0:T(8,128)S(1)} %pad_add_fusion.2), channel_id=1, source_target_pairs={{0,4},{1,5},{2,6},{3,7},{4,0},{5,1},{6,2},{7,3},{8,12},{9,13},{10,... | collective-permute-start | bytes 98312 | tf_op jit(solution)/shard_map/ppermute | solution.py:354
  11.7 20.8 %collective-permute-start.4 = (bf16[192,1920]{1,0:T(8,128)(2,1)S(1)}, bf16[192,1920]{1,0:T(8,128)(2,1)}, u32[]{:S(2)}, u32[]{:S(2)}) collective-permute-start(bf16[192,1920]{1,0:T(8,128)(2,1)S(1)} %pad_maximum_fusion.1.refs_0_), channel_id=1, source_target_pairs={{0,1},{1,0},{2,3},{3,2},{4,5},{5,4},{6,7},{7,6},{8,9},{9,8},{10,11... | collective-permute-start | bytes 2211848 | tf_op jit(solution)/shard_map/ppermute | solution.py:350
  14.2 4.3 %collective-permute-start.2 = (s32[64,256]{1,0:T(8,128)S(1)}, s32[64,256]{1,0:T(8,128)S(1)}, u32[]{:S(2)}, u32[]{:S(2)}) collective-permute-start(s32[64,256]{1,0:T(8,128)S(1)} %pad_add_fusion.1), channel_id=1, source_target_pairs={{0,2},{1,3},{2,0},{3,1},{4,6},{5,7},{6,4},{7,5},{8,10},{9,11},{10,... | collective-permute-start | bytes 196616 | tf_op jit(solution)/shard_map/ppermute | solution.py:354
  26.8 12.2 %collective-permute-start.5 = (bf16[192,1024]{1,0:T(8,128)(2,1)}, bf16[192,1024]{1,0:T(8,128)(2,1)S(1)}, u32[]{:S(2)}, u32[]{:S(2)}) collective-permute-start(bf16[192,1024]{1,0:T(8,128)(2,1)} %slice.16), channel_id=1, source_target_pairs={{0,1},{1,0},{2,3},{3,2},{4,5},{5,4},{6,7},{7,6},{8,9},{9,8},{10,11... | collective-permute-start | bytes 1179656 | tf_op jit(solution)/shard_map/ppermute | solution.py:350
  30.3 20.5 %collective-permute-start.11 = (bf16[192,1920]{1,0:T(8,128)(2,1)}, bf16[192,1920]{1,0:T(8,128)(2,1)S(1)}, u32[]{:S(2)}, u32[]{:S(2)}) collective-permute-start(bf16[192,1920]{1,0:T(8,128)(2,1)} %pad_maximum_fusion.3), channel_id=1, source_target_pairs={{0,16},{1,17},{2,18},{3,19},{4,20},{5,21},{6,22},{7,23},{8,24},{9,... | collective-permute-start | bytes 2211848 | tf_op jit(solution)/shard_map/ppermute | solution.py:350
  31.9 14.5 %collective-permute-start.6 = (bf16[192,896]{1,0:T(8,128)(2,1)S(1)}, bf16[192,896]{1,0:T(8,128)(2,1)S(1)}, u32[]{:S(2)}, u32[]{:S(2)}) collective-permute-start(bf16[192,896]{1,0:T(8,128)(2,1)S(1)} %slice.17), channel_id=1, source_target_pairs={{0,1},{1,0},{2,3},{3,2},{4,5},{5,4},{6,7},{7,6},{8,9},{9,8},{10,11... | collective-permute-start | bytes 1032200 | tf_op jit(solution)/shard_map/ppermute | solution.py:350
  39.0 4.6 %copy-start.7 = (bf16[96,1920]{1,0:T(8,128)(2,1)S(1)}, bf16[96,1920]{1,0:T(8,128)(2,1)}, u32[]{:S(2)}) copy-start(bf16[96,1920]{1,0:T(8,128)(2,1)} %get-tuple-element.55) | copy-start | bytes 1105924
  39.0 4.6 %copy-start.8 = (bf16[96,1920]{1,0:T(8,128)(2,1)S(1)}, bf16[96,1920]{1,0:T(8,128)(2,1)}, u32[]{:S(2)}) copy-start(bf16[96,1920]{1,0:T(8,128)(2,1)} %get-tuple-element.63) | copy-start | bytes 1105924
  41.7 18.0 %collective-permute-start.7 = (s16[2080,128]{1,0:T(8,128)(2,1)S(1)}, s16[2080,128]{1,0:T(8,128)(2,1)S(1)}, u32[]{:S(2)}, u32[]{:S(2)}) collective-permute-start(s16[2080,128]{1,0:T(8,128)(2,1)S(1)} %get-tuple-element.34), channel_id=1, source_target_pairs={{0,2},{1,3},{2,0},{3,1},{4,6},{5,7},{6,4},{7,5},{8,10},{9,11},{10,... | collective-permute-start | bytes 1597448 | tf_op jit(solution)/shard_map/ppermute | solution.py:354
  43.7 36.9 %collective-permute-start.12 = (bf16[192,1920]{1,0:T(8,128)(2,1)S(1)}, bf16[192,1920]{1,0:T(8,128)(2,1)S(1)}, u32[]{:S(2)}, u32[]{:S(2)}) collective-permute-start(bf16[192,1920]{1,0:T(8,128)(2,1)S(1)} %pad_maximum_fusion.2.refs_0_), channel_id=1, source_target_pairs={{0,1},{1,0},{2,3},{3,2},{4,5},{5,4},{6,7},{7,6},{8,9},{9,8},{10,11... | collective-permute-start | bytes 2211848 | tf_op jit(solution)/shard_map/ppermute | solution.py:350
  48.9 21.0 %collective-permute-start.8 = (s16[1824,128]{1,0:T(8,128)(2,1)S(1)}, s16[1824,128]{1,0:T(8,128)(2,1)S(1)}, u32[]{:S(2)}, u32[]{:S(2)}) collective-permute-start(s16[1824,128]{1,0:T(8,128)(2,1)S(1)} %get-tuple-element.36), channel_id=1, source_target_pairs={{0,2},{1,3},{2,0},{3,1},{4,6},{5,7},{6,4},{7,5},{8,10},{9,11},{10,... | collective-permute-start | bytes 1400840 | tf_op jit(solution)/shard_map/ppermute | solution.py:354
  50.9 29.7 %collective-permute-start.13 = (bf16[192,1024]{1,0:T(8,128)(2,1)S(1)}, bf16[192,1024]{1,0:T(8,128)(2,1)S(1)}, u32[]{:S(2)}, u32[]{:S(2)}) collective-permute-start(bf16[192,1024]{1,0:T(8,128)(2,1)S(1)} %slice.18), channel_id=1, source_target_pairs={{0,1},{1,0},{2,3},{3,2},{4,5},{5,4},{6,7},{7,6},{8,9},{9,8},{10,11... | collective-permute-start | bytes 1179656 | tf_op jit(solution)/shard_map/ppermute | solution.py:350
  52.5 30.4 %collective-permute-start.17 = (bf16[192,896]{1,0:T(8,128)(2,1)S(1)}, bf16[192,896]{1,0:T(8,128)(2,1)S(1)}, u32[]{:S(2)}, u32[]{:S(2)}) collective-permute-start(bf16[192,896]{1,0:T(8,128)(2,1)S(1)} %slice.19), channel_id=1, source_target_pairs={{0,1},{1,0},{2,3},{3,2},{4,5},{5,4},{6,7},{7,6},{8,9},{9,8},{10,11... | collective-permute-start | bytes 1032200 | tf_op jit(solution)/shard_map/ppermute | solution.py:350
  59.9 17.0 %collective-permute-start.9 = (s16[1040,128]{1,0:T(8,128)(2,1)S(1)}, s16[1040,128]{1,0:T(8,128)(2,1)S(1)}, u32[]{:S(2)}, u32[]{:S(2)}) collective-permute-start(s16[1040,128]{1,0:T(8,128)(2,1)S(1)} %combine.8), channel_id=1, source_target_pairs={{0,4},{1,5},{2,6},{3,7},{4,0},{5,1},{6,2},{7,3},{8,12},{9,13},{10,... | collective-permute-start | bytes 798728 | tf_op jit(solution)/shard_map/ppermute | solution.py:354
  70.1 14.2 %collective-permute-start.18 = (s16[912,128]{1,0:T(8,128)(2,1)S(1)}, s16[912,128]{1,0:T(8,128)(2,1)S(1)}, u32[]{:S(2)}, u32[]{:S(2)}) collective-permute-start(s16[912,128]{1,0:T(8,128)(2,1)S(1)} %combine.9), channel_id=1, source_target_pairs={{0,4},{1,5},{2,6},{3,7},{4,0},{5,1},{6,2},{7,3},{8,12},{9,13},{10,... | collective-permute-start | bytes 700424 | tf_op jit(solution)/shard_map/ppermute | solution.py:354
  77.1 9.7 %collective-permute-start.15 = (s16[1040,128]{1,0:T(8,128)(2,1)S(1)}, s16[1040,128]{1,0:T(8,128)(2,1)}, u32[]{:S(2)}, u32[]{:S(2)}) collective-permute-start(s16[1040,128]{1,0:T(8,128)(2,1)S(1)} %combine.10.refs_0_), channel_id=1, source_target_pairs={{0,16},{1,17},{2,18},{3,19},{4,20},{5,21},{6,22},{7,23},{8,24},{9,... | collective-permute-start | bytes 798728 | tf_op jit(solution)/shard_map/ppermute | solution.py:350
  82.9 9.5 %collective-permute-start.19 = (s16[2080,128]{1,0:T(8,128)(2,1)}, s16[2080,128]{1,0:T(8,128)(2,1)S(1)}, u32[]{:S(2)}, u32[]{:S(2)}) collective-permute-start(s16[2080,128]{1,0:T(8,128)(2,1)} %get-tuple-element.48), channel_id=1, source_target_pairs={{0,2},{1,3},{2,0},{3,1},{4,6},{5,7},{6,4},{7,5},{8,10},{9,11},{10,... | collective-permute-start | bytes 1597448 | tf_op jit(solution)/shard_map/ppermute | solution.py:354
  84.2 0.8 copy-start
  84.2 1.6 %copy-start.2 = (f32[896,128]{1,0:T(8,128)}, f32[896,128]{1,0:T(8,128)S(1)}, u32[]{:S(2)}) copy-start(f32[896,128]{1,0:T(8,128)S(1)} %get-tuple-element.45.own_ref) | copy-start | bytes 1376260
  84.3 6.8 %copy-start.4 = (s16[1824,128]{1,0:T(8,128)(2,1)}, s16[1824,128]{1,0:T(8,128)(2,1)S(1)}, u32[]{:S(2)}) copy-start(s16[1824,128]{1,0:T(8,128)(2,1)S(1)} %get-tuple-element.51) | copy-start | bytes 1400836
  85.0 6.1 %collective-permute-start.21 = (s16[912,128]{1,0:T(8,128)(2,1)S(1)}, s16[912,128]{1,0:T(8,128)(2,1)S(1)}, u32[]{:S(2)}, u32[]{:S(2)}) collective-permute-start(s16[912,128]{1,0:T(8,128)(2,1)S(1)} %combine.11.refs_4_), channel_id=1, source_target_pairs={{0,16},{1,17},{2,18},{3,19},{4,20},{5,21},{6,22},{7,23},{8,24},{9,... | collective-permute-start | bytes 700424 | tf_op jit(solution)/shard_map/ppermute | solution.py:350
  85.9 10.1 %collective-permute-start.14 = (s16[1040,128]{1,0:T(8,128)(2,1)S(1)}, s16[1040,128]{1,0:T(8,128)(2,1)S(1)}, u32[]{:S(2)}, u32[]{:S(2)}) collective-permute-start(s16[1040,128]{1,0:T(8,128)(2,1)S(1)} %combine.10.refs_0_), channel_id=1, source_target_pairs={{0,8},{1,9},{2,10},{3,11},{4,12},{5,13},{6,14},{7,15},{8,0},{9,1},... | collective-permute-start | bytes 798728 | tf_op jit(solution)/shard_map/ppermute | solution.py:350
  86.9 9.1 %collective-permute-start.16 = (s16[1040,128]{1,0:T(8,128)(2,1)}, s16[1040,128]{1,0:T(8,128)(2,1)S(1)}, u32[]{:S(2)}, u32[]{:S(2)}) collective-permute-start(s16[1040,128]{1,0:T(8,128)(2,1)} %collective-permute-done.15.refs_2_), channel_id=1, source_target_pairs={{0,8},{1,9},{2,10},{3,11},{4,12},{5,13},{6,14},{7,15},{8,0},{9,1},... | collective-permute-start | bytes 798728 | tf_op jit(solution)/shard_map/ppermute | solution.py:350
  86.9 6.6 %collective-permute-start.20 = (s16[912,128]{1,0:T(8,128)(2,1)S(1)}, s16[912,128]{1,0:T(8,128)(2,1)S(1)}, u32[]{:S(2)}, u32[]{:S(2)}) collective-permute-start(s16[912,128]{1,0:T(8,128)(2,1)S(1)} %combine.11.refs_4_), channel_id=1, source_target_pairs={{0,8},{1,9},{2,10},{3,11},{4,12},{5,13},{6,14},{7,15},{8,0},{9,1},... | collective-permute-start | bytes 700424 | tf_op jit(solution)/shard_map/ppermute | solution.py:350
  91.1 4.9 %collective-permute-start.22 = (s16[912,128]{1,0:T(8,128)(2,1)S(1)}, s16[912,128]{1,0:T(8,128)(2,1)S(1)}, u32[]{:S(2)}, u32[]{:S(2)}) collective-permute-start(s16[912,128]{1,0:T(8,128)(2,1)S(1)} %collective-permute-done.21.refs_6_), channel_id=1, source_target_pairs={{0,8},{1,9},{2,10},{3,11},{4,12},{5,13},{6,14},{7,15},{8,0},{9,1},... | collective-permute-start | bytes 700424 | tf_op jit(solution)/shard_map/ppermute | solution.py:350
  92.4 18.1 %collective-permute-start.27 = (s16[1824,128]{1,0:T(8,128)(2,1)}, s16[1824,128]{1,0:T(8,128)(2,1)S(1)}, u32[]{:S(2)}, u32[]{:S(2)}) collective-permute-start(s16[1824,128]{1,0:T(8,128)(2,1)} %copy-done.4), channel_id=1, source_target_pairs={{0,2},{1,3},{2,0},{3,1},{4,6},{5,7},{6,4},{7,5},{8,10},{9,11},{10,... | collective-permute-start | bytes 1400840 | tf_op jit(solution)/shard_map/ppermute | solution.py:354
  93.5 17.1 %copy-start.1 = (f32[896,128]{1,0:T(8,128)S(1)}, f32[896,128]{1,0:T(8,128)}, u32[]{:S(2)}) copy-start(f32[896,128]{1,0:T(8,128)} %copy-done) | copy-start | bytes 1376260
  93.5 17.9 %collective-permute-start.23 = (s16[1040,128]{1,0:T(8,128)(2,1)S(1)}, s16[1040,128]{1,0:T(8,128)(2,1)S(1)}, u32[]{:S(2)}, u32[]{:S(2)}) collective-permute-start(s16[1040,128]{1,0:T(8,128)(2,1)S(1)} %combine.12), channel_id=1, source_target_pairs={{0,4},{1,5},{2,6},{3,7},{4,0},{5,1},{6,2},{7,3},{8,12},{9,13},{10,... | collective-permute-start | bytes 798728 | tf_op jit(solution)/shard_map/ppermute | solution.py:354
  108.8 13.8 %copy-start.3 = (f32[896,128]{1,0:T(8,128)S(1)}, f32[896,128]{1,0:T(8,128)}, u32[]{:S(2)}) copy-start(f32[896,128]{1,0:T(8,128)} %copy-done.2) | copy-start | bytes 1376260
  110.7 11.9 %collective-permute-start.28 = (s16[912,128]{1,0:T(8,128)(2,1)S(1)}, s16[912,128]{1,0:T(8,128)(2,1)S(1)}, u32[]{:S(2)}, u32[]{:S(2)}) collective-permute-start(s16[912,128]{1,0:T(8,128)(2,1)S(1)} %combine.14), channel_id=1, source_target_pairs={{0,4},{1,5},{2,6},{3,7},{4,0},{5,1},{6,2},{7,3},{8,12},{9,13},{10,... | collective-permute-start | bytes 700424 | tf_op jit(solution)/shard_map/ppermute | solution.py:354
  111.6 12.7 %collective-permute-start.25 = (s16[1040,128]{1,0:T(8,128)(2,1)S(1)}, s16[1040,128]{1,0:T(8,128)(2,1)S(1)}, u32[]{:S(2)}, u32[]{:S(2)}) collective-permute-start(s16[1040,128]{1,0:T(8,128)(2,1)S(1)} %combine.13.refs_0_), channel_id=1, source_target_pairs={{0,16},{1,17},{2,18},{3,19},{4,20},{5,21},{6,22},{7,23},{8,24},{9,... | collective-permute-start | bytes 798728 | tf_op jit(solution)/shard_map/ppermute | solution.py:350
  122.8 7.7 %collective-permute-start.30 = (s16[912,128]{1,0:T(8,128)(2,1)S(1)}, s16[912,128]{1,0:T(8,128)(2,1)S(1)}, u32[]{:S(2)}, u32[]{:S(2)}) collective-permute-start(s16[912,128]{1,0:T(8,128)(2,1)S(1)} %combine.15.refs_4_), channel_id=1, source_target_pairs={{0,16},{1,17},{2,18},{3,19},{4,20},{5,21},{6,22},{7,23},{8,24},{9,... | collective-permute-start | bytes 700424 | tf_op jit(solution)/shard_map/ppermute | solution.py:350
  124.3 6.3 %collective-permute-start.24 = (s16[1040,128]{1,0:T(8,128)(2,1)S(1)}, s16[1040,128]{1,0:T(8,128)(2,1)S(1)}, u32[]{:S(2)}, u32[]{:S(2)}) collective-permute-start(s16[1040,128]{1,0:T(8,128)(2,1)S(1)} %combine.13.refs_0_), channel_id=1, source_target_pairs={{0,8},{1,9},{2,10},{3,11},{4,12},{5,13},{6,14},{7,15},{8,0},{9,1},... | collective-permute-start | bytes 798728 | tf_op jit(solution)/shard_map/ppermute | solution.py:350
  124.3 7.7 %collective-permute-start.26 = (s16[1040,128]{1,0:T(8,128)(2,1)S(1)}, s16[1040,128]{1,0:T(8,128)(2,1)S(1)}, u32[]{:S(2)}, u32[]{:S(2)}) collective-permute-start(s16[1040,128]{1,0:T(8,128)(2,1)S(1)} %collective-permute-done.25.refs_2_), channel_id=1, source_target_pairs={{0,8},{1,9},{2,10},{3,11},{4,12},{5,13},{6,14},{7,15},{8,0},{9,1},... | collective-permute-start | bytes 798728 | tf_op jit(solution)/shard_map/ppermute | solution.py:350
  124.8 5.8 %collective-permute-start.29 = (s16[912,128]{1,0:T(8,128)(2,1)S(1)}, s16[912,128]{1,0:T(8,128)(2,1)S(1)}, u32[]{:S(2)}, u32[]{:S(2)}) collective-permute-start(s16[912,128]{1,0:T(8,128)(2,1)S(1)} %combine.15.refs_4_), channel_id=1, source_target_pairs={{0,8},{1,9},{2,10},{3,11},{4,12},{5,13},{6,14},{7,15},{8,0},{9,1},... | collective-permute-start | bytes 700424 | tf_op jit(solution)/shard_map/ppermute | solution.py:350
  130.5 1.5 %collective-permute-start.31 = (s16[912,128]{1,0:T(8,128)(2,1)S(1)}, s16[912,128]{1,0:T(8,128)(2,1)S(1)}, u32[]{:S(2)}, u32[]{:S(2)}) collective-permute-start(s16[912,128]{1,0:T(8,128)(2,1)S(1)} %collective-permute-done.30.refs_6_), channel_id=1, source_target_pairs={{0,8},{1,9},{2,10},{3,11},{4,12},{5,13},{6,14},{7,15},{8,0},{9,1},... | collective-permute-start | bytes 700424 | tf_op jit(solution)/shard_map/ppermute | solution.py:350

commit v10 on v9

--- a/solution.py
+++ b/solution.py
@@ -323,7 +323,7 @@
         ),
         out_shape=jax.ShapeDtypeStruct(shape, jnp.float32),
         compiler_params=params(),
-        cost_estimate=cost(LANES * ages * ages * rank * 140, shape[0] * shape[1] * 4),
+        cost_estimate=cost(LANES * ages * ages * rank * 16, shape[0] * shape[1] * 4),
         name="covariance",
     )(places, *pieces)
 
@@ -368,21 +368,24 @@
     def exchange(array, *more):
         return [half(array, core, *more), move(half(array, (core + 1) % CORES, *more), 0, 1)]
 
-    def along_x(both):
+    def along_x(both, first, count):
         tiles = both[0].shape[1] // LANES
-        size = (rows, each_of(tiles) * LANES)
+        size = (rows, count * LANES)
 
         def part(group):
-            return jnp.concatenate([lax.dynamic_slice(b, (0, start_of(group, tiles) * LANES), size) for b in both], axis=0)
+            start = (start_of(group, tiles) + first) * LANES
+            return jnp.concatenate([lax.dynamic_slice(b, (0, start), size) for b in both], axis=0)
 
         cut = [part((x + dx) % xs) for dx in range(xs)]
         return [move(value, dx, 0) for dx, value in enumerate(cut)], cut[-1]
 
     load_both = exchange(factors, last_tile)
-    load_x, load_cut = along_x(load_both)
+    load_tiles = split(each_of(load_both[0].shape[1] // LANES), LOAD_FIRST)
+    xa, cut_a = along_x(load_both, 0, load_tiles[0])
+    xb, _ = along_x(load_both, *load_tiles)
 
     queries = jnp.concatenate([intersection_tracts.T, intersection_weights.T], axis=0)
-    queries = after(queries, load_cut)
+    queries = after(queries, cut_a)
     queries = jnp.concatenate([queries, z_swap(queries, 2)], axis=1)
     queries = jnp.concatenate([queries, z_swap(queries, 1)], axis=1)
     bases = jnp.stack([
@@ -423,13 +426,11 @@
 
     mean_width = estimates.shape[1] // LANES // CORES
     load_width = factors.shape[1] // LANES // CORES + 1
-    load_tiles = split(each_of(load_width), LOAD_FIRST)
     mean_tiles = split(each_of(mean_width), MEAN_FIRST)
     (first_a, first_b), (first_c, first_d) = load_tiles, mean_tiles
-    mean_x, _ = along_x(exchange(after(estimates, load_both[1])))
-    load_y = along_y(load_x[0], 0, first_a + first_b)
-    data_a = merge([load_y] + [along_y(value, 0, first_a, w) for value in load_x[1:]])
-    data_b = merge([later(load_y, first_a)] + [along_y(value, first_a, first_b) for value in load_x[1:]])
+    mean_x, _ = along_x(exchange(after(estimates, load_both[1])), 0, first_c + first_d)
+    data_a = merge([along_y(xa[0], 0, first_a)] + [along_y(value, 0, first_a, w) for value in xa[1:]])
+    data_b = merge([along_y(value, 0, first_b, xa[-1]) for value in xb])
     own_a, near_a, middle_a, far_a = along_z(data_a, first_a, False)
     mean_y = along_y(mean_x[0], 0, first_c + first_d, data_a[-1][0])
     there = data_b[-1][0]

time: 136 us -> 141 us (1.037)
  waiting for transfers between devices: 60.8 us -> 68.6 us
  starting transfers between devices: 34.9 us -> 38.8 us
  local copies, waits for them, and re-layouts: 5.21 us -> 2.34 us
  Pallas kernels: 31.9 us -> 30 us
  other arithmetic: 2.16 us -> 0.44 us
    ppermute x22 -> x24, waiting for transfers between devices: 24.1 us -> 38.6 us  [move(): return lax.ppermute(value, ('geo', 'dist'), perm)]
    ppermute x10, waiting for transfers between devices: 36.7 us -> 30 us  [z_swap(): return lax.ppermute(value, 'dist', perm)]
    ppermute x10, starting transfers between devices: 13.9 us -> 19.1 us  [z_swap(): return lax.ppermute(value, 'dist', perm)]
    pallas_call x4, Pallas kernels: 8.74 us -> 6.45 us  [partial_sums(): pl.pallas_call(functools.partial(sums_kernel, offsets, has_var), grid_spe...]
    dynamic_slice x4 -> x6, local copies, waits for them, and re-layouts: 2.04 us -> 0.52 us  [part(): lax.dynamic_slice(b, (0, start), size)]
    ppermute x22 -> x24, starting transfers between devices: 21 us -> 19.7 us  [move(): return lax.ppermute(value, ('geo', 'dist'), perm)]
  transfers between devices with their start and end apart: 32 -> 34, of which waited for: 16 -> 14; matrix products, arithmetic and copies ran while one was open for 3% -> 1% of each run, Pallas kernels for 21% -> 19%
where the time goes in v10:
time: 141 us
  waiting for transfers between devices  68.6 us (49%)
  starting transfers between devices  38.8 us (28%)
  Pallas kernels  30 us (21%)
  local copies, waits for them, and re-layouts  2.34 us (2%)
    ppermute x24, waiting for transfers between devices, move(): return lax.ppermute(value, ('geo', 'dist'), perm)  38.6 us
    ppermute x10, waiting for transfers between devices, z_swap(): return lax.ppermute(value, 'dist', perm)  30 us
    ppermute x24, starting transfers between devices, move(): return lax.ppermute(value, ('geo', 'dist'), perm)  19.7 us
    ppermute x10, starting transfers between devices, z_swap(): return lax.ppermute(value, 'dist', perm)  19.1 us
    pallas_call x1, Pallas kernels, covariance(): pl.pallas_call(functools.partial(covariance_kernel, tiles, total, ages, r...  13.2 us
    pallas_call x4, Pallas kernels, partial_sums(): pl.pallas_call(functools.partial(sums_kernel, offsets, has_var), grid_spe...  6.45 us
    pallas_call x1, Pallas kernels, build_weights(): pl.pallas_call(functools.partial(weights_kernel, rows), grid_spec=pltpu.P...  4.87 us
    pallas_call x1, Pallas kernels, marginal(): pl.pallas_call(functools.partial(marginal_kernel, tiles), grid_spec=pltpu...  3.83 us
  transfers between devices with their start and end apart: 34, of which 14 were waited for; matrix products, arithmetic and copies ran while one was open for 1% of the time, Pallas kernels for 19%

profile of v10, /device:TPU:0, one launch (start us, length us, event | category | flops | bytes accessed | tf_op | source)
XLA Modules:
  0.0 141.2 jit_solution(2951493544370526357)
XLA Ops:
  0.7 1.4 %constant_dynamic-slice_fusion.14 = (bf16[96,3712]{1,0:T(8,128)(2,1)S(1)}, bf16[96,3712]{1,0:T(8,128)(2,1)S(1)}) fusion(bf16[96,7424]{1,0:T(8,128)(2,1)} %param.6, s32[]{:T(128)S(6)} %select_n.178, s32[]{:T(128)S(6)} %select_n.182), kind=kLoop, calls=%fused_computation.27 | loop fusion | bytes 2850824 | tf_op jit(solution)/shard_map/dynamic_slice | solution.py:360
  2.3 0.5 collective-permute-start
  3.1 1.6 %collective-permute-done = bf16[96,3840]{1,0:T(8,128)(2,1)S(1)} collective-permute-done((bf16[96,3840]{1,0:T(8,128)(2,1)S(1)}, bf16[96,3840]{1,0:T(8,128)(2,1)S(1)}, u32[]{:S(2)}, u32[]{:S(2)}) %collective-permute-start) | collective-permute-done | bytes 737312 | tf_op jit(solution)/shard_map/ppermute | solution.py:350
  4.8 2.9 %collective-permute-start.3 = (bf16[192,1024]{1,0:T(8,128)(2,1)S(1)}, bf16[192,1024]{1,0:T(8,128)(2,1)S(1)}, u32[]{:S(2)}, u32[]{:S(2)}) collective-permute-start(bf16[192,1024]{1,0:T(8,128)(2,1)S(1)} %pad_maximum_fusion.2), channel_id=1, source_target_pairs={{0,16},{1,17},{2,18},{3,19},{4,20},{5,21},{6,22},{7,23},{8,24},{9,... | collective-permute-start | bytes 1179656 | tf_op jit(solution)/shard_map/ppermute | solution.py:350
  7.7 2.6 %collective-permute-start.1 = (s32[64,128]{1,0:T(8,128)S(1)}, s32[64,128]{1,0:T(8,128)S(1)}, u32[]{:S(2)}, u32[]{:S(2)}) collective-permute-start(s32[64,128]{1,0:T(8,128)S(1)} %pad_add_fusion.2), channel_id=1, source_target_pairs={{0,4},{1,5},{2,6},{3,7},{4,0},{5,1},{6,2},{7,3},{8,12},{9,13},{10,... | collective-permute-start | bytes 98312 | tf_op jit(solution)/shard_map/ppermute | solution.py:354
  10.4 0.6 collective-permute-start.6
  11.0 1.5 %collective-permute-start.4 = (bf16[192,1024]{1,0:T(8,128)(2,1)S(1)}, bf16[192,1024]{1,0:T(8,128)(2,1)S(1)}, u32[]{:S(2)}, u32[]{:S(2)}) collective-permute-start(bf16[192,1024]{1,0:T(8,128)(2,1)S(1)} %pad_maximum_fusion.3.refs_0_), channel_id=1, source_target_pairs={{0,1},{1,0},{2,3},{3,2},{4,5},{5,4},{6,7},{7,6},{8,9},{9,8},{10,11... | collective-permute-start | bytes 1179656 | tf_op jit(solution)/shard_map/ppermute | solution.py:350
  12.8 1.5 %collective-permute-start.2 = (s32[64,256]{1,0:T(8,128)S(1)}, s32[64,256]{1,0:T(8,128)S(1)}, u32[]{:S(2)}, u32[]{:S(2)}) collective-permute-start(s32[64,256]{1,0:T(8,128)S(1)} %pad_add_fusion.1), channel_id=1, source_target_pairs={{0,2},{1,3},{2,0},{3,1},{4,6},{5,7},{6,4},{7,5},{8,10},{9,11},{10,... | collective-permute-start | bytes 196616 | tf_op jit(solution)/shard_map/ppermute | solution.py:354
  14.3 0.3 constant_dynamic-slice_fusion.1
  14.6 2.6 %collective-permute-done.2 = s32[64,256]{1,0:T(8,128)S(1)} collective-permute-done((s32[64,256]{1,0:T(8,128)S(1)}, s32[64,256]{1,0:T(8,128)S(1)}, u32[]{:S(2)}, u32[]{:S(2)}) %collective-permute-start.2) | collective-permute-done | bytes 65568 | tf_op jit(solution)/shard_map/ppermute | solution.py:354
  17.3 4.9 %build_weights.1.w_ref = bf16[768,512]{1,0:T(8,128)(2,1)S(1)} custom-call(s32[8]{0:T(128)S(1)} %stack.92.base_ref, s32[64,512]{1,0:T(8,128)S(1)} %pad_add_fusion.query_ref), custom_call_target="tpu_custom_call" | custom-call | flops 5033164800 | bytes 786432 | tf_op jit(solution)/shard_map/build_weights/pallas_call | solution.py:93
  22.2 1.4 collective-permute-start.5
  23.7 0.7 collective-permute-start.13
  24.5 1.8 %collective-permute-start.7 = (bf16[192,896]{1,0:T(8,128)(2,1)S(1)}, bf16[192,896]{1,0:T(8,128)(2,1)S(1)}, u32[]{:S(2)}, u32[]{:S(2)}) collective-permute-start(bf16[192,896]{1,0:T(8,128)(2,1)S(1)} %pad_maximum_fusion.4.refs_0_), channel_id=1, source_target_pairs={{0,1},{1,0},{2,3},{3,2},{4,5},{5,4},{6,7},{7,6},{8,9},{9,8},{10,11... | collective-permute-start | bytes 1032200 | tf_op jit(solution)/shard_map/ppermute | solution.py:350
  26.3 0.3 collective-permute-start.8
  26.6 7.7 %collective-permute-done.5.refs_3_ = bf16[192,1024]{1,0:T(8,128)(2,1)S(1)} collective-permute-done((bf16[192,1024]{1,0:T(8,128)(2,1)S(1)}, bf16[192,1024]{1,0:T(8,128)(2,1)S(1)}, u32[]{:S(2)}, u32[]{:S(2)}) %collective-permute-start.5) | collective-permute-done | bytes 393248 | tf_op jit(solution)/shard_map/ppermute | solution.py:350
  34.2 1.5 %partial_sums.4 = (f32[1024,128]{1,0:T(8,128)S(1)}, f32[1024,128]{1,0:T(8,128)S(1)}, s16[2080,128]{1,0:T(8,128)(2,1)S(1)}) custom-call(s32[1]{0:T(128)} %bitcast.6.flag_ref, bf16[768,512]{1,0:T(8,128)(2,1)S(1)} %build_weights.1.w_ref, bf16[192,1024]{1,0:T(8,128)(2,1)S(1)} %pad_maximum_fusion.3.refs_0_, bf16[192,1024]{1,0:T(8,128)(2,1)S(1)} %collective-permute-done.3.refs_1_, ...), custom_call_target="tpu_custom_call" | custom-call | flops 805306368 | bytes 2883584 | tf_op jit(solution)/shard_map/partial_sums/pallas_call | solution.py:170
  35.8 1.6 %collective-permute-start.9 = (s16[2080,128]{1,0:T(8,128)(2,1)S(1)}, s16[2080,128]{1,0:T(8,128)(2,1)S(1)}, u32[]{:S(2)}, u32[]{:S(2)}) collective-permute-start(s16[2080,128]{1,0:T(8,128)(2,1)S(1)} %get-tuple-element.38), channel_id=1, source_target_pairs={{0,2},{1,3},{2,0},{3,1},{4,6},{5,7},{6,4},{7,5},{8,10},{9,11},{10,... | collective-permute-start | bytes 1597448 | tf_op jit(solution)/shard_map/ppermute | solution.py:354
  37.5 1.2 collective-permute-start.14
  38.6 3.0 %collective-permute-done.7.refs_2_ = bf16[192,896]{1,0:T(8,128)(2,1)S(1)} collective-permute-done((bf16[192,896]{1,0:T(8,128)(2,1)S(1)}, bf16[192,896]{1,0:T(8,128)(2,1)S(1)}, u32[]{:S(2)}, u32[]{:S(2)}) %collective-permute-start.7) | collective-permute-done | bytes 344096 | tf_op jit(solution)/shard_map/ppermute | solution.py:350
  41.6 7.4 %collective-permute-done.8.refs_3_ = bf16[192,896]{1,0:T(8,128)(2,1)S(1)} collective-permute-done((bf16[192,896]{1,0:T(8,128)(2,1)S(1)}, bf16[192,896]{1,0:T(8,128)(2,1)S(1)}, u32[]{:S(2)}, u32[]{:S(2)}) %collective-permute-start.8) | collective-permute-done | bytes 344096 | tf_op jit(solution)/shard_map/ppermute | solution.py:350
  49.0 1.4 partial_sums.5
  50.4 1.6 %collective-permute-start.10 = (s16[1824,128]{1,0:T(8,128)(2,1)S(1)}, s16[1824,128]{1,0:T(8,128)(2,1)S(1)}, u32[]{:S(2)}, u32[]{:S(2)}) collective-permute-start(s16[1824,128]{1,0:T(8,128)(2,1)S(1)} %get-tuple-element.40), channel_id=1, source_target_pairs={{0,2},{1,3},{2,0},{3,1},{4,6},{5,7},{6,4},{7,5},{8,10},{9,11},{10,... | collective-permute-start | bytes 1400840 | tf_op jit(solution)/shard_map/ppermute | solution.py:354
  52.0 1.2 collective-permute-start.15
  53.4 2.9 %collective-permute-start.11 = (s16[1040,128]{1,0:T(8,128)(2,1)S(1)}, s16[1040,128]{1,0:T(8,128)(2,1)S(1)}, u32[]{:S(2)}, u32[]{:S(2)}) collective-permute-start(s16[1040,128]{1,0:T(8,128)(2,1)S(1)} %combine.8), channel_id=1, source_target_pairs={{0,4},{1,5},{2,6},{3,7},{4,0},{5,1},{6,2},{7,3},{8,12},{9,13},{10,... | collective-permute-start | bytes 798728 | tf_op jit(solution)/shard_map/ppermute | solution.py:354
  56.4 0.6 collective-permute-start.19
  56.9 9.2 %collective-permute-done.10.refs_0_ = s16[1824,128]{1,0:T(8,128)(2,1)S(1)} collective-permute-done((s16[1824,128]{1,0:T(8,128)(2,1)S(1)}, s16[1824,128]{1,0:T(8,128)(2,1)S(1)}, u32[]{:S(2)}, u32[]{:S(2)}) %collective-permute-start.10) | collective-permute-done | bytes 466976 | tf_op jit(solution)/shard_map/ppermute | solution.py:354
  66.4 6.9 %collective-permute-done.15.refs_3_ = bf16[192,1024]{1,0:T(8,128)(2,1)S(1)} collective-permute-done((bf16[192,1024]{1,0:T(8,128)(2,1)S(1)}, bf16[192,1024]{1,0:T(8,128)(2,1)S(1)}, u32[]{:S(2)}, u32[]{:S(2)}) %collective-permute-start.15) | collective-permute-done | bytes 393248 | tf_op jit(solution)/shard_map/ppermute | solution.py:350
  73.2 1.5 %partial_sums.6 = (f32[1024,128]{1,0:T(8,128)S(1)}, f32[1024,128]{1,0:T(8,128)S(1)}, s16[2080,128]{1,0:T(8,128)(2,1)S(1)}) custom-call(s32[1]{0:T(128)} %bitcast.6.flag_ref, bf16[768,512]{1,0:T(8,128)(2,1)S(1)} %build_weights.1.w_ref, bf16[192,1920]{1,0:T(8,128)(2,1)S(1)} %pad_maximum_fusion.refs_0_, bf16[192,1920]{1,0:T(8,128)(2,1)S(1)} %collective-permute-done.13.refs_1_, ...), custom_call_target="tpu_custom_call" | custom-call | flops 805306368 | bytes 2883584 | tf_op jit(solution)/shard_map/partial_sums/pallas_call | solution.py:170
  74.7 1.6 %collective-permute-start.21 = (s16[2080,128]{1,0:T(8,128)(2,1)S(1)}, s16[2080,128]{1,0:T(8,128)(2,1)S(1)}, u32[]{:S(2)}, u32[]{:S(2)}) collective-permute-start(s16[2080,128]{1,0:T(8,128)(2,1)S(1)} %get-tuple-element.52), channel_id=1, source_target_pairs={{0,2},{1,3},{2,0},{3,1},{4,6},{5,7},{6,4},{7,5},{8,10},{9,11},{10,... | collective-permute-start | bytes 1597448 | tf_op jit(solution)/shard_map/ppermute | solution.py:354
  76.3 2.4 %collective-permute-start.20 = (s16[912,128]{1,0:T(8,128)(2,1)S(1)}, s16[912,128]{1,0:T(8,128)(2,1)S(1)}, u32[]{:S(2)}, u32[]{:S(2)}) collective-permute-start(s16[912,128]{1,0:T(8,128)(2,1)S(1)} %combine.9), channel_id=1, source_target_pairs={{0,4},{1,5},{2,6},{3,7},{4,0},{5,1},{6,2},{7,3},{8,12},{9,13},{10,... | collective-permute-start | bytes 700424 | tf_op jit(solution)/shard_map/ppermute | solution.py:354
  78.8 0.3 combine.10.refs_0_
  79.0 0.6 collective-permute-start.17
  79.6 2.1 %partial_sums.7 = (f32[896,128]{1,0:T(8,128)S(1)}, f32[896,128]{1,0:T(8,128)S(1)}, s16[1824,128]{1,0:T(8,128)(2,1)}) custom-call(s32[1]{0:T(128)} %bitcast.6.flag_ref, bf16[768,512]{1,0:T(8,128)(2,1)S(1)} %build_weights.1.w_ref, bf16[192,1920]{1,0:T(8,128)(2,1)S(1)} %pad_maximum_fusion.refs_0_, bf16[192,1920]{1,0:T(8,128)(2,1)S(1)} %collective-permute-done.13.refs_1_, ...), custom_call_target="tpu_custom_call" | custom-call | flops 704643072 | bytes 2523136 | tf_op jit(solution)/shard_map/partial_sums/pallas_call | solution.py:170
  81.7 9.9 %collective-permute-done.20.refs_1_ = s16[912,128]{1,0:T(8,128)(2,1)S(1)} collective-permute-done((s16[912,128]{1,0:T(8,128)(2,1)S(1)}, s16[912,128]{1,0:T(8,128)(2,1)S(1)}, u32[]{:S(2)}, u32[]{:S(2)}) %collective-permute-start.20) | collective-permute-done | bytes 233504 | tf_op jit(solution)/shard_map/ppermute | solution.py:354
  91.9 2.5 %collective-permute-start.23 = (s16[912,128]{1,0:T(8,128)(2,1)S(1)}, s16[912,128]{1,0:T(8,128)(2,1)}, u32[]{:S(2)}, u32[]{:S(2)}) collective-permute-start(s16[912,128]{1,0:T(8,128)(2,1)S(1)} %combine.11.refs_4_), channel_id=1, source_target_pairs={{0,16},{1,17},{2,18},{3,19},{4,20},{5,21},{6,22},{7,23},{8,24},{9,... | collective-permute-start | bytes 700424 | tf_op jit(solution)/shard_map/ppermute | solution.py:350
  94.3 0.5 collective-permute-start.18
  94.8 3.6 %collective-permute-done.23.refs_6_ = s16[912,128]{1,0:T(8,128)(2,1)} collective-permute-done((s16[912,128]{1,0:T(8,128)(2,1)S(1)}, s16[912,128]{1,0:T(8,128)(2,1)}, u32[]{:S(2)}, u32[]{:S(2)}) %collective-permute-start.23) | collective-permute-done | bytes 233504 | tf_op jit(solution)/shard_map/ppermute | solution.py:350
  98.5 0.5 collective-permute-start.24
  99.3 3.4 %collective-permute-start.25 = (s16[1040,128]{1,0:T(8,128)(2,1)S(1)}, s16[1040,128]{1,0:T(8,128)(2,1)S(1)}, u32[]{:S(2)}, u32[]{:S(2)}) collective-permute-start(s16[1040,128]{1,0:T(8,128)(2,1)S(1)} %combine.12), channel_id=1, source_target_pairs={{0,4},{1,5},{2,6},{3,7},{4,0},{5,1},{6,2},{7,3},{8,12},{9,13},{10,... | collective-permute-start | bytes 798728 | tf_op jit(solution)/shard_map/ppermute | solution.py:354
  102.7 13.2 %covariance.1 = f32[13456,128]{1,0:T(8,128)} custom-call(s32[8]{0:T(128)S(1)} %stack.97.place_ref, s16[1040,128]{1,0:T(8,128)(2,1)S(1)} %combine.10.refs_0_, s16[1040,128]{1,0:T(8,128)(2,1)} %collective-permute-done.16.refs_1_, s16[1040,128]{1,0:T(8,128)(2,1)} %collective-permute-done.17.refs_2_, s16[1040,128]{1,0:T(8,128)(2,1)} %collective-permute-done.18.refs_3_, ...), custom_call_target="tpu_custom_call" | custom-call | flops 1763704832 | bytes 6889472 | tf_op jit(solution)/shard_map/covariance/pallas_call | solution.py:311
  116.1 1.3 collective-permute-start.30
  117.7 2.1 %collective-permute-start.27 = (s16[1040,128]{1,0:T(8,128)(2,1)S(1)}, s16[1040,128]{1,0:T(8,128)(2,1)S(1)}, u32[]{:S(2)}, u32[]{:S(2)}) collective-permute-start(s16[1040,128]{1,0:T(8,128)(2,1)S(1)} %combine.13.refs_0_), channel_id=1, source_target_pairs={{0,16},{1,17},{2,18},{3,19},{4,20},{5,21},{6,22},{7,23},{8,24},{9,... | collective-permute-start | bytes 798728 | tf_op jit(solution)/shard_map/ppermute | solution.py:350
  119.8 8.1 %collective-permute-done.30.refs_1_ = s16[912,128]{1,0:T(8,128)(2,1)S(1)} collective-permute-done((s16[912,128]{1,0:T(8,128)(2,1)S(1)}, s16[912,128]{1,0:T(8,128)(2,1)S(1)}, u32[]{:S(2)}, u32[]{:S(2)}) %collective-permute-start.30) | collective-permute-done | bytes 233504 | tf_op jit(solution)/shard_map/ppermute | solution.py:354
  128.4 0.5 collective-permute-start.28
  128.9 6.9 %collective-permute-done.32.refs_6_ = s16[912,128]{1,0:T(8,128)(2,1)S(1)} collective-permute-done((s16[912,128]{1,0:T(8,128)(2,1)S(1)}, s16[912,128]{1,0:T(8,128)(2,1)S(1)}, u32[]{:S(2)}, u32[]{:S(2)}) %collective-permute-start.32) | collective-permute-done | bytes 233504 | tf_op jit(solution)/shard_map/ppermute | solution.py:350
  136.0 1.4 collective-permute-done.33.refs_7_
  137.4 3.8 %marginal.1 = f32[128,7424]{1,0:T(8,128)} custom-call(s32[8]{0:T(128)S(1)} %stack.83.place_ref, s16[1040,128]{1,0:T(8,128)(2,1)S(1)} %combine.13.refs_0_, s16[1040,128]{1,0:T(8,128)(2,1)S(1)} %collective-permute-done.26.refs_1_, s16[1040,128]{1,0:T(8,128)(2,1)S(1)} %collective-permute-done.27.refs_2_, s16[1040,128]{1,0:T(8,128)(2,1)S(1)} %collective-permute-done.28.refs_3_, ...), custom_call_target="tpu_custom_call" | custom-call | flops 3801088 | bytes 5701632 | tf_op jit(solution)/shard_map/marginal/pallas_call | solution.py:238
  (66 shorter events, 3.0 us)
Async XLA Ops:
  0.6 1.5 %copy-start.1 = (bf16[96,116]{1,0:T(8,128)(2,1)S(1)}, bf16[96,116]{1,0:T(8,128)(2,1)}, u32[]{:S(2)}) copy-start(bf16[96,116]{1,0:T(8,128)(2,1)} %param.7) | copy-start | bytes 66820
  2.1 0.8 copy-start.2
  2.1 0.8 copy-start.3
  2.3 2.4 %collective-permute-start = (bf16[96,3840]{1,0:T(8,128)(2,1)S(1)}, bf16[96,3840]{1,0:T(8,128)(2,1)S(1)}, u32[]{:S(2)}, u32[]{:S(2)}) collective-permute-start(bf16[96,3840]{1,0:T(8,128)(2,1)S(1)} %get-tuple-element.73), channel_id=1, source_target_pairs={{0,8},{1,9},{2,10},{3,11},{4,12},{5,13},{6,14},{7,15},{8,0},{9,1},... | collective-permute-start | bytes 2211848 | tf_op jit(solution)/shard_map/ppermute | solution.py:350
  4.7 7.8 %copy-start = (bf16[96,7424]{1,0:T(8,128)(2,1)S(1)}, bf16[96,7424]{1,0:T(8,128)(2,1)}, u32[]{:S(2)}) copy-start(bf16[96,7424]{1,0:T(8,128)(2,1)} %param.5) | copy-start | bytes 4276228
  4.8 17.3 %collective-permute-start.3 = (bf16[192,1024]{1,0:T(8,128)(2,1)S(1)}, bf16[192,1024]{1,0:T(8,128)(2,1)S(1)}, u32[]{:S(2)}, u32[]{:S(2)}) collective-permute-start(bf16[192,1024]{1,0:T(8,128)(2,1)S(1)} %pad_maximum_fusion.2), channel_id=1, source_target_pairs={{0,16},{1,17},{2,18},{3,19},{4,20},{5,21},{6,22},{7,23},{8,24},{9,... | collective-permute-start | bytes 1179656 | tf_op jit(solution)/shard_map/ppermute | solution.py:350
  7.7 5.1 %collective-permute-start.1 = (s32[64,128]{1,0:T(8,128)S(1)}, s32[64,128]{1,0:T(8,128)S(1)}, u32[]{:S(2)}, u32[]{:S(2)}) collective-permute-start(s32[64,128]{1,0:T(8,128)S(1)} %pad_add_fusion.2), channel_id=1, source_target_pairs={{0,4},{1,5},{2,6},{3,7},{4,0},{5,1},{6,2},{7,3},{8,12},{9,13},{10,... | collective-permute-start | bytes 98312 | tf_op jit(solution)/shard_map/ppermute | solution.py:354
  10.4 14.1 %collective-permute-start.6 = (bf16[192,896]{1,0:T(8,128)(2,1)S(1)}, bf16[192,896]{1,0:T(8,128)(2,1)S(1)}, u32[]{:S(2)}, u32[]{:S(2)}) collective-permute-start(bf16[192,896]{1,0:T(8,128)(2,1)S(1)} %pad_maximum_fusion.5), channel_id=1, source_target_pairs={{0,16},{1,17},{2,18},{3,19},{4,20},{5,21},{6,22},{7,23},{8,24},{9,... | collective-permute-start | bytes 1032200 | tf_op jit(solution)/shard_map/ppermute | solution.py:350
  11.0 15.5 %collective-permute-start.4 = (bf16[192,1024]{1,0:T(8,128)(2,1)S(1)}, bf16[192,1024]{1,0:T(8,128)(2,1)S(1)}, u32[]{:S(2)}, u32[]{:S(2)}) collective-permute-start(bf16[192,1024]{1,0:T(8,128)(2,1)S(1)} %pad_maximum_fusion.3.refs_0_), channel_id=1, source_target_pairs={{0,1},{1,0},{2,3},{3,2},{4,5},{5,4},{6,7},{7,6},{8,9},{9,8},{10,11... | collective-permute-start | bytes 1179656 | tf_op jit(solution)/shard_map/ppermute | solution.py:350
  12.6 11.0 %collective-permute-start.12 = (bf16[96,3712]{1,0:T(8,128)(2,1)S(1)}, bf16[96,3712]{1,0:T(8,128)(2,1)S(1)}, u32[]{:S(2)}, u32[]{:S(2)}) collective-permute-start(bf16[96,3712]{1,0:T(8,128)(2,1)S(1)} %constant_dynamic-slice_fusion.3), channel_id=1, source_target_pairs={{0,8},{1,9},{2,10},{3,11},{4,12},{5,13},{6,14},{7,15},{8,0},{9,1},... | collective-permute-start | bytes 2138120 | tf_op jit(solution)/shard_map/ppermute | solution.py:350
  12.8 4.4 %collective-permute-start.2 = (s32[64,256]{1,0:T(8,128)S(1)}, s32[64,256]{1,0:T(8,128)S(1)}, u32[]{:S(2)}, u32[]{:S(2)}) collective-permute-start(s32[64,256]{1,0:T(8,128)S(1)} %pad_add_fusion.1), channel_id=1, source_target_pairs={{0,2},{1,3},{2,0},{3,1},{4,6},{5,7},{6,4},{7,5},{8,10},{9,11},{10,... | collective-permute-start | bytes 196616 | tf_op jit(solution)/shard_map/ppermute | solution.py:354
  22.2 12.1 %collective-permute-start.5 = (bf16[192,1024]{1,0:T(8,128)(2,1)S(1)}, bf16[192,1024]{1,0:T(8,128)(2,1)S(1)}, u32[]{:S(2)}, u32[]{:S(2)}) collective-permute-start(bf16[192,1024]{1,0:T(8,128)(2,1)S(1)} %collective-permute-done.3.refs_1_), channel_id=1, source_target_pairs={{0,1},{1,0},{2,3},{3,2},{4,5},{5,4},{6,7},{7,6},{8,9},{9,8},{10,11... | collective-permute-start | bytes 1179656 | tf_op jit(solution)/shard_map/ppermute | solution.py:350
  23.7 28.3 %collective-permute-start.13 = (bf16[192,1920]{1,0:T(8,128)(2,1)S(1)}, bf16[192,1920]{1,0:T(8,128)(2,1)S(1)}, u32[]{:S(2)}, u32[]{:S(2)}) collective-permute-start(bf16[192,1920]{1,0:T(8,128)(2,1)S(1)} %pad_maximum_fusion.1), channel_id=1, source_target_pairs={{0,16},{1,17},{2,18},{3,19},{4,20},{5,21},{6,22},{7,23},{8,24},{9,... | collective-permute-start | bytes 2211848 | tf_op jit(solution)/shard_map/ppermute | solution.py:350
  24.5 17.1 %collective-permute-start.7 = (bf16[192,896]{1,0:T(8,128)(2,1)S(1)}, bf16[192,896]{1,0:T(8,128)(2,1)S(1)}, u32[]{:S(2)}, u32[]{:S(2)}) collective-permute-start(bf16[192,896]{1,0:T(8,128)(2,1)S(1)} %pad_maximum_fusion.4.refs_0_), channel_id=1, source_target_pairs={{0,1},{1,0},{2,3},{3,2},{4,5},{5,4},{6,7},{7,6},{8,9},{9,8},{10,11... | collective-permute-start | bytes 1032200 | tf_op jit(solution)/shard_map/ppermute | solution.py:350
  26.3 22.7 %collective-permute-start.8 = (bf16[192,896]{1,0:T(8,128)(2,1)S(1)}, bf16[192,896]{1,0:T(8,128)(2,1)S(1)}, u32[]{:S(2)}, u32[]{:S(2)}) collective-permute-start(bf16[192,896]{1,0:T(8,128)(2,1)S(1)} %collective-permute-done.6.refs_1_), channel_id=1, source_target_pairs={{0,1},{1,0},{2,3},{3,2},{4,5},{5,4},{6,7},{7,6},{8,9},{9,8},{10,11... | collective-permute-start | bytes 1032200 | tf_op jit(solution)/shard_map/ppermute | solution.py:350
  35.8 17.5 %collective-permute-start.9 = (s16[2080,128]{1,0:T(8,128)(2,1)S(1)}, s16[2080,128]{1,0:T(8,128)(2,1)S(1)}, u32[]{:S(2)}, u32[]{:S(2)}) collective-permute-start(s16[2080,128]{1,0:T(8,128)(2,1)S(1)} %get-tuple-element.38), channel_id=1, source_target_pairs={{0,2},{1,3},{2,0},{3,1},{4,6},{5,7},{6,4},{7,5},{8,10},{9,11},{10,... | collective-permute-start | bytes 1597448 | tf_op jit(solution)/shard_map/ppermute | solution.py:354
  37.5 28.9 %collective-permute-start.14 = (bf16[192,1920]{1,0:T(8,128)(2,1)S(1)}, bf16[192,1920]{1,0:T(8,128)(2,1)S(1)}, u32[]{:S(2)}, u32[]{:S(2)}) collective-permute-start(bf16[192,1920]{1,0:T(8,128)(2,1)S(1)} %pad_maximum_fusion.refs_0_), channel_id=1, source_target_pairs={{0,1},{1,0},{2,3},{3,2},{4,5},{5,4},{6,7},{7,6},{8,9},{9,8},{10,11... | collective-permute-start | bytes 2211848 | tf_op jit(solution)/shard_map/ppermute | solution.py:350
  50.4 15.8 %collective-permute-start.10 = (s16[1824,128]{1,0:T(8,128)(2,1)S(1)}, s16[1824,128]{1,0:T(8,128)(2,1)S(1)}, u32[]{:S(2)}, u32[]{:S(2)}) collective-permute-start(s16[1824,128]{1,0:T(8,128)(2,1)S(1)} %get-tuple-element.40), channel_id=1, source_target_pairs={{0,2},{1,3},{2,0},{3,1},{4,6},{5,7},{6,4},{7,5},{8,10},{9,11},{10,... | collective-permute-start | bytes 1400840 | tf_op jit(solution)/shard_map/ppermute | solution.py:354
  52.0 21.2 %collective-permute-start.15 = (bf16[192,1024]{1,0:T(8,128)(2,1)S(1)}, bf16[192,1024]{1,0:T(8,128)(2,1)S(1)}, u32[]{:S(2)}, u32[]{:S(2)}) collective-permute-start(bf16[192,1024]{1,0:T(8,128)(2,1)S(1)} %slice.8), channel_id=1, source_target_pairs={{0,1},{1,0},{2,3},{3,2},{4,5},{5,4},{6,7},{7,6},{8,9},{9,8},{10,11... | collective-permute-start | bytes 1179656 | tf_op jit(solution)/shard_map/ppermute | solution.py:350
  53.4 12.9 %collective-permute-start.11 = (s16[1040,128]{1,0:T(8,128)(2,1)S(1)}, s16[1040,128]{1,0:T(8,128)(2,1)S(1)}, u32[]{:S(2)}, u32[]{:S(2)}) collective-permute-start(s16[1040,128]{1,0:T(8,128)(2,1)S(1)} %combine.8), channel_id=1, source_target_pairs={{0,4},{1,5},{2,6},{3,7},{4,0},{5,1},{6,2},{7,3},{8,12},{9,13},{10,... | collective-permute-start | bytes 798728 | tf_op jit(solution)/shard_map/ppermute | solution.py:354
  56.4 23.3 %collective-permute-start.19 = (bf16[192,896]{1,0:T(8,128)(2,1)S(1)}, bf16[192,896]{1,0:T(8,128)(2,1)S(1)}, u32[]{:S(2)}, u32[]{:S(2)}) collective-permute-start(bf16[192,896]{1,0:T(8,128)(2,1)S(1)} %slice.9), channel_id=1, source_target_pairs={{0,1},{1,0},{2,3},{3,2},{4,5},{5,4},{6,7},{7,6},{8,9},{9,8},{10,11... | collective-permute-start | bytes 1032200 | tf_op jit(solution)/shard_map/ppermute | solution.py:350
  74.7 23.8 %collective-permute-start.21 = (s16[2080,128]{1,0:T(8,128)(2,1)S(1)}, s16[2080,128]{1,0:T(8,128)(2,1)S(1)}, u32[]{:S(2)}, u32[]{:S(2)}) collective-permute-start(s16[2080,128]{1,0:T(8,128)(2,1)S(1)} %get-tuple-element.52), channel_id=1, source_target_pairs={{0,2},{1,3},{2,0},{3,1},{4,6},{5,7},{6,4},{7,5},{8,10},{9,11},{10,... | collective-permute-start | bytes 1597448 | tf_op jit(solution)/shard_map/ppermute | solution.py:354
  76.3 15.3 %collective-permute-start.20 = (s16[912,128]{1,0:T(8,128)(2,1)S(1)}, s16[912,128]{1,0:T(8,128)(2,1)S(1)}, u32[]{:S(2)}, u32[]{:S(2)}) collective-permute-start(s16[912,128]{1,0:T(8,128)(2,1)S(1)} %combine.9), channel_id=1, source_target_pairs={{0,4},{1,5},{2,6},{3,7},{4,0},{5,1},{6,2},{7,3},{8,12},{9,13},{10,... | collective-permute-start | bytes 700424 | tf_op jit(solution)/shard_map/ppermute | solution.py:354
  79.0 15.3 %collective-permute-start.17 = (s16[1040,128]{1,0:T(8,128)(2,1)S(1)}, s16[1040,128]{1,0:T(8,128)(2,1)}, u32[]{:S(2)}, u32[]{:S(2)}) collective-permute-start(s16[1040,128]{1,0:T(8,128)(2,1)S(1)} %combine.10.refs_0_), channel_id=1, source_target_pairs={{0,16},{1,17},{2,18},{3,19},{4,20},{5,21},{6,22},{7,23},{8,24},{9,... | collective-permute-start | bytes 798728 | tf_op jit(solution)/shard_map/ppermute | solution.py:350
  91.9 6.6 %collective-permute-start.23 = (s16[912,128]{1,0:T(8,128)(2,1)S(1)}, s16[912,128]{1,0:T(8,128)(2,1)}, u32[]{:S(2)}, u32[]{:S(2)}) collective-permute-start(s16[912,128]{1,0:T(8,128)(2,1)S(1)} %combine.11.refs_4_), channel_id=1, source_target_pairs={{0,16},{1,17},{2,18},{3,19},{4,20},{5,21},{6,22},{7,23},{8,24},{9,... | collective-permute-start | bytes 700424 | tf_op jit(solution)/shard_map/ppermute | solution.py:350
  94.3 21.6 %collective-permute-start.29 = (s16[1824,128]{1,0:T(8,128)(2,1)}, s16[1824,128]{1,0:T(8,128)(2,1)S(1)}, u32[]{:S(2)}, u32[]{:S(2)}) collective-permute-start(s16[1824,128]{1,0:T(8,128)(2,1)} %get-tuple-element.55), channel_id=1, source_target_pairs={{0,2},{1,3},{2,0},{3,1},{4,6},{5,7},{6,4},{7,5},{8,10},{9,11},{10,... | collective-permute-start | bytes 1400840 | tf_op jit(solution)/shard_map/ppermute | solution.py:354
  94.3 5.0 %collective-permute-start.16 = (s16[1040,128]{1,0:T(8,128)(2,1)S(1)}, s16[1040,128]{1,0:T(8,128)(2,1)}, u32[]{:S(2)}, u32[]{:S(2)}) collective-permute-start(s16[1040,128]{1,0:T(8,128)(2,1)S(1)} %combine.10.refs_0_), channel_id=1, source_target_pairs={{0,8},{1,9},{2,10},{3,11},{4,12},{5,13},{6,14},{7,15},{8,0},{9,1},... | collective-permute-start | bytes 798728 | tf_op jit(solution)/shard_map/ppermute | solution.py:350
  94.3 8.4 %collective-permute-start.18 = (s16[1040,128]{1,0:T(8,128)(2,1)}, s16[1040,128]{1,0:T(8,128)(2,1)}, u32[]{:S(2)}, u32[]{:S(2)}) collective-permute-start(s16[1040,128]{1,0:T(8,128)(2,1)} %collective-permute-done.17.refs_2_), channel_id=1, source_target_pairs={{0,8},{1,9},{2,10},{3,11},{4,12},{5,13},{6,14},{7,15},{8,0},{9,1},... | collective-permute-start | bytes 798728 | tf_op jit(solution)/shard_map/ppermute | solution.py:350
  98.5 4.3 %collective-permute-start.22 = (s16[912,128]{1,0:T(8,128)(2,1)S(1)}, s16[912,128]{1,0:T(8,128)(2,1)}, u32[]{:S(2)}, u32[]{:S(2)}) collective-permute-start(s16[912,128]{1,0:T(8,128)(2,1)S(1)} %combine.11.refs_4_), channel_id=1, source_target_pairs={{0,8},{1,9},{2,10},{3,11},{4,12},{5,13},{6,14},{7,15},{8,0},{9,1},... | collective-permute-start | bytes 700424 | tf_op jit(solution)/shard_map/ppermute | solution.py:350
  98.5 4.3 %collective-permute-start.24 = (s16[912,128]{1,0:T(8,128)(2,1)}, s16[912,128]{1,0:T(8,128)(2,1)}, u32[]{:S(2)}, u32[]{:S(2)}) collective-permute-start(s16[912,128]{1,0:T(8,128)(2,1)} %collective-permute-done.23.refs_6_), channel_id=1, source_target_pairs={{0,8},{1,9},{2,10},{3,11},{4,12},{5,13},{6,14},{7,15},{8,0},{9,1},... | collective-permute-start | bytes 700424 | tf_op jit(solution)/shard_map/ppermute | solution.py:350
  99.3 18.2 %collective-permute-start.25 = (s16[1040,128]{1,0:T(8,128)(2,1)S(1)}, s16[1040,128]{1,0:T(8,128)(2,1)S(1)}, u32[]{:S(2)}, u32[]{:S(2)}) collective-permute-start(s16[1040,128]{1,0:T(8,128)(2,1)S(1)} %combine.12), channel_id=1, source_target_pairs={{0,4},{1,5},{2,6},{3,7},{4,0},{5,1},{6,2},{7,3},{8,12},{9,13},{10,... | collective-permute-start | bytes 798728 | tf_op jit(solution)/shard_map/ppermute | solution.py:354
  116.1 11.8 %collective-permute-start.30 = (s16[912,128]{1,0:T(8,128)(2,1)S(1)}, s16[912,128]{1,0:T(8,128)(2,1)S(1)}, u32[]{:S(2)}, u32[]{:S(2)}) collective-permute-start(s16[912,128]{1,0:T(8,128)(2,1)S(1)} %combine.14), channel_id=1, source_target_pairs={{0,4},{1,5},{2,6},{3,7},{4,0},{5,1},{6,2},{7,3},{8,12},{9,13},{10,... | collective-permute-start | bytes 700424 | tf_op jit(solution)/shard_map/ppermute | solution.py:354
  117.7 10.6 %collective-permute-start.27 = (s16[1040,128]{1,0:T(8,128)(2,1)S(1)}, s16[1040,128]{1,0:T(8,128)(2,1)S(1)}, u32[]{:S(2)}, u32[]{:S(2)}) collective-permute-start(s16[1040,128]{1,0:T(8,128)(2,1)S(1)} %combine.13.refs_0_), channel_id=1, source_target_pairs={{0,16},{1,17},{2,18},{3,19},{4,20},{5,21},{6,22},{7,23},{8,24},{9,... | collective-permute-start | bytes 798728 | tf_op jit(solution)/shard_map/ppermute | solution.py:350
  128.2 7.7 %collective-permute-start.32 = (s16[912,128]{1,0:T(8,128)(2,1)S(1)}, s16[912,128]{1,0:T(8,128)(2,1)S(1)}, u32[]{:S(2)}, u32[]{:S(2)}) collective-permute-start(s16[912,128]{1,0:T(8,128)(2,1)S(1)} %combine.15.refs_4_), channel_id=1, source_target_pairs={{0,16},{1,17},{2,18},{3,19},{4,20},{5,21},{6,22},{7,23},{8,24},{9,... | collective-permute-start | bytes 700424 | tf_op jit(solution)/shard_map/ppermute | solution.py:350
  128.3 7.6 %collective-permute-start.26 = (s16[1040,128]{1,0:T(8,128)(2,1)S(1)}, s16[1040,128]{1,0:T(8,128)(2,1)S(1)}, u32[]{:S(2)}, u32[]{:S(2)}) collective-permute-start(s16[1040,128]{1,0:T(8,128)(2,1)S(1)} %combine.13.refs_0_), channel_id=1, source_target_pairs={{0,8},{1,9},{2,10},{3,11},{4,12},{5,13},{6,14},{7,15},{8,0},{9,1},... | collective-permute-start | bytes 798728 | tf_op jit(solution)/shard_map/ppermute | solution.py:350
  128.4 9.0 %collective-permute-start.28 = (s16[1040,128]{1,0:T(8,128)(2,1)S(1)}, s16[1040,128]{1,0:T(8,128)(2,1)S(1)}, u32[]{:S(2)}, u32[]{:S(2)}) collective-permute-start(s16[1040,128]{1,0:T(8,128)(2,1)S(1)} %collective-permute-done.27.refs_2_), channel_id=1, source_target_pairs={{0,8},{1,9},{2,10},{3,11},{4,12},{5,13},{6,14},{7,15},{8,0},{9,1},... | collective-permute-start | bytes 798728 | tf_op jit(solution)/shard_map/ppermute | solution.py:350
  128.9 7.1 %collective-permute-start.31 = (s16[912,128]{1,0:T(8,128)(2,1)S(1)}, s16[912,128]{1,0:T(8,128)(2,1)S(1)}, u32[]{:S(2)}, u32[]{:S(2)}) collective-permute-start(s16[912,128]{1,0:T(8,128)(2,1)S(1)} %combine.15.refs_4_), channel_id=1, source_target_pairs={{0,8},{1,9},{2,10},{3,11},{4,12},{5,13},{6,14},{7,15},{8,0},{9,1},... | collective-permute-start | bytes 700424 | tf_op jit(solution)/shard_map/ppermute | solution.py:350
  135.9 1.5 %collective-permute-start.33 = (s16[912,128]{1,0:T(8,128)(2,1)S(1)}, s16[912,128]{1,0:T(8,128)(2,1)S(1)}, u32[]{:S(2)}, u32[]{:S(2)}) collective-permute-start(s16[912,128]{1,0:T(8,128)(2,1)S(1)} %collective-permute-done.32.refs_6_), channel_id=1, source_target_pairs={{0,8},{1,9},{2,10},{3,11},{4,12},{5,13},{6,14},{7,15},{8,0},{9,1},... | collective-permute-start | bytes 700424 | tf_op jit(solution)/shard_map/ppermute | solution.py:350

commit v11 on v10

--- a/solution.py
+++ b/solution.py
@@ -439,14 +439,12 @@
     data_d = merge([later(mean_y, first_c)] + [along_y(value, first_c, first_d, there) for value in mean_x[1:]])
     own_c, near_c, middle_c, far_c = along_z(data_c, first_c, False, (middle_b, far_a))
     mine_a, load_a = spread(own_a, near_a, far_a)
-    own_d, opposite_d, sent_d = partial_sums(flag, after(w, own_c), data_d, first_d, False)
-    near_d = z_swap(sent_d, 1)
-    mine_b, load_b = spread(after(own_b, own_d), near_b, far_b)
-    load_pieces = load_a + [after(load_b[0], middle_c, own_d)] + load_b[1:]
+    own_d, near_d, middle_d, far_d = along_z(data_d, first_d, False, (own_c,), (middle_c,))
+    mine_b, load_b = spread(after(own_b, middle_c), near_b, far_b)
+    load_pieces = load_a + [after(load_b[0], middle_d)] + load_b[1:]
     cov = covariance(places(load_width), load_pieces, load_tiles, load_width * CORES, ages, rank)
-    far_d = z_swap(combine(after(opposite_d, cov), (near_d, 1)), 2)
-    mine_c, mean_c = spread(after(own_c, cov), near_c, far_c)
-    mine_d, mean_d = spread(own_d, near_d, far_d)
+    mine_c, mean_c = spread(own_c, near_c, far_c)
+    mine_d, mean_d = spread(after(own_d, cov), near_d, far_d)
     mean_pieces = mean_c + mean_d
     mean = marginal(places(mean_width), mean_pieces, mean_tiles, mean_width * CORES)
     return mean, cov.T

time: 141 us -> 139 us (0.986)
  waiting for transfers between devices: 68.6 us -> 62.6 us
  local copies, waits for them, and re-layouts: 2.34 us -> 3.99 us
    ppermute x24, waiting for transfers between devices: 38.6 us -> 33.5 us  [move(): return lax.ppermute(value, ('geo', 'dist'), perm)]
    unnamed x8 -> x12, local copies, waits for them, and re-layouts: 0.02 us -> 1.68 us
    pallas_call x8, Pallas kernels: 1.67 us -> 3.31 us  [combine(): pl.pallas_call(functools.partial(combine_kernel, [unit * shape[0] for _,...]
  transfers between devices with their start and end apart: 34 -> 34, of which waited for: 14 -> 15; matrix products, arithmetic and copies ran while one was open for 1% -> 1% of each run, Pallas kernels for 19% -> 19%
where the time goes in v11:
time: 139 us
  waiting for transfers between devices  62.6 us (45%)
  starting transfers between devices  40.2 us (29%)
  Pallas kernels  30.7 us (22%)
  local copies, waits for them, and re-layouts  3.99 us (3%)
    ppermute x24, waiting for transfers between devices, move(): return lax.ppermute(value, ('geo', 'dist'), perm)  33.5 us
    ppermute x10, waiting for transfers between devices, z_swap(): return lax.ppermute(value, 'dist', perm)  29 us
    ppermute x10, starting transfers between devices, z_swap(): return lax.ppermute(value, 'dist', perm)  20.4 us
    ppermute x24, starting transfers between devices, move(): return lax.ppermute(value, ('geo', 'dist'), perm)  19.8 us
    pallas_call x1, Pallas kernels, covariance(): pl.pallas_call(functools.partial(covariance_kernel, tiles, total, ages, r...  13 us
    pallas_call x4, Pallas kernels, partial_sums(): pl.pallas_call(functools.partial(sums_kernel, offsets, has_var), grid_spe...  5.66 us
    pallas_call x1, Pallas kernels, build_weights(): pl.pallas_call(functools.partial(weights_kernel, rows), grid_spec=pltpu.P...  4.87 us
    pallas_call x1, Pallas kernels, marginal(): pl.pallas_call(functools.partial(marginal_kernel, tiles), grid_spec=pltpu...  3.83 us
  transfers between devices with their start and end apart: 34, of which 15 were waited for; matrix products, arithmetic and copies ran while one was open for 1% of the time, Pallas kernels for 19%

profile of v11, /device:TPU:0, one launch (start us, length us, event | category | flops | bytes accessed | tf_op | source)
XLA Modules:
  0.0 138.9 jit_solution(16755310192348693688)
XLA Ops:
  0.7 1.4 %constant_dynamic-slice_fusion.14 = (bf16[96,3712]{1,0:T(8,128)(2,1)S(1)}, bf16[96,3712]{1,0:T(8,128)(2,1)S(1)}) fusion(bf16[96,7424]{1,0:T(8,128)(2,1)} %param.6, s32[]{:T(128)S(6)} %select_n.178, s32[]{:T(128)S(6)} %select_n.182), kind=kLoop, calls=%fused_computation.27 | loop fusion | bytes 2850824 | tf_op jit(solution)/shard_map/dynamic_slice | solution.py:360
  2.3 0.5 collective-permute-start
  3.0 1.6 %collective-permute-done = bf16[96,3840]{1,0:T(8,128)(2,1)S(1)} collective-permute-done((bf16[96,3840]{1,0:T(8,128)(2,1)S(1)}, bf16[96,3840]{1,0:T(8,128)(2,1)S(1)}, u32[]{:S(2)}, u32[]{:S(2)}) %collective-permute-start) | collective-permute-done | bytes 737312 | tf_op jit(solution)/shard_map/ppermute | solution.py:350
  4.8 2.9 %collective-permute-start.3 = (bf16[192,1024]{1,0:T(8,128)(2,1)S(1)}, bf16[192,1024]{1,0:T(8,128)(2,1)S(1)}, u32[]{:S(2)}, u32[]{:S(2)}) collective-permute-start(bf16[192,1024]{1,0:T(8,128)(2,1)S(1)} %pad_maximum_fusion.2), channel_id=1, source_target_pairs={{0,16},{1,17},{2,18},{3,19},{4,20},{5,21},{6,22},{7,23},{8,24},{9,... | collective-permute-start | bytes 1179656 | tf_op jit(solution)/shard_map/ppermute | solution.py:350
  7.7 2.6 %collective-permute-start.1 = (s32[64,128]{1,0:T(8,128)S(1)}, s32[64,128]{1,0:T(8,128)S(1)}, u32[]{:S(2)}, u32[]{:S(2)}) collective-permute-start(s32[64,128]{1,0:T(8,128)S(1)} %pad_add_fusion.2), channel_id=1, source_target_pairs={{0,4},{1,5},{2,6},{3,7},{4,0},{5,1},{6,2},{7,3},{8,12},{9,13},{10,... | collective-permute-start | bytes 98312 | tf_op jit(solution)/shard_map/ppermute | solution.py:354
  10.4 0.6 collective-permute-start.6
  11.0 1.5 %collective-permute-start.4 = (bf16[192,1024]{1,0:T(8,128)(2,1)S(1)}, bf16[192,1024]{1,0:T(8,128)(2,1)S(1)}, u32[]{:S(2)}, u32[]{:S(2)}) collective-permute-start(bf16[192,1024]{1,0:T(8,128)(2,1)S(1)} %pad_maximum_fusion.3.refs_0_), channel_id=1, source_target_pairs={{0,1},{1,0},{2,3},{3,2},{4,5},{5,4},{6,7},{7,6},{8,9},{9,8},{10,11... | collective-permute-start | bytes 1179656 | tf_op jit(solution)/shard_map/ppermute | solution.py:350
  12.8 1.5 %collective-permute-start.2 = (s32[64,256]{1,0:T(8,128)S(1)}, s32[64,256]{1,0:T(8,128)S(1)}, u32[]{:S(2)}, u32[]{:S(2)}) collective-permute-start(s32[64,256]{1,0:T(8,128)S(1)} %pad_add_fusion.1), channel_id=1, source_target_pairs={{0,2},{1,3},{2,0},{3,1},{4,6},{5,7},{6,4},{7,5},{8,10},{9,11},{10,... | collective-permute-start | bytes 196616 | tf_op jit(solution)/shard_map/ppermute | solution.py:354
  14.6 2.6 %collective-permute-done.2 = s32[64,256]{1,0:T(8,128)S(1)} collective-permute-done((s32[64,256]{1,0:T(8,128)S(1)}, s32[64,256]{1,0:T(8,128)S(1)}, u32[]{:S(2)}, u32[]{:S(2)}) %collective-permute-start.2) | collective-permute-done | bytes 65568 | tf_op jit(solution)/shard_map/ppermute | solution.py:354
  17.3 4.9 %build_weights.1.w_ref = bf16[768,512]{1,0:T(8,128)(2,1)S(1)} custom-call(s32[8]{0:T(128)S(1)} %stack.92.base_ref, s32[64,512]{1,0:T(8,128)S(1)} %pad_add_fusion.query_ref), custom_call_target="tpu_custom_call" | custom-call | flops 5033164800 | bytes 786432 | tf_op jit(solution)/shard_map/build_weights/pallas_call | solution.py:93
  22.2 1.4 %collective-permute-start.5 = (bf16[192,1024]{1,0:T(8,128)(2,1)S(1)}, bf16[192,1024]{1,0:T(8,128)(2,1)S(1)}, u32[]{:S(2)}, u32[]{:S(2)}) collective-permute-start(bf16[192,1024]{1,0:T(8,128)(2,1)S(1)} %collective-permute-done.3.refs_1_), channel_id=1, source_target_pairs={{0,1},{1,0},{2,3},{3,2},{4,5},{5,4},{6,7},{7,6},{8,9},{9,8},{10,11... | collective-permute-start | bytes 1179656 | tf_op jit(solution)/shard_map/ppermute | solution.py:350
  23.7 0.7 collective-permute-start.13
  24.5 1.8 %collective-permute-start.7 = (bf16[192,896]{1,0:T(8,128)(2,1)S(1)}, bf16[192,896]{1,0:T(8,128)(2,1)S(1)}, u32[]{:S(2)}, u32[]{:S(2)}) collective-permute-start(bf16[192,896]{1,0:T(8,128)(2,1)S(1)} %pad_maximum_fusion.4.refs_0_), channel_id=1, source_target_pairs={{0,1},{1,0},{2,3},{3,2},{4,5},{5,4},{6,7},{7,6},{8,9},{9,8},{10,11... | collective-permute-start | bytes 1032200 | tf_op jit(solution)/shard_map/ppermute | solution.py:350
  26.6 7.7 %collective-permute-done.5.refs_3_ = bf16[192,1024]{1,0:T(8,128)(2,1)S(1)} collective-permute-done((bf16[192,1024]{1,0:T(8,128)(2,1)S(1)}, bf16[192,1024]{1,0:T(8,128)(2,1)S(1)}, u32[]{:S(2)}, u32[]{:S(2)}) %collective-permute-start.5) | collective-permute-done | bytes 393248 | tf_op jit(solution)/shard_map/ppermute | solution.py:350
  34.2 1.5 %partial_sums.4 = (f32[1024,128]{1,0:T(8,128)S(1)}, f32[1024,128]{1,0:T(8,128)S(1)}, s16[2080,128]{1,0:T(8,128)(2,1)S(1)}) custom-call(s32[1]{0:T(128)} %bitcast.6.flag_ref, bf16[768,512]{1,0:T(8,128)(2,1)S(1)} %build_weights.1.w_ref, bf16[192,1024]{1,0:T(8,128)(2,1)S(1)} %pad_maximum_fusion.3.refs_0_, bf16[192,1024]{1,0:T(8,128)(2,1)S(1)} %collective-permute-done.3.refs_1_, ...), custom_call_target="tpu_custom_call" | custom-call | flops 805306368 | bytes 2883584 | tf_op jit(solution)/shard_map/partial_sums/pallas_call | solution.py:170
  35.8 1.6 %collective-permute-start.9 = (s16[2080,128]{1,0:T(8,128)(2,1)S(1)}, s16[2080,128]{1,0:T(8,128)(2,1)S(1)}, u32[]{:S(2)}, u32[]{:S(2)}) collective-permute-start(s16[2080,128]{1,0:T(8,128)(2,1)S(1)} %get-tuple-element.38), channel_id=1, source_target_pairs={{0,2},{1,3},{2,0},{3,1},{4,6},{5,7},{6,4},{7,5},{8,10},{9,11},{10,... | collective-permute-start | bytes 1597448 | tf_op jit(solution)/shard_map/ppermute | solution.py:354
  37.5 1.2 collective-permute-start.14
  38.7 3.0 %collective-permute-done.7.refs_2_ = bf16[192,896]{1,0:T(8,128)(2,1)S(1)} collective-permute-done((bf16[192,896]{1,0:T(8,128)(2,1)S(1)}, bf16[192,896]{1,0:T(8,128)(2,1)S(1)}, u32[]{:S(2)}, u32[]{:S(2)}) %collective-permute-start.7) | collective-permute-done | bytes 344096 | tf_op jit(solution)/shard_map/ppermute | solution.py:350
  41.6 7.4 %collective-permute-done.8.refs_3_ = bf16[192,896]{1,0:T(8,128)(2,1)S(1)} collective-permute-done((bf16[192,896]{1,0:T(8,128)(2,1)S(1)}, bf16[192,896]{1,0:T(8,128)(2,1)S(1)}, u32[]{:S(2)}, u32[]{:S(2)}) %collective-permute-start.8) | collective-permute-done | bytes 344096 | tf_op jit(solution)/shard_map/ppermute | solution.py:350
  49.0 1.4 partial_sums.5
  50.4 1.6 %collective-permute-start.10 = (s16[1824,128]{1,0:T(8,128)(2,1)S(1)}, s16[1824,128]{1,0:T(8,128)(2,1)S(1)}, u32[]{:S(2)}, u32[]{:S(2)}) collective-permute-start(s16[1824,128]{1,0:T(8,128)(2,1)S(1)} %get-tuple-element.40), channel_id=1, source_target_pairs={{0,2},{1,3},{2,0},{3,1},{4,6},{5,7},{6,4},{7,5},{8,10},{9,11},{10,... | collective-permute-start | bytes 1400840 | tf_op jit(solution)/shard_map/ppermute | solution.py:354
  52.0 1.2 collective-permute-start.15
  53.4 2.9 %collective-permute-start.11 = (s16[1040,128]{1,0:T(8,128)(2,1)S(1)}, s16[1040,128]{1,0:T(8,128)(2,1)S(1)}, u32[]{:S(2)}, u32[]{:S(2)}) collective-permute-start(s16[1040,128]{1,0:T(8,128)(2,1)S(1)} %combine.8), channel_id=1, source_target_pairs={{0,4},{1,5},{2,6},{3,7},{4,0},{5,1},{6,2},{7,3},{8,12},{9,13},{10,... | collective-permute-start | bytes 798728 | tf_op jit(solution)/shard_map/ppermute | solution.py:354
  56.4 0.6 collective-permute-start.21
  56.9 9.2 %collective-permute-done.10.refs_0_ = s16[1824,128]{1,0:T(8,128)(2,1)S(1)} collective-permute-done((s16[1824,128]{1,0:T(8,128)(2,1)S(1)}, s16[1824,128]{1,0:T(8,128)(2,1)S(1)}, u32[]{:S(2)}, u32[]{:S(2)}) %collective-permute-start.10) | collective-permute-done | bytes 466976 | tf_op jit(solution)/shard_map/ppermute | solution.py:354
  66.4 6.9 %collective-permute-done.15.refs_3_ = bf16[192,1024]{1,0:T(8,128)(2,1)S(1)} collective-permute-done((bf16[192,1024]{1,0:T(8,128)(2,1)S(1)}, bf16[192,1024]{1,0:T(8,128)(2,1)S(1)}, u32[]{:S(2)}, u32[]{:S(2)}) %collective-permute-start.15) | collective-permute-done | bytes 393248 | tf_op jit(solution)/shard_map/ppermute | solution.py:350
  73.2 1.5 %partial_sums.6 = (f32[1024,128]{1,0:T(8,128)S(1)}, f32[1024,128]{1,0:T(8,128)S(1)}, s16[2080,128]{1,0:T(8,128)(2,1)S(1)}) custom-call(s32[1]{0:T(128)} %bitcast.6.flag_ref, bf16[768,512]{1,0:T(8,128)(2,1)S(1)} %build_weights.1.w_ref, bf16[192,1920]{1,0:T(8,128)(2,1)S(1)} %pad_maximum_fusion.refs_0_, bf16[192,1920]{1,0:T(8,128)(2,1)S(1)} %collective-permute-done.13.refs_1_, ...), custom_call_target="tpu_custom_call" | custom-call | flops 805306368 | bytes 2883584 | tf_op jit(solution)/shard_map/partial_sums/pallas_call | solution.py:170
  74.7 1.6 %collective-permute-start.16 = (s16[2080,128]{1,0:T(8,128)(2,1)S(1)}, s16[2080,128]{1,0:T(8,128)(2,1)S(1)}, u32[]{:S(2)}, u32[]{:S(2)}) collective-permute-start(s16[2080,128]{1,0:T(8,128)(2,1)S(1)} %get-tuple-element.46), channel_id=1, source_target_pairs={{0,2},{1,3},{2,0},{3,1},{4,6},{5,7},{6,4},{7,5},{8,10},{9,11},{10,... | collective-permute-start | bytes 1597448 | tf_op jit(solution)/shard_map/ppermute | solution.py:354
  76.3 2.4 %collective-permute-start.25 = (s16[912,128]{1,0:T(8,128)(2,1)S(1)}, s16[912,128]{1,0:T(8,128)(2,1)S(1)}, u32[]{:S(2)}, u32[]{:S(2)}) collective-permute-start(s16[912,128]{1,0:T(8,128)(2,1)S(1)} %combine.9), channel_id=1, source_target_pairs={{0,4},{1,5},{2,6},{3,7},{4,0},{5,1},{6,2},{7,3},{8,12},{9,13},{10,... | collective-permute-start | bytes 700424 | tf_op jit(solution)/shard_map/ppermute | solution.py:354
  79.2 1.3 partial_sums.7
  80.5 1.7 %collective-permute-start.26 = (s16[1824,128]{1,0:T(8,128)(2,1)S(1)}, s16[1824,128]{1,0:T(8,128)(2,1)S(1)}, u32[]{:S(2)}, u32[]{:S(2)}) collective-permute-start(s16[1824,128]{1,0:T(8,128)(2,1)S(1)} %get-tuple-element.55), channel_id=1, source_target_pairs={{0,2},{1,3},{2,0},{3,1},{4,6},{5,7},{6,4},{7,5},{8,10},{9,11},{10,... | collective-permute-start | bytes 1400840 | tf_op jit(solution)/shard_map/ppermute | solution.py:354
  82.5 1.5 %collective-permute-start.23 = (s16[1040,128]{1,0:T(8,128)(2,1)S(1)}, s16[1040,128]{1,0:T(8,128)(2,1)S(1)}, u32[]{:S(2)}, u32[]{:S(2)}) collective-permute-start(s16[1040,128]{1,0:T(8,128)(2,1)S(1)} %combine.12.refs_0_), channel_id=1, source_target_pairs={{0,16},{1,17},{2,18},{3,19},{4,20},{5,21},{6,22},{7,23},{8,24},{9,... | collective-permute-start | bytes 798728 | tf_op jit(solution)/shard_map/ppermute | solution.py:350
  84.0 9.6 %collective-permute-done.16.refs_0_ = s16[2080,128]{1,0:T(8,128)(2,1)S(1)} collective-permute-done((s16[2080,128]{1,0:T(8,128)(2,1)S(1)}, s16[2080,128]{1,0:T(8,128)(2,1)S(1)}, u32[]{:S(2)}, u32[]{:S(2)}) %collective-permute-start.16) | collective-permute-done | bytes 532512 | tf_op jit(solution)/shard_map/ppermute | solution.py:354
  94.1 1.8 %collective-permute-start.28 = (s16[912,128]{1,0:T(8,128)(2,1)S(1)}, s16[912,128]{1,0:T(8,128)(2,1)}, u32[]{:S(2)}, u32[]{:S(2)}) collective-permute-start(s16[912,128]{1,0:T(8,128)(2,1)S(1)} %combine.13.refs_4_), channel_id=1, source_target_pairs={{0,16},{1,17},{2,18},{3,19},{4,20},{5,21},{6,22},{7,23},{8,24},{9,... | collective-permute-start | bytes 700424 | tf_op jit(solution)/shard_map/ppermute | solution.py:350
  95.9 3.1 %collective-permute-start.17 = (s16[1040,128]{1,0:T(8,128)(2,1)S(1)}, s16[1040,128]{1,0:T(8,128)(2,1)S(1)}, u32[]{:S(2)}, u32[]{:S(2)}) collective-permute-start(s16[1040,128]{1,0:T(8,128)(2,1)S(1)} %combine.10), channel_id=1, source_target_pairs={{0,4},{1,5},{2,6},{3,7},{4,0},{5,1},{6,2},{7,3},{8,12},{9,13},{10,... | collective-permute-start | bytes 798728 | tf_op jit(solution)/shard_map/ppermute | solution.py:354
  99.6 7.4 %collective-permute-done.26.refs_0_ = s16[1824,128]{1,0:T(8,128)(2,1)S(1)} collective-permute-done((s16[1824,128]{1,0:T(8,128)(2,1)S(1)}, s16[1824,128]{1,0:T(8,128)(2,1)S(1)}, u32[]{:S(2)}, u32[]{:S(2)}) %collective-permute-start.26) | collective-permute-done | bytes 466976 | tf_op jit(solution)/shard_map/ppermute | solution.py:354
  106.9 0.5 collective-permute-start.29
  107.4 0.9 combine.14
  108.3 0.7 copy-done
  109.0 1.3 collective-permute-start.30
  110.4 1.0 copy-done.1
  111.6 1.5 %collective-permute-start.19 = (s16[1040,128]{1,0:T(8,128)(2,1)S(1)}, s16[1040,128]{1,0:T(8,128)(2,1)S(1)}, u32[]{:S(2)}, u32[]{:S(2)}) collective-permute-start(s16[1040,128]{1,0:T(8,128)(2,1)S(1)} %combine.11.refs_0_), channel_id=1, source_target_pairs={{0,16},{1,17},{2,18},{3,19},{4,20},{5,21},{6,22},{7,23},{8,24},{9,... | collective-permute-start | bytes 798728 | tf_op jit(solution)/shard_map/ppermute | solution.py:350
  113.2 13.0 %covariance.1 = f32[13456,128]{1,0:T(8,128)} custom-call(s32[8]{0:T(128)S(1)} %stack.97.place_ref, s16[1040,128]{1,0:T(8,128)(2,1)S(1)} %combine.12.refs_0_, s16[1040,128]{1,0:T(8,128)(2,1)S(1)} %collective-permute-done.22.refs_1_, s16[1040,128]{1,0:T(8,128)(2,1)S(1)} %collective-permute-done.23.refs_2_, ...), custom_call_target="tpu_custom_call" | custom-call | flops 1763704832 | bytes 6889472 | tf_op jit(solution)/shard_map/covariance/pallas_call | solution.py:311
  126.2 1.2 combine.15.refs_4_
  127.3 0.6 collective-permute-start.32
  128.5 5.0 %collective-permute-done.32.refs_6_ = s16[912,128]{1,0:T(8,128)(2,1)S(1)} collective-permute-done((s16[912,128]{1,0:T(8,128)(2,1)S(1)}, s16[912,128]{1,0:T(8,128)(2,1)S(1)}, u32[]{:S(2)}, u32[]{:S(2)}) %collective-permute-start.32) | collective-permute-done | bytes 233504 | tf_op jit(solution)/shard_map/ppermute | solution.py:350
  133.7 1.4 collective-permute-done.33.refs_7_
  135.0 3.8 %marginal.1 = f32[128,7424]{1,0:T(8,128)} custom-call(s32[8]{0:T(128)S(1)} %stack.83.place_ref, s16[1040,128]{1,0:T(8,128)(2,1)S(1)} %combine.11.refs_0_, s16[1040,128]{1,0:T(8,128)(2,1)S(1)} %collective-permute-done.18.refs_1_, s16[1040,128]{1,0:T(8,128)(2,1)S(1)} %collective-permute-done.19.refs_2_, s16[1040,128]{1,0:T(8,128)(2,1)S(1)} %collective-permute-done.20.refs_3_, ...), custom_call_target="tpu_custom_call" | custom-call | flops 3801088 | bytes 5701632 | tf_op jit(solution)/shard_map/marginal/pallas_call | solution.py:238
  (70 shorter events, 4.8 us)
Async XLA Ops:
  0.6 1.5 %copy-start.3 = (bf16[96,116]{1,0:T(8,128)(2,1)S(1)}, bf16[96,116]{1,0:T(8,128)(2,1)}, u32[]{:S(2)}) copy-start(bf16[96,116]{1,0:T(8,128)(2,1)} %param.7) | copy-start | bytes 66820
  2.1 0.8 copy-start.4
  2.1 0.8 copy-start.5
  2.3 2.4 %collective-permute-start = (bf16[96,3840]{1,0:T(8,128)(2,1)S(1)}, bf16[96,3840]{1,0:T(8,128)(2,1)S(1)}, u32[]{:S(2)}, u32[]{:S(2)}) collective-permute-start(bf16[96,3840]{1,0:T(8,128)(2,1)S(1)} %get-tuple-element.73), channel_id=1, source_target_pairs={{0,8},{1,9},{2,10},{3,11},{4,12},{5,13},{6,14},{7,15},{8,0},{9,1},... | collective-permute-start | bytes 2211848 | tf_op jit(solution)/shard_map/ppermute | solution.py:350
  4.7 7.8 %copy-start.2 = (bf16[96,7424]{1,0:T(8,128)(2,1)S(1)}, bf16[96,7424]{1,0:T(8,128)(2,1)}, u32[]{:S(2)}) copy-start(bf16[96,7424]{1,0:T(8,128)(2,1)} %param.5) | copy-start | bytes 4276228
  4.8 17.3 %collective-permute-start.3 = (bf16[192,1024]{1,0:T(8,128)(2,1)S(1)}, bf16[192,1024]{1,0:T(8,128)(2,1)S(1)}, u32[]{:S(2)}, u32[]{:S(2)}) collective-permute-start(bf16[192,1024]{1,0:T(8,128)(2,1)S(1)} %pad_maximum_fusion.2), channel_id=1, source_target_pairs={{0,16},{1,17},{2,18},{3,19},{4,20},{5,21},{6,22},{7,23},{8,24},{9,... | collective-permute-start | bytes 1179656 | tf_op jit(solution)/shard_map/ppermute | solution.py:350
  7.7 5.1 %collective-permute-start.1 = (s32[64,128]{1,0:T(8,128)S(1)}, s32[64,128]{1,0:T(8,128)S(1)}, u32[]{:S(2)}, u32[]{:S(2)}) collective-permute-start(s32[64,128]{1,0:T(8,128)S(1)} %pad_add_fusion.2), channel_id=1, source_target_pairs={{0,4},{1,5},{2,6},{3,7},{4,0},{5,1},{6,2},{7,3},{8,12},{9,13},{10,... | collective-permute-start | bytes 98312 | tf_op jit(solution)/shard_map/ppermute | solution.py:354
  10.4 14.1 %collective-permute-start.6 = (bf16[192,896]{1,0:T(8,128)(2,1)S(1)}, bf16[192,896]{1,0:T(8,128)(2,1)S(1)}, u32[]{:S(2)}, u32[]{:S(2)}) collective-permute-start(bf16[192,896]{1,0:T(8,128)(2,1)S(1)} %pad_maximum_fusion.5), channel_id=1, source_target_pairs={{0,16},{1,17},{2,18},{3,19},{4,20},{5,21},{6,22},{7,23},{8,24},{9,... | collective-permute-start | bytes 1032200 | tf_op jit(solution)/shard_map/ppermute | solution.py:350
  11.0 15.5 %collective-permute-start.4 = (bf16[192,1024]{1,0:T(8,128)(2,1)S(1)}, bf16[192,1024]{1,0:T(8,128)(2,1)S(1)}, u32[]{:S(2)}, u32[]{:S(2)}) collective-permute-start(bf16[192,1024]{1,0:T(8,128)(2,1)S(1)} %pad_maximum_fusion.3.refs_0_), channel_id=1, source_target_pairs={{0,1},{1,0},{2,3},{3,2},{4,5},{5,4},{6,7},{7,6},{8,9},{9,8},{10,11... | collective-permute-start | bytes 1179656 | tf_op jit(solution)/shard_map/ppermute | solution.py:350
  12.6 11.0 %collective-permute-start.12 = (bf16[96,3712]{1,0:T(8,128)(2,1)S(1)}, bf16[96,3712]{1,0:T(8,128)(2,1)S(1)}, u32[]{:S(2)}, u32[]{:S(2)}) collective-permute-start(bf16[96,3712]{1,0:T(8,128)(2,1)S(1)} %constant_dynamic-slice_fusion.3), channel_id=1, source_target_pairs={{0,8},{1,9},{2,10},{3,11},{4,12},{5,13},{6,14},{7,15},{8,0},{9,1},... | collective-permute-start | bytes 2138120 | tf_op jit(solution)/shard_map/ppermute | solution.py:350
  12.8 4.4 %collective-permute-start.2 = (s32[64,256]{1,0:T(8,128)S(1)}, s32[64,256]{1,0:T(8,128)S(1)}, u32[]{:S(2)}, u32[]{:S(2)}) collective-permute-start(s32[64,256]{1,0:T(8,128)S(1)} %pad_add_fusion.1), channel_id=1, source_target_pairs={{0,2},{1,3},{2,0},{3,1},{4,6},{5,7},{6,4},{7,5},{8,10},{9,11},{10,... | collective-permute-start | bytes 196616 | tf_op jit(solution)/shard_map/ppermute | solution.py:354
  22.2 12.1 %collective-permute-start.5 = (bf16[192,1024]{1,0:T(8,128)(2,1)S(1)}, bf16[192,1024]{1,0:T(8,128)(2,1)S(1)}, u32[]{:S(2)}, u32[]{:S(2)}) collective-permute-start(bf16[192,1024]{1,0:T(8,128)(2,1)S(1)} %collective-permute-done.3.refs_1_), channel_id=1, source_target_pairs={{0,1},{1,0},{2,3},{3,2},{4,5},{5,4},{6,7},{7,6},{8,9},{9,8},{10,11... | collective-permute-start | bytes 1179656 | tf_op jit(solution)/shard_map/ppermute | solution.py:350
  23.7 28.3 %collective-permute-start.13 = (bf16[192,1920]{1,0:T(8,128)(2,1)S(1)}, bf16[192,1920]{1,0:T(8,128)(2,1)S(1)}, u32[]{:S(2)}, u32[]{:S(2)}) collective-permute-start(bf16[192,1920]{1,0:T(8,128)(2,1)S(1)} %pad_maximum_fusion.1), channel_id=1, source_target_pairs={{0,16},{1,17},{2,18},{3,19},{4,20},{5,21},{6,22},{7,23},{8,24},{9,... | collective-permute-start | bytes 2211848 | tf_op jit(solution)/shard_map/ppermute | solution.py:350
  24.5 17.1 %collective-permute-start.7 = (bf16[192,896]{1,0:T(8,128)(2,1)S(1)}, bf16[192,896]{1,0:T(8,128)(2,1)S(1)}, u32[]{:S(2)}, u32[]{:S(2)}) collective-permute-start(bf16[192,896]{1,0:T(8,128)(2,1)S(1)} %pad_maximum_fusion.4.refs_0_), channel_id=1, source_target_pairs={{0,1},{1,0},{2,3},{3,2},{4,5},{5,4},{6,7},{7,6},{8,9},{9,8},{10,11... | collective-permute-start | bytes 1032200 | tf_op jit(solution)/shard_map/ppermute | solution.py:350
  26.3 22.7 %collective-permute-start.8 = (bf16[192,896]{1,0:T(8,128)(2,1)S(1)}, bf16[192,896]{1,0:T(8,128)(2,1)S(1)}, u32[]{:S(2)}, u32[]{:S(2)}) collective-permute-start(bf16[192,896]{1,0:T(8,128)(2,1)S(1)} %collective-permute-done.6.refs_1_), channel_id=1, source_target_pairs={{0,1},{1,0},{2,3},{3,2},{4,5},{5,4},{6,7},{7,6},{8,9},{9,8},{10,11... | collective-permute-start | bytes 1032200 | tf_op jit(solution)/shard_map/ppermute | solution.py:350
  35.8 17.5 %collective-permute-start.9 = (s16[2080,128]{1,0:T(8,128)(2,1)S(1)}, s16[2080,128]{1,0:T(8,128)(2,1)S(1)}, u32[]{:S(2)}, u32[]{:S(2)}) collective-permute-start(s16[2080,128]{1,0:T(8,128)(2,1)S(1)} %get-tuple-element.38), channel_id=1, source_target_pairs={{0,2},{1,3},{2,0},{3,1},{4,6},{5,7},{6,4},{7,5},{8,10},{9,11},{10,... | collective-permute-start | bytes 1597448 | tf_op jit(solution)/shard_map/ppermute | solution.py:354
  37.5 28.9 %collective-permute-start.14 = (bf16[192,1920]{1,0:T(8,128)(2,1)S(1)}, bf16[192,1920]{1,0:T(8,128)(2,1)S(1)}, u32[]{:S(2)}, u32[]{:S(2)}) collective-permute-start(bf16[192,1920]{1,0:T(8,128)(2,1)S(1)} %pad_maximum_fusion.refs_0_), channel_id=1, source_target_pairs={{0,1},{1,0},{2,3},{3,2},{4,5},{5,4},{6,7},{7,6},{8,9},{9,8},{10,11... | collective-permute-start | bytes 2211848 | tf_op jit(solution)/shard_map/ppermute | solution.py:350
  50.4 15.8 %collective-permute-start.10 = (s16[1824,128]{1,0:T(8,128)(2,1)S(1)}, s16[1824,128]{1,0:T(8,128)(2,1)S(1)}, u32[]{:S(2)}, u32[]{:S(2)}) collective-permute-start(s16[1824,128]{1,0:T(8,128)(2,1)S(1)} %get-tuple-element.40), channel_id=1, source_target_pairs={{0,2},{1,3},{2,0},{3,1},{4,6},{5,7},{6,4},{7,5},{8,10},{9,11},{10,... | collective-permute-start | bytes 1400840 | tf_op jit(solution)/shard_map/ppermute | solution.py:354
  52.0 21.2 %collective-permute-start.15 = (bf16[192,1024]{1,0:T(8,128)(2,1)S(1)}, bf16[192,1024]{1,0:T(8,128)(2,1)S(1)}, u32[]{:S(2)}, u32[]{:S(2)}) collective-permute-start(bf16[192,1024]{1,0:T(8,128)(2,1)S(1)} %slice.8), channel_id=1, source_target_pairs={{0,1},{1,0},{2,3},{3,2},{4,5},{5,4},{6,7},{7,6},{8,9},{9,8},{10,11... | collective-permute-start | bytes 1179656 | tf_op jit(solution)/shard_map/ppermute | solution.py:350
  53.4 12.9 %collective-permute-start.11 = (s16[1040,128]{1,0:T(8,128)(2,1)S(1)}, s16[1040,128]{1,0:T(8,128)(2,1)S(1)}, u32[]{:S(2)}, u32[]{:S(2)}) collective-permute-start(s16[1040,128]{1,0:T(8,128)(2,1)S(1)} %combine.8), channel_id=1, source_target_pairs={{0,4},{1,5},{2,6},{3,7},{4,0},{5,1},{6,2},{7,3},{8,12},{9,13},{10,... | collective-permute-start | bytes 798728 | tf_op jit(solution)/shard_map/ppermute | solution.py:354
  56.4 22.9 %collective-permute-start.21 = (bf16[192,896]{1,0:T(8,128)(2,1)S(1)}, bf16[192,896]{1,0:T(8,128)(2,1)S(1)}, u32[]{:S(2)}, u32[]{:S(2)}) collective-permute-start(bf16[192,896]{1,0:T(8,128)(2,1)S(1)} %slice.9), channel_id=1, source_target_pairs={{0,1},{1,0},{2,3},{3,2},{4,5},{5,4},{6,7},{7,6},{8,9},{9,8},{10,11... | collective-permute-start | bytes 1032200 | tf_op jit(solution)/shard_map/ppermute | solution.py:350
  74.7 18.9 %collective-permute-start.16 = (s16[2080,128]{1,0:T(8,128)(2,1)S(1)}, s16[2080,128]{1,0:T(8,128)(2,1)S(1)}, u32[]{:S(2)}, u32[]{:S(2)}) collective-permute-start(s16[2080,128]{1,0:T(8,128)(2,1)S(1)} %get-tuple-element.46), channel_id=1, source_target_pairs={{0,2},{1,3},{2,0},{3,1},{4,6},{5,7},{6,4},{7,5},{8,10},{9,11},{10,... | collective-permute-start | bytes 1597448 | tf_op jit(solution)/shard_map/ppermute | solution.py:354
  76.3 17.6 %collective-permute-start.25 = (s16[912,128]{1,0:T(8,128)(2,1)S(1)}, s16[912,128]{1,0:T(8,128)(2,1)S(1)}, u32[]{:S(2)}, u32[]{:S(2)}) collective-permute-start(s16[912,128]{1,0:T(8,128)(2,1)S(1)} %combine.9), channel_id=1, source_target_pairs={{0,4},{1,5},{2,6},{3,7},{4,0},{5,1},{6,2},{7,3},{8,12},{9,13},{10,... | collective-permute-start | bytes 700424 | tf_op jit(solution)/shard_map/ppermute | solution.py:354
  80.5 26.4 %collective-permute-start.26 = (s16[1824,128]{1,0:T(8,128)(2,1)S(1)}, s16[1824,128]{1,0:T(8,128)(2,1)S(1)}, u32[]{:S(2)}, u32[]{:S(2)}) collective-permute-start(s16[1824,128]{1,0:T(8,128)(2,1)S(1)} %get-tuple-element.55), channel_id=1, source_target_pairs={{0,2},{1,3},{2,0},{3,1},{4,6},{5,7},{6,4},{7,5},{8,10},{9,11},{10,... | collective-permute-start | bytes 1400840 | tf_op jit(solution)/shard_map/ppermute | solution.py:354
  82.5 16.6 %collective-permute-start.23 = (s16[1040,128]{1,0:T(8,128)(2,1)S(1)}, s16[1040,128]{1,0:T(8,128)(2,1)S(1)}, u32[]{:S(2)}, u32[]{:S(2)}) collective-permute-start(s16[1040,128]{1,0:T(8,128)(2,1)S(1)} %combine.12.refs_0_), channel_id=1, source_target_pairs={{0,16},{1,17},{2,18},{3,19},{4,20},{5,21},{6,22},{7,23},{8,24},{9,... | collective-permute-start | bytes 798728 | tf_op jit(solution)/shard_map/ppermute | solution.py:350
  94.1 12.8 %collective-permute-start.28 = (s16[912,128]{1,0:T(8,128)(2,1)S(1)}, s16[912,128]{1,0:T(8,128)(2,1)}, u32[]{:S(2)}, u32[]{:S(2)}) collective-permute-start(s16[912,128]{1,0:T(8,128)(2,1)S(1)} %combine.13.refs_4_), channel_id=1, source_target_pairs={{0,16},{1,17},{2,18},{3,19},{4,20},{5,21},{6,22},{7,23},{8,24},{9,... | collective-permute-start | bytes 700424 | tf_op jit(solution)/shard_map/ppermute | solution.py:350
  95.9 12.4 %collective-permute-start.17 = (s16[1040,128]{1,0:T(8,128)(2,1)S(1)}, s16[1040,128]{1,0:T(8,128)(2,1)S(1)}, u32[]{:S(2)}, u32[]{:S(2)}) collective-permute-start(s16[1040,128]{1,0:T(8,128)(2,1)S(1)} %combine.10), channel_id=1, source_target_pairs={{0,4},{1,5},{2,6},{3,7},{4,0},{5,1},{6,2},{7,3},{8,12},{9,13},{10,... | collective-permute-start | bytes 798728 | tf_op jit(solution)/shard_map/ppermute | solution.py:354
  99.1 12.5 %collective-permute-start.22 = (s16[1040,128]{1,0:T(8,128)(2,1)S(1)}, s16[1040,128]{1,0:T(8,128)(2,1)S(1)}, u32[]{:S(2)}, u32[]{:S(2)}) collective-permute-start(s16[1040,128]{1,0:T(8,128)(2,1)S(1)} %combine.12.refs_0_), channel_id=1, source_target_pairs={{0,8},{1,9},{2,10},{3,11},{4,12},{5,13},{6,14},{7,15},{8,0},{9,1},... | collective-permute-start | bytes 798728 | tf_op jit(solution)/shard_map/ppermute | solution.py:350
  99.1 14.1 %collective-permute-start.24 = (s16[1040,128]{1,0:T(8,128)(2,1)S(1)}, s16[1040,128]{1,0:T(8,128)(2,1)S(1)}, u32[]{:S(2)}, u32[]{:S(2)}) collective-permute-start(s16[1040,128]{1,0:T(8,128)(2,1)S(1)} %collective-permute-done.23.refs_2_), channel_id=1, source_target_pairs={{0,8},{1,9},{2,10},{3,11},{4,12},{5,13},{6,14},{7,15},{8,0},{9,1},... | collective-permute-start | bytes 798728 | tf_op jit(solution)/shard_map/ppermute | solution.py:350
  106.9 6.2 %collective-permute-start.27 = (s16[912,128]{1,0:T(8,128)(2,1)S(1)}, s16[912,128]{1,0:T(8,128)(2,1)}, u32[]{:S(2)}, u32[]{:S(2)}) collective-permute-start(s16[912,128]{1,0:T(8,128)(2,1)S(1)} %combine.13.refs_4_), channel_id=1, source_target_pairs={{0,8},{1,9},{2,10},{3,11},{4,12},{5,13},{6,14},{7,15},{8,0},{9,1},... | collective-permute-start | bytes 700424 | tf_op jit(solution)/shard_map/ppermute | solution.py:350
  106.9 6.2 %collective-permute-start.29 = (s16[912,128]{1,0:T(8,128)(2,1)}, s16[912,128]{1,0:T(8,128)(2,1)}, u32[]{:S(2)}, u32[]{:S(2)}) collective-permute-start(s16[912,128]{1,0:T(8,128)(2,1)} %collective-permute-done.28.refs_6_), channel_id=1, source_target_pairs={{0,8},{1,9},{2,10},{3,11},{4,12},{5,13},{6,14},{7,15},{8,0},{9,1},... | collective-permute-start | bytes 700424 | tf_op jit(solution)/shard_map/ppermute | solution.py:350
  108.3 0.7 copy-start
  109.0 17.2 %collective-permute-start.30 = (s16[912,128]{1,0:T(8,128)(2,1)}, s16[912,128]{1,0:T(8,128)(2,1)}, u32[]{:S(2)}, u32[]{:S(2)}) collective-permute-start(s16[912,128]{1,0:T(8,128)(2,1)} %combine.14), channel_id=1, source_target_pairs={{0,4},{1,5},{2,6},{3,7},{4,0},{5,1},{6,2},{7,3},{8,12},{9,13},{10,... | collective-permute-start | bytes 700424 | tf_op jit(solution)/shard_map/ppermute | solution.py:354
  110.4 1.0 copy-start.1
  111.6 16.4 %collective-permute-start.19 = (s16[1040,128]{1,0:T(8,128)(2,1)S(1)}, s16[1040,128]{1,0:T(8,128)(2,1)S(1)}, u32[]{:S(2)}, u32[]{:S(2)}) collective-permute-start(s16[1040,128]{1,0:T(8,128)(2,1)S(1)} %combine.11.refs_0_), channel_id=1, source_target_pairs={{0,16},{1,17},{2,18},{3,19},{4,20},{5,21},{6,22},{7,23},{8,24},{9,... | collective-permute-start | bytes 798728 | tf_op jit(solution)/shard_map/ppermute | solution.py:350
  127.3 6.2 %collective-permute-start.32 = (s16[912,128]{1,0:T(8,128)(2,1)S(1)}, s16[912,128]{1,0:T(8,128)(2,1)S(1)}, u32[]{:S(2)}, u32[]{:S(2)}) collective-permute-start(s16[912,128]{1,0:T(8,128)(2,1)S(1)} %combine.15.refs_4_), channel_id=1, source_target_pairs={{0,16},{1,17},{2,18},{3,19},{4,20},{5,21},{6,22},{7,23},{8,24},{9,... | collective-permute-start | bytes 700424 | tf_op jit(solution)/shard_map/ppermute | solution.py:350
  128.0 5.7 %collective-permute-start.18 = (s16[1040,128]{1,0:T(8,128)(2,1)S(1)}, s16[1040,128]{1,0:T(8,128)(2,1)S(1)}, u32[]{:S(2)}, u32[]{:S(2)}) collective-permute-start(s16[1040,128]{1,0:T(8,128)(2,1)S(1)} %combine.11.refs_0_), channel_id=1, source_target_pairs={{0,8},{1,9},{2,10},{3,11},{4,12},{5,13},{6,14},{7,15},{8,0},{9,1},... | collective-permute-start | bytes 798728 | tf_op jit(solution)/shard_map/ppermute | solution.py:350
  128.0 5.7 %collective-permute-start.20 = (s16[1040,128]{1,0:T(8,128)(2,1)S(1)}, s16[1040,128]{1,0:T(8,128)(2,1)S(1)}, u32[]{:S(2)}, u32[]{:S(2)}) collective-permute-start(s16[1040,128]{1,0:T(8,128)(2,1)S(1)} %collective-permute-done.19.refs_2_), channel_id=1, source_target_pairs={{0,8},{1,9},{2,10},{3,11},{4,12},{5,13},{6,14},{7,15},{8,0},{9,1},... | collective-permute-start | bytes 798728 | tf_op jit(solution)/shard_map/ppermute | solution.py:350
  128.5 5.1 %collective-permute-start.31 = (s16[912,128]{1,0:T(8,128)(2,1)S(1)}, s16[912,128]{1,0:T(8,128)(2,1)S(1)}, u32[]{:S(2)}, u32[]{:S(2)}) collective-permute-start(s16[912,128]{1,0:T(8,128)(2,1)S(1)} %combine.15.refs_4_), channel_id=1, source_target_pairs={{0,8},{1,9},{2,10},{3,11},{4,12},{5,13},{6,14},{7,15},{8,0},{9,1},... | collective-permute-start | bytes 700424 | tf_op jit(solution)/shard_map/ppermute | solution.py:350
  133.5 1.5 %collective-permute-start.33 = (s16[912,128]{1,0:T(8,128)(2,1)S(1)}, s16[912,128]{1,0:T(8,128)(2,1)S(1)}, u32[]{:S(2)}, u32[]{:S(2)}) collective-permute-start(s16[912,128]{1,0:T(8,128)(2,1)S(1)} %collective-permute-done.32.refs_6_), channel_id=1, source_target_pairs={{0,8},{1,9},{2,10},{3,11},{4,12},{5,13},{6,14},{7,15},{8,0},{9,1},... | collective-permute-start | bytes 700424 | tf_op jit(solution)/shard_map/ppermute | solution.py:350

commit v12 on v10

--- a/solution.py
+++ b/solution.py
@@ -437,11 +437,11 @@
     own_b, near_b, middle_b, far_b = along_z(data_b, first_b, True, (own_a,), (middle_a,))
     data_c = merge([mean_y] + [along_y(value, 0, first_c, there) for value in mean_x[1:]])
     data_d = merge([later(mean_y, first_c)] + [along_y(value, first_c, first_d, there) for value in mean_x[1:]])
-    own_c, near_c, middle_c, far_c = along_z(data_c, first_c, False, (middle_b, far_a))
+    own_c, near_c, middle_c, far_c = along_z(data_c, first_c, False, (middle_b, far_a, far_b))
     mine_a, load_a = spread(own_a, near_a, far_a)
+    mine_b, load_b = spread(after(own_b, own_c), near_b, far_b)
     own_d, opposite_d, sent_d = partial_sums(flag, after(w, own_c), data_d, first_d, False)
     near_d = z_swap(sent_d, 1)
-    mine_b, load_b = spread(after(own_b, own_d), near_b, far_b)
     load_pieces = load_a + [after(load_b[0], middle_c, own_d)] + load_b[1:]
     cov = covariance(places(load_width), load_pieces, load_tiles, load_width * CORES, ages, rank)
     far_d = z_swap(combine(after(opposite_d, cov), (near_d, 1)), 2)

time: 141 us -> 137 us (0.972)
  waiting for transfers between devices: 68.6 us -> 62.5 us
  starting transfers between devices: 38.8 us -> 35.1 us
  local copies, waits for them, and re-layouts: 2.34 us -> 5.68 us
    ppermute x24, waiting for transfers between devices: 38.6 us -> 30.7 us  [move(): return lax.ppermute(value, ('geo', 'dist'), perm)]
    ppermute x10, starting transfers between devices: 19.1 us -> 15.1 us  [z_swap(): return lax.ppermute(value, 'dist', perm)]
    unnamed x8 -> x20, local copies, waits for them, and re-layouts: 0.02 us -> 1.88 us
    ppermute x10, waiting for transfers between devices: 30 us -> 31.9 us  [z_swap(): return lax.ppermute(value, 'dist', perm)]
    dynamic_slice x6, local copies, waits for them, and re-layouts: 0.52 us -> 2.01 us  [part(): lax.dynamic_slice(b, (0, start), size)]
  transfers between devices with their start and end apart: 34 -> 34, of which waited for: 14 -> 13; matrix products, arithmetic and copies ran while one was open for 1% -> 2% of each run, Pallas kernels for 19% -> 19%
where the time goes in v12:
time: 137 us
  waiting for transfers between devices  62.5 us (46%)
  starting transfers between devices  35.1 us (26%)
  Pallas kernels  31 us (23%)
  local copies, waits for them, and re-layouts  5.68 us (4%)
    ppermute x10, waiting for transfers between devices, z_swap(): return lax.ppermute(value, 'dist', perm)  31.9 us
    ppermute x24, waiting for transfers between devices, move(): return lax.ppermute(value, ('geo', 'dist'), perm)  30.7 us
    ppermute x24, starting transfers between devices, move(): return lax.ppermute(value, ('geo', 'dist'), perm)  20 us
    ppermute x10, starting transfers between devices, z_swap(): return lax.ppermute(value, 'dist', perm)  15.1 us
    pallas_call x1, Pallas kernels, covariance(): pl.pallas_call(functools.partial(covariance_kernel, tiles, total, ages, r...  13 us
    pallas_call x4, Pallas kernels, partial_sums(): pl.pallas_call(functools.partial(sums_kernel, offsets, has_var), grid_spe...  7.64 us
    pallas_call x1, Pallas kernels, build_weights(): pl.pallas_call(functools.partial(weights_kernel, rows), grid_spec=pltpu.P...  4.89 us
    pallas_call x1, Pallas kernels, marginal(): pl.pallas_call(functools.partial(marginal_kernel, tiles), grid_spec=pltpu...  3.83 us
  transfers between devices with their start and end apart: 34, of which 13 were waited for; matrix products, arithmetic and copies ran while one was open for 2% of the time, Pallas kernels for 19%

profile of v12, /device:TPU:0, one launch (start us, length us, event | category | flops | bytes accessed | tf_op | source)
XLA Modules:
  0.0 136.6 jit_solution(15644476416950851530)
XLA Ops:
  0.7 1.4 %constant_dynamic-slice_fusion.14 = (bf16[96,3712]{1,0:T(8,128)(2,1)S(1)}, bf16[96,3712]{1,0:T(8,128)(2,1)S(1)}) fusion(bf16[96,7424]{1,0:T(8,128)(2,1)} %param.6, s32[]{:T(128)S(6)} %select_n.178, s32[]{:T(128)S(6)} %select_n.182), kind=kLoop, calls=%fused_computation.27 | loop fusion | bytes 2850824 | tf_op jit(solution)/shard_map/dynamic_slice | solution.py:360
  2.3 0.5 collective-permute-start
  3.1 1.6 %collective-permute-done = bf16[96,3840]{1,0:T(8,128)(2,1)S(1)} collective-permute-done((bf16[96,3840]{1,0:T(8,128)(2,1)S(1)}, bf16[96,3840]{1,0:T(8,128)(2,1)S(1)}, u32[]{:S(2)}, u32[]{:S(2)}) %collective-permute-start) | collective-permute-done | bytes 737312 | tf_op jit(solution)/shard_map/ppermute | solution.py:350
  4.8 2.9 %collective-permute-start.3 = (bf16[192,1024]{1,0:T(8,128)(2,1)S(1)}, bf16[192,1024]{1,0:T(8,128)(2,1)S(1)}, u32[]{:S(2)}, u32[]{:S(2)}) collective-permute-start(bf16[192,1024]{1,0:T(8,128)(2,1)S(1)} %pad_maximum_fusion.2), channel_id=1, source_target_pairs={{0,16},{1,17},{2,18},{3,19},{4,20},{5,21},{6,22},{7,23},{8,24},{9,... | collective-permute-start | bytes 1179656 | tf_op jit(solution)/shard_map/ppermute | solution.py:350
  7.7 2.6 %collective-permute-start.1 = (s32[64,128]{1,0:T(8,128)S(1)}, s32[64,128]{1,0:T(8,128)S(1)}, u32[]{:S(2)}, u32[]{:S(2)}) collective-permute-start(s32[64,128]{1,0:T(8,128)S(1)} %pad_add_fusion.2), channel_id=1, source_target_pairs={{0,4},{1,5},{2,6},{3,7},{4,0},{5,1},{6,2},{7,3},{8,12},{9,13},{10,... | collective-permute-start | bytes 98312 | tf_op jit(solution)/shard_map/ppermute | solution.py:354
  10.4 0.6 collective-permute-start.6
  11.0 1.5 %collective-permute-start.4 = (bf16[192,1024]{1,0:T(8,128)(2,1)S(1)}, bf16[192,1024]{1,0:T(8,128)(2,1)S(1)}, u32[]{:S(2)}, u32[]{:S(2)}) collective-permute-start(bf16[192,1024]{1,0:T(8,128)(2,1)S(1)} %pad_maximum_fusion.3.refs_0_), channel_id=1, source_target_pairs={{0,1},{1,0},{2,3},{3,2},{4,5},{5,4},{6,7},{7,6},{8,9},{9,8},{10,11... | collective-permute-start | bytes 1179656 | tf_op jit(solution)/shard_map/ppermute | solution.py:350
  12.8 1.5 %collective-permute-start.2 = (s32[64,256]{1,0:T(8,128)S(1)}, s32[64,256]{1,0:T(8,128)S(1)}, u32[]{:S(2)}, u32[]{:S(2)}) collective-permute-start(s32[64,256]{1,0:T(8,128)S(1)} %pad_add_fusion.1), channel_id=1, source_target_pairs={{0,2},{1,3},{2,0},{3,1},{4,6},{5,7},{6,4},{7,5},{8,10},{9,11},{10,... | collective-permute-start | bytes 196616 | tf_op jit(solution)/shard_map/ppermute | solution.py:354
  14.3 1.0 constant_dynamic-slice_fusion.1
  15.4 1.9 %collective-permute-done.2 = s32[64,256]{1,0:T(8,128)S(1)} collective-permute-done((s32[64,256]{1,0:T(8,128)S(1)}, s32[64,256]{1,0:T(8,128)S(1)}, u32[]{:S(2)}, u32[]{:S(2)}) %collective-permute-start.2) | collective-permute-done | bytes 65568 | tf_op jit(solution)/shard_map/ppermute | solution.py:354
  17.3 4.9 %build_weights.1.w_ref = bf16[768,512]{1,0:T(8,128)(2,1)S(1)} custom-call(s32[8]{0:T(128)S(1)} %stack.92.base_ref, s32[64,512]{1,0:T(8,128)S(1)} %pad_add_fusion.query_ref), custom_call_target="tpu_custom_call" | custom-call | flops 5033164800 | bytes 786432 | tf_op jit(solution)/shard_map/build_weights/pallas_call | solution.py:93
  22.2 1.4 %collective-permute-start.5 = (bf16[192,1024]{1,0:T(8,128)(2,1)S(1)}, bf16[192,1024]{1,0:T(8,128)(2,1)S(1)}, u32[]{:S(2)}, u32[]{:S(2)}) collective-permute-start(bf16[192,1024]{1,0:T(8,128)(2,1)S(1)} %collective-permute-done.3.refs_1_), channel_id=1, source_target_pairs={{0,1},{1,0},{2,3},{3,2},{4,5},{5,4},{6,7},{7,6},{8,9},{9,8},{10,11... | collective-permute-start | bytes 1179656 | tf_op jit(solution)/shard_map/ppermute | solution.py:350
  23.6 0.8 constant_dynamic-slice_fusion
  24.4 0.9 pad_maximum_fusion.1
  25.3 0.7 collective-permute-start.14
  26.0 1.6 %collective-permute-start.7 = (bf16[192,896]{1,0:T(8,128)(2,1)S(1)}, bf16[192,896]{1,0:T(8,128)(2,1)}, u32[]{:S(2)}, u32[]{:S(2)}) collective-permute-start(bf16[192,896]{1,0:T(8,128)(2,1)S(1)} %pad_maximum_fusion.4.refs_0_), channel_id=1, source_target_pairs={{0,1},{1,0},{2,3},{3,2},{4,5},{5,4},{6,7},{7,6},{8,9},{9,8},{10,11... | collective-permute-start | bytes 1032200 | tf_op jit(solution)/shard_map/ppermute | solution.py:350
  27.6 0.5 collective-permute-start.8
  28.1 6.1 %collective-permute-done.5.refs_3_ = bf16[192,1024]{1,0:T(8,128)(2,1)S(1)} collective-permute-done((bf16[192,1024]{1,0:T(8,128)(2,1)S(1)}, bf16[192,1024]{1,0:T(8,128)(2,1)S(1)}, u32[]{:S(2)}, u32[]{:S(2)}) %collective-permute-start.5) | collective-permute-done | bytes 393248 | tf_op jit(solution)/shard_map/ppermute | solution.py:350
  34.3 1.5 %partial_sums.4 = (f32[1024,128]{1,0:T(8,128)S(1)}, f32[1024,128]{1,0:T(8,128)S(1)}, s16[2080,128]{1,0:T(8,128)(2,1)S(1)}) custom-call(s32[1]{0:T(128)} %bitcast.6.flag_ref, bf16[768,512]{1,0:T(8,128)(2,1)S(1)} %build_weights.1.w_ref, bf16[192,1024]{1,0:T(8,128)(2,1)S(1)} %pad_maximum_fusion.3.refs_0_, bf16[192,1024]{1,0:T(8,128)(2,1)S(1)} %collective-permute-done.3.refs_1_, ...), custom_call_target="tpu_custom_call" | custom-call | flops 805306368 | bytes 2883584 | tf_op jit(solution)/shard_map/partial_sums/pallas_call | solution.py:170
  35.8 1.6 %collective-permute-start.9 = (s16[2080,128]{1,0:T(8,128)(2,1)S(1)}, s16[2080,128]{1,0:T(8,128)(2,1)S(1)}, u32[]{:S(2)}, u32[]{:S(2)}) collective-permute-start(s16[2080,128]{1,0:T(8,128)(2,1)S(1)} %get-tuple-element.38), channel_id=1, source_target_pairs={{0,2},{1,3},{2,0},{3,1},{4,6},{5,7},{6,4},{7,5},{8,10},{9,11},{10,... | collective-permute-start | bytes 1597448 | tf_op jit(solution)/shard_map/ppermute | solution.py:354
  37.5 1.2 collective-permute-start.15
  38.7 3.1 %collective-permute-done.7.refs_2_ = bf16[192,896]{1,0:T(8,128)(2,1)} collective-permute-done((bf16[192,896]{1,0:T(8,128)(2,1)S(1)}, bf16[192,896]{1,0:T(8,128)(2,1)}, u32[]{:S(2)}, u32[]{:S(2)}) %collective-permute-start.7) | collective-permute-done | bytes 344096 | tf_op jit(solution)/shard_map/ppermute | solution.py:350
  41.7 7.4 %collective-permute-done.8.refs_3_ = bf16[192,896]{1,0:T(8,128)(2,1)} collective-permute-done((bf16[192,896]{1,0:T(8,128)(2,1)}, bf16[192,896]{1,0:T(8,128)(2,1)}, u32[]{:S(2)}, u32[]{:S(2)}) %collective-permute-start.8) | collective-permute-done | bytes 344096 | tf_op jit(solution)/shard_map/ppermute | solution.py:350
  49.1 2.6 %partial_sums.5 = (f32[896,128]{1,0:T(8,128)S(1)}, f32[896,128]{1,0:T(8,128)S(1)}, s16[1824,128]{1,0:T(8,128)(2,1)S(1)}) custom-call(s32[1]{0:T(128)} %bitcast.6.flag_ref, bf16[768,512]{1,0:T(8,128)(2,1)S(1)} %build_weights.1.w_ref, bf16[192,896]{1,0:T(8,128)(2,1)S(1)} %pad_maximum_fusion.4.refs_0_, bf16[192,896]{1,0:T(8,128)(2,1)} %collective-permute-done.6.refs_1_, ...), custom_call_target="tpu_custom_call" | custom-call | flops 704643072 | bytes 2523136 | tf_op jit(solution)/shard_map/partial_sums/pallas_call | solution.py:170
  51.7 1.6 %collective-permute-start.10 = (s16[1824,128]{1,0:T(8,128)(2,1)S(1)}, s16[1824,128]{1,0:T(8,128)(2,1)S(1)}, u32[]{:S(2)}, u32[]{:S(2)}) collective-permute-start(s16[1824,128]{1,0:T(8,128)(2,1)S(1)} %get-tuple-element.40), channel_id=1, source_target_pairs={{0,2},{1,3},{2,0},{3,1},{4,6},{5,7},{6,4},{7,5},{8,10},{9,11},{10,... | collective-permute-start | bytes 1400840 | tf_op jit(solution)/shard_map/ppermute | solution.py:354
  53.3 1.2 collective-permute-start.16
  54.7 2.9 %collective-permute-start.11 = (s16[1040,128]{1,0:T(8,128)(2,1)S(1)}, s16[1040,128]{1,0:T(8,128)(2,1)S(1)}, u32[]{:S(2)}, u32[]{:S(2)}) collective-permute-start(s16[1040,128]{1,0:T(8,128)(2,1)S(1)} %combine.8), channel_id=1, source_target_pairs={{0,4},{1,5},{2,6},{3,7},{4,0},{5,1},{6,2},{7,3},{8,12},{9,13},{10,... | collective-permute-start | bytes 798728 | tf_op jit(solution)/shard_map/ppermute | solution.py:354
  57.6 9.8 %collective-permute-done.10.refs_0_ = s16[1824,128]{1,0:T(8,128)(2,1)S(1)} collective-permute-done((s16[1824,128]{1,0:T(8,128)(2,1)S(1)}, s16[1824,128]{1,0:T(8,128)(2,1)S(1)}, u32[]{:S(2)}, u32[]{:S(2)}) %collective-permute-start.10) | collective-permute-done | bytes 466976 | tf_op jit(solution)/shard_map/ppermute | solution.py:354
  67.7 9.3 %collective-permute-done.12.refs_1_ = s16[912,128]{1,0:T(8,128)(2,1)S(1)} collective-permute-done((s16[912,128]{1,0:T(8,128)(2,1)S(1)}, s16[912,128]{1,0:T(8,128)(2,1)S(1)}, u32[]{:S(2)}, u32[]{:S(2)}) %collective-permute-start.12) | collective-permute-done | bytes 233504 | tf_op jit(solution)/shard_map/ppermute | solution.py:354
  77.0 1.5 %partial_sums.6 = (f32[1024,128]{1,0:T(8,128)S(1)}, f32[1024,128]{1,0:T(8,128)S(1)}, s16[2080,128]{1,0:T(8,128)(2,1)S(1)}) custom-call(s32[1]{0:T(128)} %bitcast.6.flag_ref, bf16[768,512]{1,0:T(8,128)(2,1)S(1)} %build_weights.1.w_ref, bf16[192,1920]{1,0:T(8,128)(2,1)S(1)} %pad_maximum_fusion.refs_0_, bf16[192,1920]{1,0:T(8,128)(2,1)S(1)} %collective-permute-done.14.refs_1_, ...), custom_call_target="tpu_custom_call" | custom-call | flops 805306368 | bytes 2883584 | tf_op jit(solution)/shard_map/partial_sums/pallas_call | solution.py:170
  78.5 0.6 collective-permute-start.20
  79.6 2.0 %collective-permute-start.18 = (s16[1040,128]{1,0:T(8,128)(2,1)S(1)}, s16[1040,128]{1,0:T(8,128)(2,1)}, u32[]{:S(2)}, u32[]{:S(2)}) collective-permute-start(s16[1040,128]{1,0:T(8,128)(2,1)S(1)} %combine.10.refs_0_), channel_id=1, source_target_pairs={{0,16},{1,17},{2,18},{3,19},{4,20},{5,21},{6,22},{7,23},{8,24},{9,... | collective-permute-start | bytes 798728 | tf_op jit(solution)/shard_map/ppermute | solution.py:350
  82.0 6.2 %collective-permute-done.21.refs_3_ = bf16[192,896]{1,0:T(8,128)(2,1)S(1)} collective-permute-done((bf16[192,896]{1,0:T(8,128)(2,1)S(1)}, bf16[192,896]{1,0:T(8,128)(2,1)S(1)}, u32[]{:S(2)}, u32[]{:S(2)}) %collective-permute-start.21) | collective-permute-done | bytes 344096 | tf_op jit(solution)/shard_map/ppermute | solution.py:350
  88.2 2.1 %partial_sums.7 = (f32[896,128]{1,0:T(8,128)S(1)}, f32[896,128]{1,0:T(8,128)S(1)}, s16[1824,128]{1,0:T(8,128)(2,1)}) custom-call(s32[1]{0:T(128)} %bitcast.6.flag_ref, bf16[768,512]{1,0:T(8,128)(2,1)S(1)} %build_weights.1.w_ref, bf16[192,1920]{1,0:T(8,128)(2,1)S(1)} %pad_maximum_fusion.refs_0_, bf16[192,1920]{1,0:T(8,128)(2,1)S(1)} %collective-permute-done.14.refs_1_, ...), custom_call_target="tpu_custom_call" | custom-call | flops 704643072 | bytes 2523136 | tf_op jit(solution)/shard_map/partial_sums/pallas_call | solution.py:170
  90.3 0.8 copy-done.2
  91.1 0.5 collective-permute-start.29
  91.5 0.5 collective-permute-start.19
  92.4 0.5 collective-permute-start.24
  93.0 1.0 copy-done.1
  94.2 3.5 %collective-permute-start.25 = (s16[1040,128]{1,0:T(8,128)(2,1)S(1)}, s16[1040,128]{1,0:T(8,128)(2,1)S(1)}, u32[]{:S(2)}, u32[]{:S(2)}) collective-permute-start(s16[1040,128]{1,0:T(8,128)(2,1)S(1)} %combine.12), channel_id=1, source_target_pairs={{0,4},{1,5},{2,6},{3,7},{4,0},{5,1},{6,2},{7,3},{8,12},{9,13},{10,... | collective-permute-start | bytes 798728 | tf_op jit(solution)/shard_map/ppermute | solution.py:354
  97.7 13.0 %covariance.1 = f32[13456,128]{1,0:T(8,128)} custom-call(s32[8]{0:T(128)S(1)} %stack.97.place_ref, s16[1040,128]{1,0:T(8,128)(2,1)S(1)} %combine.10.refs_0_, s16[1040,128]{1,0:T(8,128)(2,1)S(1)} %collective-permute-done.17.refs_1_, s16[1040,128]{1,0:T(8,128)(2,1)} %collective-permute-done.18.refs_2_, s16[1040,128]{1,0:T(8,128)(2,1)S(1)} %collective-permute-done.19.refs_3_, ...), custom_call_target="tpu_custom_call" | custom-call | flops 1763704832 | bytes 6889472 | tf_op jit(solution)/shard_map/covariance/pallas_call | solution.py:311
  111.4 2.0 %collective-permute-start.27 = (s16[1040,128]{1,0:T(8,128)(2,1)S(1)}, s16[1040,128]{1,0:T(8,128)(2,1)S(1)}, u32[]{:S(2)}, u32[]{:S(2)}) collective-permute-start(s16[1040,128]{1,0:T(8,128)(2,1)S(1)} %combine.13.refs_0_), channel_id=1, source_target_pairs={{0,16},{1,17},{2,18},{3,19},{4,20},{5,21},{6,22},{7,23},{8,24},{9,... | collective-permute-start | bytes 798728 | tf_op jit(solution)/shard_map/ppermute | solution.py:350
  113.4 10.7 %collective-permute-done.30.refs_1_ = s16[912,128]{1,0:T(8,128)(2,1)S(1)} collective-permute-done((s16[912,128]{1,0:T(8,128)(2,1)S(1)}, s16[912,128]{1,0:T(8,128)(2,1)S(1)}, u32[]{:S(2)}, u32[]{:S(2)}) %collective-permute-start.30) | collective-permute-done | bytes 233504 | tf_op jit(solution)/shard_map/ppermute | solution.py:354
  124.4 1.8 %collective-permute-start.32 = (s16[912,128]{1,0:T(8,128)(2,1)S(1)}, s16[912,128]{1,0:T(8,128)(2,1)S(1)}, u32[]{:S(2)}, u32[]{:S(2)}) collective-permute-start(s16[912,128]{1,0:T(8,128)(2,1)S(1)} %combine.15.refs_4_), channel_id=1, source_target_pairs={{0,16},{1,17},{2,18},{3,19},{4,20},{5,21},{6,22},{7,23},{8,24},{9,... | collective-permute-start | bytes 700424 | tf_op jit(solution)/shard_map/ppermute | solution.py:350
  126.2 0.5 collective-permute-start.28
  126.7 4.5 %collective-permute-done.32.refs_6_ = s16[912,128]{1,0:T(8,128)(2,1)S(1)} collective-permute-done((s16[912,128]{1,0:T(8,128)(2,1)S(1)}, s16[912,128]{1,0:T(8,128)(2,1)S(1)}, u32[]{:S(2)}, u32[]{:S(2)}) %collective-permute-start.32) | collective-permute-done | bytes 233504 | tf_op jit(solution)/shard_map/ppermute | solution.py:350
  131.3 1.4 %collective-permute-done.33.refs_7_ = s16[912,128]{1,0:T(8,128)(2,1)S(1)} collective-permute-done((s16[912,128]{1,0:T(8,128)(2,1)S(1)}, s16[912,128]{1,0:T(8,128)(2,1)S(1)}, u32[]{:S(2)}, u32[]{:S(2)}) %collective-permute-start.33) | collective-permute-done | bytes 233504 | tf_op jit(solution)/shard_map/ppermute | solution.py:350
  132.7 3.8 %marginal.1 = f32[128,7424]{1,0:T(8,128)} custom-call(s32[8]{0:T(128)S(1)} %stack.83.place_ref, s16[1040,128]{1,0:T(8,128)(2,1)S(1)} %combine.13.refs_0_, s16[1040,128]{1,0:T(8,128)(2,1)S(1)} %collective-permute-done.26.refs_1_, s16[1040,128]{1,0:T(8,128)(2,1)S(1)} %collective-permute-done.27.refs_2_, s16[1040,128]{1,0:T(8,128)(2,1)S(1)} %collective-permute-done.28.refs_3_, ...), custom_call_target="tpu_custom_call" | custom-call | flops 3801088 | bytes 5701632 | tf_op jit(solution)/shard_map/marginal/pallas_call | solution.py:238
  (78 shorter events, 4.0 us)
Async XLA Ops:
  0.6 1.5 %copy-start.7 = (bf16[96,116]{1,0:T(8,128)(2,1)S(1)}, bf16[96,116]{1,0:T(8,128)(2,1)}, u32[]{:S(2)}) copy-start(bf16[96,116]{1,0:T(8,128)(2,1)} %param.7) | copy-start | bytes 66820
  2.1 0.8 copy-start.8
  2.1 0.8 copy-start.9
  2.3 2.4 %collective-permute-start = (bf16[96,3840]{1,0:T(8,128)(2,1)S(1)}, bf16[96,3840]{1,0:T(8,128)(2,1)S(1)}, u32[]{:S(2)}, u32[]{:S(2)}) collective-permute-start(bf16[96,3840]{1,0:T(8,128)(2,1)S(1)} %get-tuple-element.73), channel_id=1, source_target_pairs={{0,8},{1,9},{2,10},{3,11},{4,12},{5,13},{6,14},{7,15},{8,0},{9,1},... | collective-permute-start | bytes 2211848 | tf_op jit(solution)/shard_map/ppermute | solution.py:350
  4.7 7.8 %copy-start.4 = (bf16[96,7424]{1,0:T(8,128)(2,1)S(1)}, bf16[96,7424]{1,0:T(8,128)(2,1)}, u32[]{:S(2)}) copy-start(bf16[96,7424]{1,0:T(8,128)(2,1)} %param.5) | copy-start | bytes 4276228
  4.8 17.3 %collective-permute-start.3 = (bf16[192,1024]{1,0:T(8,128)(2,1)S(1)}, bf16[192,1024]{1,0:T(8,128)(2,1)S(1)}, u32[]{:S(2)}, u32[]{:S(2)}) collective-permute-start(bf16[192,1024]{1,0:T(8,128)(2,1)S(1)} %pad_maximum_fusion.2), channel_id=1, source_target_pairs={{0,16},{1,17},{2,18},{3,19},{4,20},{5,21},{6,22},{7,23},{8,24},{9,... | collective-permute-start | bytes 1179656 | tf_op jit(solution)/shard_map/ppermute | solution.py:350
  7.7 5.1 %collective-permute-start.1 = (s32[64,128]{1,0:T(8,128)S(1)}, s32[64,128]{1,0:T(8,128)S(1)}, u32[]{:S(2)}, u32[]{:S(2)}) collective-permute-start(s32[64,128]{1,0:T(8,128)S(1)} %pad_add_fusion.2), channel_id=1, source_target_pairs={{0,4},{1,5},{2,6},{3,7},{4,0},{5,1},{6,2},{7,3},{8,12},{9,13},{10,... | collective-permute-start | bytes 98312 | tf_op jit(solution)/shard_map/ppermute | solution.py:354
  10.4 15.6 %collective-permute-start.6 = (bf16[192,896]{1,0:T(8,128)(2,1)S(1)}, bf16[192,896]{1,0:T(8,128)(2,1)}, u32[]{:S(2)}, u32[]{:S(2)}) collective-permute-start(bf16[192,896]{1,0:T(8,128)(2,1)S(1)} %pad_maximum_fusion.5), channel_id=1, source_target_pairs={{0,16},{1,17},{2,18},{3,19},{4,20},{5,21},{6,22},{7,23},{8,24},{9,... | collective-permute-start | bytes 1032200 | tf_op jit(solution)/shard_map/ppermute | solution.py:350
  11.0 17.1 %collective-permute-start.4 = (bf16[192,1024]{1,0:T(8,128)(2,1)S(1)}, bf16[192,1024]{1,0:T(8,128)(2,1)S(1)}, u32[]{:S(2)}, u32[]{:S(2)}) collective-permute-start(bf16[192,1024]{1,0:T(8,128)(2,1)S(1)} %pad_maximum_fusion.3.refs_0_), channel_id=1, source_target_pairs={{0,1},{1,0},{2,3},{3,2},{4,5},{5,4},{6,7},{7,6},{8,9},{9,8},{10,11... | collective-permute-start | bytes 1179656 | tf_op jit(solution)/shard_map/ppermute | solution.py:350
  12.6 11.0 %collective-permute-start.13 = (bf16[96,3712]{1,0:T(8,128)(2,1)S(1)}, bf16[96,3712]{1,0:T(8,128)(2,1)S(1)}, u32[]{:S(2)}, u32[]{:S(2)}) collective-permute-start(bf16[96,3712]{1,0:T(8,128)(2,1)S(1)} %constant_dynamic-slice_fusion.3), channel_id=1, source_target_pairs={{0,8},{1,9},{2,10},{3,11},{4,12},{5,13},{6,14},{7,15},{8,0},{9,1},... | collective-permute-start | bytes 2138120 | tf_op jit(solution)/shard_map/ppermute | solution.py:350
  12.8 4.4 %collective-permute-start.2 = (s32[64,256]{1,0:T(8,128)S(1)}, s32[64,256]{1,0:T(8,128)S(1)}, u32[]{:S(2)}, u32[]{:S(2)}) collective-permute-start(s32[64,256]{1,0:T(8,128)S(1)} %pad_add_fusion.1), channel_id=1, source_target_pairs={{0,2},{1,3},{2,0},{3,1},{4,6},{5,7},{6,4},{7,5},{8,10},{9,11},{10,... | collective-permute-start | bytes 196616 | tf_op jit(solution)/shard_map/ppermute | solution.py:354
  22.2 12.1 %collective-permute-start.5 = (bf16[192,1024]{1,0:T(8,128)(2,1)S(1)}, bf16[192,1024]{1,0:T(8,128)(2,1)S(1)}, u32[]{:S(2)}, u32[]{:S(2)}) collective-permute-start(bf16[192,1024]{1,0:T(8,128)(2,1)S(1)} %collective-permute-done.3.refs_1_), channel_id=1, source_target_pairs={{0,1},{1,0},{2,3},{3,2},{4,5},{5,4},{6,7},{7,6},{8,9},{9,8},{10,11... | collective-permute-start | bytes 1179656 | tf_op jit(solution)/shard_map/ppermute | solution.py:350
  25.3 28.0 %collective-permute-start.14 = (bf16[192,1920]{1,0:T(8,128)(2,1)}, bf16[192,1920]{1,0:T(8,128)(2,1)S(1)}, u32[]{:S(2)}, u32[]{:S(2)}) collective-permute-start(bf16[192,1920]{1,0:T(8,128)(2,1)} %pad_maximum_fusion.1), channel_id=1, source_target_pairs={{0,16},{1,17},{2,18},{3,19},{4,20},{5,21},{6,22},{7,23},{8,24},{9,... | collective-permute-start | bytes 2211848 | tf_op jit(solution)/shard_map/ppermute | solution.py:350
  26.0 15.7 %collective-permute-start.7 = (bf16[192,896]{1,0:T(8,128)(2,1)S(1)}, bf16[192,896]{1,0:T(8,128)(2,1)}, u32[]{:S(2)}, u32[]{:S(2)}) collective-permute-start(bf16[192,896]{1,0:T(8,128)(2,1)S(1)} %pad_maximum_fusion.4.refs_0_), channel_id=1, source_target_pairs={{0,1},{1,0},{2,3},{3,2},{4,5},{5,4},{6,7},{7,6},{8,9},{9,8},{10,11... | collective-permute-start | bytes 1032200 | tf_op jit(solution)/shard_map/ppermute | solution.py:350
  27.6 21.5 %collective-permute-start.8 = (bf16[192,896]{1,0:T(8,128)(2,1)}, bf16[192,896]{1,0:T(8,128)(2,1)}, u32[]{:S(2)}, u32[]{:S(2)}) collective-permute-start(bf16[192,896]{1,0:T(8,128)(2,1)} %collective-permute-done.6.refs_1_), channel_id=1, source_target_pairs={{0,1},{1,0},{2,3},{3,2},{4,5},{5,4},{6,7},{7,6},{8,9},{9,8},{10,11... | collective-permute-start | bytes 1032200 | tf_op jit(solution)/shard_map/ppermute | solution.py:350
  34.3 3.1 %copy-start.5 = (bf16[96,1920]{1,0:T(8,128)(2,1)S(1)}, bf16[96,1920]{1,0:T(8,128)(2,1)}, u32[]{:S(2)}) copy-start(bf16[96,1920]{1,0:T(8,128)(2,1)} %get-tuple-element.59) | copy-start | bytes 1105924
  34.3 3.1 %copy-start.6 = (bf16[96,1920]{1,0:T(8,128)(2,1)S(1)}, bf16[96,1920]{1,0:T(8,128)(2,1)}, u32[]{:S(2)}) copy-start(bf16[96,1920]{1,0:T(8,128)(2,1)} %get-tuple-element.71) | copy-start | bytes 1105924
  35.8 18.8 %collective-permute-start.9 = (s16[2080,128]{1,0:T(8,128)(2,1)S(1)}, s16[2080,128]{1,0:T(8,128)(2,1)S(1)}, u32[]{:S(2)}, u32[]{:S(2)}) collective-permute-start(s16[2080,128]{1,0:T(8,128)(2,1)S(1)} %get-tuple-element.38), channel_id=1, source_target_pairs={{0,2},{1,3},{2,0},{3,1},{4,6},{5,7},{6,4},{7,5},{8,10},{9,11},{10,... | collective-permute-start | bytes 1597448 | tf_op jit(solution)/shard_map/ppermute | solution.py:354
  37.5 39.5 %collective-permute-start.15 = (bf16[192,1920]{1,0:T(8,128)(2,1)S(1)}, bf16[192,1920]{1,0:T(8,128)(2,1)S(1)}, u32[]{:S(2)}, u32[]{:S(2)}) collective-permute-start(bf16[192,1920]{1,0:T(8,128)(2,1)S(1)} %pad_maximum_fusion.refs_0_), channel_id=1, source_target_pairs={{0,1},{1,0},{2,3},{3,2},{4,5},{5,4},{6,7},{7,6},{8,9},{9,8},{10,11... | collective-permute-start | bytes 2211848 | tf_op jit(solution)/shard_map/ppermute | solution.py:350
  51.7 15.8 %collective-permute-start.10 = (s16[1824,128]{1,0:T(8,128)(2,1)S(1)}, s16[1824,128]{1,0:T(8,128)(2,1)S(1)}, u32[]{:S(2)}, u32[]{:S(2)}) collective-permute-start(s16[1824,128]{1,0:T(8,128)(2,1)S(1)} %get-tuple-element.40), channel_id=1, source_target_pairs={{0,2},{1,3},{2,0},{3,1},{4,6},{5,7},{6,4},{7,5},{8,10},{9,11},{10,... | collective-permute-start | bytes 1400840 | tf_op jit(solution)/shard_map/ppermute | solution.py:354
  53.3 23.7 %collective-permute-start.16 = (bf16[192,1024]{1,0:T(8,128)(2,1)S(1)}, bf16[192,1024]{1,0:T(8,128)(2,1)S(1)}, u32[]{:S(2)}, u32[]{:S(2)}) collective-permute-start(bf16[192,1024]{1,0:T(8,128)(2,1)S(1)} %slice.8), channel_id=1, source_target_pairs={{0,1},{1,0},{2,3},{3,2},{4,5},{5,4},{6,7},{7,6},{8,9},{9,8},{10,11... | collective-permute-start | bytes 1179656 | tf_op jit(solution)/shard_map/ppermute | solution.py:350
  54.7 22.2 %collective-permute-start.11 = (s16[1040,128]{1,0:T(8,128)(2,1)S(1)}, s16[1040,128]{1,0:T(8,128)(2,1)S(1)}, u32[]{:S(2)}, u32[]{:S(2)}) collective-permute-start(s16[1040,128]{1,0:T(8,128)(2,1)S(1)} %combine.8), channel_id=1, source_target_pairs={{0,4},{1,5},{2,6},{3,7},{4,0},{5,1},{6,2},{7,3},{8,12},{9,13},{10,... | collective-permute-start | bytes 798728 | tf_op jit(solution)/shard_map/ppermute | solution.py:354
  67.6 9.3 %collective-permute-start.12 = (s16[912,128]{1,0:T(8,128)(2,1)S(1)}, s16[912,128]{1,0:T(8,128)(2,1)S(1)}, u32[]{:S(2)}, u32[]{:S(2)}) collective-permute-start(s16[912,128]{1,0:T(8,128)(2,1)S(1)} %combine.9), channel_id=1, source_target_pairs={{0,4},{1,5},{2,6},{3,7},{4,0},{5,1},{6,2},{7,3},{8,12},{9,13},{10,... | collective-permute-start | bytes 700424 | tf_op jit(solution)/shard_map/ppermute | solution.py:354
  78.5 3.1 %copy-start = (f32[1024,128]{1,0:T(8,128)}, f32[1024,128]{1,0:T(8,128)S(1)}, u32[]{:S(2)}) copy-start(f32[1024,128]{1,0:T(8,128)S(1)} %get-tuple-element.48.own_ref) | copy-start | bytes 1572868
  78.5 13.9 %collective-permute-start.20 = (s16[2080,128]{1,0:T(8,128)(2,1)S(1)}, s16[2080,128]{1,0:T(8,128)(2,1)S(1)}, u32[]{:S(2)}, u32[]{:S(2)}) collective-permute-start(s16[2080,128]{1,0:T(8,128)(2,1)S(1)} %get-tuple-element.49), channel_id=1, source_target_pairs={{0,2},{1,3},{2,0},{3,1},{4,6},{5,7},{6,4},{7,5},{8,10},{9,11},{10,... | collective-permute-start | bytes 1597448 | tf_op jit(solution)/shard_map/ppermute | solution.py:354
  79.1 9.1 %collective-permute-start.21 = (bf16[192,896]{1,0:T(8,128)(2,1)S(1)}, bf16[192,896]{1,0:T(8,128)(2,1)S(1)}, u32[]{:S(2)}, u32[]{:S(2)}) collective-permute-start(bf16[192,896]{1,0:T(8,128)(2,1)S(1)} %slice.9), channel_id=1, source_target_pairs={{0,1},{1,0},{2,3},{3,2},{4,5},{5,4},{6,7},{7,6},{8,9},{9,8},{10,11... | collective-permute-start | bytes 1032200 | tf_op jit(solution)/shard_map/ppermute | solution.py:350
  79.6 12.0 %collective-permute-start.18 = (s16[1040,128]{1,0:T(8,128)(2,1)S(1)}, s16[1040,128]{1,0:T(8,128)(2,1)}, u32[]{:S(2)}, u32[]{:S(2)}) collective-permute-start(s16[1040,128]{1,0:T(8,128)(2,1)S(1)} %combine.10.refs_0_), channel_id=1, source_target_pairs={{0,16},{1,17},{2,18},{3,19},{4,20},{5,21},{6,22},{7,23},{8,24},{9,... | collective-permute-start | bytes 798728 | tf_op jit(solution)/shard_map/ppermute | solution.py:350
  81.8 10.6 %collective-permute-start.23 = (s16[912,128]{1,0:T(8,128)(2,1)S(1)}, s16[912,128]{1,0:T(8,128)(2,1)}, u32[]{:S(2)}, u32[]{:S(2)}) collective-permute-start(s16[912,128]{1,0:T(8,128)(2,1)S(1)} %combine.11.refs_4_), channel_id=1, source_target_pairs={{0,16},{1,17},{2,18},{3,19},{4,20},{5,21},{6,22},{7,23},{8,24},{9,... | collective-permute-start | bytes 700424 | tf_op jit(solution)/shard_map/ppermute | solution.py:350
  90.3 0.8 copy-start.2
  91.1 19.6 %collective-permute-start.29 = (s16[1824,128]{1,0:T(8,128)(2,1)}, s16[1824,128]{1,0:T(8,128)(2,1)S(1)}, u32[]{:S(2)}, u32[]{:S(2)}) collective-permute-start(s16[1824,128]{1,0:T(8,128)(2,1)} %get-tuple-element.55), channel_id=1, source_target_pairs={{0,2},{1,3},{2,0},{3,1},{4,6},{5,7},{6,4},{7,5},{8,10},{9,11},{10,... | collective-permute-start | bytes 1400840 | tf_op jit(solution)/shard_map/ppermute | solution.py:354
  91.5 2.7 %collective-permute-start.17 = (s16[1040,128]{1,0:T(8,128)(2,1)S(1)}, s16[1040,128]{1,0:T(8,128)(2,1)S(1)}, u32[]{:S(2)}, u32[]{:S(2)}) collective-permute-start(s16[1040,128]{1,0:T(8,128)(2,1)S(1)} %combine.10.refs_0_), channel_id=1, source_target_pairs={{0,8},{1,9},{2,10},{3,11},{4,12},{5,13},{6,14},{7,15},{8,0},{9,1},... | collective-permute-start | bytes 798728 | tf_op jit(solution)/shard_map/ppermute | solution.py:350
  91.5 6.1 %collective-permute-start.19 = (s16[1040,128]{1,0:T(8,128)(2,1)}, s16[1040,128]{1,0:T(8,128)(2,1)S(1)}, u32[]{:S(2)}, u32[]{:S(2)}) collective-permute-start(s16[1040,128]{1,0:T(8,128)(2,1)} %collective-permute-done.18.refs_2_), channel_id=1, source_target_pairs={{0,8},{1,9},{2,10},{3,11},{4,12},{5,13},{6,14},{7,15},{8,0},{9,1},... | collective-permute-start | bytes 798728 | tf_op jit(solution)/shard_map/ppermute | solution.py:350
  92.4 5.3 %collective-permute-start.22 = (s16[912,128]{1,0:T(8,128)(2,1)S(1)}, s16[912,128]{1,0:T(8,128)(2,1)S(1)}, u32[]{:S(2)}, u32[]{:S(2)}) collective-permute-start(s16[912,128]{1,0:T(8,128)(2,1)S(1)} %combine.11.refs_4_), channel_id=1, source_target_pairs={{0,8},{1,9},{2,10},{3,11},{4,12},{5,13},{6,14},{7,15},{8,0},{9,1},... | collective-permute-start | bytes 700424 | tf_op jit(solution)/shard_map/ppermute | solution.py:350
  92.4 5.3 %collective-permute-start.24 = (s16[912,128]{1,0:T(8,128)(2,1)}, s16[912,128]{1,0:T(8,128)(2,1)}, u32[]{:S(2)}, u32[]{:S(2)}) collective-permute-start(s16[912,128]{1,0:T(8,128)(2,1)} %collective-permute-done.23.refs_6_), channel_id=1, source_target_pairs={{0,8},{1,9},{2,10},{3,11},{4,12},{5,13},{6,14},{7,15},{8,0},{9,1},... | collective-permute-start | bytes 700424 | tf_op jit(solution)/shard_map/ppermute | solution.py:350
  93.0 1.0 copy-start.1
  94.2 16.9 %collective-permute-start.25 = (s16[1040,128]{1,0:T(8,128)(2,1)S(1)}, s16[1040,128]{1,0:T(8,128)(2,1)S(1)}, u32[]{:S(2)}, u32[]{:S(2)}) collective-permute-start(s16[1040,128]{1,0:T(8,128)(2,1)S(1)} %combine.12), channel_id=1, source_target_pairs={{0,4},{1,5},{2,6},{3,7},{4,0},{5,1},{6,2},{7,3},{8,12},{9,13},{10,... | collective-permute-start | bytes 798728 | tf_op jit(solution)/shard_map/ppermute | solution.py:354
  110.7 13.5 %copy-start.3 = (f32[896,128]{1,0:T(8,128)S(1)}, f32[896,128]{1,0:T(8,128)}, u32[]{:S(2)}) copy-start(f32[896,128]{1,0:T(8,128)} %copy-done.2) | copy-start | bytes 1376260
  110.8 13.3 %collective-permute-start.30 = (s16[912,128]{1,0:T(8,128)(2,1)S(1)}, s16[912,128]{1,0:T(8,128)(2,1)S(1)}, u32[]{:S(2)}, u32[]{:S(2)}) collective-permute-start(s16[912,128]{1,0:T(8,128)(2,1)S(1)} %combine.14), channel_id=1, source_target_pairs={{0,4},{1,5},{2,6},{3,7},{4,0},{5,1},{6,2},{7,3},{8,12},{9,13},{10,... | collective-permute-start | bytes 700424 | tf_op jit(solution)/shard_map/ppermute | solution.py:354
  111.4 14.8 %collective-permute-start.27 = (s16[1040,128]{1,0:T(8,128)(2,1)S(1)}, s16[1040,128]{1,0:T(8,128)(2,1)S(1)}, u32[]{:S(2)}, u32[]{:S(2)}) collective-permute-start(s16[1040,128]{1,0:T(8,128)(2,1)S(1)} %combine.13.refs_0_), channel_id=1, source_target_pairs={{0,16},{1,17},{2,18},{3,19},{4,20},{5,21},{6,22},{7,23},{8,24},{9,... | collective-permute-start | bytes 798728 | tf_op jit(solution)/shard_map/ppermute | solution.py:350
  124.4 6.9 %collective-permute-start.32 = (s16[912,128]{1,0:T(8,128)(2,1)S(1)}, s16[912,128]{1,0:T(8,128)(2,1)S(1)}, u32[]{:S(2)}, u32[]{:S(2)}) collective-permute-start(s16[912,128]{1,0:T(8,128)(2,1)S(1)} %combine.15.refs_4_), channel_id=1, source_target_pairs={{0,16},{1,17},{2,18},{3,19},{4,20},{5,21},{6,22},{7,23},{8,24},{9,... | collective-permute-start | bytes 700424 | tf_op jit(solution)/shard_map/ppermute | solution.py:350
  126.2 5.1 %collective-permute-start.26 = (s16[1040,128]{1,0:T(8,128)(2,1)S(1)}, s16[1040,128]{1,0:T(8,128)(2,1)S(1)}, u32[]{:S(2)}, u32[]{:S(2)}) collective-permute-start(s16[1040,128]{1,0:T(8,128)(2,1)S(1)} %combine.13.refs_0_), channel_id=1, source_target_pairs={{0,8},{1,9},{2,10},{3,11},{4,12},{5,13},{6,14},{7,15},{8,0},{9,1},... | collective-permute-start | bytes 798728 | tf_op jit(solution)/shard_map/ppermute | solution.py:350
  126.2 6.5 %collective-permute-start.28 = (s16[1040,128]{1,0:T(8,128)(2,1)S(1)}, s16[1040,128]{1,0:T(8,128)(2,1)S(1)}, u32[]{:S(2)}, u32[]{:S(2)}) collective-permute-start(s16[1040,128]{1,0:T(8,128)(2,1)S(1)} %collective-permute-done.27.refs_2_), channel_id=1, source_target_pairs={{0,8},{1,9},{2,10},{3,11},{4,12},{5,13},{6,14},{7,15},{8,0},{9,1},... | collective-permute-start | bytes 798728 | tf_op jit(solution)/shard_map/ppermute | solution.py:350
  126.7 4.6 %collective-permute-start.31 = (s16[912,128]{1,0:T(8,128)(2,1)S(1)}, s16[912,128]{1,0:T(8,128)(2,1)S(1)}, u32[]{:S(2)}, u32[]{:S(2)}) collective-permute-start(s16[912,128]{1,0:T(8,128)(2,1)S(1)} %combine.15.refs_4_), channel_id=1, source_target_pairs={{0,8},{1,9},{2,10},{3,11},{4,12},{5,13},{6,14},{7,15},{8,0},{9,1},... | collective-permute-start | bytes 700424 | tf_op jit(solution)/shard_map/ppermute | solution.py:350
  131.2 1.5 %collective-permute-start.33 = (s16[912,128]{1,0:T(8,128)(2,1)S(1)}, s16[912,128]{1,0:T(8,128)(2,1)S(1)}, u32[]{:S(2)}, u32[]{:S(2)}) collective-permute-start(s16[912,128]{1,0:T(8,128)(2,1)S(1)} %collective-permute-done.32.refs_6_), channel_id=1, source_target_pairs={{0,8},{1,9},{2,10},{3,11},{4,12},{5,13},{6,14},{7,15},{8,0},{9,1},... | collective-permute-start | bytes 700424 | tf_op jit(solution)/shard_map/ppermute | solution.py:350

commit v13 on v12

--- a/solution.py
+++ b/solution.py
@@ -442,11 +442,12 @@
     mine_b, load_b = spread(after(own_b, own_c), near_b, far_b)
     own_d, opposite_d, sent_d = partial_sums(flag, after(w, own_c), data_d, first_d, False)
     near_d = z_swap(sent_d, 1)
-    load_pieces = load_a + [after(load_b[0], middle_c, own_d)] + load_b[1:]
+    middle_d = combine(after(opposite_d, middle_c), (near_d, 1))
+    far_d = z_swap(middle_d, 2)
+    load_pieces = load_a + [after(load_b[0], middle_d)] + load_b[1:]
     cov = covariance(places(load_width), load_pieces, load_tiles, load_width * CORES, ages, rank)
-    far_d = z_swap(combine(after(opposite_d, cov), (near_d, 1)), 2)
     mine_c, mean_c = spread(after(own_c, cov), near_c, far_c)
-    mine_d, mean_d = spread(own_d, near_d, far_d)
+    mine_d, mean_d = spread(after(own_d, cov), near_d, far_d)
     mean_pieces = mean_c + mean_d
     mean = marginal(places(mean_width), mean_pieces, mean_tiles, mean_width * CORES)
     return mean, cov.T

time: 137 us -> 140 us (1.022)
  Pallas kernels: 31 us -> 33.4 us
  waiting for transfers between devices: 62.5 us -> 64.4 us
  local copies, waits for them, and re-layouts: 5.68 us -> 3.8 us
    ppermute x24, waiting for transfers between devices: 30.7 us -> 34.5 us  [move(): return lax.ppermute(value, ('geo', 'dist'), perm)]
    pallas_call x8, Pallas kernels: 1.67 us -> 4.99 us  [combine(): pl.pallas_call(functools.partial(combine_kernel, [unit * shape[0] for _,...]
    ppermute x10, waiting for transfers between devices: 31.9 us -> 29.9 us  [z_swap(): return lax.ppermute(value, 'dist', perm)]
    unnamed x20 -> x12, local copies, waits for them, and re-layouts: 1.88 us -> 0.03 us
  transfers between devices with their start and end apart: 34 -> 34, of which waited for: 13 -> 17; matrix products, arithmetic and copies ran while one was open for 2% -> 2% of each run, Pallas kernels for 19% -> 21%
where the time goes in v13:
time: 140 us
  waiting for transfers between devices  64.4 us (46%)
  starting transfers between devices  35.9 us (26%)
  Pallas kernels  33.4 us (24%)
  local copies, waits for them, and re-layouts  3.8 us (3%)
    ppermute x24, waiting for transfers between devices, move(): return lax.ppermute(value, ('geo', 'dist'), perm)  34.5 us
    ppermute x10, waiting for transfers between devices, z_swap(): return lax.ppermute(value, 'dist', perm)  29.9 us
    ppermute x24, starting transfers between devices, move(): return lax.ppermute(value, ('geo', 'dist'), perm)  20.2 us
    ppermute x10, starting transfers between devices, z_swap(): return lax.ppermute(value, 'dist', perm)  15.7 us
    pallas_call x1, Pallas kernels, covariance(): pl.pallas_call(functools.partial(covariance_kernel, tiles, total, ages, r...  12.9 us
    pallas_call x4, Pallas kernels, partial_sums(): pl.pallas_call(functools.partial(sums_kernel, offsets, has_var), grid_spe...  6.83 us
    pallas_call x8, Pallas kernels, combine(): pl.pallas_call(functools.partial(combine_kernel, [unit * shape[0] for _,...  4.99 us
    pallas_call x1, Pallas kernels, build_weights(): pl.pallas_call(functools.partial(weights_kernel, rows), grid_spec=pltpu.P...  4.89 us
  transfers between devices with their start and end apart: 34, of which 17 were waited for; matrix products, arithmetic and copies ran while one was open for 2% of the time, Pallas kernels for 21%

profile of v13, /device:TPU:0, one launch (start us, length us, event | category | flops | bytes accessed | tf_op | source)
XLA Modules:
  0.0 139.8 jit_solution(15228579398891228903)
XLA Ops:
  0.7 1.4 %constant_dynamic-slice_fusion.14 = (bf16[96,3712]{1,0:T(8,128)(2,1)S(1)}, bf16[96,3712]{1,0:T(8,128)(2,1)S(1)}) fusion(bf16[96,7424]{1,0:T(8,128)(2,1)} %param.6, s32[]{:T(128)S(6)} %select_n.178, s32[]{:T(128)S(6)} %select_n.182), kind=kLoop, calls=%fused_computation.27 | loop fusion | bytes 2850824 | tf_op jit(solution)/shard_map/dynamic_slice | solution.py:360
  3.1 1.6 %collective-permute-done = bf16[96,3840]{1,0:T(8,128)(2,1)S(1)} collective-permute-done((bf16[96,3840]{1,0:T(8,128)(2,1)S(1)}, bf16[96,3840]{1,0:T(8,128)(2,1)S(1)}, u32[]{:S(2)}, u32[]{:S(2)}) %collective-permute-start) | collective-permute-done | bytes 737312 | tf_op jit(solution)/shard_map/ppermute | solution.py:350
  4.8 2.9 %collective-permute-start.3 = (bf16[192,1024]{1,0:T(8,128)(2,1)S(1)}, bf16[192,1024]{1,0:T(8,128)(2,1)S(1)}, u32[]{:S(2)}, u32[]{:S(2)}) collective-permute-start(bf16[192,1024]{1,0:T(8,128)(2,1)S(1)} %pad_maximum_fusion.2), channel_id=1, source_target_pairs={{0,16},{1,17},{2,18},{3,19},{4,20},{5,21},{6,22},{7,23},{8,24},{9,... | collective-permute-start | bytes 1179656 | tf_op jit(solution)/shard_map/ppermute | solution.py:350
  7.7 2.6 %collective-permute-start.1 = (s32[64,128]{1,0:T(8,128)S(1)}, s32[64,128]{1,0:T(8,128)S(1)}, u32[]{:S(2)}, u32[]{:S(2)}) collective-permute-start(s32[64,128]{1,0:T(8,128)S(1)} %pad_add_fusion.2), channel_id=1, source_target_pairs={{0,4},{1,5},{2,6},{3,7},{4,0},{5,1},{6,2},{7,3},{8,12},{9,13},{10,... | collective-permute-start | bytes 98312 | tf_op jit(solution)/shard_map/ppermute | solution.py:354
  10.4 0.6 collective-permute-start.6
  11.0 1.5 %collective-permute-start.4 = (bf16[192,1024]{1,0:T(8,128)(2,1)S(1)}, bf16[192,1024]{1,0:T(8,128)(2,1)S(1)}, u32[]{:S(2)}, u32[]{:S(2)}) collective-permute-start(bf16[192,1024]{1,0:T(8,128)(2,1)S(1)} %pad_maximum_fusion.3.refs_0_), channel_id=1, source_target_pairs={{0,1},{1,0},{2,3},{3,2},{4,5},{5,4},{6,7},{7,6},{8,9},{9,8},{10,11... | collective-permute-start | bytes 1179656 | tf_op jit(solution)/shard_map/ppermute | solution.py:350
  12.8 1.5 %collective-permute-start.2 = (s32[64,256]{1,0:T(8,128)S(1)}, s32[64,256]{1,0:T(8,128)S(1)}, u32[]{:S(2)}, u32[]{:S(2)}) collective-permute-start(s32[64,256]{1,0:T(8,128)S(1)} %pad_add_fusion.1), channel_id=1, source_target_pairs={{0,2},{1,3},{2,0},{3,1},{4,6},{5,7},{6,4},{7,5},{8,10},{9,11},{10,... | collective-permute-start | bytes 196616 | tf_op jit(solution)/shard_map/ppermute | solution.py:354
  14.3 1.0 constant_dynamic-slice_fusion.1
  15.4 1.9 %collective-permute-done.2 = s32[64,256]{1,0:T(8,128)S(1)} collective-permute-done((s32[64,256]{1,0:T(8,128)S(1)}, s32[64,256]{1,0:T(8,128)S(1)}, u32[]{:S(2)}, u32[]{:S(2)}) %collective-permute-start.2) | collective-permute-done | bytes 65568 | tf_op jit(solution)/shard_map/ppermute | solution.py:354
  17.3 4.9 %build_weights.1.w_ref = bf16[768,512]{1,0:T(8,128)(2,1)S(1)} custom-call(s32[8]{0:T(128)S(1)} %stack.92.base_ref, s32[64,512]{1,0:T(8,128)S(1)} %pad_add_fusion.query_ref), custom_call_target="tpu_custom_call" | custom-call | flops 5033164800 | bytes 786432 | tf_op jit(solution)/shard_map/build_weights/pallas_call | solution.py:93
  22.2 1.4 %collective-permute-start.5 = (bf16[192,1024]{1,0:T(8,128)(2,1)S(1)}, bf16[192,1024]{1,0:T(8,128)(2,1)S(1)}, u32[]{:S(2)}, u32[]{:S(2)}) collective-permute-start(bf16[192,1024]{1,0:T(8,128)(2,1)S(1)} %collective-permute-done.3.refs_1_), channel_id=1, source_target_pairs={{0,1},{1,0},{2,3},{3,2},{4,5},{5,4},{6,7},{7,6},{8,9},{9,8},{10,11... | collective-permute-start | bytes 1179656 | tf_op jit(solution)/shard_map/ppermute | solution.py:350
  23.6 0.8 constant_dynamic-slice_fusion
  24.4 0.9 pad_maximum_fusion.1
  25.3 0.7 collective-permute-start.14
  26.0 1.6 %collective-permute-start.7 = (bf16[192,896]{1,0:T(8,128)(2,1)S(1)}, bf16[192,896]{1,0:T(8,128)(2,1)}, u32[]{:S(2)}, u32[]{:S(2)}) collective-permute-start(bf16[192,896]{1,0:T(8,128)(2,1)S(1)} %pad_maximum_fusion.4.refs_0_), channel_id=1, source_target_pairs={{0,1},{1,0},{2,3},{3,2},{4,5},{5,4},{6,7},{7,6},{8,9},{9,8},{10,11... | collective-permute-start | bytes 1032200 | tf_op jit(solution)/shard_map/ppermute | solution.py:350
  28.1 6.1 %collective-permute-done.5.refs_3_ = bf16[192,1024]{1,0:T(8,128)(2,1)S(1)} collective-permute-done((bf16[192,1024]{1,0:T(8,128)(2,1)S(1)}, bf16[192,1024]{1,0:T(8,128)(2,1)S(1)}, u32[]{:S(2)}, u32[]{:S(2)}) %collective-permute-start.5) | collective-permute-done | bytes 393248 | tf_op jit(solution)/shard_map/ppermute | solution.py:350
  34.3 1.5 %partial_sums.4 = (f32[1024,128]{1,0:T(8,128)S(1)}, f32[1024,128]{1,0:T(8,128)S(1)}, s16[2080,128]{1,0:T(8,128)(2,1)S(1)}) custom-call(s32[1]{0:T(128)} %bitcast.6.flag_ref, bf16[768,512]{1,0:T(8,128)(2,1)S(1)} %build_weights.1.w_ref, bf16[192,1024]{1,0:T(8,128)(2,1)S(1)} %pad_maximum_fusion.3.refs_0_, bf16[192,1024]{1,0:T(8,128)(2,1)S(1)} %collective-permute-done.3.refs_1_, ...), custom_call_target="tpu_custom_call" | custom-call | flops 805306368 | bytes 2883584 | tf_op jit(solution)/shard_map/partial_sums/pallas_call | solution.py:170
  35.8 1.6 %collective-permute-start.9 = (s16[2080,128]{1,0:T(8,128)(2,1)S(1)}, s16[2080,128]{1,0:T(8,128)(2,1)S(1)}, u32[]{:S(2)}, u32[]{:S(2)}) collective-permute-start(s16[2080,128]{1,0:T(8,128)(2,1)S(1)} %get-tuple-element.39), channel_id=1, source_target_pairs={{0,2},{1,3},{2,0},{3,1},{4,6},{5,7},{6,4},{7,5},{8,10},{9,11},{10,... | collective-permute-start | bytes 1597448 | tf_op jit(solution)/shard_map/ppermute | solution.py:354
  37.5 1.2 collective-permute-start.15
  38.7 3.1 %collective-permute-done.7.refs_2_ = bf16[192,896]{1,0:T(8,128)(2,1)} collective-permute-done((bf16[192,896]{1,0:T(8,128)(2,1)S(1)}, bf16[192,896]{1,0:T(8,128)(2,1)}, u32[]{:S(2)}, u32[]{:S(2)}) %collective-permute-start.7) | collective-permute-done | bytes 344096 | tf_op jit(solution)/shard_map/ppermute | solution.py:350
  41.7 7.4 %collective-permute-done.8.refs_3_ = bf16[192,896]{1,0:T(8,128)(2,1)} collective-permute-done((bf16[192,896]{1,0:T(8,128)(2,1)}, bf16[192,896]{1,0:T(8,128)(2,1)}, u32[]{:S(2)}, u32[]{:S(2)}) %collective-permute-start.8) | collective-permute-done | bytes 344096 | tf_op jit(solution)/shard_map/ppermute | solution.py:350
  49.1 2.6 %partial_sums.5 = (f32[896,128]{1,0:T(8,128)S(1)}, f32[896,128]{1,0:T(8,128)S(1)}, s16[1824,128]{1,0:T(8,128)(2,1)S(1)}) custom-call(s32[1]{0:T(128)} %bitcast.6.flag_ref, bf16[768,512]{1,0:T(8,128)(2,1)S(1)} %build_weights.1.w_ref, bf16[192,896]{1,0:T(8,128)(2,1)S(1)} %pad_maximum_fusion.4.refs_0_, bf16[192,896]{1,0:T(8,128)(2,1)} %collective-permute-done.6.refs_1_, ...), custom_call_target="tpu_custom_call" | custom-call | flops 704643072 | bytes 2523136 | tf_op jit(solution)/shard_map/partial_sums/pallas_call | solution.py:170
  51.7 1.6 %collective-permute-start.10 = (s16[1824,128]{1,0:T(8,128)(2,1)S(1)}, s16[1824,128]{1,0:T(8,128)(2,1)S(1)}, u32[]{:S(2)}, u32[]{:S(2)}) collective-permute-start(s16[1824,128]{1,0:T(8,128)(2,1)S(1)} %get-tuple-element.41), channel_id=1, source_target_pairs={{0,2},{1,3},{2,0},{3,1},{4,6},{5,7},{6,4},{7,5},{8,10},{9,11},{10,... | collective-permute-start | bytes 1400840 | tf_op jit(solution)/shard_map/ppermute | solution.py:354
  53.3 1.2 collective-permute-start.16
  54.7 2.9 %collective-permute-start.11 = (s16[1040,128]{1,0:T(8,128)(2,1)S(1)}, s16[1040,128]{1,0:T(8,128)(2,1)S(1)}, u32[]{:S(2)}, u32[]{:S(2)}) collective-permute-start(s16[1040,128]{1,0:T(8,128)(2,1)S(1)} %combine.8), channel_id=1, source_target_pairs={{0,4},{1,5},{2,6},{3,7},{4,0},{5,1},{6,2},{7,3},{8,12},{9,13},{10,... | collective-permute-start | bytes 798728 | tf_op jit(solution)/shard_map/ppermute | solution.py:354
  57.6 9.8 %collective-permute-done.10.refs_0_ = s16[1824,128]{1,0:T(8,128)(2,1)S(1)} collective-permute-done((s16[1824,128]{1,0:T(8,128)(2,1)S(1)}, s16[1824,128]{1,0:T(8,128)(2,1)S(1)}, u32[]{:S(2)}, u32[]{:S(2)}) %collective-permute-start.10) | collective-permute-done | bytes 466976 | tf_op jit(solution)/shard_map/ppermute | solution.py:354
  67.8 9.2 %collective-permute-done.12.refs_1_ = s16[912,128]{1,0:T(8,128)(2,1)S(1)} collective-permute-done((s16[912,128]{1,0:T(8,128)(2,1)S(1)}, s16[912,128]{1,0:T(8,128)(2,1)S(1)}, u32[]{:S(2)}, u32[]{:S(2)}) %collective-permute-start.12) | collective-permute-done | bytes 233504 | tf_op jit(solution)/shard_map/ppermute | solution.py:354
  77.0 1.5 %partial_sums.6 = (f32[1024,128]{1,0:T(8,128)S(1)}, f32[1024,128]{1,0:T(8,128)S(1)}, s16[2080,128]{1,0:T(8,128)(2,1)S(1)}) custom-call(s32[1]{0:T(128)} %bitcast.6.flag_ref, bf16[768,512]{1,0:T(8,128)(2,1)S(1)} %build_weights.1.w_ref, bf16[192,1920]{1,0:T(8,128)(2,1)S(1)} %pad_maximum_fusion.refs_0_, bf16[192,1920]{1,0:T(8,128)(2,1)S(1)} %collective-permute-done.14.refs_1_, ...), custom_call_target="tpu_custom_call" | custom-call | flops 805306368 | bytes 2883584 | tf_op jit(solution)/shard_map/partial_sums/pallas_call | solution.py:170
  78.5 0.6 collective-permute-start.21
  79.3 1.3 partial_sums.7
  80.5 1.7 %collective-permute-start.22 = (s16[1824,128]{1,0:T(8,128)(2,1)S(1)}, s16[1824,128]{1,0:T(8,128)(2,1)S(1)}, u32[]{:S(2)}, u32[]{:S(2)}) collective-permute-start(s16[1824,128]{1,0:T(8,128)(2,1)S(1)} %get-tuple-element.55), channel_id=1, source_target_pairs={{0,2},{1,3},{2,0},{3,1},{4,6},{5,7},{6,4},{7,5},{8,10},{9,11},{10,... | collective-permute-start | bytes 1400840 | tf_op jit(solution)/shard_map/ppermute | solution.py:354
  82.5 2.0 %collective-permute-start.18 = (s16[1040,128]{1,0:T(8,128)(2,1)S(1)}, s16[1040,128]{1,0:T(8,128)(2,1)S(1)}, u32[]{:S(2)}, u32[]{:S(2)}) collective-permute-start(s16[1040,128]{1,0:T(8,128)(2,1)S(1)} %combine.10.refs_0_), channel_id=1, source_target_pairs={{0,16},{1,17},{2,18},{3,19},{4,20},{5,21},{6,22},{7,23},{8,24},{9,... | collective-permute-start | bytes 798728 | tf_op jit(solution)/shard_map/ppermute | solution.py:350
  84.9 7.0 %collective-permute-done.18.refs_2_ = s16[1040,128]{1,0:T(8,128)(2,1)S(1)} collective-permute-done((s16[1040,128]{1,0:T(8,128)(2,1)S(1)}, s16[1040,128]{1,0:T(8,128)(2,1)S(1)}, u32[]{:S(2)}, u32[]{:S(2)}) %collective-permute-start.18) | collective-permute-done | bytes 266272 | tf_op jit(solution)/shard_map/ppermute | solution.py:350
  91.9 2.5 %collective-permute-done.24.refs_6_ = s16[912,128]{1,0:T(8,128)(2,1)S(1)} collective-permute-done((s16[912,128]{1,0:T(8,128)(2,1)S(1)}, s16[912,128]{1,0:T(8,128)(2,1)S(1)}, u32[]{:S(2)}, u32[]{:S(2)}) %collective-permute-start.24) | collective-permute-done | bytes 233504 | tf_op jit(solution)/shard_map/ppermute | solution.py:350
  94.9 0.9 combine.12
  95.8 5.0 %collective-permute-done.22.refs_0_ = s16[1824,128]{1,0:T(8,128)(2,1)S(1)} collective-permute-done((s16[1824,128]{1,0:T(8,128)(2,1)S(1)}, s16[1824,128]{1,0:T(8,128)(2,1)S(1)}, u32[]{:S(2)}, u32[]{:S(2)}) %collective-permute-start.22) | collective-permute-done | bytes 466976 | tf_op jit(solution)/shard_map/ppermute | solution.py:354
  100.8 3.2 %collective-permute-start.26 = (s16[1040,128]{1,0:T(8,128)(2,1)}, s16[1040,128]{1,0:T(8,128)(2,1)}, u32[]{:S(2)}, u32[]{:S(2)}) collective-permute-start(s16[1040,128]{1,0:T(8,128)(2,1)} %combine.12), channel_id=1, source_target_pairs={{0,4},{1,5},{2,6},{3,7},{4,0},{5,1},{6,2},{7,3},{8,12},{9,13},{10,... | collective-permute-start | bytes 798728 | tf_op jit(solution)/shard_map/ppermute | solution.py:354
  104.0 0.9 combine.13
  105.0 12.9 %covariance.1 = f32[13456,128]{1,0:T(8,128)} custom-call(s32[8]{0:T(128)S(1)} %stack.97.place_ref, s16[1040,128]{1,0:T(8,128)(2,1)S(1)} %combine.10.refs_0_, s16[1040,128]{1,0:T(8,128)(2,1)S(1)} %collective-permute-done.17.refs_1_, s16[1040,128]{1,0:T(8,128)(2,1)S(1)} %collective-permute-done.18.refs_2_, ...), custom_call_target="tpu_custom_call" | custom-call | flops 1763704832 | bytes 6889472 | tf_op jit(solution)/shard_map/covariance/pallas_call | solution.py:311
  117.9 3.4 %collective-permute-done.26.refs_1_ = s16[1040,128]{1,0:T(8,128)(2,1)} collective-permute-done((s16[1040,128]{1,0:T(8,128)(2,1)}, s16[1040,128]{1,0:T(8,128)(2,1)}, u32[]{:S(2)}, u32[]{:S(2)}) %collective-permute-start.26) | collective-permute-done | bytes 266272 | tf_op jit(solution)/shard_map/ppermute | solution.py:354
  121.3 1.2 combine.14.refs_0_
  122.6 2.3 %collective-permute-start.28 = (s16[1040,128]{1,0:T(8,128)(2,1)S(1)}, s16[1040,128]{1,0:T(8,128)(2,1)S(1)}, u32[]{:S(2)}, u32[]{:S(2)}) collective-permute-start(s16[1040,128]{1,0:T(8,128)(2,1)S(1)} %combine.14.refs_0_), channel_id=1, source_target_pairs={{0,16},{1,17},{2,18},{3,19},{4,20},{5,21},{6,22},{7,23},{8,24},{9,... | collective-permute-start | bytes 798728 | tf_op jit(solution)/shard_map/ppermute | solution.py:350
  125.3 1.2 combine.15.refs_4_
  126.5 2.3 %collective-permute-start.32 = (s16[912,128]{1,0:T(8,128)(2,1)S(1)}, s16[912,128]{1,0:T(8,128)(2,1)S(1)}, u32[]{:S(2)}, u32[]{:S(2)}) collective-permute-start(s16[912,128]{1,0:T(8,128)(2,1)S(1)} %combine.15.refs_4_), channel_id=1, source_target_pairs={{0,16},{1,17},{2,18},{3,19},{4,20},{5,21},{6,22},{7,23},{8,24},{9,... | collective-permute-start | bytes 700424 | tf_op jit(solution)/shard_map/ppermute | solution.py:350
  128.8 1.3 collective-permute-done.28.refs_2_
  130.7 3.8 %collective-permute-done.32.refs_6_ = s16[912,128]{1,0:T(8,128)(2,1)S(1)} collective-permute-done((s16[912,128]{1,0:T(8,128)(2,1)S(1)}, s16[912,128]{1,0:T(8,128)(2,1)S(1)}, u32[]{:S(2)}, u32[]{:S(2)}) %collective-permute-start.32) | collective-permute-done | bytes 233504 | tf_op jit(solution)/shard_map/ppermute | solution.py:350
  134.6 1.4 collective-permute-done.33.refs_7_
  136.0 3.8 %marginal.1 = f32[128,7424]{1,0:T(8,128)} custom-call(s32[8]{0:T(128)S(1)} %stack.83.place_ref, s16[1040,128]{1,0:T(8,128)(2,1)S(1)} %combine.14.refs_0_, s16[1040,128]{1,0:T(8,128)(2,1)S(1)} %collective-permute-done.27.refs_1_, s16[1040,128]{1,0:T(8,128)(2,1)S(1)} %collective-permute-done.28.refs_2_, s16[1040,128]{1,0:T(8,128)(2,1)S(1)} %collective-permute-done.29.refs_3_, ...), custom_call_target="tpu_custom_call" | custom-call | flops 3801088 | bytes 5701632 | tf_op jit(solution)/shard_map/marginal/pallas_call | solution.py:238
  (70 shorter events, 5.0 us)
Async XLA Ops:
  0.6 1.5 %copy-start.3 = (bf16[96,116]{1,0:T(8,128)(2,1)S(1)}, bf16[96,116]{1,0:T(8,128)(2,1)}, u32[]{:S(2)}) copy-start(bf16[96,116]{1,0:T(8,128)(2,1)} %param.7) | copy-start | bytes 66820
  2.1 0.8 copy-start.4
  2.1 0.8 copy-start.5
  2.3 2.4 %collective-permute-start = (bf16[96,3840]{1,0:T(8,128)(2,1)S(1)}, bf16[96,3840]{1,0:T(8,128)(2,1)S(1)}, u32[]{:S(2)}, u32[]{:S(2)}) collective-permute-start(bf16[96,3840]{1,0:T(8,128)(2,1)S(1)} %get-tuple-element.75), channel_id=1, source_target_pairs={{0,8},{1,9},{2,10},{3,11},{4,12},{5,13},{6,14},{7,15},{8,0},{9,1},... | collective-permute-start | bytes 2211848 | tf_op jit(solution)/shard_map/ppermute | solution.py:350
  4.7 7.8 %copy-start = (bf16[96,7424]{1,0:T(8,128)(2,1)S(1)}, bf16[96,7424]{1,0:T(8,128)(2,1)}, u32[]{:S(2)}) copy-start(bf16[96,7424]{1,0:T(8,128)(2,1)} %param.5) | copy-start | bytes 4276228
  4.8 17.3 %collective-permute-start.3 = (bf16[192,1024]{1,0:T(8,128)(2,1)S(1)}, bf16[192,1024]{1,0:T(8,128)(2,1)S(1)}, u32[]{:S(2)}, u32[]{:S(2)}) collective-permute-start(bf16[192,1024]{1,0:T(8,128)(2,1)S(1)} %pad_maximum_fusion.2), channel_id=1, source_target_pairs={{0,16},{1,17},{2,18},{3,19},{4,20},{5,21},{6,22},{7,23},{8,24},{9,... | collective-permute-start | bytes 1179656 | tf_op jit(solution)/shard_map/ppermute | solution.py:350
  7.7 5.1 %collective-permute-start.1 = (s32[64,128]{1,0:T(8,128)S(1)}, s32[64,128]{1,0:T(8,128)S(1)}, u32[]{:S(2)}, u32[]{:S(2)}) collective-permute-start(s32[64,128]{1,0:T(8,128)S(1)} %pad_add_fusion.2), channel_id=1, source_target_pairs={{0,4},{1,5},{2,6},{3,7},{4,0},{5,1},{6,2},{7,3},{8,12},{9,13},{10,... | collective-permute-start | bytes 98312 | tf_op jit(solution)/shard_map/ppermute | solution.py:354
  10.4 15.6 %collective-permute-start.6 = (bf16[192,896]{1,0:T(8,128)(2,1)S(1)}, bf16[192,896]{1,0:T(8,128)(2,1)}, u32[]{:S(2)}, u32[]{:S(2)}) collective-permute-start(bf16[192,896]{1,0:T(8,128)(2,1)S(1)} %pad_maximum_fusion.5), channel_id=1, source_target_pairs={{0,16},{1,17},{2,18},{3,19},{4,20},{5,21},{6,22},{7,23},{8,24},{9,... | collective-permute-start | bytes 1032200 | tf_op jit(solution)/shard_map/ppermute | solution.py:350
  11.0 17.1 %collective-permute-start.4 = (bf16[192,1024]{1,0:T(8,128)(2,1)S(1)}, bf16[192,1024]{1,0:T(8,128)(2,1)S(1)}, u32[]{:S(2)}, u32[]{:S(2)}) collective-permute-start(bf16[192,1024]{1,0:T(8,128)(2,1)S(1)} %pad_maximum_fusion.3.refs_0_), channel_id=1, source_target_pairs={{0,1},{1,0},{2,3},{3,2},{4,5},{5,4},{6,7},{7,6},{8,9},{9,8},{10,11... | collective-permute-start | bytes 1179656 | tf_op jit(solution)/shard_map/ppermute | solution.py:350
  12.6 11.0 %collective-permute-start.13 = (bf16[96,3712]{1,0:T(8,128)(2,1)S(1)}, bf16[96,3712]{1,0:T(8,128)(2,1)S(1)}, u32[]{:S(2)}, u32[]{:S(2)}) collective-permute-start(bf16[96,3712]{1,0:T(8,128)(2,1)S(1)} %constant_dynamic-slice_fusion.3), channel_id=1, source_target_pairs={{0,8},{1,9},{2,10},{3,11},{4,12},{5,13},{6,14},{7,15},{8,0},{9,1},... | collective-permute-start | bytes 2138120 | tf_op jit(solution)/shard_map/ppermute | solution.py:350
  12.8 4.4 %collective-permute-start.2 = (s32[64,256]{1,0:T(8,128)S(1)}, s32[64,256]{1,0:T(8,128)S(1)}, u32[]{:S(2)}, u32[]{:S(2)}) collective-permute-start(s32[64,256]{1,0:T(8,128)S(1)} %pad_add_fusion.1), channel_id=1, source_target_pairs={{0,2},{1,3},{2,0},{3,1},{4,6},{5,7},{6,4},{7,5},{8,10},{9,11},{10,... | collective-permute-start | bytes 196616 | tf_op jit(solution)/shard_map/ppermute | solution.py:354
  22.2 12.1 %collective-permute-start.5 = (bf16[192,1024]{1,0:T(8,128)(2,1)S(1)}, bf16[192,1024]{1,0:T(8,128)(2,1)S(1)}, u32[]{:S(2)}, u32[]{:S(2)}) collective-permute-start(bf16[192,1024]{1,0:T(8,128)(2,1)S(1)} %collective-permute-done.3.refs_1_), channel_id=1, source_target_pairs={{0,1},{1,0},{2,3},{3,2},{4,5},{5,4},{6,7},{7,6},{8,9},{9,8},{10,11... | collective-permute-start | bytes 1179656 | tf_op jit(solution)/shard_map/ppermute | solution.py:350
  25.3 28.0 %collective-permute-start.14 = (bf16[192,1920]{1,0:T(8,128)(2,1)}, bf16[192,1920]{1,0:T(8,128)(2,1)S(1)}, u32[]{:S(2)}, u32[]{:S(2)}) collective-permute-start(bf16[192,1920]{1,0:T(8,128)(2,1)} %pad_maximum_fusion.1), channel_id=1, source_target_pairs={{0,16},{1,17},{2,18},{3,19},{4,20},{5,21},{6,22},{7,23},{8,24},{9,... | collective-permute-start | bytes 2211848 | tf_op jit(solution)/shard_map/ppermute | solution.py:350
  26.0 15.7 %collective-permute-start.7 = (bf16[192,896]{1,0:T(8,128)(2,1)S(1)}, bf16[192,896]{1,0:T(8,128)(2,1)}, u32[]{:S(2)}, u32[]{:S(2)}) collective-permute-start(bf16[192,896]{1,0:T(8,128)(2,1)S(1)} %pad_maximum_fusion.4.refs_0_), channel_id=1, source_target_pairs={{0,1},{1,0},{2,3},{3,2},{4,5},{5,4},{6,7},{7,6},{8,9},{9,8},{10,11... | collective-permute-start | bytes 1032200 | tf_op jit(solution)/shard_map/ppermute | solution.py:350
  27.6 21.5 %collective-permute-start.8 = (bf16[192,896]{1,0:T(8,128)(2,1)}, bf16[192,896]{1,0:T(8,128)(2,1)}, u32[]{:S(2)}, u32[]{:S(2)}) collective-permute-start(bf16[192,896]{1,0:T(8,128)(2,1)} %collective-permute-done.6.refs_1_), channel_id=1, source_target_pairs={{0,1},{1,0},{2,3},{3,2},{4,5},{5,4},{6,7},{7,6},{8,9},{9,8},{10,11... | collective-permute-start | bytes 1032200 | tf_op jit(solution)/shard_map/ppermute | solution.py:350
  34.3 3.1 %copy-start.1 = (bf16[96,1920]{1,0:T(8,128)(2,1)S(1)}, bf16[96,1920]{1,0:T(8,128)(2,1)}, u32[]{:S(2)}) copy-start(bf16[96,1920]{1,0:T(8,128)(2,1)} %get-tuple-element.61) | copy-start | bytes 1105924
  34.3 3.1 %copy-start.2 = (bf16[96,1920]{1,0:T(8,128)(2,1)S(1)}, bf16[96,1920]{1,0:T(8,128)(2,1)}, u32[]{:S(2)}) copy-start(bf16[96,1920]{1,0:T(8,128)(2,1)} %get-tuple-element.73) | copy-start | bytes 1105924
  35.8 18.8 %collective-permute-start.9 = (s16[2080,128]{1,0:T(8,128)(2,1)S(1)}, s16[2080,128]{1,0:T(8,128)(2,1)S(1)}, u32[]{:S(2)}, u32[]{:S(2)}) collective-permute-start(s16[2080,128]{1,0:T(8,128)(2,1)S(1)} %get-tuple-element.39), channel_id=1, source_target_pairs={{0,2},{1,3},{2,0},{3,1},{4,6},{5,7},{6,4},{7,5},{8,10},{9,11},{10,... | collective-permute-start | bytes 1597448 | tf_op jit(solution)/shard_map/ppermute | solution.py:354
  37.5 39.5 %collective-permute-start.15 = (bf16[192,1920]{1,0:T(8,128)(2,1)S(1)}, bf16[192,1920]{1,0:T(8,128)(2,1)S(1)}, u32[]{:S(2)}, u32[]{:S(2)}) collective-permute-start(bf16[192,1920]{1,0:T(8,128)(2,1)S(1)} %pad_maximum_fusion.refs_0_), channel_id=1, source_target_pairs={{0,1},{1,0},{2,3},{3,2},{4,5},{5,4},{6,7},{7,6},{8,9},{9,8},{10,11... | collective-permute-start | bytes 2211848 | tf_op jit(solution)/shard_map/ppermute | solution.py:350
  51.7 15.8 %collective-permute-start.10 = (s16[1824,128]{1,0:T(8,128)(2,1)S(1)}, s16[1824,128]{1,0:T(8,128)(2,1)S(1)}, u32[]{:S(2)}, u32[]{:S(2)}) collective-permute-start(s16[1824,128]{1,0:T(8,128)(2,1)S(1)} %get-tuple-element.41), channel_id=1, source_target_pairs={{0,2},{1,3},{2,0},{3,1},{4,6},{5,7},{6,4},{7,5},{8,10},{9,11},{10,... | collective-permute-start | bytes 1400840 | tf_op jit(solution)/shard_map/ppermute | solution.py:354
  53.3 23.7 %collective-permute-start.16 = (bf16[192,1024]{1,0:T(8,128)(2,1)S(1)}, bf16[192,1024]{1,0:T(8,128)(2,1)S(1)}, u32[]{:S(2)}, u32[]{:S(2)}) collective-permute-start(bf16[192,1024]{1,0:T(8,128)(2,1)S(1)} %slice.8), channel_id=1, source_target_pairs={{0,1},{1,0},{2,3},{3,2},{4,5},{5,4},{6,7},{7,6},{8,9},{9,8},{10,11... | collective-permute-start | bytes 1179656 | tf_op jit(solution)/shard_map/ppermute | solution.py:350
  54.7 22.2 %collective-permute-start.11 = (s16[1040,128]{1,0:T(8,128)(2,1)S(1)}, s16[1040,128]{1,0:T(8,128)(2,1)S(1)}, u32[]{:S(2)}, u32[]{:S(2)}) collective-permute-start(s16[1040,128]{1,0:T(8,128)(2,1)S(1)} %combine.8), channel_id=1, source_target_pairs={{0,4},{1,5},{2,6},{3,7},{4,0},{5,1},{6,2},{7,3},{8,12},{9,13},{10,... | collective-permute-start | bytes 798728 | tf_op jit(solution)/shard_map/ppermute | solution.py:354
  67.6 9.3 %collective-permute-start.12 = (s16[912,128]{1,0:T(8,128)(2,1)S(1)}, s16[912,128]{1,0:T(8,128)(2,1)S(1)}, u32[]{:S(2)}, u32[]{:S(2)}) collective-permute-start(s16[912,128]{1,0:T(8,128)(2,1)S(1)} %combine.9), channel_id=1, source_target_pairs={{0,4},{1,5},{2,6},{3,7},{4,0},{5,1},{6,2},{7,3},{8,12},{9,13},{10,... | collective-permute-start | bytes 700424 | tf_op jit(solution)/shard_map/ppermute | solution.py:354
  67.8 11.5 %collective-permute-start.20 = (bf16[192,896]{1,0:T(8,128)(2,1)S(1)}, bf16[192,896]{1,0:T(8,128)(2,1)S(1)}, u32[]{:S(2)}, u32[]{:S(2)}) collective-permute-start(bf16[192,896]{1,0:T(8,128)(2,1)S(1)} %slice.9), channel_id=1, source_target_pairs={{0,1},{1,0},{2,3},{3,2},{4,5},{5,4},{6,7},{7,6},{8,9},{9,8},{10,11... | collective-permute-start | bytes 1032200 | tf_op jit(solution)/shard_map/ppermute | solution.py:350
  78.5 15.9 %collective-permute-start.21 = (s16[2080,128]{1,0:T(8,128)(2,1)S(1)}, s16[2080,128]{1,0:T(8,128)(2,1)S(1)}, u32[]{:S(2)}, u32[]{:S(2)}) collective-permute-start(s16[2080,128]{1,0:T(8,128)(2,1)S(1)} %get-tuple-element.53), channel_id=1, source_target_pairs={{0,2},{1,3},{2,0},{3,1},{4,6},{5,7},{6,4},{7,5},{8,10},{9,11},{10,... | collective-permute-start | bytes 1597448 | tf_op jit(solution)/shard_map/ppermute | solution.py:354
  80.5 20.3 %collective-permute-start.22 = (s16[1824,128]{1,0:T(8,128)(2,1)S(1)}, s16[1824,128]{1,0:T(8,128)(2,1)S(1)}, u32[]{:S(2)}, u32[]{:S(2)}) collective-permute-start(s16[1824,128]{1,0:T(8,128)(2,1)S(1)} %get-tuple-element.55), channel_id=1, source_target_pairs={{0,2},{1,3},{2,0},{3,1},{4,6},{5,7},{6,4},{7,5},{8,10},{9,11},{10,... | collective-permute-start | bytes 1400840 | tf_op jit(solution)/shard_map/ppermute | solution.py:354
  82.5 9.4 %collective-permute-start.18 = (s16[1040,128]{1,0:T(8,128)(2,1)S(1)}, s16[1040,128]{1,0:T(8,128)(2,1)S(1)}, u32[]{:S(2)}, u32[]{:S(2)}) collective-permute-start(s16[1040,128]{1,0:T(8,128)(2,1)S(1)} %combine.10.refs_0_), channel_id=1, source_target_pairs={{0,16},{1,17},{2,18},{3,19},{4,20},{5,21},{6,22},{7,23},{8,24},{9,... | collective-permute-start | bytes 798728 | tf_op jit(solution)/shard_map/ppermute | solution.py:350
  84.7 9.7 %collective-permute-start.24 = (s16[912,128]{1,0:T(8,128)(2,1)S(1)}, s16[912,128]{1,0:T(8,128)(2,1)S(1)}, u32[]{:S(2)}, u32[]{:S(2)}) collective-permute-start(s16[912,128]{1,0:T(8,128)(2,1)S(1)} %combine.11.refs_4_), channel_id=1, source_target_pairs={{0,16},{1,17},{2,18},{3,19},{4,20},{5,21},{6,22},{7,23},{8,24},{9,... | collective-permute-start | bytes 700424 | tf_op jit(solution)/shard_map/ppermute | solution.py:350
  84.9 20.0 %collective-permute-start.17 = (s16[1040,128]{1,0:T(8,128)(2,1)S(1)}, s16[1040,128]{1,0:T(8,128)(2,1)S(1)}, u32[]{:S(2)}, u32[]{:S(2)}) collective-permute-start(s16[1040,128]{1,0:T(8,128)(2,1)S(1)} %combine.10.refs_0_), channel_id=1, source_target_pairs={{0,8},{1,9},{2,10},{3,11},{4,12},{5,13},{6,14},{7,15},{8,0},{9,1},... | collective-permute-start | bytes 798728 | tf_op jit(solution)/shard_map/ppermute | solution.py:350
  91.9 13.1 %collective-permute-start.19 = (s16[1040,128]{1,0:T(8,128)(2,1)S(1)}, s16[1040,128]{1,0:T(8,128)(2,1)S(1)}, u32[]{:S(2)}, u32[]{:S(2)}) collective-permute-start(s16[1040,128]{1,0:T(8,128)(2,1)S(1)} %collective-permute-done.18.refs_2_), channel_id=1, source_target_pairs={{0,8},{1,9},{2,10},{3,11},{4,12},{5,13},{6,14},{7,15},{8,0},{9,1},... | collective-permute-start | bytes 798728 | tf_op jit(solution)/shard_map/ppermute | solution.py:350
  94.4 10.6 %collective-permute-start.23 = (s16[912,128]{1,0:T(8,128)(2,1)S(1)}, s16[912,128]{1,0:T(8,128)(2,1)}, u32[]{:S(2)}, u32[]{:S(2)}) collective-permute-start(s16[912,128]{1,0:T(8,128)(2,1)S(1)} %combine.11.refs_4_), channel_id=1, source_target_pairs={{0,8},{1,9},{2,10},{3,11},{4,12},{5,13},{6,14},{7,15},{8,0},{9,1},... | collective-permute-start | bytes 700424 | tf_op jit(solution)/shard_map/ppermute | solution.py:350
  94.4 10.6 %collective-permute-start.25 = (s16[912,128]{1,0:T(8,128)(2,1)S(1)}, s16[912,128]{1,0:T(8,128)(2,1)}, u32[]{:S(2)}, u32[]{:S(2)}) collective-permute-start(s16[912,128]{1,0:T(8,128)(2,1)S(1)} %collective-permute-done.24.refs_6_), channel_id=1, source_target_pairs={{0,8},{1,9},{2,10},{3,11},{4,12},{5,13},{6,14},{7,15},{8,0},{9,1},... | collective-permute-start | bytes 700424 | tf_op jit(solution)/shard_map/ppermute | solution.py:350
  100.8 20.5 %collective-permute-start.26 = (s16[1040,128]{1,0:T(8,128)(2,1)}, s16[1040,128]{1,0:T(8,128)(2,1)}, u32[]{:S(2)}, u32[]{:S(2)}) collective-permute-start(s16[1040,128]{1,0:T(8,128)(2,1)} %combine.12), channel_id=1, source_target_pairs={{0,4},{1,5},{2,6},{3,7},{4,0},{5,1},{6,2},{7,3},{8,12},{9,13},{10,... | collective-permute-start | bytes 798728 | tf_op jit(solution)/shard_map/ppermute | solution.py:354
  104.9 20.4 %collective-permute-start.30 = (s16[912,128]{1,0:T(8,128)(2,1)}, s16[912,128]{1,0:T(8,128)(2,1)}, u32[]{:S(2)}, u32[]{:S(2)}) collective-permute-start(s16[912,128]{1,0:T(8,128)(2,1)} %combine.13), channel_id=1, source_target_pairs={{0,4},{1,5},{2,6},{3,7},{4,0},{5,1},{6,2},{7,3},{8,12},{9,13},{10,... | collective-permute-start | bytes 700424 | tf_op jit(solution)/shard_map/ppermute | solution.py:354
  122.6 7.6 %collective-permute-start.28 = (s16[1040,128]{1,0:T(8,128)(2,1)S(1)}, s16[1040,128]{1,0:T(8,128)(2,1)S(1)}, u32[]{:S(2)}, u32[]{:S(2)}) collective-permute-start(s16[1040,128]{1,0:T(8,128)(2,1)S(1)} %combine.14.refs_0_), channel_id=1, source_target_pairs={{0,16},{1,17},{2,18},{3,19},{4,20},{5,21},{6,22},{7,23},{8,24},{9,... | collective-permute-start | bytes 798728 | tf_op jit(solution)/shard_map/ppermute | solution.py:350
  126.5 8.0 %collective-permute-start.32 = (s16[912,128]{1,0:T(8,128)(2,1)S(1)}, s16[912,128]{1,0:T(8,128)(2,1)S(1)}, u32[]{:S(2)}, u32[]{:S(2)}) collective-permute-start(s16[912,128]{1,0:T(8,128)(2,1)S(1)} %combine.15.refs_4_), channel_id=1, source_target_pairs={{0,16},{1,17},{2,18},{3,19},{4,20},{5,21},{6,22},{7,23},{8,24},{9,... | collective-permute-start | bytes 700424 | tf_op jit(solution)/shard_map/ppermute | solution.py:350
  128.8 5.8 %collective-permute-start.27 = (s16[1040,128]{1,0:T(8,128)(2,1)S(1)}, s16[1040,128]{1,0:T(8,128)(2,1)S(1)}, u32[]{:S(2)}, u32[]{:S(2)}) collective-permute-start(s16[1040,128]{1,0:T(8,128)(2,1)S(1)} %combine.14.refs_0_), channel_id=1, source_target_pairs={{0,8},{1,9},{2,10},{3,11},{4,12},{5,13},{6,14},{7,15},{8,0},{9,1},... | collective-permute-start | bytes 798728 | tf_op jit(solution)/shard_map/ppermute | solution.py:350
  130.2 5.8 %collective-permute-start.29 = (s16[1040,128]{1,0:T(8,128)(2,1)S(1)}, s16[1040,128]{1,0:T(8,128)(2,1)S(1)}, u32[]{:S(2)}, u32[]{:S(2)}) collective-permute-start(s16[1040,128]{1,0:T(8,128)(2,1)S(1)} %collective-permute-done.28.refs_2_), channel_id=1, source_target_pairs={{0,8},{1,9},{2,10},{3,11},{4,12},{5,13},{6,14},{7,15},{8,0},{9,1},... | collective-permute-start | bytes 798728 | tf_op jit(solution)/shard_map/ppermute | solution.py:350
  130.2 4.4 %collective-permute-start.31 = (s16[912,128]{1,0:T(8,128)(2,1)S(1)}, s16[912,128]{1,0:T(8,128)(2,1)S(1)}, u32[]{:S(2)}, u32[]{:S(2)}) collective-permute-start(s16[912,128]{1,0:T(8,128)(2,1)S(1)} %combine.15.refs_4_), channel_id=1, source_target_pairs={{0,8},{1,9},{2,10},{3,11},{4,12},{5,13},{6,14},{7,15},{8,0},{9,1},... | collective-permute-start | bytes 700424 | tf_op jit(solution)/shard_map/ppermute | solution.py:350
  134.5 1.5 %collective-permute-start.33 = (s16[912,128]{1,0:T(8,128)(2,1)S(1)}, s16[912,128]{1,0:T(8,128)(2,1)S(1)}, u32[]{:S(2)}, u32[]{:S(2)}) collective-permute-start(s16[912,128]{1,0:T(8,128)(2,1)S(1)} %collective-permute-done.32.refs_6_), channel_id=1, source_target_pairs={{0,8},{1,9},{2,10},{3,11},{4,12},{5,13},{6,14},{7,15},{8,0},{9,1},... | collective-permute-start | bytes 700424 | tf_op jit(solution)/shard_map/ppermute | solution.py:350
